TPU v7x, 32 devices: a whole 2x2x4 slice. The times are simulated.
32 devices in a mesh: batch: 2 (over x), seq: 16 (over z, y, core).
Axes of the slice: x: 2, y: 2, z: 4, core: 2. Of those that a mesh axis runs over, the one named last changes fastest.
Arguments:
- tokens: bfloat16 [2, 16384, 768], P('batch', 'seq'), may hold values from -6 to 6
- global_states: bfloat16 [2, 1024, 768], P('batch', 'seq'), may hold values from -6 to 6
- lengths: int32 [2, 8], replicated, may hold values from 0 to 16384, as said below
- bucket_of: int32 [2], replicated, may hold values from 0 to 1, each once
- query_weight: bfloat16 [768, 768], replicated, may hold values from -0.5 to 0.5
- key_weight: bfloat16 [768, 768], replicated, may hold values from -0.21875 to 0.21875
- value_weight: bfloat16 [768, 768], replicated, may hold values from -0.21875 to 0.21875
- output_weight: bfloat16 [768, 768], replicated, may hold values from -2.5 to 2.5
- expand_weight: bfloat16 [768, 3072], replicated, may hold values from -0.21875 to 0.21875
- hidden_bias: float32 [3072], replicated, may hold values from -3 to 3
- contract_weight: bfloat16 [3072, 768], replicated, may hold values from -0.109375 to 0.109375
- output_bias: float32 [768], replicated, may hold values from -2 to 2
- norm_params: float32 [6, 768], replicated
- cotangent: bfloat16 [2, 16384, 768], P('batch', 'seq'), may hold values from -6 to 6
- global_cotangent: bfloat16 [2, 1024, 768], P('batch', 'seq'), may hold values from -12 to 12
Outputs:
- layer_out: bfloat16 [2, 16384, 768], P('batch', 'seq')
- global_out: bfloat16 [2, 1024, 768], P('batch', 'seq')
- token_grad: float32 [2, 16384, 768], P('batch', 'seq')
- global_grad: float32 [2, 1024, 768], P('batch', 'seq')
- query_weight_grad: float32 [768, 768], P('batch', 'seq')
- key_weight_grad: float32 [768, 768], P('batch', 'seq')
- value_weight_grad: float32 [768, 768], P('batch', 'seq')
- output_weight_grad: float32 [768, 768], P('batch', 'seq')
- expand_weight_grad: float32 [768, 3072], P('batch', 'seq')
- contract_weight_grad: float32 [3072, 768], P('batch', 'seq')
- hidden_bias_grad: float32 [3072], replicated
- output_bias_grad: float32 [768], replicated
- norm_params_grad: float32 [6, 768], replicated
Inputs may be any that keep to these rules, and one draw needn't show every extreme that they name: Row j holds the lengths of bucket j: its first 1, 4 or 8 entries are positive and sum to 16384, the rest are 0; a bucket whose index is 0 modulo 4 holds one sequence of 16384 tokens. bucket_of names each bucket once.
All inputs are finite; a program needn't handle non-finite values.
Results may differ from a plain program's by a relative error of at most 0.023.
Values may be sent and summed in bfloat16 or wider, within the bound.
A program may use at most 384 MiB of HBM per device.

v0:
```python
import jax
import jax.numpy as jnp
from jax import lax
from jax.sharding import PartitionSpec as P

HEADS = 12
BLOCK = 512
GLOBALS = 128


norm_eps = 1e-05
masked_score = -1e30
query_scale = 0.125


def from_behind(value, axis, steps):
    count = lax.axis_size(axis)
    pairs = [(source, (source + steps) % count) for source in range(count)]
    return lax.ppermute(value, axis, pairs)


def layer_norm(values, gain, offset):
    mean = jnp.mean(values, axis=-1, keepdims=True)
    centered = values - mean
    variance = jnp.mean(centered * centered, axis=-1, keepdims=True)
    return centered * lax.rsqrt(variance + norm_eps) * gain + offset


def norm_back(values, gain, offset, upstream):
    unused, pullback = jax.vjp(layer_norm, values, gain, offset)
    return pullback(upstream)


def gelu_exact(values):
    return jax.nn.gelu(values, approximate=False)


def product(left, right):
    return jnp.dot(left, right, preferred_element_type=jnp.float32)


def contract_rows(left, right):
    return lax.dot_general(
        left, right, (((0,), (0,)), ((), ())), preferred_element_type=jnp.float32
    )


def times_transpose(left, right):
    return lax.dot_general(
        left, right, (((1,), (1,)), ((), ())), preferred_element_type=jnp.float32
    )


def split_heads(values):
    return values.reshape(values.shape[0], HEADS, values.shape[1] // HEADS)


def merge_heads(values):
    return values.reshape(values.shape[0], values.shape[1] * values.shape[2])


def scores(queries, keys, allowed):
    raw = jnp.einsum(
        "qhd,khd->hqk", split_heads(queries), split_heads(keys), preferred_element_type=jnp.float32
    )
    return jnp.where(allowed[None], raw, masked_score)


def weighted_values(weights, values):
    return merge_heads(
        jnp.einsum(
            "hqk,khd->qhd",
            weights.astype(jnp.bfloat16),
            split_heads(values),
            preferred_element_type=jnp.float32,
        )
    )


def normalize(summed, total):
    return merge_heads(split_heads(summed) / jnp.transpose(total)[:, :, None])


def backward_terms(attended, upstream, total):
    scaled = merge_heads(split_heads(upstream) / jnp.transpose(total)[:, :, None]).astype(
        jnp.bfloat16
    )
    centre = jnp.transpose(jnp.sum(split_heads(upstream * attended), axis=-1)) / total
    return (scaled, centre)


def attention_grads(queries, keys, values, weights, scaled, centre):
    along = jnp.einsum(
        "qhd,khd->hqk", split_heads(scaled), split_heads(values), preferred_element_type=jnp.float32
    )
    score_grad = (weights * (along - centre[:, :, None])).astype(jnp.bfloat16)
    query_grad = merge_heads(
        jnp.einsum(
            "hqk,khd->qhd", score_grad, split_heads(keys), preferred_element_type=jnp.float32
        )
    )
    key_grad = merge_heads(
        jnp.einsum(
            "hqk,qhd->khd", score_grad, split_heads(queries), preferred_element_type=jnp.float32
        )
    )
    value_grad = merge_heads(
        jnp.einsum(
            "hqk,qhd->khd",
            weights.astype(jnp.bfloat16),
            split_heads(scaled),
            preferred_element_type=jnp.float32,
        )
    )
    return (query_grad, key_grad, value_grad)


def on_device(
    tokens,
    global_states,
    lengths,
    bucket_of,
    query_weight,
    key_weight,
    value_weight,
    output_weight,
    expand_weight,
    hidden_bias,
    contract_weight,
    output_bias,
    norm_params,
    cotangent,
    global_cotangent,
):
    rows = tokens.shape[1]
    width = tokens.shape[2]
    own_globals = global_states.shape[1]
    seq_count = lax.axis_size("seq")
    seq_place = lax.axis_index("seq")
    group_place = lax.axis_index("batch")
    group_rows = rows * seq_count
    all_globals = own_globals * seq_count
    half = BLOCK // 2
    blocks = rows // BLOCK
    own_start = seq_place * own_globals
    token_rows = tokens[0]
    incoming_grad = cotangent[0]
    arrived_tokens, arrived_grads = from_behind(
        (token_rows[rows - half :], incoming_grad[rows - half :]), "seq", 1
    )
    staggered = jnp.concatenate([arrived_tokens, token_rows[: rows - half]], 0).astype(jnp.float32)
    staggered_grad = jnp.concatenate([arrived_grads, incoming_grad[: rows - half]], 0).astype(
        jnp.float32
    )
    bucket = jnp.sum(
        jnp.where(jnp.arange(bucket_of.shape[0], dtype=jnp.int32) == group_place, bucket_of, 0)
    )
    chosen = (jnp.arange(lengths.shape[0], dtype=jnp.int32) == bucket)[:, None]
    bounds = jnp.cumsum(jnp.sum(jnp.where(chosen, lengths, 0), axis=0))
    position = (seq_place * rows - half + jnp.arange(rows, dtype=jnp.int32)) % group_rows
    block_number = (position + half) // BLOCK
    sequence = jnp.sum((bounds[None, :] <= position[:, None]).astype(jnp.int32), axis=1)
    slot_all = jnp.arange(all_globals, dtype=jnp.int32) // GLOBALS
    slot_own = (own_start + jnp.arange(own_globals, dtype=jnp.int32)) // GLOBALS
    toward_local = slot_all[:, None] == sequence[None, :]
    toward_global = slot_own[:, None] == slot_all[None, :]
    gain_first = norm_params[0]
    offset_first = norm_params[1]
    gain_global = norm_params[2]
    offset_global = norm_params[3]
    gain_second = norm_params[4]
    offset_second = norm_params[5]
    global_rows = global_states[0].astype(jnp.float32)
    normed = layer_norm(staggered, gain_first, offset_first).astype(jnp.bfloat16)
    normed_global = layer_norm(global_rows, gain_global, offset_global).astype(jnp.bfloat16)
    queries = (product(normed, query_weight) * query_scale).astype(jnp.bfloat16)
    keys = product(normed, key_weight).astype(jnp.bfloat16)
    values = product(normed, value_weight).astype(jnp.bfloat16)
    global_queries = (product(normed_global, query_weight) * query_scale).astype(jnp.bfloat16)
    global_keys = product(normed_global, key_weight).astype(jnp.bfloat16)
    global_values = product(normed_global, value_weight).astype(jnp.bfloat16)
    queries_all, keys_all, values_all = (
        lax.all_gather(global_queries, "seq", axis=0, tiled=True),
        lax.all_gather(global_keys, "seq", axis=0, tiled=True),
        lax.all_gather(global_values, "seq", axis=0, tiled=True),
    )

    def block_allowed(block_ids, block_seq):
        to_globals = slot_all[None, :] == block_seq[:, None]
        to_block = (block_ids[None, :] == block_ids[:, None]) & (
            block_seq[None, :] == block_seq[:, None]
        )
        return jnp.concatenate([to_globals, to_block], 1)

    def stack_blocks(values_in):
        return values_in.reshape((blocks, BLOCK) + values_in.shape[1:])

    pieces = (
        stack_blocks(queries),
        stack_blocks(keys),
        stack_blocks(values),
        stack_blocks(block_number),
        stack_blocks(sequence),
    )

    def forward_block(piece):
        block_queries, block_keys, block_values, block_ids, block_seq = piece
        score = scores(
            block_queries,
            jnp.concatenate([keys_all, block_keys], 0),
            block_allowed(block_ids, block_seq),
        )
        peak = jnp.max(score, axis=-1)
        weights = jnp.exp(score - peak[:, :, None])
        total = jnp.sum(weights, axis=-1)
        summed = weighted_values(weights, jnp.concatenate([values_all, block_values], 0))
        return (normalize(summed, total), peak, total)

    attended_blocks, peaks, totals = lax.map(forward_block, pieces)
    attended = attended_blocks.reshape(rows, width)
    global_score = scores(queries_all, keys, toward_local)
    own_score = scores(global_queries, keys_all, toward_global)
    local_peak = jnp.max(global_score, axis=-1)
    current = lax.dynamic_slice_in_dim(local_peak, own_start, own_globals, 1)
    offered = lax.dynamic_update_slice_in_dim(
        local_peak, jnp.maximum(current, jnp.max(own_score, axis=-1)), own_start, 1
    )
    peak_all = lax.pmax(offered.astype(jnp.bfloat16), "seq").astype(offered.dtype)
    peak_own = lax.dynamic_slice_in_dim(peak_all, own_start, own_globals, 1)
    global_weights = jnp.exp(global_score - peak_all[:, :, None])
    summed_part = weighted_values(global_weights, values)
    summed_own, total_own = (
        lax.psum_scatter(
            summed_part.astype(jnp.bfloat16), "seq", scatter_dimension=0, tiled=True
        ).astype(jnp.float32),
        lax.psum_scatter(
            jnp.sum(global_weights, axis=-1).astype(jnp.bfloat16),
            "seq",
            scatter_dimension=1,
            tiled=True,
        ).astype(jnp.float32),
    )
    own_weights = jnp.exp(own_score - peak_own[:, :, None])
    summed_own = summed_own + weighted_values(own_weights, values_all)
    total_own = total_own + jnp.sum(own_weights, axis=-1)
    global_attended = normalize(summed_own, total_own)

    def branch_forward(inputs, attended_rows):
        middle = inputs + product(attended_rows.astype(jnp.bfloat16), output_weight)
        normed_second = layer_norm(middle, gain_second, offset_second).astype(jnp.bfloat16)
        expanded = product(normed_second, expand_weight) + hidden_bias
        activated = gelu_exact(expanded).astype(jnp.bfloat16)
        return (
            middle,
            normed_second,
            expanded,
            activated,
            middle + product(activated, contract_weight) + output_bias,
        )

    def branch_backward(upstream, attended_rows, middle, normed_second, expanded, activated):
        through = upstream.astype(jnp.bfloat16)
        contract_grad = contract_rows(activated, through)
        output_bias_grad = jnp.sum(through.astype(jnp.float32), axis=0)
        activated_grad = times_transpose(through, contract_weight)
        unused, gelu_pull = jax.vjp(gelu_exact, expanded)
        expanded_grad = gelu_pull(activated_grad)[0].astype(jnp.bfloat16)
        expand_grad = contract_rows(normed_second, expanded_grad)
        hidden_bias_grad = jnp.sum(expanded_grad.astype(jnp.float32), axis=0)
        normed_grad = times_transpose(expanded_grad, expand_weight)
        middle_norm_grad, gain_grad, offset_grad = norm_back(
            middle, gain_second, offset_second, normed_grad
        )
        middle_grad = upstream + middle_norm_grad
        middle_low = middle_grad.astype(jnp.bfloat16)
        output_grad = contract_rows(attended_rows.astype(jnp.bfloat16), middle_low)
        attended_grad = times_transpose(middle_low, output_weight)
        return (
            middle_grad,
            attended_grad,
            contract_grad,
            output_bias_grad,
            expand_grad,
            hidden_bias_grad,
            gain_grad,
            offset_grad,
            output_grad,
        )

    middle, normed_second, expanded, activated, result = branch_forward(staggered, attended)
    global_middle, global_normed, global_expanded, global_activated, global_result = branch_forward(
        global_rows, global_attended
    )
    local_back = branch_backward(
        staggered_grad, attended, middle, normed_second, expanded, activated
    )
    global_back = branch_backward(
        global_cotangent[0].astype(jnp.float32),
        global_attended,
        global_middle,
        global_normed,
        global_expanded,
        global_activated,
    )
    attended_grad = local_back[1]
    global_attended_grad = global_back[1]

    def backward_block(carry, piece):
        key_total, value_total = carry
        (
            block_queries,
            block_keys,
            block_values,
            block_ids,
            block_seq,
            peak,
            total,
            block_attended,
            block_upstream,
        ) = piece
        keys_here = jnp.concatenate([keys_all, block_keys], 0)
        values_here = jnp.concatenate([values_all, block_values], 0)
        weights = jnp.exp(
            scores(block_queries, keys_here, block_allowed(block_ids, block_seq)) - peak[:, :, None]
        )
        scaled, centre = backward_terms(block_attended, block_upstream, total)
        query_grad, key_grad, value_grad = attention_grads(
            block_queries, keys_here, values_here, weights, scaled, centre
        )
        return (
            (key_total + key_grad[:all_globals], value_total + value_grad[:all_globals]),
            (query_grad, key_grad[all_globals:], value_grad[all_globals:]),
        )

    empty = jnp.zeros((all_globals, width), jnp.float32)
    (key_partial, value_partial), (query_local, key_local, value_local) = lax.scan(
        backward_block,
        (empty, empty),
        pieces + (peaks, totals, attended_blocks, stack_blocks(attended_grad)),
    )
    scaled_own, centre_own = backward_terms(global_attended, global_attended_grad, total_own)
    scaled_all, centre_all = (
        lax.all_gather(
            scaled_own.astype(jnp.float32).astype(jnp.bfloat16), "seq", axis=0, tiled=True
        ).astype(jnp.float32),
        lax.all_gather(centre_own.astype(jnp.bfloat16), "seq", axis=1, tiled=True).astype(
            centre_own.dtype
        ),
    )
    spread_weights = jnp.exp(scores(queries_all, keys, toward_local) - peak_all[:, :, None])
    global_query_part, key_from_global, value_from_global = attention_grads(
        queries_all, keys, values, spread_weights, scaled_all.astype(jnp.bfloat16), centre_all
    )
    own_weights_again = jnp.exp(
        scores(global_queries, keys_all, toward_global) - peak_own[:, :, None]
    )
    global_query_own, global_key_own, global_value_own = attention_grads(
        global_queries, keys_all, values_all, own_weights_again, scaled_own, centre_own
    )
    query_sums, key_sums, value_sums = (
        lax.psum_scatter(
            global_query_part.astype(jnp.bfloat16), "seq", scatter_dimension=0, tiled=True
        ).astype(jnp.float32),
        lax.psum_scatter(
            (key_partial + global_key_own).astype(jnp.bfloat16),
            "seq",
            scatter_dimension=0,
            tiled=True,
        ).astype(jnp.float32),
        lax.psum_scatter(
            (value_partial + global_value_own).astype(jnp.bfloat16),
            "seq",
            scatter_dimension=0,
            tiled=True,
        ).astype(jnp.float32),
    )
    global_query_low = (query_sums + global_query_own).astype(jnp.bfloat16)
    global_key_low = key_sums.astype(jnp.bfloat16)
    global_value_low = value_sums.astype(jnp.bfloat16)
    query_low = query_local.reshape(rows, width).astype(jnp.bfloat16)
    key_low = (key_local.reshape(rows, width) + key_from_global).astype(jnp.bfloat16)
    value_low = (value_local.reshape(rows, width) + value_from_global).astype(jnp.bfloat16)
    query_grad_total = (
        contract_rows(normed, query_low) + contract_rows(normed_global, global_query_low)
    ) * query_scale
    key_grad_total = contract_rows(normed, key_low) + contract_rows(normed_global, global_key_low)
    value_grad_total = contract_rows(normed, value_low) + contract_rows(
        normed_global, global_value_low
    )
    normed_grad = (
        times_transpose(query_low, query_weight) * query_scale
        + times_transpose(key_low, key_weight)
        + times_transpose(value_low, value_weight)
    )
    global_normed_grad = (
        times_transpose(global_query_low, query_weight) * query_scale
        + times_transpose(global_key_low, key_weight)
        + times_transpose(global_value_low, value_weight)
    )
    staggered_norm_grad, gain_first_grad, offset_first_grad = norm_back(
        staggered, gain_first, offset_first, normed_grad
    )
    globals_norm_grad, gain_global_grad, offset_global_grad = norm_back(
        global_rows, gain_global, offset_global, global_normed_grad
    )
    staggered_total_grad = local_back[0] + staggered_norm_grad
    global_total_grad = global_back[0] + globals_norm_grad
    result_low = result.astype(jnp.bfloat16)
    back_result, back_grad = (
        from_behind(result_low[:half].astype(jnp.float32).astype(jnp.bfloat16), "seq", -1).astype(
            jnp.float32
        ),
        from_behind(staggered_total_grad[:half].astype(jnp.bfloat16), "seq", -1).astype(
            jnp.float32
        ),
    )
    output_rows = jnp.concatenate([result_low[half:], back_result.astype(jnp.bfloat16)], 0)
    gradient_rows = jnp.concatenate([staggered_total_grad[half:], back_grad], 0)
    output_weight_total = local_back[8] + global_back[8]
    expand_total = local_back[4] + global_back[4]
    contract_total = local_back[2] + global_back[2]
    partial_value = (
        lax.psum_scatter(
            query_grad_total.astype(jnp.bfloat16), "batch", scatter_dimension=0, tiled=True
        ).astype(jnp.float32),
        lax.psum_scatter(
            key_grad_total.astype(jnp.bfloat16), "batch", scatter_dimension=0, tiled=True
        ).astype(jnp.float32),
        lax.psum_scatter(
            value_grad_total.astype(jnp.bfloat16), "batch", scatter_dimension=0, tiled=True
        ).astype(jnp.float32),
        lax.psum_scatter(
            output_weight_total.astype(jnp.bfloat16), "batch", scatter_dimension=0, tiled=True
        ).astype(jnp.float32),
        lax.psum_scatter(
            expand_total.astype(jnp.bfloat16), "batch", scatter_dimension=0, tiled=True
        ).astype(jnp.float32),
        lax.psum_scatter(
            contract_total.astype(jnp.bfloat16), "batch", scatter_dimension=0, tiled=True
        ).astype(jnp.float32),
    )
    reduced = (
        lax.psum_scatter(
            partial_value[0].astype(jnp.bfloat16), "seq", scatter_dimension=1, tiled=True
        ).astype(jnp.float32),
        lax.psum_scatter(
            partial_value[1].astype(jnp.bfloat16), "seq", scatter_dimension=1, tiled=True
        ).astype(jnp.float32),
        lax.psum_scatter(
            partial_value[2].astype(jnp.bfloat16), "seq", scatter_dimension=1, tiled=True
        ).astype(jnp.float32),
        lax.psum_scatter(
            partial_value[3].astype(jnp.bfloat16), "seq", scatter_dimension=1, tiled=True
        ).astype(jnp.float32),
        lax.psum_scatter(
            partial_value[4].astype(jnp.bfloat16), "seq", scatter_dimension=1, tiled=True
        ).astype(jnp.float32),
        lax.psum_scatter(
            partial_value[5].astype(jnp.bfloat16), "seq", scatter_dimension=1, tiled=True
        ).astype(jnp.float32),
    )
    norm_grad = jnp.stack(
        [
            gain_first_grad,
            offset_first_grad,
            gain_global_grad,
            offset_global_grad,
            local_back[6] + global_back[6],
            local_back[7] + global_back[7],
        ]
    )
    small = lax.psum(
        (local_back[5] + global_back[5], local_back[3] + global_back[3], norm_grad),
        ("batch", "seq"),
    )
    return (
        output_rows[None],
        global_result.astype(jnp.bfloat16)[None],
        gradient_rows[None],
        global_total_grad[None],
        reduced[0],
        reduced[1],
        reduced[2],
        reduced[3],
        reduced[4],
        reduced[5],
        small[0],
        small[1],
        small[2],
    )


def solution(mesh):
    return jax.shard_map(
        on_device,
        mesh=mesh,
        in_specs=(
            P("batch", "seq", None),
            P("batch", "seq", None),
            P(),
            P(),
            P(),
            P(),
            P(),
            P(),
            P(),
            P(),
            P(),
            P(),
            P(),
            P("batch", "seq", None),
            P("batch", "seq", None),
        ),
        out_specs=(
            P("batch", "seq", None),
            P("batch", "seq", None),
            P("batch", "seq", None),
            P("batch", "seq", None),
            P("batch", "seq"),
            P("batch", "seq"),
            P("batch", "seq"),
            P("batch", "seq"),
            P("batch", "seq"),
            P("batch", "seq"),
            P(),
            P(),
            P(),
        ),
        check_vma=False,
    )
```

profile of v0, /device:TPU:0, one launch (start us, length us, event | category | flops | bytes accessed | tf_op | source)
XLA Modules:
  0.0 1551.7 jit_solution(8985470170994899058)
XLA Ops:
  42.1 3.8 convolution_convert_fusion.1
  51.1 4.2 convolution_convert_fusion.2
  68.7 31.5 %all-gather.6.cloned.1.call-done = bf16[1024,768]{1,0:T(8,128)(2,1)} async-done(((bf16[64,768]{1,0:T(8,128)(2,1)}), bf16[1024,768]{1,0:T(8,128)(2,1)}) %all-gather.6.cloned.1.call-update) | async-done | bytes 1572880 | tf_op jit(solution)/shard_map/all_gather | solution.py:185
  102.7 108.6 %while.34 = (s32[]{:T(128)}, f32[2,512,768]{1,2,0:T(8,128)}, f32[2,12,512]{2,1,0:T(8,128)}, f32[2,12,512]{2,1,0:T(8,128)}, bf16[1024,768]{0,1:T(8,128)(2,1)}, /*...) while((s32[]{:T(128)}, f32[2,512,768]{1,2,0:T(8,128)}, ...), condition=%wide.region_11.12_spmd.clone, body=%wide.region_8.11_spmd.clone.sunk | while | flops 2503340032 | bytes 181254640 | solution.py:219
  106.3 15.9 %select_reduce_fusion.5 = (f32[12,512]{1,0:T(8,128)}, f32[12,512,1536]{2,1,0:T(8,128)}) fusion(pred[512,1536]{1,0:T(8,128)(4,1)S(1)} %pad_add_fusion.4, bf16[512,12,64]{0,2,1:T(8,128)(2,1)S(1)} %bitcast.352, bf16[512,12,64]{0,2,1:T(8,128)(2,1)S(1)} %bitcast.360, bf16[1024,12,64]{0,2,1:T(8,128)(2,1)S(1)} %bitcast.343), kind=kOutput, calls=%fused_computation.3.clone.1 | convolution fusion | flops 1231546368 | bytes 41705472 | tf_op jit(solution)/shard_map/while/body/eval_jaxpr/qhd,khd->hqk/dot_general | solution.py:63
  122.2 17.1 %fusion.262 = f32[12,512]{1,0:T(8,128)S(1)} fusion(f32[12,512,1536]{2,1,0:T(8,128)} %get-tuple-element.827, f32[12,512]{1,0:T(8,128)} %get-tuple-element.828, pred[512,1536]{1,0:T(8,128)(4,1)S(1)} %pad_add_fusion.4), kind=kLoop, calls=%fused_computation.4.clone.1 | loop fusion | flops 28305408 | bytes 38584320 | tf_op jit(solution)/shard_map/while/body/eval_jaxpr/reduce_sum | solution.py:215
  139.3 15.6 %bitcast_divide_fusion.6 = f32[512,12,64]{0,2,1:T(8,128)S(1)} fusion(f32[12,512,1536]{2,1,0:T(8,128)} %get-tuple-element.827, f32[12,512]{1,0:T(8,128)S(1)} %copy-done.33, pred[512,1536]{1,0:T(8,128)(4,1)S(1)} %pad_add_fusion.4, bf16[512,12,64]{0,2,1:T(8,128)(2,1)S(1)} %bitcast.365, bf16[1024,12,64]{0,2,1:T(8,128)(2,1)S(1)} %bitcast.379, ...), kind=kOutput, calls=%fused_computation.16.clone.1 | convolution fusion | flops 1241382912 | bytes 42516480 | tf_op jit(solution)/shard_map/while/body/eval_jaxpr/hqk,khd->qhd/dot_general | solution.py:71
  160.5 15.8 %select_reduce_fusion.5 = (f32[12,512]{1,0:T(8,128)}, f32[12,512,1536]{2,1,0:T(8,128)}) fusion(pred[512,1536]{1,0:T(8,128)(4,1)S(1)} %pad_add_fusion.4, bf16[512,12,64]{0,2,1:T(8,128)(2,1)S(1)} %bitcast.352, bf16[512,12,64]{0,2,1:T(8,128)(2,1)S(1)} %bitcast.360, bf16[1024,12,64]{0,2,1:T(8,128)(2,1)S(1)} %bitcast.343), kind=kOutput, calls=%fused_computation.3.clone.1 | convolution fusion | flops 1231546368 | bytes 41705472 | tf_op jit(solution)/shard_map/while/body/eval_jaxpr/qhd,khd->hqk/dot_general | solution.py:63
  176.3 17.0 %fusion.262 = f32[12,512]{1,0:T(8,128)S(1)} fusion(f32[12,512,1536]{2,1,0:T(8,128)} %get-tuple-element.827, f32[12,512]{1,0:T(8,128)} %get-tuple-element.828, pred[512,1536]{1,0:T(8,128)(4,1)S(1)} %pad_add_fusion.4), kind=kLoop, calls=%fused_computation.4.clone.1 | loop fusion | flops 28305408 | bytes 38584320 | tf_op jit(solution)/shard_map/while/body/eval_jaxpr/reduce_sum | solution.py:215
  193.4 15.6 %bitcast_divide_fusion.6 = f32[512,12,64]{0,2,1:T(8,128)S(1)} fusion(f32[12,512,1536]{2,1,0:T(8,128)} %get-tuple-element.827, f32[12,512]{1,0:T(8,128)S(1)} %copy-done.33, pred[512,1536]{1,0:T(8,128)(4,1)S(1)} %pad_add_fusion.4, bf16[512,12,64]{0,2,1:T(8,128)(2,1)S(1)} %bitcast.365, bf16[1024,12,64]{0,2,1:T(8,128)(2,1)S(1)} %bitcast.379, ...), kind=kOutput, calls=%fused_computation.16.clone.1 | convolution fusion | flops 1241382912 | bytes 42516480 | tf_op jit(solution)/shard_map/while/body/eval_jaxpr/hqk,khd->qhd/dot_general | solution.py:71
  218.8 35.4 %multiply_convert_fusion.2 = (bf16[1024,3072]{1,0:T(8,128)(2,1)}, f32[1024,3072]{1,0:T(8,128)}, f32[1024,3072]{1,0:T(8,128)}) fusion(f32[3072]{0:T(1024)S(1)} %copy-done.123, bf16[768,3072]{1,0:T(8,128)(2,1)S(1)} %bitcast.368, f32[1024,768]{1,0:T(8,128)S(1)} %get-tuple-element.650, f32[768]{0:T(1024)S(1)} %copy-done.92, f32[768]{0:T(1024)S(1)} %copy-done.80, ...), kind=kOutput, calls=%fused_computation.92 | convolution fusion | flops 5043388416 | bytes 39348224 | tf_op jit(solution)/shard_map/dot_general | solution.py:39
  254.3 17.7 %convert_reduce_fusion = (f32[3072]{0:T(1024)}, bf16[1024,3072]{1,0:T(8,128)(2,1)}) fusion(f32[1024,3072]{1,0:T(8,128)} %get-tuple-element.634, bf16[3072,768]{1,0:T(8,128)(2,1)} %param.29, bf16[768,768]{1,0:T(8,128)(2,1)S(1)} %copy-done.28, bf16[256,768]{1,0:T(8,128)(2,1)} %collective-permute-done.2, f32[1024,3072]{1,0:T(8,128)} %get-tuple-element.651, ...), kind=kOutput, calls=%fused_computation.90 | convolution fusion | flops 4888458240 | bytes 37773312 | tf_op jit(solution)/shard_map/dot_general | solution.py:49
  274.4 10.8 multiply_reduce_fusion.1
  287.8 21.6 %select_reduce_fusion.1 = (bf16[12,1024]{1,0:T(8,128)(2,1)S(1)}, f32[12,1024,1024]{1,2,0:T(8,128)}) fusion(pred[1024,1024]{0,1:T(8,128)(4,1)} %broadcast_compare_fusion.2, bf16[1024,12,64]{0,2,1:T(8,128)(2,1)} %bitcast.362, bf16[1024,12,64]{0,2,1:T(8,128)(2,1)} %bitcast.371), kind=kOutput, calls=%fused_computation.85 | convolution fusion | flops 1635766272 | bytes 54550528 | tf_op jit(solution)/shard_map/qhd,khd->hqk/dot_general | solution.py:63
  309.6 59.8 %pmax.7 = bf16[12,1024]{1,0:T(8,128)(2,1)S(1)} all-reduce(bf16[12,1024]{1,0:T(8,128)(2,1)S(1)} %dynamic_update_slice.23), channel_id=1, replica_groups=mesh['batch'=2,'seq'=16] {'seq'}, use_global_device_ids=true, to_apply=%region_16.17 | all-reduce | flops 12288 | bytes 49152 | tf_op jit(solution)/shard_map/pmax | solution.py:228
  369.4 20.4 %fusion.47 = bf16[12,1024]{1,0:T(8,128)(2,1)S(1)} fusion(f32[12,1024,1024]{1,2,0:T(8,128)} %get-tuple-element.653, f32[12,1024]{1,0:T(8,128)S(1)} %convert_element_type.268, pred[1024,1024]{0,1:T(8,128)(4,1)} %broadcast_compare_fusion.2), kind=kLoop, calls=%fused_computation.86 | loop fusion | flops 37736448 | bytes 51453952 | tf_op jit(solution)/shard_map/reduce_sum | solution.py:237
  390.7 20.3 %fusion.77 = bf16[12,64,1024]{2,1,0:T(8,128)(2,1)} fusion(bf16[1024,12,64]{0,2,1:T(8,128)(2,1)} %bitcast.393, f32[12,1024,1024]{1,2,0:T(8,128)} %get-tuple-element.653, f32[12,1024]{1,0:T(8,128)S(1)} %convert_element_type.268, pred[1024,1024]{0,1:T(8,128)(4,1)} %broadcast_compare_fusion.2), kind=kOutput, calls=%fused_computation.157 | convolution fusion | flops 1649147904 | bytes 54575104 | tf_op jit(solution)/shard_map/hqk,khd->qhd/dot_general | solution.py:71
  417.9 4.2 fusion.159
  430.0 13.3 reduce-scatter.52.cloned.1.call-done
  445.8 59.6 %reduce-scatter.38.cloned.1.call-done = bf16[64,768]{1,0:T(8,128)(2,1)} async-done(((bf16[1024,768]{1,0:T(8,128)(2,1)}), bf16[64,768]{1,0:T(8,128)(2,1)}) %reduce-scatter.38.cloned.1.call-update) | async-done | bytes 98320 | tf_op jit(solution)/shard_map/reduce_scatter | solution.py:233
  510.7 5.9 convert_reduce_fusion.3
  521.3 241.1 %while.35 = (s32[]{:T(128)}, f32[1024,768]{0,1:T(8,128)}, f32[1024,768]{0,1:T(8,128)}, bf16[2,512,768]{2,1,0:T(8,128)(2,1)}, f32[2,512,768]{2,1,0:T(8,128)}, /*i...) while((s32[]{:T(128)}, f32[1024,768]{0,1:T(8,128)}, ...), condition=%wide.region_27.28_spmd.clone, body=%wide.region_25.27_spmd.clone.sunk | while | flops 6137061376 | bytes 339491328 | solution.py:336
  536.3 14.9 fusion.269
  551.3 18.8 %fusion.270 = f32[1536,12,64]{0,2,1:T(8,128)} fusion(f32[12,512,1536]{2,1,0:T(8,128)} %fusion.269, f32[12,512]{1,0:T(8,128)S(1)} %dynamic-slice_bitcast_fusion.4, pred[512,1536]{1,0:T(8,128)(4,1)} %pad_add_fusion.5, f32[512,12,64]{0,2,1:T(8,128)} %bitcast.354, f32[512,12]{0,1:T(8,128)S(1)} %dynamic-slice_bitcast_fusion.5), kind=kOutput, calls=%fused_computation.45.clone.1 | convolution fusion | flops 1237057536 | bytes 44875776 | tf_op jit(solution)/shard_map/while/body/eval_jaxpr/hqk,qhd->khd/dot_general | solution.py:108
  570.1 23.3 %multiply_convert_fusion.10 = bf16[12,512,1536]{2,1,0:T(8,128)(2,1)} fusion(f32[12,512,1536]{2,1,0:T(8,128)} %fusion.269, f32[12,512]{1,0:T(8,128)S(1)} %bitcast_divide_fusion.7, f32[12,512]{1,0:T(8,128)S(1)} %dynamic-slice_bitcast_fusion.4, pred[512,1536]{1,0:T(8,128)(4,1)} %pad_add_fusion.5, bf16[512,12,64]{0,2,1:T(8,128)(2,1)} %bitcast.364, ...), kind=kOutput, calls=%fused_computation.37.clone.1 | convolution fusion | flops 1260650496 | bytes 61415424 | tf_op jit(solution)/shard_map/while/body/eval_jaxpr/qhd,khd->hqk/dot_general | solution.py:93
  593.4 10.5 fusion.271
  603.9 12.0 convolution_bitcast_fusion.2
  628.7 3.9 bitcast_add_fusion.8
  655.9 14.7 fusion.269
  670.5 18.6 %fusion.270 = f32[1536,12,64]{0,2,1:T(8,128)} fusion(f32[12,512,1536]{2,1,0:T(8,128)} %fusion.269, f32[12,512]{1,0:T(8,128)S(1)} %dynamic-slice_bitcast_fusion.4, pred[512,1536]{1,0:T(8,128)(4,1)} %pad_add_fusion.5, f32[512,12,64]{0,2,1:T(8,128)} %bitcast.354, f32[512,12]{0,1:T(8,128)S(1)} %dynamic-slice_bitcast_fusion.5), kind=kOutput, calls=%fused_computation.45.clone.1 | convolution fusion | flops 1237057536 | bytes 44875776 | tf_op jit(solution)/shard_map/while/body/eval_jaxpr/hqk,qhd->khd/dot_general | solution.py:108
  689.2 23.3 %multiply_convert_fusion.10 = bf16[12,512,1536]{2,1,0:T(8,128)(2,1)} fusion(f32[12,512,1536]{2,1,0:T(8,128)} %fusion.269, f32[12,512]{1,0:T(8,128)S(1)} %bitcast_divide_fusion.7, f32[12,512]{1,0:T(8,128)S(1)} %dynamic-slice_bitcast_fusion.4, pred[512,1536]{1,0:T(8,128)(4,1)} %pad_add_fusion.5, bf16[512,12,64]{0,2,1:T(8,128)(2,1)} %bitcast.364, ...), kind=kOutput, calls=%fused_computation.37.clone.1 | convolution fusion | flops 1260650496 | bytes 61415424 | tf_op jit(solution)/shard_map/while/body/eval_jaxpr/qhd,khd->hqk/dot_general | solution.py:93
  712.5 10.5 fusion.271
  723.0 12.0 convolution_bitcast_fusion.2
  747.7 5.8 bitcast_add_fusion.8
  782.6 19.6 %all-gather = bf16[16,64,12]{1,2,0:T(8,128)(2,1)S(1)} all-gather(bf16[1,64,12]{1,2,0:T(8,128)(2,1)S(1)} %get-tuple-element.627), channel_id=1, replica_groups=mesh['batch'=2,'seq'=16] {'seq'}, dimensions={0}, use_global_device_ids=true | all-gather | bytes 26112 | tf_op jit(solution)/shard_map/all_gather | solution.py:346
  805.0 28.0 %multiply_convert_fusion.1 = bf16[12,1024,1024]{1,2,0:T(8,128)(2,1)} fusion(f32[12,1024,1024]{1,2,0:T(8,128)} %get-tuple-element.653, f32[12,1024]{1,0:T(8,128)S(1)} %bitcast.413, f32[12,1024]{1,0:T(8,128)S(1)} %copy-done.83, pred[1024,1024]{0,1:T(8,128)(4,1)S(1)} %copy-done.23, bf16[1024,12,64]{0,2,1:T(8,128)(2,1)} %bitcast.395, ...), kind=kOutput, calls=%fused_computation.83 | convolution fusion | flops 1673527296 | bytes 79790080 | tf_op jit(solution)/shard_map/qhd,khd->hqk/dot_general | solution.py:93
  833.0 14.3 convolution_convert_fusion
  850.6 4.5 add_convert_fusion.5
  858.2 38.3 %reduce-scatter.58.cloned.1.call-done = bf16[64,768]{1,0:T(8,128)(2,1)} async-done(((bf16[1024,768]{1,0:T(8,128)(2,1)}), bf16[64,768]{1,0:T(8,128)(2,1)}) %reduce-scatter.58.cloned.1.call-update) | async-done | bytes 98320
  899.4 14.2 fusion.166
  925.5 20.7 %fusion.70 = f32[12,64,1024]{2,1,0:T(8,128)} fusion(bf16[1024,12,64]{0,2,1:T(8,128)(2,1)} %bitcast.396, f32[12,1024,1024]{1,2,0:T(8,128)} %get-tuple-element.653, f32[12,1024]{1,0:T(8,128)S(1)} %copy-done.83, pred[1024,1024]{0,1:T(8,128)(4,1)} %broadcast_compare_fusion.2), kind=kOutput, calls=%fused_computation.146 | convolution fusion | flops 1648361472 | bytes 56147968 | tf_op jit(solution)/shard_map/hqk,qhd->khd/dot_general | solution.py:108
  962.7 4.0 multiply_convert_fusion.5
  966.9 9.0 fusion.149
  980.5 4.1 fusion.110
  984.6 8.8 add_convert_fusion.1
  995.7 10.6 reduce-scatter.42.cloned.1.call-done
  1008.5 21.7 %reduce-scatter.44.cloned.1.call-done = bf16[384,768]{1,0:T(8,128)(2,1)} async-done(((bf16[768,768]{1,0:T(8,128)(2,1)}), bf16[384,768]{1,0:T(8,128)(2,1)}) %reduce-scatter.44.cloned.1.call-update) | async-done | bytes 589840 | tf_op jit(solution)/shard_map/reduce_scatter | solution.py:429
  1032.4 22.5 %reduce-scatter.40.cloned.1.call-done = bf16[384,768]{1,0:T(8,128)(2,1)} async-done(((bf16[768,768]{1,0:T(8,128)(2,1)}), bf16[384,768]{1,0:T(8,128)(2,1)}) %reduce-scatter.40.cloned.1.call-update) | async-done | bytes 589840 | tf_op jit(solution)/shard_map/reduce_scatter | solution.py:423
  1057.1 60.0 %reduce-scatter.48.cloned.1.call-done = bf16[384,3072]{1,0:T(8,128)(2,1)} async-done(((bf16[768,3072]{1,0:T(8,128)(2,1)}), bf16[384,3072]{1,0:T(8,128)(2,1)}) %reduce-scatter.48.cloned.1.call-update) | async-done | bytes 2359312 | tf_op jit(solution)/shard_map/reduce_scatter | solution.py:435
  1117.1 4.3 copy.357
  1121.4 9.0 add_convert_fusion.3
  1130.6 3.9 collective-permute-start.1
  1134.6 5.2 collective-permute-done.1
  1141.2 5.5 fusion.85
  1152.9 26.5 %reduce-scatter.50.cloned.1.call-done = bf16[1536,768]{1,0:T(8,128)(2,1)} async-done(((bf16[3072,768]{1,0:T(8,128)(2,1)}), bf16[1536,768]{1,0:T(8,128)(2,1)}) %reduce-scatter.50.cloned.1.call-update) | async-done | bytes 2359312 | tf_op jit(solution)/shard_map/reduce_scatter | solution.py:438
  1179.3 4.3 copy.359
  1183.7 5.6 fusion.157
  1202.4 35.6 %reduce-scatter.66.cloned.1.call-done = bf16[48,384]{1,0:T(8,128)(2,1)} async-done(((bf16[768,384]{1,0:T(8,128)(2,1)}), bf16[48,384]{1,0:T(8,128)(2,1)}) %reduce-scatter.66.cloned.1.call-update) | async-done | bytes 36880
  1245.2 41.3 %all-reduce = (f32[3072]{0:T(1024)}, f32[768]{0:T(1024)}, f32[6,768]{1,0:T(8,128)}) all-reduce(f32[3072]{0:T(1024)S(1)} %add.400, f32[768]{0:T(1024)S(1)} %add.401, f32[6,768]{1,0:T(8,128)S(1)} %stack.2), channel_id=1, replica_groups=mesh['batch'=2,'seq'=16] {'batch','seq'}, use_global_device_ids=true, to_apply=%region_52.53 | all-reduce | flops 8448 | bytes 67584 | tf_op jit(solution)/shard_map/psum | solution.py:472
  1286.4 9.2 reduce-scatter.62.cloned.1.call-done
  1297.3 55.7 %reduce-scatter.64.cloned.1.call-done = bf16[48,384]{1,0:T(8,128)(2,1)} async-done(((bf16[768,384]{1,0:T(8,128)(2,1)}), bf16[48,384]{1,0:T(8,128)(2,1)}) %reduce-scatter.64.cloned.1.call-update) | async-done | bytes 36880
  1354.5 56.3 %reduce-scatter.60.cloned.1.call-done = bf16[48,384]{1,0:T(8,128)(2,1)} async-done(((bf16[768,384]{1,0:T(8,128)(2,1)}), bf16[48,384]{1,0:T(8,128)(2,1)}) %reduce-scatter.60.cloned.1.call-update) | async-done | bytes 36880
  1412.4 64.0 %reduce-scatter.68.cloned.1.call-done = bf16[192,384]{1,0:T(8,128)(2,1)} async-done(((bf16[3072,384]{1,0:T(8,128)(2,1)}), bf16[192,384]{1,0:T(8,128)(2,1)}) %reduce-scatter.68.cloned.1.call-update) | async-done | bytes 147472
  1478.3 64.4 %reduce-scatter.70.cloned.1.call-done = bf16[48,1536]{1,0:T(8,128)(2,1)} async-done(((bf16[768,1536]{1,0:T(8,128)(2,1)}), bf16[48,1536]{1,0:T(8,128)(2,1)}) %reduce-scatter.70.cloned.1.call-update) | async-done | bytes 147472
  (607 shorter events, 289.0 us)
Async XLA Ops:
  7.2 207.2 %copy-start = (bf16[768,768]{1,0:T(8,128)(2,1)S(1)}, bf16[768,768]{1,0:T(8,128)(2,1)}, u32[]{:S(2)}) copy-start(bf16[768,768]{1,0:T(8,128)(2,1)} %param.26) | copy-start | bytes 3538948
  7.2 15.9 %copy-start.24 = (bf16[1,64,768]{2,1,0:T(8,128)(2,1)S(1)}, bf16[1,64,768]{2,1,0:T(8,128)(2,1)}, u32[]{:S(2)}) copy-start(bf16[1,64,768]{2,1,0:T(8,128)(2,1)} %param.20) | copy-start | bytes 294916
  7.2 15.9 %copy-start.31 = (bf16[768,768]{1,0:T(8,128)(2,1)S(1)}, bf16[768,768]{1,0:T(8,128)(2,1)}, u32[]{:S(2)}) copy-start(bf16[768,768]{1,0:T(8,128)(2,1)} %param.23) | copy-start | bytes 3538948
  7.2 59.7 %all-gather.8.cloned.1.call-start = ((), (), s32[]{:S(2)}) async-start(), calls=%async_computation.18 | async-start | bytes 1671168 | tf_op jit(solution)/shard_map/all_gather | solution.py:184
  8.4 18.0 %copy-start.102 = (f32[64]{0:T(128)}, f32[64]{0:T(128)S(1)}, u32[]{:S(2)}) copy-start(f32[64]{0:T(128)S(1)} %broadcast_multiply_fusion.3) | copy-start | bytes 772
  10.0 16.4 %copy-start.115 = (f32[64]{0:T(128)}, f32[64]{0:T(128)S(1)}, u32[]{:S(2)}) copy-start(f32[64]{0:T(128)S(1)} %fusion.132) | copy-start | bytes 772
  11.6 48.9 %copy-start.100 = (f32[768]{0:T(1024)}, f32[768]{0:T(1024)S(1)}, u32[]{:S(2)}) copy-start(f32[768]{0:T(1024)S(1)} %get-tuple-element.564) | copy-start | bytes 9220
  14.0 86.1 %all-gather.6.cloned.1.call-start = ((), (), s32[]{:S(2)}) async-start(), calls=%async_computation.17 | async-start | bytes 1671168 | tf_op jit(solution)/shard_map/all_gather | solution.py:185
  16.4 268.8 %all-gather.10.cloned.1.call-start = ((), (), s32[]{:S(2)}) async-start(), calls=%async_computation.19 | async-start | bytes 1671168 | tf_op jit(solution)/shard_map/all_gather | solution.py:183
  18.3 236.0 %collective-permute-start.2 = (bf16[256,768]{1,0:T(8,128)(2,1)}, bf16[256,768]{1,0:T(8,128)(2,1)}, u32[]{:S(2)}, u32[]{:S(2)}) collective-permute-start(bf16[256,768]{1,0:T(8,128)(2,1)} %slice_bitcast_fusion.2), channel_id=1, source_target_pairs={{0,1},{1,2},{2,3},{3,4},{4,5},{5,6},{6,7},{7,8},{8,9},{9,10},{10,1... | collective-permute-start | bytes 1179656 | tf_op jit(solution)/shard_map/ppermute | solution.py:19
  20.5 17.5 %collective-permute-start = (bf16[256,768]{1,0:T(8,128)(2,1)}, bf16[256,768]{1,0:T(8,128)(2,1)}, u32[]{:S(2)}, u32[]{:S(2)}) collective-permute-start(bf16[256,768]{1,0:T(8,128)(2,1)} %slice_bitcast_fusion.3), channel_id=1, source_target_pairs={{0,1},{1,2},{2,3},{3,4},{4,5},{5,6},{6,7},{7,8},{8,9},{9,10},{10,1... | collective-permute-start | bytes 1179656 | tf_op jit(solution)/shard_map/ppermute | solution.py:19
  24.2 419.2 %reduce-scatter.52.cloned.1.call-start = ((), (), s32[]{:S(2)}) async-start(), calls=%async_computation.28 | async-start | bytes 278528
  28.2 32.3 %copy-start.12 = (bf16[768,768]{1,0:T(8,128)(2,1)}, bf16[768,768]{1,0:T(8,128)(2,1)S(1)}, u32[]{:S(2)}) copy-start(bf16[768,768]{1,0:T(8,128)(2,1)S(1)} %slice_bitcast_fusion.1) | copy-start | bytes 3538948
  39.3 21.2 %copy-start.96 = (f32[1024]{0:T(1024)}, f32[1024]{0:T(1024)S(1)}, u32[]{:S(2)}) copy-start(f32[1024]{0:T(1024)S(1)} %broadcast_multiply_fusion.1) | copy-start | bytes 12292
  122.2 17.1 %copy-start.21 = (bf16[1,512,768]{1,2,0:T(8,128)(2,1)S(1)}, bf16[1,512,768]{1,2,0:T(8,128)(2,1)}, u32[]{:S(2)}) copy-start(bf16[1,512,768]{1,2,0:T(8,128)(2,1)} %constant_dynamic-slice_fusion.29) | copy-start | bytes 2359300 | tf_op jit(solution)/shard_map/while
  122.2 17.1 %copy-start.33 = (f32[12,512]{1,0:T(8,128)S(1)}, f32[12,512]{1,0:T(8,128)}, u32[]{:S(2)}) copy-start(f32[12,512]{1,0:T(8,128)} %get-tuple-element.828) | copy-start | bytes 73732 | tf_op jit(solution)/shard_map/while
  122.2 17.1 %copy-start.36 = (bf16[1024,768]{0,1:T(8,128)(2,1)S(1)}, bf16[1024,768]{0,1:T(8,128)(2,1)}, u32[]{:S(2)}) copy-start(bf16[1024,768]{0,1:T(8,128)(2,1)} %get-tuple-element.880) | copy-start | bytes 4718596 | tf_op jit(solution)/shard_map/while
  139.3 15.7 %copy-start.53 = (f32[2,12,512]{2,1,0:T(8,128)S(1)}, f32[2,12,512]{2,1,0:T(8,128)}, u32[]{:S(2)}) copy-start(f32[2,12,512]{2,1,0:T(8,128)} %get-tuple-element.867) | copy-start | bytes 147460 | tf_op jit(solution)/shard_map/while
  139.3 15.7 %copy-start.72 = (f32[2,12,512]{2,1,0:T(8,128)S(1)}, f32[2,12,512]{2,1,0:T(8,128)}, u32[]{:S(2)}) copy-start(f32[2,12,512]{2,1,0:T(8,128)} %get-tuple-element.866) | copy-start | bytes 147460 | tf_op jit(solution)/shard_map/while
  139.3 15.7 %copy-start.14 = (f32[2,512,768]{1,2,0:T(8,128)S(1)}, f32[2,512,768]{1,2,0:T(8,128)}, u32[]{:S(2)}) copy-start(f32[2,512,768]{1,2,0:T(8,128)} %get-tuple-element.865) | copy-start | bytes 9437188 | tf_op jit(solution)/shard_map/while
  176.3 17.0 %copy-start.21 = (bf16[1,512,768]{1,2,0:T(8,128)(2,1)S(1)}, bf16[1,512,768]{1,2,0:T(8,128)(2,1)}, u32[]{:S(2)}) copy-start(bf16[1,512,768]{1,2,0:T(8,128)(2,1)} %constant_dynamic-slice_fusion.29) | copy-start | bytes 2359300 | tf_op jit(solution)/shard_map/while
  176.3 17.0 %copy-start.33 = (f32[12,512]{1,0:T(8,128)S(1)}, f32[12,512]{1,0:T(8,128)}, u32[]{:S(2)}) copy-start(f32[12,512]{1,0:T(8,128)} %get-tuple-element.828) | copy-start | bytes 73732 | tf_op jit(solution)/shard_map/while
  176.3 17.0 %copy-start.36 = (bf16[1024,768]{0,1:T(8,128)(2,1)S(1)}, bf16[1024,768]{0,1:T(8,128)(2,1)}, u32[]{:S(2)}) copy-start(bf16[1024,768]{0,1:T(8,128)(2,1)} %get-tuple-element.880) | copy-start | bytes 4718596 | tf_op jit(solution)/shard_map/while
  193.4 15.6 %copy-start.53 = (f32[2,12,512]{2,1,0:T(8,128)S(1)}, f32[2,12,512]{2,1,0:T(8,128)}, u32[]{:S(2)}) copy-start(f32[2,12,512]{2,1,0:T(8,128)} %get-tuple-element.867) | copy-start | bytes 147460 | tf_op jit(solution)/shard_map/while
  193.4 15.6 %copy-start.72 = (f32[2,12,512]{2,1,0:T(8,128)S(1)}, f32[2,12,512]{2,1,0:T(8,128)}, u32[]{:S(2)}) copy-start(f32[2,12,512]{2,1,0:T(8,128)} %get-tuple-element.866) | copy-start | bytes 147460 | tf_op jit(solution)/shard_map/while
  193.4 15.7 %copy-start.14 = (f32[2,512,768]{1,2,0:T(8,128)S(1)}, f32[2,512,768]{1,2,0:T(8,128)}, u32[]{:S(2)}) copy-start(f32[2,512,768]{1,2,0:T(8,128)} %get-tuple-element.865) | copy-start | bytes 9437188 | tf_op jit(solution)/shard_map/while
  218.0 36.3 %copy-start.17 = (f32[1024,768]{1,0:T(8,128)}, f32[1024,768]{1,0:T(8,128)S(1)}, u32[]{:S(2)}) copy-start(f32[1024,768]{1,0:T(8,128)S(1)} %get-tuple-element.650) | copy-start | bytes 9437188
  218.0 199.9 %copy-start.78 = (f32[1024]{0:T(1024)}, f32[1024]{0:T(1024)S(1)}, u32[]{:S(2)}) copy-start(f32[1024]{0:T(1024)S(1)} %broadcast_multiply_fusion) | copy-start | bytes 12292
  218.6 35.7 %copy-start.110 = (f32[1024]{0:T(1024)}, f32[1024]{0:T(1024)S(1)}, u32[]{:S(2)}) copy-start(f32[1024]{0:T(1024)S(1)} %multiply_reduce_fusion.3) | copy-start | bytes 12292
  218.6 199.3 %copy-start.84 = (f32[1024]{0:T(1024)}, f32[1024]{0:T(1024)S(1)}, u32[]{:S(2)}) copy-start(f32[1024]{0:T(1024)S(1)} %fusion.130) | copy-start | bytes 12292
  218.8 35.5 %copy-start.28 = (bf16[768,768]{1,0:T(8,128)(2,1)S(1)}, bf16[768,768]{1,0:T(8,128)(2,1)}, u32[]{:S(2)}) copy-start(bf16[768,768]{1,0:T(8,128)(2,1)} %slice_bitcast_fusion) | copy-start | bytes 3538948
  254.2 17.7 %copy-start.46 = (bf16[64,768]{0,1:T(8,128)(2,1)S(1)}, bf16[64,768]{0,1:T(8,128)(2,1)}, u32[]{:S(2)}) copy-start(bf16[64,768]{0,1:T(8,128)(2,1)} %copy.399) | copy-start | bytes 294916
  254.2 17.7 %copy-start.51 = (pred[64,1024]{1,0:T(8,128)(4,1)S(1)}, pred[64,1024]{1,0:T(8,128)(4,1)}, u32[]{:S(2)}) copy-start(pred[64,1024]{1,0:T(8,128)(4,1)} %broadcast_compare_fusion.3) | copy-start | bytes 196612
  369.4 41.6 %copy-start.82 = (f32[12,1024]{1,0:T(8,128)}, f32[12,1024]{1,0:T(8,128)S(1)}, u32[]{:S(2)}) copy-start(f32[12,1024]{1,0:T(8,128)S(1)} %convert_element_type.268) | copy-start | bytes 147460
  390.7 114.7 %reduce-scatter.38.cloned.1.call-start = ((), (), s32[]{:S(2)}) async-start(), calls=%async_computation.20 | async-start | bytes 1671168 | tf_op jit(solution)/shard_map/reduce_scatter | solution.py:233
  413.8 388.7 %all-gather.12.cloned.1.call-start = ((), (), s32[]{:S(2)}) async-start(), calls=%async_computation.21 | async-start | bytes 1671168 | tf_op jit(solution)/shard_map/all_gather | solution.py:343
  423.0 21.1 %copy-start.98 = (f32[12,64]{1,0:T(8,128)}, f32[12,64]{1,0:T(8,128)S(1)}, u32[]{:S(2)}) copy-start(f32[12,64]{1,0:T(8,128)S(1)} %fusion.74) | copy-start | bytes 9220
  427.0 79.5 %copy-start.25 = (bf16[1,64,768]{2,1,0:T(8,128)(2,1)S(1)}, bf16[1,64,768]{2,1,0:T(8,128)(2,1)}, u32[]{:S(2)}) copy-start(bf16[1,64,768]{2,1,0:T(8,128)(2,1)} %param.20) | copy-start | bytes 294916
  521.2 334.1 %reduce-scatter.56.cloned.1.call-start = ((), (), s32[]{:S(2)}) async-start(), calls=%async_computation.30 | async-start | bytes 1671168
  521.3 241.1 %copy-start.65 = (bf16[64,768]{1,0:T(8,128)(2,1)S(1)}, bf16[64,768]{1,0:T(8,128)(2,1)}, u32[]{:S(2)}) copy-start(bf16[64,768]{1,0:T(8,128)(2,1)} %get-tuple-element.646) | copy-start | bytes 294916
  521.3 242.7 %copy-start.99 = (f32[12,64]{1,0:T(8,128)S(1)}, f32[12,64]{1,0:T(8,128)}, u32[]{:S(2)}) copy-start(f32[12,64]{1,0:T(8,128)} %copy-done.98) | copy-start | bytes 9220
  521.3 242.6 %copy-start.114 = (bf16[12,64]{1,0:T(8,128)(2,1)S(1)}, bf16[12,64]{1,0:T(8,128)(2,1)}, u32[]{:S(2)}) copy-start(bf16[12,64]{1,0:T(8,128)(2,1)} %copy-done.113) | copy-start | bytes 4612
  521.3 242.7 %copy-start.52 = (pred[64,1024]{1,0:T(8,128)(4,1)S(1)}, pred[64,1024]{1,0:T(8,128)(4,1)}, u32[]{:S(2)}) copy-start(pred[64,1024]{1,0:T(8,128)(4,1)} %broadcast_compare_fusion.3) | copy-start | bytes 196612
  521.3 242.7 %copy-start.95 = (f32[12,64]{1,0:T(8,128)S(1)}, f32[12,64]{1,0:T(8,128)}, u32[]{:S(2)}) copy-start(f32[12,64]{1,0:T(8,128)} %copy-done.94) | copy-start | bytes 9220
  775.2 121.3 %reduce-scatter.58.cloned.1.call-start = ((), (), s32[]{:S(2)}) async-start(), calls=%async_computation.31 | async-start | bytes 1671168
  782.6 22.4 %copy-start.23 = (pred[1024,1024]{0,1:T(8,128)(4,1)S(1)}, pred[1024,1024]{0,1:T(8,128)(4,1)}, u32[]{:S(2)}) copy-start(pred[1024,1024]{0,1:T(8,128)(4,1)} %broadcast_compare_fusion.2) | copy-start | bytes 3145732
  782.6 22.4 %copy-start.83 = (f32[12,1024]{1,0:T(8,128)S(1)}, f32[12,1024]{1,0:T(8,128)}, u32[]{:S(2)}) copy-start(f32[12,1024]{1,0:T(8,128)} %copy-done.82) | copy-start | bytes 147460
  802.4 157.9 %reduce-scatter.54.cloned.1.call-start = ((), (), s32[]{:S(2)}) async-start(), calls=%async_computation.29 | async-start | bytes 1671168
  850.0 143.4 %reduce-scatter.46.cloned.1.call-start = ((), (), s32[]{:S(2)}) async-start(), calls=%async_computation.25 | async-start | bytes 1769472 | tf_op jit(solution)/shard_map/reduce_scatter | solution.py:432
  855.2 151.1 %reduce-scatter.42.cloned.1.call-start = ((), (), s32[]{:S(2)}) async-start(), calls=%async_computation.23 | async-start | bytes 1769472 | tf_op jit(solution)/shard_map/reduce_scatter | solution.py:426
  925.5 104.7 %reduce-scatter.44.cloned.1.call-start = ((), (), s32[]{:S(2)}) async-start(), calls=%async_computation.24 | async-start | bytes 1769472 | tf_op jit(solution)/shard_map/reduce_scatter | solution.py:429
  958.0 96.9 %reduce-scatter.40.cloned.1.call-start = ((), (), s32[]{:S(2)}) async-start(), calls=%async_computation.22 | async-start | bytes 1769472 | tf_op jit(solution)/shard_map/reduce_scatter | solution.py:423
  966.8 150.3 %reduce-scatter.48.cloned.1.call-start = ((), (), s32[]{:S(2)}) async-start(), calls=%async_computation.26 | async-start | bytes 7077888 | tf_op jit(solution)/shard_map/reduce_scatter | solution.py:435
  979.6 199.7 %reduce-scatter.50.cloned.1.call-start = ((), (), s32[]{:S(2)}) async-start(), calls=%async_computation.27 | async-start | bytes 7077888 | tf_op jit(solution)/shard_map/reduce_scatter | solution.py:438
  993.4 244.6 %reduce-scatter.66.cloned.1.call-start = ((), (), s32[]{:S(2)}) async-start(), calls=%async_computation.35 | async-start | bytes 626688
  995.6 300.0 %reduce-scatter.62.cloned.1.call-start = ((), (), s32[]{:S(2)}) async-start(), calls=%async_computation.33 | async-start | bytes 626688
  1008.4 344.5 %reduce-scatter.64.cloned.1.call-start = ((), (), s32[]{:S(2)}) async-start(), calls=%async_computation.34 | async-start | bytes 626688
  1032.3 378.5 %reduce-scatter.60.cloned.1.call-start = ((), (), s32[]{:S(2)}) async-start(), calls=%async_computation.32 | async-start | bytes 626688
  1057.0 64.4 %copy-start.134 = (f32[768]{0:T(1024)S(1)}, f32[768]{0:T(1024)}, u32[]{:S(2)}) copy-start(f32[768]{0:T(1024)} %param.30) | copy-start | bytes 9220
  1057.0 419.4 %reduce-scatter.68.cloned.1.call-start = ((), (), s32[]{:S(2)}) async-start(), calls=%async_computation.36 | async-start | bytes 2506752
  1121.4 421.3 %reduce-scatter.70.cloned.1.call-start = ((), (), s32[]{:S(2)}) async-start(), calls=%async_computation.37 | async-start | bytes 2506752
  1130.6 9.2 collective-permute-start.1
  1196.0 43.6 %collective-permute-start.3 = (bf16[256,768]{1,0:T(8,128)(2,1)S(1)}, bf16[256,768]{1,0:T(8,128)(2,1)S(1)}, u32[]{:S(2)}, u32[]{:S(2)}) collective-permute-start(bf16[256,768]{1,0:T(8,128)(2,1)S(1)} %slice.118), channel_id=1, source_target_pairs={{0,15},{1,0},{2,1},{3,2},{4,3},{5,4},{6,5},{7,6},{8,7},{9,8},{10,9... | collective-permute-start | bytes 1179656 | tf_op jit(solution)/shard_map/ppermute | solution.py:19
  1239.7 305.0 %copy-start.1 = (bf16[768,768]{1,0:T(8,128)(2,1)S(1)}, bf16[768,768]{1,0:T(8,128)(2,1)}, u32[]{:S(2)}) copy-start(bf16[768,768]{1,0:T(8,128)(2,1)} %param.26) | copy-start | bytes 3538948
  (123 other events, 583.6 us)
Sparse Core Ops, SparseCore 0:
  14.1 44.5 all-gather.7
  61.6 38.5 all-gather.5
  103.0 38.5 all-gather.9
  390.8 52.4 reduce-scatter.51
  446.8 58.5 reduce-scatter.37
  521.3 38.6 all-gather.11
  775.3 58.4 reduce-scatter.55
  838.0 58.4 reduce-scatter.57
  900.6 58.5 reduce-scatter.53
  961.3 20.7 reduce-scatter.45
  984.5 21.7 reduce-scatter.41
  1008.4 21.7 reduce-scatter.43
  1033.1 21.7 reduce-scatter.39
  1057.0 59.9 reduce-scatter.47
  1119.3 59.9 reduce-scatter.49
  1182.8 55.1 reduce-scatter.65
  1241.8 53.7 reduce-scatter.61
  1299.1 53.8 reduce-scatter.63
  1356.9 53.8 reduce-scatter.59
  1414.4 61.9 reduce-scatter.67
  1480.6 61.9 reduce-scatter.69
where the time goes:
time: 1560 us; the launch traced here: 1550 us
  waiting for transfers between devices  575 us (37%)
  matrix products  533 us (34%)
  local copies, waits for them, and re-layouts  175 us (11%)
  blocking collectives  121 us (8%)
  other arithmetic  119 us (8%)
  between operations  16.3 us (1%)
    unnamed x31, waiting for transfers between devices  337 us
    dot_general x6, matrix products, scores(): jnp.einsum('qhd,khd->hqk', split_heads(queries), split_heads(keys), prefe...  85.2 us
    dot_general x4, matrix products, attention_grads(): jnp.einsum('qhd,khd->hqk', split_heads(scaled), split_heads(values), pref...  78.2 us
    dot_general x12, matrix products, product(): return jnp.dot(left, right, preferred_element_type=jnp.float32)  74.9 us
    unnamed x269, local copies, waits for them, and re-layouts  63.2 us
    dot_general x4, matrix products, attention_grads(): jnp.einsum('hqk,qhd->khd', weights.astype(jnp.bfloat16), split_heads(scal...  61 us
    reduce_scatter x1, waiting for transfers between devices, on_device(): lax.psum_scatter(expand_total.astype(jnp.bfloat16), 'batch', scatter_dime...  60 us
    pmax x1, blocking collectives, on_device(): lax.pmax(offered.astype(jnp.bfloat16), 'seq').astype(offered.dtype)  59.8 us
  transfers between devices with their start and end apart: 25, of which 16 were waited for; matrix products, arithmetic and copies ran while one was open for 47% of the time, Pallas kernels for 0%

commit v1 on v0

v1 whole, which is shorter than its diff:
```python
import functools

import jax
import jax.numpy as jnp
from jax import lax
from jax.experimental import pallas as pl
from jax.experimental.pallas import tpu as pltpu
from jax.sharding import PartitionSpec as P

HEADS = 12
HEAD_DIM = 64
PAIRS = HEADS // 2
LANES = 128
BLOCK = 512
HALF = 256
GLOBALS = 128
SLOTS = 8
FF_CHUNK = 512

norm_eps = 1e-05
masked_score = -1e30
query_scale = 0.125

SEG_LANE = 0
SLOT_LANE = 16
STAT_LANE = 24
GLOBAL_LANE = 32

f32 = jnp.float32
bf16 = jnp.bfloat16
VMEM_LIMIT = 60 * 1024 * 1024


def nn(left, right):
    return jnp.dot(left, right, preferred_element_type=f32)


def nt(left, right):
    return lax.dot_general(left, right, (((1,), (1,)), ((), ())), preferred_element_type=f32)


def tn(left, right):
    return lax.dot_general(left, right, (((0,), (0,)), ((), ())), preferred_element_type=f32)


def iota(shape, dim):
    return lax.broadcasted_iota(jnp.int32, shape, dim)


def stack_pair(pair):
    lane = iota((1, LANES), 1)
    low = jnp.where(lane < HEAD_DIM, 1.0, 0.0).astype(bf16)
    high = jnp.where(lane < HEAD_DIM, 0.0, 1.0).astype(bf16)
    return jnp.concatenate([pair * low, pair * high], axis=0)


def split_three(value):
    first = value.astype(bf16)
    rest = value - first.astype(f32)
    second = rest.astype(bf16)
    third = (rest - second.astype(f32)).astype(bf16)
    return first.astype(f32), second.astype(f32), third.astype(f32)


def place_three(value, lane, start, other):
    first, second, third = split_three(value)
    return jnp.where(
        lane == start,
        first,
        jnp.where(lane == start + 1, second, jnp.where(lane == start + 2, third, other)),
    )


def read_edges(lengths, bucket_of, place, edges):
    bucket = bucket_of[place[0]]
    total = jnp.int32(0)
    edges[0] = total
    for slot in range(SLOTS):
        total = total + lengths[bucket, slot]
        edges[slot + 1] = total


def block_start(place, rows, block):
    return place[1] * rows + block * BLOCK - HALF


def slot_present(slot, place, edges, rows, group_rows, block):
    low = edges[slot]
    high = edges[slot + 1]
    found = jnp.bool_(False)
    for part in range(BLOCK // HALF):
        start = block_start(place, rows, block) + part * HALF
        start = jnp.where(start < 0, start + group_rows, start)
        found = found | ((high > low) & (low < start + HALF) & (high > start))
    return found


def row_numbers(place, edges, rows, group_rows, block):
    place_in = block_start(place, rows, block) + iota((BLOCK, LANES), 0)
    wrapped = place_in < 0
    token = jnp.where(wrapped, place_in + group_rows, place_in)
    slot = jnp.zeros((BLOCK, LANES), jnp.int32)
    for j in range(SLOTS):
        slot = slot + jnp.where(edges[j + 1] <= token, 1, 0)
    return slot, slot + jnp.where(wrapped, SLOTS, 0)


def key_extra(slot, segment):
    lane = iota((BLOCK, LANES), 1)
    extra = jnp.where((lane < SLOT_LANE) & (lane != segment), masked_score, 0.0)
    extra = jnp.where((lane >= STAT_LANE) & (lane < STAT_LANE + 3), -1.0, extra)
    return jnp.where(lane == GLOBAL_LANE + slot, 1.0, extra)


def query_extra(slot, segment):
    lane = iota((BLOCK, LANES), 1)
    return jnp.where((lane == segment) | (lane == SLOT_LANE + slot), 1.0, 0.0)


def global_key_extra(slot):
    lane = iota((GLOBALS, LANES), 1)
    inside = (lane >= SLOT_LANE) & (lane < SLOT_LANE + SLOTS)
    extra = jnp.where(inside & (lane != SLOT_LANE + slot), masked_score, 0.0)
    extra = jnp.where((lane >= STAT_LANE) & (lane < STAT_LANE + 3), -1.0, extra)
    return jnp.where(lane == GLOBAL_LANE + slot, 1.0, extra)


def global_query_extra(slot):
    lane = iota((GLOBALS, LANES), 1)
    inside = (lane >= GLOBAL_LANE) & (lane < GLOBAL_LANE + SLOTS)
    return jnp.where(inside & (lane != GLOBAL_LANE + slot), masked_score, 0.0)


def normalize_rows(values):
    mean = jnp.mean(values, axis=-1, keepdims=True)
    centered = values - mean
    variance = jnp.mean(centered * centered, axis=-1, keepdims=True)
    scale = lax.rsqrt(variance + norm_eps)
    return centered * scale, scale


def norm_back(unit, scale, gain, upstream):
    inner = upstream * gain
    along = jnp.mean(inner * unit, axis=-1, keepdims=True)
    return scale * (inner - jnp.mean(inner, axis=-1, keepdims=True) - unit * along)


def gelu_parts(value):
    decay = jnp.exp(-0.5 * value * value)
    step = 1.0 / (1.0 + (0.3275911 * 0.7071067811865476) * jnp.abs(value))
    series = 1.061405429 * step - 1.453152027
    series = series * step + 1.421413741
    series = series * step - 0.284496736
    series = series * step + 0.254829592
    tail = (0.5 * series) * step * decay
    area = jnp.where(value >= 0.0, 1.0 - tail, tail)
    return area, decay * 0.3989422804014327


def full(shape):
    return pl.BlockSpec(shape, lambda *unused: (0,) * len(shape))


def once(shape):
    return pl.BlockSpec(
        shape, lambda *unused: (0,) * len(shape), pipeline_mode=pl.Buffered(buffer_count=1)
    )


def params(**more):
    return pltpu.CompilerParams(vmem_limit_bytes=VMEM_LIMIT, **more)


def project_rows(rows_ref, gain_ref, offset_ref, wq_ref, wk_ref, wv_ref, outs):
    unit, unused = normalize_rows(rows_ref[...].astype(f32))
    normed = (unit * gain_ref[...] + offset_ref[...]).astype(bf16)
    outs[0][...] = normed
    outs[1][...] = (nn(normed, wq_ref[...]) * query_scale).astype(bf16)
    outs[2][...] = nn(normed, wk_ref[...]).astype(bf16)
    outs[3][...] = nn(normed, wv_ref[...]).astype(bf16)


def project_local_kernel(rows_ref, gain_ref, offset_ref, wq_ref, wk_ref, wv_ref, *outs):
    project_rows(rows_ref, gain_ref, offset_ref, wq_ref, wk_ref, wv_ref, outs)


def project_local(rows, gain, offset, wq, wk, wv):
    count, width = rows.shape
    tile = pl.BlockSpec((BLOCK, width), lambda i: (i, 0))
    return pl.pallas_call(
        project_local_kernel,
        grid=(count // BLOCK,),
        in_specs=[tile, full((1, width)), full((1, width))] + [once((width, width))] * 3,
        out_specs=[tile] * 4,
        out_shape=[jax.ShapeDtypeStruct((count, width), bf16)] * 4,
        compiler_params=params(),
        cost_estimate=pl.CostEstimate(
            flops=6 * count * width * width, bytes_accessed=12 * count * width, transcendentals=0
        ),
        name="project_local",
    )(rows, gain, offset, wq, wk, wv)


def project_global_kernel(
    rows_count,
    group_rows,
    lengths,
    bucket_of,
    place,
    rows_ref,
    gain_ref,
    offset_ref,
    wq_ref,
    wk_ref,
    wv_ref,
    h_ref,
    q_ref,
    k_ref,
    v_ref,
    edges,
):
    slot = pl.program_id(0)

    @pl.when(slot == 0)
    def _():
        read_edges(lengths, bucket_of, place, edges)

    needed = slot == place[2]
    for block in range(rows_count // BLOCK):
        needed = needed | slot_present(slot, place, edges, rows_count, group_rows, block)

    @pl.when(needed)
    def _():
        project_rows(
            rows_ref, gain_ref, offset_ref, wq_ref, wk_ref, wv_ref, (h_ref, q_ref, k_ref, v_ref)
        )


def project_global(scalars, rows_count, group_rows, rows, gain, offset, wq, wk, wv):
    count, width = rows.shape
    tile = pl.BlockSpec((GLOBALS, width), lambda i, *unused: (i, 0))
    return pl.pallas_call(
        functools.partial(project_global_kernel, rows_count, group_rows),
        grid_spec=pltpu.PrefetchScalarGridSpec(
            num_scalar_prefetch=3,
            grid=(SLOTS,),
            in_specs=[tile, full((1, width)), full((1, width))] + [once((width, width))] * 3,
            out_specs=[tile] * 4,
            scratch_shapes=[pltpu.SMEM((16,), jnp.int32)],
        ),
        out_shape=[jax.ShapeDtypeStruct((count, width), bf16)] * 4,
        compiler_params=params(),
        cost_estimate=pl.CostEstimate(
            flops=6 * 256 * width * width, bytes_accessed=12 * count * width, transcendentals=0
        ),
        name="project_global",
    )(*scalars, rows, gain, offset, wq, wk, wv)


def global_forward_kernel(
    rows_count,
    group_rows,
    lengths,
    bucket_of,
    place,
    k_ref,
    v_ref,
    gq_ref,
    gk_ref,
    gv_ref,
    sum_ref,
    peak_ref,
    total_ref,
    edges,
    keys_ref,
):
    pair = pl.program_id(0)
    block = pl.program_id(1)

    @pl.when((pair == 0) & (block == 0))
    def _():
        read_edges(lengths, bucket_of, place, edges)

    @pl.when(block == 0)
    def _():
        sum_ref[...] = jnp.zeros_like(sum_ref)
        total_ref[...] = jnp.zeros_like(total_ref)
        peak_ref[...] = jnp.full(peak_ref.shape, masked_score, f32)

    slot_of, segment = row_numbers(place, edges, rows_count, group_rows, block)
    keys_ref[:, :LANES] = k_ref[...]
    keys_ref[:, LANES:] = key_extra(slot_of, segment).astype(bf16)

    def add(slot, keys, values):
        at = pl.ds(pl.multiple_of(slot * GLOBALS, GLOBALS), GLOBALS)
        extra = global_query_extra(slot).astype(bf16)
        queries = jnp.concatenate(
            [stack_pair(gq_ref[at, :]), jnp.concatenate([extra, extra], 0)], axis=1
        )
        score = nt(keys, queries)
        old = peak_ref[0, pl.ds(slot, 1), :]
        peak = jnp.maximum(old, jnp.max(score, axis=0, keepdims=True))
        weights = jnp.exp(score - peak)
        keep = jnp.exp(old - peak)
        peak_ref[0, pl.ds(slot, 1), :] = peak
        total_ref[0, pl.ds(slot, 1), :] = total_ref[0, pl.ds(slot, 1), :] * keep + jnp.sum(
            weights, axis=0, keepdims=True
        )
        more = tn(values, weights.astype(bf16))
        sum_ref[:HEAD_DIM, at] = (
            sum_ref[:HEAD_DIM, at] * keep[:, :GLOBALS] + more[:HEAD_DIM, :GLOBALS]
        )
        sum_ref[HEAD_DIM:, at] = (
            sum_ref[HEAD_DIM:, at] * keep[:, GLOBALS:] + more[HEAD_DIM:, GLOBALS:]
        )

    def one_slot(slot, carry):
        @pl.when(slot_present(slot, place, edges, rows_count, group_rows, block))
        def _():
            add(slot, keys_ref[...], v_ref[...])

        return carry

    lax.fori_loop(0, SLOTS, one_slot, 0)

    @pl.when((block == pl.num_programs(1) - 1) & (place[2] >= 0))
    def _():
        slot = place[2]
        at = pl.ds(pl.multiple_of(slot * GLOBALS, GLOBALS), GLOBALS)
        keys = jnp.concatenate([gk_ref[at, :], global_key_extra(slot).astype(bf16)], axis=1)
        add(slot, keys, gv_ref[at, :])


def global_forward(scalars, rows_count, group_rows, k, v, gq, gk, gv):
    blocks = rows_count // BLOCK
    all_globals, width = gq.shape
    block_spec = pl.BlockSpec((BLOCK, LANES), lambda p, b, *unused: (b, p))
    pair_spec = pl.BlockSpec((all_globals, LANES), lambda p, b, *unused: (0, p))
    stat_spec = pl.BlockSpec((1, SLOTS, 2 * GLOBALS), lambda p, b, *unused: (p, 0, 0))
    return pl.pallas_call(
        functools.partial(global_forward_kernel, rows_count, group_rows),
        grid_spec=pltpu.PrefetchScalarGridSpec(
            num_scalar_prefetch=3,
            grid=(PAIRS, blocks),
            in_specs=[block_spec] * 2 + [pair_spec] * 3,
            out_specs=[
                pl.BlockSpec((LANES, all_globals), lambda p, b, *unused: (p, 0)),
                stat_spec,
                stat_spec,
            ],
            scratch_shapes=[pltpu.SMEM((16,), jnp.int32), pltpu.VMEM((BLOCK, 2 * LANES), bf16)],
        ),
        out_shape=[
            jax.ShapeDtypeStruct((width, all_globals), f32),
            jax.ShapeDtypeStruct((PAIRS, SLOTS, 2 * GLOBALS), f32),
            jax.ShapeDtypeStruct((PAIRS, SLOTS, 2 * GLOBALS), f32),
        ],
        compiler_params=params(),
        cost_estimate=pl.CostEstimate(
            flops=4 * 4 * rows_count * GLOBALS * width,
            bytes_accessed=10 * all_globals * width,
            transcendentals=HEADS * rows_count * GLOBALS,
        ),
        name="global_forward",
    )(*scalars, k, v, gq, gk, gv)


def local_forward_kernel(
    rows_count,
    group_rows,
    lengths,
    bucket_of,
    place,
    q_ref,
    k_ref,
    v_ref,
    gk_ref,
    gv_ref,
    o_ref,
    extra_ref,
    edges,
    queries_ref,
    score_ref,
    sum_ref,
):
    pair = pl.program_id(0)
    block = pl.program_id(1)

    @pl.when((pair == 0) & (block == 0))
    def _():
        read_edges(lengths, bucket_of, place, edges)

    slot_of, segment = row_numbers(place, edges, rows_count, group_rows, block)
    extra = query_extra(slot_of, segment)
    extra = jnp.concatenate([extra, extra], 0)
    slot_both = jnp.concatenate([slot_of, slot_of], 0)
    queries_ref[:, :LANES] = stack_pair(q_ref[...])
    queries_ref[:, LANES:] = extra.astype(bf16)
    queries = queries_ref[...]
    keys = jnp.concatenate([k_ref[...], key_extra(slot_of, segment).astype(bf16)], axis=1)
    score = nt(queries, keys)
    score_ref[...] = jnp.full(score_ref.shape, masked_score, f32)

    def score_slot(slot, carry):
        @pl.when(slot_present(slot, place, edges, rows_count, group_rows, block))
        def _():
            at = pl.ds(pl.multiple_of(slot * GLOBALS, GLOBALS), GLOBALS)
            slot_keys = jnp.concatenate([gk_ref[at, :], global_key_extra(slot).astype(bf16)], 1)
            score_ref[...] = jnp.maximum(score_ref[...], nt(queries_ref[...], slot_keys))

        return carry

    lax.fori_loop(0, SLOTS, score_slot, 0)
    far_score = score_ref[...]
    peak = jnp.maximum(
        jnp.max(score, axis=1, keepdims=True), jnp.max(far_score, axis=1, keepdims=True)
    )
    weights = jnp.exp(score - peak)
    far_weights = jnp.exp(far_score - peak)
    total = jnp.sum(weights, axis=1, keepdims=True) + jnp.sum(far_weights, axis=1, keepdims=True)
    sum_ref[...] = nn(weights.astype(bf16), v_ref[...])
    score_ref[...] = far_weights

    def add_slot(slot, carry):
        @pl.when(slot_present(slot, place, edges, rows_count, group_rows, block))
        def _():
            at = pl.ds(pl.multiple_of(slot * GLOBALS, GLOBALS), GLOBALS)
            chosen = jnp.where(slot_both == slot, score_ref[...], 0.0).astype(bf16)
            sum_ref[...] = sum_ref[...] + nn(chosen, gv_ref[at, :])

        return carry

    lax.fori_loop(0, SLOTS, add_slot, 0)
    mean = sum_ref[...] / total
    lane = iota((BLOCK, LANES), 1)
    o_ref[...] = jnp.where(lane < HEAD_DIM, mean[:BLOCK], mean[BLOCK:]).astype(bf16)
    stat = peak + jnp.log(total)
    lane = iota((2 * BLOCK, LANES), 1)
    extra_ref[...] = (
        place_three(stat, lane, STAT_LANE, extra).astype(bf16).reshape(2, BLOCK, LANES)
    )


def local_forward(scalars, rows_count, group_rows, q, k, v, gk, gv):
    blocks = rows_count // BLOCK
    all_globals, width = gk.shape
    block_spec = pl.BlockSpec((BLOCK, LANES), lambda p, b, *unused: (b, p))
    pair_spec = pl.BlockSpec((all_globals, LANES), lambda p, b, *unused: (0, p))
    return pl.pallas_call(
        functools.partial(local_forward_kernel, rows_count, group_rows),
        grid_spec=pltpu.PrefetchScalarGridSpec(
            num_scalar_prefetch=3,
            grid=(PAIRS, blocks),
            in_specs=[block_spec] * 3 + [pair_spec] * 2,
            out_specs=[
                block_spec,
                pl.BlockSpec((2, BLOCK, LANES), lambda p, b, *unused: (p, b, 0)),
            ],
            scratch_shapes=[
                pltpu.SMEM((16,), jnp.int32),
                pltpu.VMEM((2 * BLOCK, 2 * LANES), bf16),
                pltpu.VMEM((2 * BLOCK, LANES), f32),
                pltpu.VMEM((2 * BLOCK, LANES), f32),
            ],
        ),
        out_shape=[
            jax.ShapeDtypeStruct((rows_count, width), bf16),
            jax.ShapeDtypeStruct((HEADS, rows_count, LANES), bf16),
        ],
        compiler_params=params(),
        cost_estimate=pl.CostEstimate(
            flops=16 * rows_count * (BLOCK + GLOBALS) * width,
            bytes_accessed=16 * rows_count * width,
            transcendentals=HEADS * rows_count * (BLOCK + GLOBALS),
        ),
        name="local_forward",
    )(*scalars, q, k, v, gk, gv)


def branch_kernel(
    tile,
    x_ref,
    o_ref,
    ct_ref,
    wo_ref,
    w1_ref,
    b1_ref,
    w2_ref,
    b2_ref,
    gain_ref,
    offset_ref,
    z_ref,
    dy_ref,
    do_ref,
    dw1_ref,
    dw2_ref,
    dwo_ref,
    db1_ref,
    db2_ref,
    dgain_ref,
    doffset_ref,
    y_ref,
    h_ref,
    dh_ref,
    dft_ref,
    a_ref,
    du_ref,
):
    step = pl.program_id(0)
    count, width = x_ref.shape
    tiles = count // tile

    def rows_at(i):
        return pl.ds(pl.multiple_of(i * tile, tile), tile)

    @pl.when(step == 0)
    def _():
        dft_ref[...] = ct_ref[...].T

        def start(i, carry):
            at = rows_at(i)
            y = x_ref[at, :].astype(f32) + nn(o_ref[at, :], wo_ref[...])
            unit, unused = normalize_rows(y)
            h_ref[at, :] = (unit * gain_ref[...] + offset_ref[...]).astype(bf16)
            y_ref[at, :] = y
            dh_ref[at, :] = jnp.zeros((tile, width), f32)
            return carry

        lax.fori_loop(0, tiles, start, 0)

    db1_ref[...] = jnp.zeros_like(db1_ref)

    def chunk(i, carry):
        at = rows_at(i)
        u = nn(h_ref[at, :], w1_ref[...]) + b1_ref[...]
        da = nt(ct_ref[at, :], w2_ref[...])
        area, density = gelu_parts(u)
        a = (u * area).astype(bf16)
        du = (da * (area + u * density)).astype(bf16)
        a_ref[at, :] = a
        du_ref[at, :] = du
        db1_ref[...] += jnp.sum(du.astype(f32), axis=0, keepdims=True)
        more = nn(a, w2_ref[...])

        @pl.when(step == 0)
        def _():
            dy_ref[at, :] = y_ref[at, :] + b2_ref[...] + more

        @pl.when(step > 0)
        def _():
            dy_ref[at, :] = dy_ref[at, :] + more

        dh_ref[at, :] = dh_ref[at, :] + nt(du, w1_ref[...])
        return carry

    lax.fori_loop(0, tiles, chunk, 0)
    dw1_ref[...] = tn(du_ref[...], h_ref[...]).astype(bf16)
    dw2_ref[...] = nn(dft_ref[...], a_ref[...]).astype(bf16)

    @pl.when(step == pl.num_programs(0) - 1)
    def _():
        db2_ref[...] = jnp.zeros_like(db2_ref)
        dgain_ref[...] = jnp.zeros_like(dgain_ref)
        doffset_ref[...] = jnp.zeros_like(doffset_ref)

        def finish(i, carry):
            at = rows_at(i)
            z_ref[at, :] = dy_ref[at, :].astype(bf16)
            unit, scale = normalize_rows(y_ref[at, :])
            dh = dh_ref[at, :]
            ct = ct_ref[at, :].astype(f32)
            dy = ct + norm_back(unit, scale, gain_ref[...], dh)
            dy_ref[at, :] = dy
            db2_ref[...] += jnp.sum(ct, axis=0, keepdims=True)
            doffset_ref[...] += jnp.sum(dh, axis=0, keepdims=True)
            dgain_ref[...] += jnp.sum(dh * unit, axis=0, keepdims=True)
            low = dy.astype(bf16)
            h_ref[at, :] = low
            do_ref[at, :] = nt(low, wo_ref[...]).astype(bf16)
            return carry

        lax.fori_loop(0, tiles, finish, 0)
        dwo_ref[...] = tn(h_ref[...], o_ref[...]).astype(bf16)


def branch(x, o, ct, wo, w1, b1, w2, b2, gain, offset, name):
    count, width = x.shape
    hidden = w1.shape[1]
    chunk = FF_CHUNK
    tile = min(count, 512)
    row = once((count, width))
    line = full((1, width))
    return pl.pallas_call(
        functools.partial(branch_kernel, tile),
        grid=(hidden // chunk,),
        in_specs=[
            row,
            row,
            row,
            once((width, width)),
            pl.BlockSpec((width, chunk), lambda j: (0, j)),
            pl.BlockSpec((1, chunk), lambda j: (0, j)),
            pl.BlockSpec((chunk, width), lambda j: (j, 0)),
            line,
            line,
            line,
        ],
        out_specs=[
            row,
            row,
            row,
            pl.BlockSpec((chunk, width), lambda j: (j, 0)),
            pl.BlockSpec((width, chunk), lambda j: (0, j)),
            full((width, width)),
            pl.BlockSpec((1, chunk), lambda j: (0, j)),
            line,
            line,
            line,
        ],
        out_shape=[
            jax.ShapeDtypeStruct((count, width), bf16),
            jax.ShapeDtypeStruct((count, width), f32),
            jax.ShapeDtypeStruct((count, width), bf16),
            jax.ShapeDtypeStruct((hidden, width), bf16),
            jax.ShapeDtypeStruct((width, hidden), bf16),
            jax.ShapeDtypeStruct((width, width), bf16),
            jax.ShapeDtypeStruct((1, hidden), f32),
            jax.ShapeDtypeStruct((1, width), f32),
            jax.ShapeDtypeStruct((1, width), f32),
            jax.ShapeDtypeStruct((1, width), f32),
        ],
        scratch_shapes=[
            pltpu.VMEM((count, width), f32),
            pltpu.VMEM((count, width), bf16),
            pltpu.VMEM((count, width), f32),
            pltpu.VMEM((width, count), bf16),
            pltpu.VMEM((count, chunk), bf16),
            pltpu.VMEM((count, chunk), bf16),
        ],
        compiler_params=params(),
        cost_estimate=pl.CostEstimate(
            flops=6 * count * width * (2 * hidden + width),
            bytes_accessed=8 * width * hidden + 16 * count * width,
            transcendentals=2 * count * hidden,
        ),
        name=name,
    )(x, o, ct, wo, w1, b1, w2, b2, gain, offset)


def local_backward_kernel(
    rows_count,
    group_rows,
    lengths,
    bucket_of,
    place,
    q_ref,
    k_ref,
    v_ref,
    do_ref,
    o_ref,
    extra_ref,
    gk_ref,
    gv_ref,
    dq_ref,
    dk_ref,
    dv_ref,
    dgk_ref,
    dgv_ref,
    edges,
    queries_ref,
    grads_ref,
    turned_ref,
):
    pair = pl.program_id(0)
    block = pl.program_id(1)

    @pl.when((pair == 0) & (block == 0))
    def _():
        read_edges(lengths, bucket_of, place, edges)

    @pl.when(block == 0)
    def _():
        dgk_ref[...] = jnp.zeros_like(dgk_ref)
        dgv_ref[...] = jnp.zeros_like(dgv_ref)

    slot_of, segment = row_numbers(place, edges, rows_count, group_rows, block)
    queries_ref[:, :LANES] = stack_pair(q_ref[...])
    queries_ref[:, LANES:] = extra_ref[...].reshape(2 * BLOCK, LANES)
    upstream = stack_pair(do_ref[...])
    attended = jnp.concatenate([o_ref[...], o_ref[...]], 0)
    centre = jnp.sum(upstream.astype(f32) * attended.astype(f32), axis=1, keepdims=True)
    lane = iota((2 * BLOCK, LANES), 1)
    grads_ref[:, :LANES] = upstream
    grads_ref[:, LANES:] = place_three(
        centre, lane, STAT_LANE, jnp.zeros((2 * BLOCK, LANES), f32)
    ).astype(bf16)

    def gradients(keys, key_columns, values):
        columns = iota(values.shape, 1)
        minus = jnp.where((columns >= STAT_LANE) & (columns < STAT_LANE + 3), -1.0, 0.0)
        weights = jnp.exp(nt(jnp.concatenate([keys, key_columns], 1), queries_ref[...]))
        along = nt(jnp.concatenate([values, minus.astype(bf16)], 1), grads_ref[...])
        score_grad = (weights * along).astype(bf16)
        value_grad = nn(weights.astype(bf16), grads_ref[:, :LANES])
        key_grad = nn(score_grad, queries_ref[:, :LANES])
        return key_grad, value_grad, tn(keys, score_grad)

    key_grad, value_grad, turned = gradients(
        k_ref[...], key_extra(slot_of, segment).astype(bf16), v_ref[...]
    )
    dk_ref[...] = key_grad
    dv_ref[...] = value_grad
    turned_ref[...] = turned

    def one_slot(slot, carry):
        @pl.when(slot_present(slot, place, edges, rows_count, group_rows, block))
        def _():
            at = pl.ds(pl.multiple_of(slot * GLOBALS, GLOBALS), GLOBALS)
            key_grad, value_grad, turned = gradients(
                gk_ref[at, :], global_key_extra(slot).astype(bf16), gv_ref[at, :]
            )
            dgk_ref[at, :] = dgk_ref[at, :] + key_grad
            dgv_ref[at, :] = dgv_ref[at, :] + value_grad
            turned_ref[...] = turned_ref[...] + turned

        return carry

    lax.fori_loop(0, SLOTS, one_slot, 0)
    both = jnp.concatenate([turned_ref[:HEAD_DIM, :BLOCK], turned_ref[HEAD_DIM:, BLOCK:]], 0)
    dq_ref[...] = both.T.astype(bf16)


def local_backward(scalars, rows_count, group_rows, q, k, v, do, o, extra, gk, gv):
    blocks = rows_count // BLOCK
    all_globals, width = gk.shape
    block_spec = pl.BlockSpec((BLOCK, LANES), lambda p, b, *unused: (b, p))
    pair_spec = pl.BlockSpec((all_globals, LANES), lambda p, b, *unused: (0, p))
    return pl.pallas_call(
        functools.partial(local_backward_kernel, rows_count, group_rows),
        grid_spec=pltpu.PrefetchScalarGridSpec(
            num_scalar_prefetch=3,
            grid=(PAIRS, blocks),
            in_specs=[block_spec] * 5
            + [pl.BlockSpec((2, BLOCK, LANES), lambda p, b, *unused: (p, b, 0))]
            + [pair_spec] * 2,
            out_specs=[block_spec] * 3 + [pair_spec] * 2,
            scratch_shapes=[
                pltpu.SMEM((16,), jnp.int32),
                pltpu.VMEM((2 * BLOCK, 2 * LANES), bf16),
                pltpu.VMEM((2 * BLOCK, 2 * LANES), bf16),
                pltpu.VMEM((LANES, 2 * BLOCK), f32),
            ],
        ),
        out_shape=[
            jax.ShapeDtypeStruct((rows_count, width), bf16),
            jax.ShapeDtypeStruct((rows_count, width), f32),
            jax.ShapeDtypeStruct((rows_count, width), f32),
            jax.ShapeDtypeStruct((all_globals, width), f32),
            jax.ShapeDtypeStruct((all_globals, width), f32),
        ],
        compiler_params=params(),
        cost_estimate=pl.CostEstimate(
            flops=40 * rows_count * (BLOCK + GLOBALS) * width,
            bytes_accessed=30 * rows_count * width,
            transcendentals=HEADS * rows_count * (BLOCK + GLOBALS),
        ),
        name="local_backward",
    )(*scalars, q, k, v, do, o, extra, gk, gv)


def global_backward_kernel(
    rows_count,
    group_rows,
    lengths,
    bucket_of,
    place,
    k_ref,
    v_ref,
    dk_ref,
    dv_ref,
    gq_ref,
    gk_ref,
    gv_ref,
    gdo_ref,
    gstat_ref,
    dgk_in_ref,
    dgv_in_ref,
    dk_out_ref,
    dv_out_ref,
    dgq_ref,
    dgk_ref,
    dgv_ref,
    edges,
    keys_ref,
    values_ref,
    dk_sum_ref,
    dv_sum_ref,
):
    pair = pl.program_id(0)
    block = pl.program_id(1)

    @pl.when((pair == 0) & (block == 0))
    def _():
        read_edges(lengths, bucket_of, place, edges)

    @pl.when(block == 0)
    def _():
        dgq_ref[...] = jnp.zeros_like(dgq_ref)
        dgk_ref[...] = dgk_in_ref[...].astype(bf16)
        dgv_ref[...] = dgv_in_ref[...].astype(bf16)

    slot_of, segment = row_numbers(place, edges, rows_count, group_rows, block)
    column = iota((BLOCK, LANES), 1)
    minus = jnp.where((column >= STAT_LANE) & (column < STAT_LANE + 3), -1.0, 0.0).astype(bf16)
    keys_ref[:, :LANES] = k_ref[...]
    keys_ref[:, LANES:] = key_extra(slot_of, segment).astype(bf16)
    values_ref[:, :LANES] = v_ref[...]
    values_ref[:, LANES:] = minus
    dk_sum_ref[...] = dk_ref[...]
    dv_sum_ref[...] = dv_ref[...]

    def gradients(slot, keys, values):
        at = pl.ds(pl.multiple_of(slot * GLOBALS, GLOBALS), GLOBALS)
        source = iota((LANES, LANES), 0)
        target = iota((LANES, LANES), 1)
        stats = gstat_ref[at, :]

        def moved(head, first):
            match = jnp.zeros((LANES, LANES), jnp.bool_)
            for piece in range(3):
                match = match | (
                    (target == STAT_LANE + piece) & (source == first + piece * HEADS + head)
                )
            return nn(stats, jnp.where(match, 1.0, 0.0).astype(bf16))

        extra = global_query_extra(slot)
        query_columns = jnp.concatenate(
            [moved(2 * pair, 0) + extra, moved(2 * pair + 1, 0) + extra], 0
        ).astype(bf16)
        grad_columns = jnp.concatenate(
            [moved(2 * pair, 3 * HEADS), moved(2 * pair + 1, 3 * HEADS)], 0
        ).astype(bf16)
        queries = stack_pair(gq_ref[at, :])
        upstream = stack_pair(gdo_ref[at, :])
        weights = jnp.exp(nt(keys, jnp.concatenate([queries, query_columns], 1)))
        along = nt(values, jnp.concatenate([upstream, grad_columns], 1))
        score_grad = (weights * along).astype(bf16)
        key_grad = nn(score_grad, queries)
        value_grad = nn(weights.astype(bf16), upstream)
        turned = tn(keys[:, :LANES], score_grad)
        turned = jnp.concatenate([turned[:HEAD_DIM, :GLOBALS], turned[HEAD_DIM:, GLOBALS:]], 0)
        dgq_ref[at, :] = dgq_ref[at, :] + turned.T
        return key_grad, value_grad

    def one_slot(slot, carry):
        @pl.when(slot_present(slot, place, edges, rows_count, group_rows, block))
        def _():
            key_grad, value_grad = gradients(slot, keys_ref[...], values_ref[...])
            dk_sum_ref[...] = dk_sum_ref[...] + key_grad
            dv_sum_ref[...] = dv_sum_ref[...] + value_grad

        return carry

    lax.fori_loop(0, SLOTS, one_slot, 0)
    dk_out_ref[...] = dk_sum_ref[...].astype(bf16)
    dv_out_ref[...] = dv_sum_ref[...].astype(bf16)

    @pl.when((block == pl.num_programs(1) - 1) & (place[2] >= 0))
    def _():
        slot = place[2]
        at = pl.ds(pl.multiple_of(slot * GLOBALS, GLOBALS), GLOBALS)
        keys = jnp.concatenate([gk_ref[at, :], global_key_extra(slot).astype(bf16)], axis=1)
        values = jnp.concatenate([gv_ref[at, :], minus[:GLOBALS]], axis=1)
        key_grad, value_grad = gradients(slot, keys, values)
        dgk_ref[at, :] = (dgk_in_ref[at, :] + key_grad).astype(bf16)
        dgv_ref[at, :] = (dgv_in_ref[at, :] + value_grad).astype(bf16)


def global_backward(scalars, rows_count, group_rows, k, v, dk, dv, gq, gk, gv, gdo, gstat, dgk, dgv):
    blocks = rows_count // BLOCK
    all_globals, width = gk.shape
    block_spec = pl.BlockSpec((BLOCK, LANES), lambda p, b, *unused: (b, p))
    pair_spec = pl.BlockSpec((all_globals, LANES), lambda p, b, *unused: (0, p))
    return pl.pallas_call(
        functools.partial(global_backward_kernel, rows_count, group_rows),
        grid_spec=pltpu.PrefetchScalarGridSpec(
            num_scalar_prefetch=3,
            grid=(PAIRS, blocks),
            in_specs=[block_spec] * 4
            + [pair_spec] * 4
            + [pl.BlockSpec((all_globals, LANES), lambda p, b, *unused: (0, 0))]
            + [pair_spec] * 2,
            out_specs=[block_spec] * 2 + [pair_spec] * 3,
            scratch_shapes=[
                pltpu.SMEM((16,), jnp.int32),
                pltpu.VMEM((BLOCK, 2 * LANES), bf16),
                pltpu.VMEM((BLOCK, 2 * LANES), bf16),
                pltpu.VMEM((BLOCK, LANES), f32),
                pltpu.VMEM((BLOCK, LANES), f32),
            ],
        ),
        out_shape=[
            jax.ShapeDtypeStruct((rows_count, width), bf16),
            jax.ShapeDtypeStruct((rows_count, width), bf16),
            jax.ShapeDtypeStruct((all_globals, width), f32),
            jax.ShapeDtypeStruct((all_globals, width), bf16),
            jax.ShapeDtypeStruct((all_globals, width), bf16),
        ],
        compiler_params=params(),
        cost_estimate=pl.CostEstimate(
            flops=40 * rows_count * GLOBALS * width,
            bytes_accessed=30 * rows_count * width,
            transcendentals=HEADS * rows_count * GLOBALS,
        ),
        name="global_backward",
    )(*scalars, k, v, dk, dv, gq, gk, gv, gdo, gstat, dgk, dgv)


def project_back_kernel(
    rows_count,
    group_rows,
    tile,
    lengths,
    bucket_of,
    place,
    x_ref,
    dy_ref,
    h_ref,
    dq_ref,
    dk_ref,
    dv_ref,
    gh_ref,
    dgq_ref,
    dgk_ref,
    dgv_ref,
    wq_ref,
    wk_ref,
    wv_ref,
    gain_ref,
    dx_ref,
    dgh_ref,
    dwq_ref,
    dwk_ref,
    dwv_ref,
    dgain_ref,
    doffset_ref,
    edges,
    sq_ref,
    sk_ref,
    sv_ref,
):
    read_edges(lengths, bucket_of, place, edges)
    count, width = x_ref.shape
    dgain_ref[...] = jnp.zeros_like(dgain_ref)
    doffset_ref[...] = jnp.zeros_like(doffset_ref)

    def back(dq, dk, dv):
        return nt(dq, wq_ref[...]) * query_scale + nt(dk, wk_ref[...]) + nt(dv, wv_ref[...])

    def one_tile(i, carry):
        at = pl.ds(pl.multiple_of(i * tile, tile), tile)
        dh = back(dq_ref[at, :], dk_ref[at, :], dv_ref[at, :])
        unit, scale = normalize_rows(x_ref[at, :].astype(f32))
        doffset_ref[...] += jnp.sum(dh, axis=0, keepdims=True)
        dgain_ref[...] += jnp.sum(dh * unit, axis=0, keepdims=True)
        dx_ref[at, :] = dy_ref[at, :] + norm_back(unit, scale, gain_ref[...], dh)
        return carry

    lax.fori_loop(0, count // tile, one_tile, 0)
    sums = (sq_ref, sk_ref, sv_ref)
    for target, source in zip(sums, (dq_ref, dk_ref, dv_ref)):
        target[...] = tn(source[...], h_ref[...])
    dgh_ref[...] = jnp.zeros_like(dgh_ref)

    def one_slot(slot, carry):
        needed = slot == place[2]
        for block in range(rows_count // BLOCK):
            needed = needed | slot_present(slot, place, edges, rows_count, group_rows, block)

        @pl.when(needed)
        def _():
            at = pl.ds(pl.multiple_of(slot * GLOBALS, GLOBALS), GLOBALS)
            grads = (dgq_ref[at, :].astype(bf16), dgk_ref[at, :], dgv_ref[at, :])
            for target, grad in zip(sums, grads):
                target[...] = target[...] + tn(grad, gh_ref[at, :])
            dgh_ref[at, :] = back(*grads).astype(bf16)

        return carry

    lax.fori_loop(0, SLOTS, one_slot, 0)
    dwq_ref[...] = (sq_ref[...] * query_scale).astype(bf16)
    dwk_ref[...] = sk_ref[...].astype(bf16)
    dwv_ref[...] = sv_ref[...].astype(bf16)


def project_back(scalars, group_rows, x, dy, h, dq, dk, dv, gh, dgq, dgk, dgv, wq, wk, wv, gain):
    count, width = x.shape
    all_globals = gh.shape[0]
    vmem = pl.BlockSpec(memory_space=pltpu.VMEM)
    smem = pl.BlockSpec(memory_space=pltpu.SMEM)
    return pl.pallas_call(
        functools.partial(project_back_kernel, count, group_rows, 512),
        in_specs=[smem] * 3 + [vmem] * 14,
        out_specs=[vmem] * 7,
        scratch_shapes=[pltpu.SMEM((16,), jnp.int32)] + [pltpu.VMEM((width, width), f32)] * 3,
        out_shape=[
            jax.ShapeDtypeStruct((count, width), f32),
            jax.ShapeDtypeStruct((all_globals, width), bf16),
            jax.ShapeDtypeStruct((width, width), bf16),
            jax.ShapeDtypeStruct((width, width), bf16),
            jax.ShapeDtypeStruct((width, width), bf16),
            jax.ShapeDtypeStruct((1, width), f32),
            jax.ShapeDtypeStruct((1, width), f32),
        ],
        compiler_params=params(),
        cost_estimate=pl.CostEstimate(
            flops=12 * count * width * width, bytes_accessed=30 * count * width, transcendentals=0
        ),
        name="project_back",
    )(*scalars, x, dy, h, dq, dk, dv, gh, dgq, dgk, dgv, wq, wk, wv, gain)


def from_behind(value, axis, steps):
    count = lax.axis_size(axis)
    pairs = [(source, (source + steps) % count) for source in range(count)]
    return lax.ppermute(value, axis, pairs)


def pieces(value):
    first = lax.reduce_precision(value, 8, 7)
    second = lax.reduce_precision(value - first, 8, 7)
    return [first.astype(bf16), second.astype(bf16), (value - first - second).astype(bf16)]


def scatter_sum(value):
    half = lax.psum_scatter(value, "batch", scatter_dimension=1, tiled=True)
    part = lax.psum_scatter(half, "seq", scatter_dimension=0, tiled=True)
    return part.T.astype(f32)


def on_device(
    tokens,
    global_states,
    lengths,
    bucket_of,
    wq,
    wk,
    wv,
    wo,
    w1,
    b1,
    w2,
    b2,
    norm_params,
    cotangent,
    global_cotangent,
):
    rows = tokens.shape[1]
    width = tokens.shape[2]
    own = global_states.shape[1]
    seq_count = lax.axis_size("seq")
    seq_place = lax.axis_index("seq")
    group_rows = rows * seq_count
    own_start = seq_place * own
    first_of_slot = own_start % GLOBALS == 0
    place = jnp.stack(
        [
            lax.axis_index("batch"),
            seq_place,
            jnp.where(first_of_slot, own_start // GLOBALS, -1),
        ]
    ).astype(jnp.int32)
    scalars = (lengths, bucket_of, place)
    norms = [norm_params[i : i + 1] for i in range(6)]
    b1_line = b1[None]
    b2_line = b2[None]

    arrived_tokens, arrived_grads = from_behind(
        (tokens[0, rows - HALF :], cotangent[0, rows - HALF :]), "seq", 1
    )
    x = jnp.concatenate([arrived_tokens, tokens[0, : rows - HALF]], 0)
    ct = jnp.concatenate([arrived_grads, cotangent[0, : rows - HALF]], 0)
    all_states = lax.all_gather(global_states[0], "seq", axis=0, tiled=True)

    h, q, k, v = project_local(x, norms[0], norms[1], wq, wk, wv)
    gh, gq, gk, gv = project_global(
        scalars, rows, group_rows, all_states, norms[2], norms[3], wq, wk, wv
    )
    part_sum, part_peak, part_total = global_forward(scalars, rows, group_rows, k, v, gq, gk, gv)

    def by_head(value):
        value = value.reshape(PAIRS, SLOTS, 2, GLOBALS).transpose(0, 2, 1, 3)
        return value.reshape(HEADS, SLOTS * GLOBALS)

    part_peak = by_head(part_peak)
    peak = jnp.max(lax.all_gather(part_peak, "seq"), axis=0)
    o, extra = local_forward(scalars, rows, group_rows, q, k, v, gk, gv)
    factor = jnp.exp(part_peak - peak)
    scaled = (part_sum.reshape(HEADS, HEAD_DIM, -1) * factor[:, None, :]).reshape(width, -1)
    payload = jnp.concatenate([scaled, by_head(part_total) * factor, jnp.zeros((4, scaled.shape[1]), f32)], 0)
    sums = lax.psum_scatter(
        payload.astype(bf16).T, "seq", scatter_dimension=0, tiled=True
    ).astype(f32)
    own_total = sums[:, width : width + HEADS]
    own_peak = lax.dynamic_slice_in_dim(peak, own_start, own, 1).T
    go = (
        (sums[:, :width].reshape(own, HEADS, HEAD_DIM) / own_total[:, :, None])
        .reshape(own, width)
        .astype(bf16)
    )
    gstat = own_peak + jnp.log(own_total)

    z, dy, do, dw1, dw2, dwo, db1, db2, dgain2, doffset2 = branch(
        x, o, ct, wo, w1, b1_line, w2, b2_line, norms[4], norms[5], "branch_local"
    )
    gz, gdy, gdo, gdw1, gdw2, gdwo, gdb1, gdb2, gdgain2, gdoffset2 = branch(
        global_states[0],
        go,
        global_cotangent[0],
        wo,
        w1,
        b1_line,
        w2,
        b2_line,
        norms[4],
        norms[5],
        "branch_global",
    )
    gcentre = jnp.sum(
        (gdo.astype(f32) * go.astype(f32)).reshape(own, HEADS, HEAD_DIM), axis=-1
    )
    message = jnp.concatenate(
        [gdo]
        + pieces(gstat)
        + pieces(gcentre)
        + [jnp.zeros((own, LANES - 6 * HEADS), bf16)],
        axis=1,
    )
    everyone = lax.all_gather(message, "seq", axis=0, tiled=True)
    dq, dk, dv, dgk, dgv = local_backward(
        scalars, rows, group_rows, q, k, v, do, o, extra, gk, gv
    )
    dk, dv, dgq, dgk, dgv = global_backward(
        scalars,
        rows,
        group_rows,
        k,
        v,
        dk,
        dv,
        gq,
        gk,
        gv,
        everyone[:, :width],
        everyone[:, width:],
        dgk,
        dgv,
    )
    dx, dgh, dwq, dwk, dwv, dgain1, doffset1 = project_back(
        scalars, group_rows, x, dy, h, dq, dk, dv, gh, dgq, dgk, dgv, wq, wk, wv, norms[0]
    )
    dgh = lax.psum_scatter(dgh, "seq", scatter_dimension=0, tiled=True).astype(f32)
    gunit, gscale = normalize_rows(global_states[0].astype(f32))
    global_grad = gdy + norm_back(gunit, gscale, norms[2], dgh)
    norm_grad = jnp.concatenate(
        [
            dgain1,
            doffset1,
            jnp.sum(dgh * gunit, axis=0, keepdims=True),
            jnp.sum(dgh, axis=0, keepdims=True),
            dgain2 + gdgain2,
            doffset2 + gdoffset2,
        ],
        0,
    )
    back_z, back_grad = from_behind((z[:HALF], dx[:HALF].astype(bf16)), "seq", -1)
    layer_out = jnp.concatenate([z[HALF:], back_z], 0)
    token_grad = jnp.concatenate([dx[HALF:], back_grad.astype(f32)], 0)
    small = lax.psum((db1[0] + gdb1[0], db2[0] + gdb2[0], norm_grad), ("batch", "seq"))
    return (
        layer_out[None],
        gz[None],
        token_grad[None],
        global_grad[None],
        scatter_sum(dwq),
        scatter_sum(dwk),
        scatter_sum(dwv),
        scatter_sum(dwo + gdwo),
        scatter_sum(dw1 + gdw1),
        scatter_sum(dw2 + gdw2),
        small[0],
        small[1],
        small[2],
    )


def solution(mesh):
    split = P("batch", "seq", None)
    return jax.shard_map(
        on_device,
        mesh=mesh,
        in_specs=(split, split) + (P(),) * 11 + (split, split),
        out_specs=(split,) * 4 + (P("batch", "seq"),) * 6 + (P(),) * 3,
        check_vma=False,
    )
```

time: 1560 us -> 1050 us (0.67)
  matrix products: 533 us -> 0 us
  Pallas kernels: 0 us -> 260 us
  local copies, waits for them, and re-layouts: 175 us -> 50.7 us
  other arithmetic: 119 us -> 44.1 us
  blocking collectives: 121 us -> 63.1 us
  waiting for transfers between devices: 575 us -> 600 us
    dot_general x62 -> x0, matrix products: 533 us -> none  [the longest x6 85.2 us: scores(): jnp.einsum('qhd,khd->hqk', split_heads(queries), split_heads(keys), prefe...]
    pallas_call x0 -> x9, Pallas kernels: none -> 260 us  [the longest x2 78.3 us: branch(): pl.pallas_call(functools.partial(branch_kernel, tile), grid=(hidden // ch...]
    reduce_scatter x7 -> x9, waiting for transfers between devices: 201 us -> 458 us  [the longest x6 296 us: scatter_sum(): part = lax.psum_scatter(half, 'seq', scatter_dimension=0, tiled=True)]
    unnamed x31 -> x21, waiting for transfers between devices: 337 us -> 99.7 us
    reduce_sum x22 -> x4, other arithmetic: 80.6 us -> 1.63 us  [the longest x1 1.12 us: on_device(): jnp.sum(dgh * gunit, axis=0, keepdims=True)]
    pmax x1 -> x0, blocking collectives: 59.8 us -> none  [on_device(): lax.pmax(offered.astype(jnp.bfloat16), 'seq').astype(offered.dtype)]
    unnamed x269 -> x59, local copies, waits for them, and re-layouts: 63.2 us -> 29.2 us
    dynamic_update_slice x15 -> x0, local copies, waits for them, and re-layouts: 22.4 us -> none  [the longest x14 22.3 us: on_device(): attended_blocks, peaks, totals = lax.map(forward_block, pieces)]
  transfers between devices with their start and end apart: 25 -> 20, of which waited for: 16 -> 16; matrix products, arithmetic and copies ran while one was open for 47% -> 7% of each run, Pallas kernels for 0% -> 20%
where the time goes in v1:
time: 1050 us; the launch traced here: 1040 us
  waiting for transfers between devices  600 us (57%)
  Pallas kernels  260 us (25%)
  blocking collectives  63.1 us (6%)
  local copies, waits for them, and re-layouts  50.7 us (5%)
  other arithmetic  44.1 us (4%)
  between operations  14.9 us (1%)
    reduce_scatter x6, waiting for transfers between devices, scatter_sum(): part = lax.psum_scatter(half, 'seq', scatter_dimension=0, tiled=True)  296 us
    unnamed x21, waiting for transfers between devices  99.7 us
    pallas_call x2, Pallas kernels, branch(): pl.pallas_call(functools.partial(branch_kernel, tile), grid=(hidden // ch...  78.3 us
    reduce_scatter x1, waiting for transfers between devices, scatter_sum(): half = lax.psum_scatter(value, 'batch', scatter_dimension=1, tiled=True)  60.1 us
    reduce_scatter x1, waiting for transfers between devices, on_device(): lax.psum_scatter(dgh, 'seq', scatter_dimension=0, tiled=True).astype(f32)  58.2 us
    reduce_scatter x1, waiting for transfers between devices, on_device(): lax.psum_scatter(payload.astype(bf16).T, 'seq', scatter_dimension=0, tile...  44.4 us
    pallas_call x1, Pallas kernels, local_backward(): pl.pallas_call(functools.partial(local_backward_kernel, rows_count, group...  43.3 us
    psum x1, blocking collectives, on_device(): lax.psum((db1[0] + gdb1[0], db2[0] + gdb2[0], norm_grad), ('batch', 'seq'))  41.2 us
  transfers between devices with their start and end apart: 20, of which 16 were waited for; matrix products, arithmetic and copies ran while one was open for 7% of the time, Pallas kernels for 20%

profile of v1, /device:TPU:0, one launch (start us, length us, event | category | flops | bytes accessed | tf_op | source)
XLA Modules:
  0.0 1038.2 jit_solution(3691241468553832904)
XLA Ops:
  9.6 1.6 slice_reduce_fusion
  11.8 1.3 slice_bitcast_fusion.1
  13.1 6.8 collective-permute-done
  19.9 1.2 pad_maximum_fusion.rows_ref.x_ref
  21.2 7.9 project_local.1
  29.1 23.6 %all-gather.6.cloned.1.call-done = bf16[1,1024,768]{2,1,0:T(8,128)(2,1)} async-done(((bf16[1,64,768]{2,1,0:T(8,128)(2,1)}), bf16[1,1024,768]{2,1,0:T(8,128)(2,1)}) %all-gather.6.cloned.1.call-update) | async-done | bytes 1572880 | tf_op jit(solution)/shard_map/all_gather | solution.py:1083
  52.7 9.7 project_global.1
  62.4 22.8 %global_forward.1 = (f32[768,1024]{1,0:T(8,128)}, f32[6,8,256]{2,1,0:T(8,128)}, f32[6,8,256]{2,1,0:T(8,128)}) custom-call(s32[2,8]{1,0:T(2,128)} %lengths.11, s32[2]{0:T(128)} %bucket_of.11, s32[3]{0:T(128)} %pad_add_fusion.place, bf16[1024,768]{1,0:T(8,128)(2,1)} %get-tuple-element.64.k_ref, bf16[1024,768]{1,0:T(8,128)(2,1)} %get-tuple-element.65.v_ref, ...), custom_call_target="tpu_custom_call" | custom-call | flops 1610612736 | bytes 7864320 | tf_op jit(solution)/shard_map/global_forward/pallas_call | solution.py:340
  85.3 3.5 copy.45
  89.2 21.9 %all_gather.10 = f32[16,12,1024]{2,1,0:T(8,128)S(1)} all-gather(f32[1,12,1024]{2,1,0:T(8,128)S(1)} %all_gather_reshape.3), channel_id=1, replica_groups=mesh['batch'=2,'seq'=16] {'seq'}, dimensions={0}, use_global_device_ids=true | all-gather | bytes 835584 | tf_op jit(solution)/shard_map/all_gather | solution.py:1096
  112.0 2.4 copy.46
  114.4 3.1 multiply_convert_fusion
  117.5 1.6 maximum_bitcast_fusion.1
  119.2 1.3 copy-done.2
  121.6 8.9 collective-permute-done.1
  130.5 1.3 pad_maximum_fusion.1.ct_ref
  131.9 44.4 %reduce-scatter.25.cloned.1.call-done = bf16[64,784]{1,0:T(8,128)(2,1)} async-done(((bf16[1024,784]{1,0:T(8,128)(2,1)}), bf16[64,784]{1,0:T(8,128)(2,1)}) %reduce-scatter.25.cloned.1.call-update) | async-done | bytes 100368 | tf_op jit(solution)/shard_map/reduce_scatter | solution.py:1101
  179.0 15.0 %branch_global.1 = (bf16[64,768]{1,0:T(8,128)(2,1)}, f32[64,768]{1,0:T(8,128)}, bf16[64,768]{1,0:T(8,128)(2,1)}, bf16[3072,768]{1,0:T(8,128)(2,1)}, bf16[768,307...) custom-call(bf16[64,768]{1,0:T(8,128)(2,1)} %bitcast.83, ...), custom_call_target="tpu_custom_call" | custom-call | flops 2038431744 | bytes 19660800 | tf_op jit(solution)/shard_map/branch_global/pallas_call | solution.py:593
  196.3 40.0 %local_forward.1 = (bf16[1024,768]{1,0:T(8,128)(2,1)}, bf16[12,1024,128]{2,1,0:T(8,128)(2,1)}) custom-call(s32[2,8]{1,0:T(2,128)} %lengths.11, s32[2]{0:T(128)} %bucket_of.11, s32[3]{0:T(128)} %pad_add_fusion.place, bf16[1024,768]{1,0:T(8,128)(2,1)} %get-tuple-element.63.q_ref, bf16[1024,768]{1,0:T(8,128)(2,1)} %get-tuple-element.64.k_ref, ...), custom_call_target="tpu_custom_call" | custom-call | flops 8053063680 | bytes 12582912 | tf_op jit(solution)/shard_map/local_forward/pallas_call | solution.py:449
  236.3 63.3 %branch_local.1 = (bf16[1024,768]{1,0:T(8,128)(2,1)}, f32[1024,768]{1,0:T(8,128)}, bf16[1024,768]{1,0:T(8,128)(2,1)}, bf16[3072,768]{1,0:T(8,128)(2,1)}, bf16[76...) custom-call(bf16[1024,768]{1,0:T(8,128)(2,1)} %pad_maximum_fusion.ro, ...), custom_call_target="tpu_custom_call" | custom-call | flops 32614907904 | bytes 31457280 | tf_op jit(solution)/shard_map/branch_local/pallas_call | solution.py:593
  299.6 1.6 add.92
  301.2 1.5 copy.55
  302.7 43.3 %local_backward.1 = (bf16[1024,768]{1,0:T(8,128)(2,1)}, f32[1024,768]{1,0:T(8,128)}, f32[1024,768]{1,0:T(8,128)}, f32[1024,768]{1,0:T(8,128)}, f32[1024,768]{1,0:T(8,128)}) custom-call(s32[2,8]{1,0:T(2,128)} %lengths.11, s32[2]{0:T(128)} %bucket_of.11, s32[3]{0:T(128)} %pad_add_fusion.place, bf16[1024,768]{1,0:T(8,128)(2,1)} %get-tuple-element.63.q_ref, ...), custom_call_target="tpu_custom_call" | custom-call | flops 20132659200 | bytes 23592960 | tf_op jit(solution)/shard_map/local_backward/pallas_call | solution.py:738
  346.1 1.7 slice.76.gstat_ref
  347.7 2.6 slice.75.gdo_ref
  350.4 33.0 %global_backward.1 = (bf16[1024,768]{1,0:T(8,128)(2,1)}, bf16[1024,768]{1,0:T(8,128)(2,1)}, f32[1024,768]{1,0:T(8,128)}, bf16[1024,768]{1,0:T(8,128)(2,1)}, bf16[1024,768]{1,0:T(8,128)(2,1)}) custom-call(s32[2,8]{1,0:T(2,128)} %lengths.11, s32[2]{0:T(128)} %bucket_of.11, s32[3]{0:T(128)} %pad_add_fusion.place, bf16[1024,768]{1,0:T(8,128)(2,1)} %get-tuple-element.64.k_ref, ...), custom_call_target="tpu_custom_call" | custom-call | flops 4026531840 | bytes 23592960 | tf_op jit(solution)/shard_map/global_backward/pallas_call | solution.py:884
  383.4 24.7 %project_back.1 = (f32[1024,768]{1,0:T(8,128)}, bf16[1024,768]{1,0:T(8,128)(2,1)}, bf16[768,768]{1,0:T(8,128)(2,1)}, bf16[768,768]{1,0:T(8,128)(2,1)}, bf16[768,...) custom-call(s32[2,8]{1,0:T(2,128)} %lengths.11, s32[2]{0:T(128)} %bucket_of.11, s32[3]{0:T(128)} %pad_add_fusion.place, ...), custom_call_target="tpu_custom_call" | custom-call | flops 7247757312 | bytes 23592960 | tf_op jit(solution)/shard_map/project_back/pallas_call | solution.py:1001
  408.1 2.7 copy.49
  410.9 1.5 copy.51
  412.4 1.5 copy.53
  414.0 8.2 add.94
  422.3 7.2 add.93
  429.5 6.6 copy.57
  436.2 2.2 copy.56
  439.2 2.2 copy.50
  441.6 13.9 %reduce-scatter.45.cloned.1.call-done = bf16[384,768]{1,0:T(8,128)(2,1)} async-done(((bf16[768,768]{1,0:T(8,128)(2,1)}), bf16[384,768]{1,0:T(8,128)(2,1)}) %reduce-scatter.45.cloned.1.call-update) | async-done | bytes 589840
  455.4 2.2 copy.52
  457.7 21.9 %reduce-scatter.47.cloned.1.call-done = bf16[384,768]{1,0:T(8,128)(2,1)} async-done(((bf16[768,768]{1,0:T(8,128)(2,1)}), bf16[384,768]{1,0:T(8,128)(2,1)}) %reduce-scatter.47.cloned.1.call-update) | async-done | bytes 589840
  479.5 2.1 copy.54
  481.8 60.1 %reduce-scatter.39.cloned.1.call-done = bf16[768,1536]{1,0:T(8,128)(2,1)} async-done(((bf16[768,3072]{1,0:T(8,128)(2,1)}), bf16[768,1536]{1,0:T(8,128)(2,1)}) %reduce-scatter.39.cloned.1.call-update) | async-done | bytes 2359312 | tf_op jit(solution)/shard_map/reduce_scatter | solution.py:1036
  541.9 62.4 %reduce-scatter.51.cloned.1.call-done = bf16[384,3072]{1,0:T(8,128)(2,1)} async-done(((bf16[768,3072]{1,0:T(8,128)(2,1)}), bf16[384,3072]{1,0:T(8,128)(2,1)}) %reduce-scatter.51.cloned.1.call-update) | async-done | bytes 2359312
  604.3 4.3 copy.58
  609.6 1.2 slice.66
  610.8 3.7 collective-permute-start.2
  614.7 1.4 slice.65
  617.7 2.1 collective-permute-done.2
  619.8 1.2 maximum_bitcast_fusion.2
  621.2 41.4 %reduce-scatter.35.cloned.1.call-done = bf16[48,384]{1,0:T(8,128)(2,1)} async-done(((bf16[768,384]{1,0:T(8,128)(2,1)}), bf16[48,384]{1,0:T(8,128)(2,1)}) %reduce-scatter.35.cloned.1.call-update) | async-done | bytes 36880 | tf_op jit(solution)/shard_map/reduce_scatter | solution.py:1037
  662.6 1.4 convert_bitcast_fusion.2
  665.3 1.9 maximum_bitcast_fusion
  667.1 58.2 %reduce-scatter.27.cloned.1.call-done = bf16[64,768]{1,0:T(8,128)(2,1)} async-done(((bf16[1024,768]{1,0:T(8,128)(2,1)}), bf16[64,768]{1,0:T(8,128)(2,1)}) %reduce-scatter.27.cloned.1.call-update) | async-done | bytes 98320 | tf_op jit(solution)/shard_map/reduce_scatter | solution.py:1162
  725.3 1.1 fusion.12
  726.5 41.2 %all-reduce = (f32[3072]{0:T(1024)}, f32[768]{0:T(1024)}, f32[6,768]{1,0:T(8,128)}) all-reduce(f32[3072]{0:T(1024)S(1)} %bitcast.98, f32[768]{0:T(1024)S(1)} %add_reduce_fusion, f32[6,768]{1,0:T(8,128)S(1)} %concatenate.28), channel_id=1, replica_groups=mesh['batch'=2,'seq'=16] {'batch','seq'}, use_global_device_ids=true, to_apply=%region_20.21 | all-reduce | flops 8448 | bytes 67584 | tf_op jit(solution)/shard_map/psum | solution.py:1179
  767.7 1.7 fusion.9
  769.4 13.2 %reduce-scatter.29.cloned.1.call-done = bf16[48,384]{1,0:T(8,128)(2,1)} async-done(((bf16[768,384]{1,0:T(8,128)(2,1)}), bf16[48,384]{1,0:T(8,128)(2,1)}) %reduce-scatter.29.cloned.1.call-update) | async-done | bytes 36880 | tf_op jit(solution)/shard_map/reduce_scatter | solution.py:1037
  782.6 1.4 convert_bitcast_fusion.5
  784.0 56.5 %reduce-scatter.31.cloned.1.call-done = bf16[48,384]{1,0:T(8,128)(2,1)} async-done(((bf16[768,384]{1,0:T(8,128)(2,1)}), bf16[48,384]{1,0:T(8,128)(2,1)}) %reduce-scatter.31.cloned.1.call-update) | async-done | bytes 36880 | tf_op jit(solution)/shard_map/reduce_scatter | solution.py:1037
  840.5 1.4 convert_bitcast_fusion.4
  842.0 55.9 %reduce-scatter.33.cloned.1.call-done = bf16[48,384]{1,0:T(8,128)(2,1)} async-done(((bf16[768,384]{1,0:T(8,128)(2,1)}), bf16[48,384]{1,0:T(8,128)(2,1)}) %reduce-scatter.33.cloned.1.call-update) | async-done | bytes 36880 | tf_op jit(solution)/shard_map/reduce_scatter | solution.py:1037
  897.9 1.4 convert_bitcast_fusion.3
  899.3 64.6 %reduce-scatter.41.cloned.1.call-done = bf16[48,1536]{1,0:T(8,128)(2,1)} async-done(((bf16[768,1536]{1,0:T(8,128)(2,1)}), bf16[48,1536]{1,0:T(8,128)(2,1)}) %reduce-scatter.41.cloned.1.call-update) | async-done | bytes 147472 | tf_op jit(solution)/shard_map/reduce_scatter | solution.py:1037
  963.9 1.6 convert_bitcast_fusion
  965.6 64.0 %reduce-scatter.37.cloned.1.call-done = bf16[192,384]{1,0:T(8,128)(2,1)} async-done(((bf16[3072,384]{1,0:T(8,128)(2,1)}), bf16[192,384]{1,0:T(8,128)(2,1)}) %reduce-scatter.37.cloned.1.call-update) | async-done | bytes 147472 | tf_op jit(solution)/shard_map/reduce_scatter | solution.py:1037
  1029.6 1.6 convert_bitcast_fusion.1
  (130 shorter events, 16.1 us)
Async XLA Ops:
  7.2 45.5 %all-gather.6.cloned.1.call-start = ((), (), s32[]{:S(2)}) async-start(), calls=%async_computation.24 | async-start | bytes 1671168 | tf_op jit(solution)/shard_map/all_gather | solution.py:1083
  7.9 168.4 %reduce-scatter.25.cloned.1.call-start = ((), (), s32[]{:S(2)}) async-start(), calls=%async_computation.14 | async-start | bytes 1949696 | tf_op jit(solution)/shard_map/reduce_scatter | solution.py:1101
  9.0 11.0 %collective-permute-start = (bf16[256,768]{1,0:T(8,128)(2,1)S(1)}, bf16[256,768]{1,0:T(8,128)(2,1)S(1)}, u32[]{:S(2)}, u32[]{:S(2)}) collective-permute-start(bf16[256,768]{1,0:T(8,128)(2,1)S(1)} %slice_bitcast_fusion.3), channel_id=1, source_target_pairs={{0,1},{1,2},{2,3},{3,4},{4,5},{5,6},{6,7},{7,8},{8,9},{9,10},{10,1... | collective-permute-start | bytes 1179656 | tf_op jit(solution)/shard_map/ppermute | solution.py:1026
  85.3 3.6 copy-start.10
  85.3 3.6 copy-start.8
  119.1 1.4 copy-start.2
  119.1 1.8 copy-start.13
  119.1 226.9 %all-gather.4.cloned.1.call-start = ((), (), s32[]{:S(2)}) async-start(), calls=%async_computation.15 | async-start | bytes 1949696 | tf_op jit(solution)/shard_map/all_gather | solution.py:1139
  120.5 10.0 collective-permute-start.1
  178.9 15.0 %copy-start.6 = (bf16[64,768]{1,0:T(8,128)(2,1)S(1)}, bf16[64,768]{1,0:T(8,128)(2,1)}, u32[]{:S(2)}) copy-start(bf16[64,768]{1,0:T(8,128)(2,1)} %fusion.13.o_ref) | copy-start | bytes 294916
  193.9 1.4 copy-start.7
  196.1 240.1 %reduce-scatter.49.cloned.1.call-start = ((), (), s32[]{:S(2)}) async-start(), calls=%async_computation.28 | async-start | bytes 1769472
  236.3 63.3 %copy-start.3 = (bf16[768,768]{1,0:T(8,128)(2,1)S(1)}, bf16[768,768]{1,0:T(8,128)(2,1)}, u32[]{:S(2)}) copy-start(bf16[768,768]{1,0:T(8,128)(2,1)} %get-tuple-element.98) | copy-start | bytes 3538948
  302.7 136.5 %reduce-scatter.43.cloned.1.call-start = ((), (), s32[]{:S(2)}) async-start(), calls=%async_computation.25 | async-start | bytes 1769472
  408.1 2.8 copy-start.5
  410.8 44.6 %reduce-scatter.45.cloned.1.call-start = ((), (), s32[]{:S(2)}) async-start(), calls=%async_computation.26 | async-start | bytes 1769472
  410.9 1.5 copy-start.4
  412.4 67.2 %reduce-scatter.47.cloned.1.call-start = ((), (), s32[]{:S(2)}) async-start(), calls=%async_computation.27 | async-start | bytes 1769472
  413.9 128.0 %reduce-scatter.39.cloned.1.call-start = ((), (), s32[]{:S(2)}) async-start(), calls=%async_computation.22 | async-start | bytes 7077888 | tf_op jit(solution)/shard_map/reduce_scatter | solution.py:1036
  422.2 182.1 %reduce-scatter.51.cloned.1.call-start = ((), (), s32[]{:S(2)}) async-start(), calls=%async_computation.29 | async-start | bytes 7077888
  436.2 226.5 %reduce-scatter.35.cloned.1.call-start = ((), (), s32[]{:S(2)}) async-start(), calls=%async_computation.20 | async-start | bytes 626688 | tf_op jit(solution)/shard_map/reduce_scatter | solution.py:1037
  438.4 286.9 %reduce-scatter.27.cloned.1.call-start = ((), (), s32[]{:S(2)}) async-start(), calls=%async_computation.16 | async-start | bytes 1671168 | tf_op jit(solution)/shard_map/reduce_scatter | solution.py:1162
  439.2 343.4 %reduce-scatter.29.cloned.1.call-start = ((), (), s32[]{:S(2)}) async-start(), calls=%async_computation.17 | async-start | bytes 626688 | tf_op jit(solution)/shard_map/reduce_scatter | solution.py:1037
  441.5 399.0 %reduce-scatter.31.cloned.1.call-start = ((), (), s32[]{:S(2)}) async-start(), calls=%async_computation.18 | async-start | bytes 626688 | tf_op jit(solution)/shard_map/reduce_scatter | solution.py:1037
  457.6 440.2 %reduce-scatter.33.cloned.1.call-start = ((), (), s32[]{:S(2)}) async-start(), calls=%async_computation.19 | async-start | bytes 626688 | tf_op jit(solution)/shard_map/reduce_scatter | solution.py:1037
  481.7 482.2 %reduce-scatter.41.cloned.1.call-start = ((), (), s32[]{:S(2)}) async-start(), calls=%async_computation.23 | async-start | bytes 2506752 | tf_op jit(solution)/shard_map/reduce_scatter | solution.py:1037
  541.9 487.7 %reduce-scatter.37.cloned.1.call-start = ((), (), s32[]{:S(2)}) async-start(), calls=%async_computation.21 | async-start | bytes 2506752 | tf_op jit(solution)/shard_map/reduce_scatter | solution.py:1037
  608.6 0.9 copy-start
  609.6 6.5 copy-start.1
  610.8 9.0 collective-permute-start.2
  616.9 4.2 copy-start.16
  616.9 4.2 copy-start.19
  616.9 4.2 copy-start.15
  616.9 4.2 copy-start.18
  616.9 4.2 copy-start.11
  616.9 4.2 copy-start.12
  616.9 4.2 copy-start.14
  616.9 4.2 copy-start.17
  616.9 47.2 %collective-permute-start.3 = (bf16[256,768]{1,0:T(8,128)(2,1)}, bf16[256,768]{1,0:T(8,128)(2,1)}, u32[]{:S(2)}, u32[]{:S(2)}) collective-permute-start(bf16[256,768]{1,0:T(8,128)(2,1)} %slice.94), channel_id=1, source_target_pairs={{0,15},{1,0},{2,1},{3,2},{4,3},{5,4},{6,5},{7,6},{8,7},{9,8},{10,9... | collective-permute-start | bytes 1179656 | tf_op jit(solution)/shard_map/ppermute | solution.py:1026
  665.2 61.2 %copy-start.20 = (f32[1,768]{1,0:T(1,128)S(1)}, f32[1,768]{1,0:T(1,128)}, u32[]{:S(2)}) copy-start(f32[1,768]{1,0:T(1,128)} %get-tuple-element.107) | copy-start | bytes 9220
  665.3 61.2 %copy-start.21 = (f32[1,768]{1,0:T(1,128)S(1)}, f32[1,768]{1,0:T(1,128)}, u32[]{:S(2)}) copy-start(f32[1,768]{1,0:T(1,128)} %get-tuple-element.108) | copy-start | bytes 9220
  665.3 102.5 %copy-start.9 = (f32[64,768]{1,0:T(8,128)S(1)}, f32[64,768]{1,0:T(8,128)}, u32[]{:S(2)}) copy-start(f32[64,768]{1,0:T(8,128)} %get-tuple-element.92) | copy-start | bytes 589828
Sparse Core Ops, SparseCore 0:
  10.3 42.3 all-gather.5
  119.3 56.9 reduce-scatter.24
  196.2 39.6 all-gather.3
  302.8 19.8 reduce-scatter.48
  410.9 19.9 reduce-scatter.42
  433.6 21.7 reduce-scatter.44
  457.8 21.7 reduce-scatter.46
  481.8 59.9 reduce-scatter.38
  544.3 59.9 reduce-scatter.50
  607.7 54.8 reduce-scatter.34
  666.7 58.5 reduce-scatter.26
  728.7 53.8 reduce-scatter.28
  786.6 53.9 reduce-scatter.30
  844.0 53.8 reduce-scatter.32
  902.0 61.9 reduce-scatter.40
  967.5 62.0 reduce-scatter.36

commit v2 on v1

v2 whole, which is shorter than its diff:
```python
import functools

import jax
import jax.numpy as jnp
from jax import lax
from jax.experimental import pallas as pl
from jax.experimental.pallas import tpu as pltpu
from jax.sharding import PartitionSpec as P

HEADS = 12
HEAD_DIM = 64
PAIRS = HEADS // 2
LANES = 128
BLOCK = 512
HALF = 256
GLOBALS = 128
SLOTS = 8
FF_CHUNK = 768

norm_eps = 1e-05
masked_score = -1e30
query_scale = 0.125

SLOT_LANE = 16
GLOBAL_LANE = 32

f32 = jnp.float32
bf16 = jnp.bfloat16
VMEM_LIMIT = 60 * 1024 * 1024


def nn(left, right):
    return jnp.dot(left, right, preferred_element_type=f32)


def nt(left, right):
    return lax.dot_general(left, right, (((1,), (1,)), ((), ())), preferred_element_type=f32)


def tn(left, right):
    return lax.dot_general(left, right, (((0,), (0,)), ((), ())), preferred_element_type=f32)


def iota(shape, dim):
    return lax.broadcasted_iota(jnp.int32, shape, dim)


def stack_pair(pair):
    lane = iota((1, LANES), 1)
    low = jnp.where(lane < HEAD_DIM, 1.0, 0.0).astype(bf16)
    high = jnp.where(lane < HEAD_DIM, 0.0, 1.0).astype(bf16)
    return jnp.concatenate([pair * low, pair * high], axis=0)


def read_edges(lengths, bucket_of, place, edges):
    bucket = bucket_of[place[0]]
    total = jnp.int32(0)
    edges[0] = total
    for slot in range(SLOTS):
        total = total + lengths[bucket, slot]
        edges[slot + 1] = total


def block_start(place, rows, block):
    return place[1] * rows + block * BLOCK - HALF


def slot_present(slot, place, edges, rows, group_rows, block):
    low = edges[slot]
    high = edges[slot + 1]
    found = jnp.bool_(False)
    for part in range(BLOCK // HALF):
        start = block_start(place, rows, block) + part * HALF
        start = jnp.where(start < 0, start + group_rows, start)
        found = found | ((high > low) & (low < start + HALF) & (high > start))
    return found


def row_numbers(place, edges, rows, group_rows, block):
    place_in = block_start(place, rows, block) + iota((BLOCK, LANES), 0)
    wrapped = place_in < 0
    token = jnp.where(wrapped, place_in + group_rows, place_in)
    slot = jnp.zeros((BLOCK, LANES), jnp.int32)
    for j in range(SLOTS):
        slot = slot + jnp.where(edges[j + 1] <= token, 1, 0)
    return slot, slot + jnp.where(wrapped, SLOTS, 0)


def key_extra(slot, segment):
    lane = iota((BLOCK, LANES), 1)
    extra = jnp.where((lane < SLOT_LANE) & (lane != segment), masked_score, 0.0)
    return jnp.where(lane == GLOBAL_LANE + slot, 1.0, extra)


def query_extra(slot, segment):
    lane = iota((BLOCK, LANES), 1)
    return jnp.where((lane == segment) | (lane == SLOT_LANE + slot), 1.0, 0.0)


def global_key_extra(slot):
    lane = iota((GLOBALS, LANES), 1)
    inside = (lane >= SLOT_LANE) & (lane < SLOT_LANE + SLOTS)
    extra = jnp.where(inside & (lane != SLOT_LANE + slot), masked_score, 0.0)
    return jnp.where(lane == GLOBAL_LANE + slot, 1.0, extra)


def global_query_extra(slot):
    lane = iota((GLOBALS, LANES), 1)
    inside = (lane >= GLOBAL_LANE) & (lane < GLOBAL_LANE + SLOTS)
    return jnp.where(inside & (lane != GLOBAL_LANE + slot), masked_score, 0.0)


def normalize_rows(values):
    mean = jnp.mean(values, axis=-1, keepdims=True)
    centered = values - mean
    variance = jnp.mean(centered * centered, axis=-1, keepdims=True)
    scale = lax.rsqrt(variance + norm_eps)
    return centered * scale, scale


def norm_back(unit, scale, gain, upstream):
    inner = upstream * gain
    along = jnp.mean(inner * unit, axis=-1, keepdims=True)
    return scale * (inner - jnp.mean(inner, axis=-1, keepdims=True) - unit * along)


def gelu_parts(value):
    decay = jnp.exp(-0.5 * value * value)
    step = 1.0 / (1.0 + (0.3275911 * 0.7071067811865476) * jnp.abs(value))
    series = 1.061405429 * step - 1.453152027
    series = series * step + 1.421413741
    series = series * step - 0.284496736
    series = series * step + 0.254829592
    tail = (0.5 * series) * step * decay
    area = jnp.where(value >= 0.0, 1.0 - tail, tail)
    return area, decay * 0.3989422804014327


def full(shape):
    return pl.BlockSpec(shape, lambda *unused: (0,) * len(shape))


def once(shape):
    return pl.BlockSpec(
        shape, lambda *unused: (0,) * len(shape), pipeline_mode=pl.Buffered(buffer_count=1)
    )


def params(**more):
    return pltpu.CompilerParams(vmem_limit_bytes=VMEM_LIMIT, **more)


STAGES = 5
MESH = pl.DeviceIdType.MESH
WEIGHTS = (("core", 1), ("y", 2), ("z0", 4), ("z1", 8))


def my_place():
    batch = lax.axis_index("batch")
    seq = lax.axis_index("seq")
    bits = {"x": batch}
    partners = {"x": (1 - batch, seq)}
    for name, weight in WEIGHTS:
        bits[name] = (seq // weight) % 2
        partners[name] = (batch, seq + weight - 2 * weight * bits[name])
    return bits, partners


def meet(devices):
    barrier = pltpu.get_barrier_semaphore()
    for device in devices:
        pl.semaphore_signal(barrier, inc=1, device_id=device, device_id_type=MESH)
    pl.semaphore_wait(barrier, len(devices))


def remote(source, target, send, recv, device):
    return pltpu.make_async_remote_copy(
        src_ref=source,
        dst_ref=target,
        send_sem=send,
        recv_sem=recv,
        device_id=device,
        device_id_type=MESH,
    )


class RowGather:
    def __init__(self, ref, cut, send_sem, recv_sem, bits, partners):
        self.ref = ref
        self.cut = cut
        self.send_sem = send_sem
        self.recv_sem = recv_sem
        self.bits = bits
        self.partners = partners

    def copies(self, number):
        core, y, z0, z1 = (self.bits[name] for name in ("core", "y", "z0", "z1"))
        ref = self.ref
        rows = pl.ds(0, ref.shape[4])
        left = pl.ds(0, self.cut)
        right = pl.ds(self.cut, ref.shape[5] - self.cut)
        if number == 0:
            moves = [
                (ref.at[z1, z0, y, core, rows, left], "z1"),
                (ref.at[z1, z0, y, core, rows, right], "y"),
            ]
        elif number == 1:
            moves = [
                (ref.at[:, z0, y, core, rows, left], "z0"),
                (ref.at[z1, z0, :, core, rows, right], "z1"),
            ]
        elif number == 2:
            moves = [
                (ref.at[:, :, y, core, rows, left], "y"),
                (ref.at[:, z0, :, core, rows, right], "z0"),
            ]
        else:
            moves = [
                (ref.at[:, :, :, core, rows, left], "core"),
                (ref.at[:, :, :, core, rows, right], "core"),
            ]
        return [
            remote(
                part,
                part,
                self.send_sem.at[number, side],
                self.recv_sem.at[number, side],
                self.partners[name],
            )
            for side, (part, name) in enumerate(moves)
        ]

    def begin(self):
        for copy in self.copies(0):
            copy.start()

    def advance(self, number):
        for copy in self.copies(number):
            copy.wait_recv()
        if number < 3:
            for copy in self.copies(number + 1):
                copy.start()

    def end(self):
        for number in range(4):
            for copy in self.copies(number):
                copy.wait_send()


ORDERS = (("core", "x", "y", "z0", "z1"), ("core", "y", "x", "z0", "z1"))


class WeightSum:
    def __init__(self, sources, landings, own, send_sem, recv_sem, own_sem, out, bits, partners):
        self.sources = sources
        self.landings = landings
        self.own = own
        self.send_sem = send_sem
        self.recv_sem = recv_sem
        self.own_sem = own_sem
        self.out = out
        self.bits = bits
        self.partners = partners

    def part(self, unit, stage, other):
        name = ORDERS[unit % 2][stage]
        side = 1 - self.bits[name] if other else self.bits[name]
        if stage == 0:
            if not other and self.own is not None:
                return self.own.at[unit]
            return self.sources[unit](side)
        ref = self.landings[stage - 1].at[unit]
        if stage == 1:
            return ref.at[:, :, :, side] if name == "x" else ref.at[:, :, side]
        if stage == 2:
            return ref.at[:, :, side]
        if stage == 3:
            return ref.at[:, side]
        return ref.at[side]

    def copy(self, unit, stage):
        return remote(
            self.part(unit, stage, True),
            self.landings[stage].at[unit],
            self.send_sem.at[unit, stage],
            self.recv_sem.at[unit, stage],
            self.partners[ORDERS[unit % 2][stage]],
        )

    def own_copy(self, unit):
        return pltpu.make_async_copy(
            self.sources[unit](self.bits["core"]), self.own.at[unit], self.own_sem.at[unit]
        )

    def begin(self, unit):
        if self.own is not None:
            self.own_copy(unit).start()
        self.copy(unit, 0).start()

    def advance(self, unit, stage, stop=False):
        if stage == 0 and self.own is not None:
            self.own_copy(unit).wait()
        self.copy(unit, stage).wait_recv()
        landing = self.landings[stage].at[unit]
        kept = self.part(unit, stage, False)
        if stage < STAGES - 1:
            add_into(landing, kept)
            if not stop:
                self.copy(unit, stage + 1).start()
        else:
            rows = landing.shape[0]
            self.out[unit * rows : (unit + 1) * rows] = landing[...].astype(f32) + kept[
                ...
            ].astype(f32)

    def sent(self, unit, stage):
        self.copy(unit, stage).wait_send()


def add_into(target, more):
    def one(i, carry):
        target[i] = target[i] + more[i]
        return carry

    lax.fori_loop(0, target.shape[0], one, 0)


def sum_scratch(units, rows, lanes, with_own):
    piece = (rows, lanes)
    dma = pltpu.SemaphoreType.DMA
    shapes = [pltpu.VMEM((units, 2, 2, 2, 2) + piece, bf16)] if with_own else []
    shapes += [
        pltpu.VMEM((units, 2, 2, 2, 2) + piece, bf16),
        pltpu.VMEM((units, 2, 2, 2) + piece, bf16),
        pltpu.VMEM((units, 2, 2) + piece, bf16),
        pltpu.VMEM((units, 2) + piece, bf16),
        pltpu.VMEM((units,) + piece, bf16),
        dma((units, STAGES)),
        dma((units, STAGES)),
    ]
    return shapes + ([dma((units,))] if with_own else [])


def project_rows(rows_ref, gain_ref, offset_ref, wq_ref, wk_ref, wv_ref, outs):
    unit, unused = normalize_rows(rows_ref[...].astype(f32))
    normed = (unit * gain_ref[...] + offset_ref[...]).astype(bf16)
    outs[0][...] = normed
    outs[1][...] = (nn(normed, wq_ref[...]) * query_scale).astype(bf16)
    outs[2][...] = nn(normed, wk_ref[...]).astype(bf16)
    outs[3][...] = nn(normed, wv_ref[...]).astype(bf16)


def project_local_kernel(rows_ref, gain_ref, offset_ref, wq_ref, wk_ref, wv_ref, *outs):
    project_rows(rows_ref, gain_ref, offset_ref, wq_ref, wk_ref, wv_ref, outs)


def project_local(rows, gain, offset, wq, wk, wv):
    count, width = rows.shape
    tile = pl.BlockSpec((BLOCK, width), lambda i: (i, 0))
    return pl.pallas_call(
        project_local_kernel,
        grid=(count // BLOCK,),
        in_specs=[tile, full((1, width)), full((1, width))] + [once((width, width))] * 3,
        out_specs=[tile] * 4,
        out_shape=[jax.ShapeDtypeStruct((count, width), bf16)] * 4,
        compiler_params=params(),
        cost_estimate=pl.CostEstimate(
            flops=6 * count * width * width, bytes_accessed=12 * count * width, transcendentals=0
        ),
        name="project_local",
    )(rows, gain, offset, wq, wk, wv)


def gather_project_kernel(
    tokens_ref,
    ct_ref,
    states_ref,
    w1_ref,
    norms_ref,
    wq_ref,
    wk_ref,
    wv_ref,
    h_ref,
    q_ref,
    k_ref,
    v_ref,
    x_ref,
    ct_out_ref,
    all_ref,
    gh_ref,
    gq_ref,
    gk_ref,
    gv_ref,
    w1t_ref,
    w1s_ref,
    halo_send,
    halo_recv,
    move_sem,
    w1_sem,
    send_sem,
    recv_sem,
):
    bits, partners = my_place()
    batch = lax.axis_index("batch")
    seq = lax.axis_index("seq")
    count = lax.axis_size("seq")
    after = (batch, lax.rem(seq + 1, count))
    before = (batch, lax.rem(seq + count - 1, count))
    rows, width = tokens_ref.shape
    own = states_ref.shape[0]
    core, y, z0, z1 = (bits[name] for name in ("core", "y", "z0", "z1"))
    w1_copy = pltpu.make_async_copy(w1_ref, w1s_ref, w1_sem)
    w1_copy.start()
    ct_copy = pltpu.make_async_copy(
        ct_ref.at[pl.ds(0, rows - HALF)], ct_out_ref.at[pl.ds(HALF, rows - HALF)], move_sem
    )
    ct_copy.start()
    all_ref[z1, z0, y, core] = states_ref[...]
    meet([partners[name] for name, unused in WEIGHTS] + [before, after])
    end = pl.ds(rows - HALF, HALF)
    start = pl.ds(0, HALF)
    halo = [
        remote(
            tokens_ref.at[end], x_ref.at[start], halo_send.at[0], halo_recv.at[0], after
        ),
        remote(
            ct_ref.at[end], ct_out_ref.at[start], halo_send.at[1], halo_recv.at[1], after
        ),
    ]
    halo[0].start()

    gather = RowGather(all_ref, width // 2, send_sem, recv_sem, bits, partners)

    def project(at):
        project_rows(
            x_ref.at[at],
            norms_ref.at[0:1],
            norms_ref.at[1:2],
            wq_ref,
            wk_ref,
            wv_ref,
            [ref.at[at] for ref in (h_ref, q_ref, k_ref, v_ref)],
        )

    gather.begin()
    halo[1].start()
    x_ref[HALF:] = tokens_ref[: rows - HALF]
    project(pl.ds(HALF, HALF))
    gather.advance(0)
    project(pl.ds(2 * HALF, HALF))
    for index in range(3, rows // HALF):
        project(pl.ds(index * HALF, HALF))
    gather.advance(1)
    halo[0].wait_recv()
    project(start)
    w1_copy.wait()

    def turn(i, carry):
        at = pl.ds(pl.multiple_of(i * HALF, HALF), HALF)
        w1t_ref[at, :] = w1s_ref[:, at].T
        return carry

    lax.fori_loop(0, w1t_ref.shape[0] // HALF, turn, 0)
    gather.advance(2)
    gather.advance(3)

    def project_states(i, carry):
        at = pl.ds(pl.multiple_of(i * HALF, HALF), HALF)
        piece = all_ref[i // 2, i % 2].reshape(HALF, width)
        unit, unused = normalize_rows(piece.astype(f32))
        normed = (unit * norms_ref[2:3] + norms_ref[3:4]).astype(bf16)
        gh_ref[at, :] = normed
        gq_ref[at, :] = (nn(normed, wq_ref[...]) * query_scale).astype(bf16)
        gk_ref[at, :] = nn(normed, wk_ref[...]).astype(bf16)
        gv_ref[at, :] = nn(normed, wv_ref[...]).astype(bf16)
        return carry

    lax.fori_loop(0, 4, project_states, 0)
    ct_copy.wait()
    halo[1].wait_recv()
    for copy in halo:
        copy.wait_send()
    gather.end()


def gather_project(tokens, ct, states, w1, norms, wq, wk, wv):
    rows, width = tokens.shape
    own = states.shape[0]
    all_globals = 16 * own
    vmem = pl.BlockSpec(memory_space=pltpu.VMEM)
    anywhere = pl.BlockSpec(memory_space=pl.ANY)
    dma = pltpu.SemaphoreType.DMA
    local = jax.ShapeDtypeStruct((rows, width), bf16)
    glob = jax.ShapeDtypeStruct((all_globals, width), bf16)
    return pl.pallas_call(
        gather_project_kernel,
        in_specs=[vmem, anywhere, vmem, anywhere] + [vmem] * 4,
        out_specs=[vmem] * 5 + [anywhere] + [vmem] * 6,
        out_shape=[local] * 6
        + [jax.ShapeDtypeStruct((2, 2, 2, 2, own, width), bf16)]
        + [glob] * 4
        + [jax.ShapeDtypeStruct((w1.shape[1], width), bf16)],
        scratch_shapes=[
            pltpu.VMEM(w1.shape, bf16),
            dma((2,)),
            dma((2,)),
            dma,
            dma,
            dma((4, 2)),
            dma((4, 2)),
        ],
        compiler_params=params(collective_id=1, has_side_effects=True),
        cost_estimate=pl.CostEstimate(
            flops=6 * (rows + all_globals) * width * width,
            bytes_accessed=24 * rows * width,
            transcendentals=0,
        ),
        name="gather_project",
    )(tokens, ct, states, w1, norms, wq, wk, wv)


def project_global_kernel(
    rows_count,
    group_rows,
    lengths,
    bucket_of,
    place,
    rows_ref,
    gain_ref,
    offset_ref,
    wq_ref,
    wk_ref,
    wv_ref,
    h_ref,
    q_ref,
    k_ref,
    v_ref,
    edges,
):
    slot = pl.program_id(0)

    @pl.when(slot == 0)
    def _():
        read_edges(lengths, bucket_of, place, edges)

    needed = slot == place[2]
    for block in range(rows_count // BLOCK):
        needed = needed | slot_present(slot, place, edges, rows_count, group_rows, block)

    @pl.when(needed)
    def _():
        project_rows(
            rows_ref, gain_ref, offset_ref, wq_ref, wk_ref, wv_ref, (h_ref, q_ref, k_ref, v_ref)
        )


def project_global(scalars, rows_count, group_rows, rows, gain, offset, wq, wk, wv):
    count, width = rows.shape
    tile = pl.BlockSpec((GLOBALS, width), lambda i, *unused: (i, 0))
    return pl.pallas_call(
        functools.partial(project_global_kernel, rows_count, group_rows),
        grid_spec=pltpu.PrefetchScalarGridSpec(
            num_scalar_prefetch=3,
            grid=(SLOTS,),
            in_specs=[tile, full((1, width)), full((1, width))] + [once((width, width))] * 3,
            out_specs=[tile] * 4,
            scratch_shapes=[pltpu.SMEM((16,), jnp.int32)],
        ),
        out_shape=[jax.ShapeDtypeStruct((count, width), bf16)] * 4,
        compiler_params=params(),
        cost_estimate=pl.CostEstimate(
            flops=6 * 256 * width * width, bytes_accessed=12 * count * width, transcendentals=0
        ),
        name="project_global",
    )(*scalars, rows, gain, offset, wq, wk, wv)


def block_columns(place, edges, rows, group_rows, block, step, blocks, query_columns, key_columns):
    @pl.when(step < blocks)
    def _():
        slot_of, segment = row_numbers(place, edges, rows, group_rows, block)
        query_columns[block] = query_extra(slot_of, segment).astype(bf16)
        key_columns[block] = key_extra(slot_of, segment).astype(bf16)


def slot_line(place, edges, rows, group_rows, block):
    token = block_start(place, rows, block) + iota((1, BLOCK), 1)
    token = jnp.where(token < 0, token + group_rows, token)
    slot = jnp.zeros((1, BLOCK), jnp.int32)
    for j in range(SLOTS):
        slot = slot + jnp.where(edges[j + 1] <= token, 1, 0)
    return slot


def side_by_side(stacked):
    return stacked[:HEAD_DIM, : stacked.shape[1] // 2], stacked[HEAD_DIM:, stacked.shape[1] // 2 :]


def slot_forward_kernel(
    rows_count,
    group_rows,
    lengths,
    bucket_of,
    place,
    q_ref,
    k_ref,
    v_ref,
    gq_ref,
    gk_ref,
    gv_ref,
    far_ref,
    far_stat_ref,
    part_ref,
    part_stat_ref,
    edges,
    query_columns,
    key_columns,
    keys_ref,
    queries_ref,
    sum_ref,
):
    pair = pl.program_id(0)
    block = pl.program_id(1)
    blocks = rows_count // BLOCK
    step = pair * blocks + block

    @pl.when(step == 0)
    def _():
        read_edges(lengths, bucket_of, place, edges)

    @pl.when(block == 0)
    def _():
        sum_ref[...] = jnp.zeros_like(sum_ref)
        part_stat_ref[...] = jnp.broadcast_to(
            jnp.where(iota((8, GLOBALS), 0) < 2, masked_score, 0.0), part_stat_ref.shape
        )

    block_columns(
        place, edges, rows_count, group_rows, block, step, blocks, query_columns, key_columns
    )
    extra = query_columns[block]
    keys_ref[:, :LANES] = k_ref[...]
    keys_ref[:, LANES:] = key_columns[block]
    queries_ref[:, :LANES] = stack_pair(q_ref[...])
    queries_ref[:BLOCK, LANES:] = extra
    queries_ref[BLOCK:, LANES:] = extra
    line = slot_line(place, edges, rows_count, group_rows, block)
    both_lines = jnp.concatenate([line, line], 1)

    def add(slot, keys, values):
        at = pl.ds(pl.multiple_of(slot * GLOBALS, GLOBALS), GLOBALS)
        extra = global_query_extra(slot).astype(bf16)
        queries = jnp.concatenate(
            [stack_pair(gq_ref[at, :]), jnp.concatenate([extra, extra], 0)], axis=1
        )
        score = nt(keys, queries)
        stat = part_stat_ref[slot, 0]
        old = jnp.concatenate([stat[0:1], stat[1:2]], axis=1)
        peak = jnp.maximum(old, jnp.max(score, axis=0, keepdims=True))
        weights = jnp.exp(score - peak)
        keep = jnp.exp(old - peak)
        total = jnp.concatenate([stat[2:3], stat[3:4]], axis=1) * keep + jnp.sum(
            weights, axis=0, keepdims=True
        )
        part_stat_ref[slot, 0] = jnp.concatenate(
            [
                peak[:, :GLOBALS],
                peak[:, GLOBALS:],
                total[:, :GLOBALS],
                total[:, GLOBALS:],
                jnp.zeros((4, GLOBALS), f32),
            ],
            axis=0,
        )
        low, high = side_by_side(tn(values, weights.astype(bf16)))
        sum_ref[slot, :HEAD_DIM] = sum_ref[slot, :HEAD_DIM] * keep[:, :GLOBALS] + low
        sum_ref[slot, HEAD_DIM:] = sum_ref[slot, HEAD_DIM:] * keep[:, GLOBALS:] + high

    far_ref[...] = jnp.zeros_like(far_ref)
    far_stat_ref[...] = jnp.zeros_like(far_stat_ref)

    def one_slot(slot, carry):
        @pl.when(slot_present(slot, place, edges, rows_count, group_rows, block))
        def _():
            add(slot, keys_ref[...], v_ref[...])
            at = pl.ds(pl.multiple_of(slot * GLOBALS, GLOBALS), GLOBALS)
            slot_keys = jnp.concatenate([gk_ref[at, :], global_key_extra(slot).astype(bf16)], 1)
            score = nt(slot_keys, queries_ref[...])
            peak = jnp.max(score, axis=0, keepdims=True)
            weights = jnp.exp(score - peak)
            total = jnp.sum(weights, axis=0, keepdims=True)
            mine = both_lines == slot
            far_stat_ref[0, 0, 0:1] = jnp.where(mine, peak, far_stat_ref[0, 0, 0:1])
            far_stat_ref[0, 0, 1:2] = jnp.where(mine, total, far_stat_ref[0, 0, 1:2])
            low, high = side_by_side(tn(gv_ref[at, :], weights.astype(bf16)))
            here = line == slot
            far_ref[:HEAD_DIM] = jnp.where(here, low, far_ref[:HEAD_DIM])
            far_ref[HEAD_DIM:] = jnp.where(here, high, far_ref[HEAD_DIM:])

        return carry

    lax.fori_loop(0, SLOTS, one_slot, 0)

    @pl.when((block == blocks - 1) & (place[2] >= 0))
    def _():
        slot = place[2]
        at = pl.ds(pl.multiple_of(slot * GLOBALS, GLOBALS), GLOBALS)
        keys = jnp.concatenate([gk_ref[at, :], global_key_extra(slot).astype(bf16)], axis=1)
        add(slot, keys, gv_ref[at, :])

    @pl.when(block == blocks - 1)
    def _():
        part_ref[:, 0] = sum_ref[...].astype(bf16)


def line_spec():
    return pl.BlockSpec((1, 1, 8, 2 * BLOCK), lambda p, b, *unused: (p, b, 0, 0))


def column_scratch(blocks):
    return [pltpu.SMEM((16,), jnp.int32)] + [pltpu.VMEM((blocks, BLOCK, LANES), bf16)] * 2


def slot_forward(scalars, rows_count, group_rows, q, k, v, gq, gk, gv):
    blocks = rows_count // BLOCK
    all_globals, width = gq.shape
    block_spec = pl.BlockSpec((BLOCK, LANES), lambda p, b, *unused: (b, p))
    pair_spec = pl.BlockSpec((all_globals, LANES), lambda p, b, *unused: (0, p))
    return pl.pallas_call(
        functools.partial(slot_forward_kernel, rows_count, group_rows),
        grid_spec=pltpu.PrefetchScalarGridSpec(
            num_scalar_prefetch=3,
            grid=(PAIRS, blocks),
            in_specs=[block_spec] * 3 + [pair_spec] * 3,
            out_specs=[
                pl.BlockSpec((LANES, BLOCK), lambda p, b, *unused: (p, b)),
                line_spec(),
                pl.BlockSpec((SLOTS, 1, LANES, GLOBALS), lambda p, b, *unused: (0, p, 0, 0)),
                pl.BlockSpec((SLOTS, 1, 8, GLOBALS), lambda p, b, *unused: (0, p, 0, 0)),
            ],
            scratch_shapes=column_scratch(blocks)
            + [
                pltpu.VMEM((BLOCK, 2 * LANES), bf16),
                pltpu.VMEM((2 * BLOCK, 2 * LANES), bf16),
                pltpu.VMEM((SLOTS, LANES, GLOBALS), f32),
            ],
        ),
        out_shape=[
            jax.ShapeDtypeStruct((width, rows_count), f32),
            jax.ShapeDtypeStruct((PAIRS, blocks, 8, 2 * BLOCK), f32),
            jax.ShapeDtypeStruct((SLOTS, PAIRS, LANES, GLOBALS), bf16),
            jax.ShapeDtypeStruct((SLOTS, PAIRS, 8, GLOBALS), f32),
        ],
        compiler_params=params(),
        cost_estimate=pl.CostEstimate(
            flops=8 * 4 * rows_count * GLOBALS * width,
            bytes_accessed=20 * all_globals * width,
            transcendentals=2 * HEADS * rows_count * GLOBALS,
        ),
        name="slot_forward",
    )(*scalars, q, k, v, gq, gk, gv)


def merge_parts(stat, sums, more_stat, more_sums):
    peak = jnp.maximum(stat[0:2], more_stat[0:2])
    keep = jnp.exp(stat[0:2] - peak)
    take = jnp.exp(more_stat[0:2] - peak)
    total = stat[2:4] * keep + more_stat[2:4] * take
    low = sums[:HEAD_DIM].astype(f32) * keep[0:1] + more_sums[:HEAD_DIM].astype(f32) * take[0:1]
    high = sums[HEAD_DIM:].astype(f32) * keep[1:2] + more_sums[HEAD_DIM:].astype(f32) * take[1:2]
    return (
        jnp.concatenate([peak, total, jnp.zeros((4, GLOBALS), f32)], 0),
        jnp.concatenate([low, high], 0),
    )


class SlotSum:
    ORDER = ("core", "y", "z0", "z1")

    def __init__(self, source, sums, stats, send_sem, recv_sem, bits, partners):
        self.source = source
        self.sums = sums
        self.stats = stats
        self.send_sem = send_sem
        self.recv_sem = recv_sem
        self.bits = bits
        self.partners = partners

    def held(self, stage, other):
        bit = self.bits[self.ORDER[stage]]
        side = 1 - bit if other else bit
        if stage == 0:
            return self.source(side)
        index = ((), (slice(None), slice(None)), (slice(None),), ())[stage] + (side,)
        return self.sums[stage - 1].at[index], self.stats[stage - 1].at[index]

    def copies(self, stage):
        partner = self.partners[self.ORDER[stage]]
        sums, stat = self.held(stage, True)
        return (
            remote(
                sums,
                self.sums[stage],
                self.send_sem.at[stage, 0],
                self.recv_sem.at[stage, 0],
                partner,
            ),
            remote(
                stat,
                self.stats[stage],
                self.send_sem.at[stage, 1],
                self.recv_sem.at[stage, 1],
                partner,
            ),
        )

    def begin(self, stage):
        for copy in self.copies(stage):
            copy.start()

    def merge(self, stage, kept=None):
        for copy in self.copies(stage):
            copy.wait_recv()
        sums, stat = self.held(stage, False) if kept is None else kept
        lead = self.sums[stage].shape[:-3]
        total = 1
        for size in lead:
            total = total * size

        def one(number, carry):
            index = []
            left = number
            for size in reversed(lead):
                index.append(left % size)
                left = left // size
            index = tuple(reversed(index))
            for which in range(PAIRS // 2):
                spot = index + (which,)
                new_stat, new_sums = merge_parts(
                    self.stats[stage][spot], self.sums[stage][spot], stat[spot], sums[spot]
                )
                self.stats[stage][spot] = new_stat
                self.sums[stage][spot] = new_sums.astype(bf16)
            return carry

        lax.fori_loop(0, total, one, 0)

    def sent(self, stage):
        for copy in self.copies(stage):
            copy.wait_send()


def local_forward_kernel(
    talk,
    rows_count,
    group_rows,
    lengths,
    bucket_of,
    place,
    q_ref,
    k_ref,
    v_ref,
    far_ref,
    far_stat_ref,
    *refs,
):
    if talk:
        part_ref, part_stat_ref, o_ref, line_ref, half_ref, half_stat_ref = refs[:6]
        own_ref, own_stat_ref = refs[6:8]
        sums_refs = refs[8:10]
        stat_refs = refs[10:12]
        edges, query_columns, key_columns, send_sem, recv_sem, own_sem = refs[12:]
    else:
        o_ref, line_ref, edges, query_columns, key_columns = refs
    pair = pl.program_id(0)
    block = pl.program_id(1)
    blocks = rows_count // BLOCK
    step = pair * blocks + block

    @pl.when(step == 0)
    def _():
        read_edges(lengths, bucket_of, place, edges)

    if talk:
        bits, partners = my_place()
        slot_sum = SlotSum(
            lambda side: (part_ref.at[:, :, :, side], part_stat_ref.at[:, :, :, side]),
            sums_refs,
            stat_refs,
            send_sem,
            recv_sem,
            bits,
            partners,
        )
        own_parts = slot_sum.held(0, False)
        own_copies = [
            pltpu.make_async_copy(own_parts[0], own_ref, own_sem.at[0]),
            pltpu.make_async_copy(own_parts[1], own_stat_ref, own_sem.at[1]),
        ]

        @pl.when(step == 0)
        def _():
            meet([partners["core"], partners["y"]])
            for copy in own_copies:
                copy.start()
            slot_sum.begin(0)

        @pl.when(step == 3)
        def _():
            for copy in own_copies:
                copy.wait()
            slot_sum.merge(0, (own_ref, own_stat_ref))
            slot_sum.begin(1)

        @pl.when(step == PAIRS * blocks - 1)
        def _():
            slot_sum.merge(1)
            half_ref[...] = sums_refs[1][...]
            half_stat_ref[...] = stat_refs[1][...]
            slot_sum.sent(0)
            slot_sum.sent(1)

    block_columns(
        place, edges, rows_count, group_rows, block, step, blocks, query_columns, key_columns
    )
    extra = query_columns[block]
    queries = jnp.concatenate(
        [stack_pair(q_ref[...]), jnp.concatenate([extra, extra], 0)], axis=1
    )
    keys = jnp.concatenate([k_ref[...], key_columns[block]], axis=1)
    score = nt(keys, queries)
    far_peak = far_stat_ref[0, 0, 0:1]
    peak = jnp.maximum(jnp.max(score, axis=0, keepdims=True), far_peak)
    weights = jnp.exp(score - peak)
    far_keep = jnp.exp(far_peak - peak)
    total = jnp.sum(weights, axis=0, keepdims=True) + far_stat_ref[0, 0, 1:2] * far_keep
    low, high = side_by_side(tn(v_ref[...], weights.astype(bf16)))
    low = (low + far_ref[:HEAD_DIM] * far_keep[:, :BLOCK]) / total[:, :BLOCK]
    high = (high + far_ref[HEAD_DIM:] * far_keep[:, BLOCK:]) / total[:, BLOCK:]
    o_ref[...] = jnp.concatenate([low, high], 0).T.astype(bf16)
    line_ref[0, 0] = jnp.broadcast_to(peak + jnp.log(total), (8, 2 * BLOCK))


def local_forward(talk, scalars, rows_count, group_rows, q, k, v, far, far_stat, part, part_stat):
    blocks = rows_count // BLOCK
    width = q.shape[1]
    block_spec = pl.BlockSpec((BLOCK, LANES), lambda p, b, *unused: (b, p))
    operands = [q, k, v, far, far_stat]
    in_specs = [block_spec] * 3 + [
        pl.BlockSpec((LANES, BLOCK), lambda p, b, *unused: (p, b)),
        line_spec(),
    ]
    out_specs = [block_spec, line_spec()]
    out_shape = [
        jax.ShapeDtypeStruct((rows_count, width), bf16),
        jax.ShapeDtypeStruct((PAIRS, blocks, 8, 2 * BLOCK), f32),
    ]
    scratch = []
    more = {}
    edges = column_scratch(blocks)
    if talk:
        cut = (2, 2, 2, 2, PAIRS // 2)
        operands += [part.reshape(cut + part.shape[2:]), part_stat.reshape(cut + part_stat.shape[2:])]
        in_specs += [pl.BlockSpec(memory_space=pl.ANY)] * 2
        shapes = [
            (2, 2, PAIRS // 2, LANES, GLOBALS),
            (2, 2, PAIRS // 2, 8, GLOBALS),
        ]
        out_specs += [full(shape) for shape in shapes]
        out_shape += [
            jax.ShapeDtypeStruct(shapes[0], bf16),
            jax.ShapeDtypeStruct(shapes[1], f32),
        ]
        leads = [(2, 2, 2), (2, 2, 2), (2, 2)]
        sums = [pltpu.VMEM(lead + shapes[0][2:], bf16) for lead in leads]
        stats = [pltpu.VMEM(lead + shapes[1][2:], f32) for lead in leads]
        dma = pltpu.SemaphoreType.DMA
        scratch = [sums[0], stats[0]] + sums[1:] + stats[1:]
        edges += [dma((2, 2)), dma((2, 2)), dma((2,))]
        more = {"collective_id": 2, "has_side_effects": True}
    return pl.pallas_call(
        functools.partial(local_forward_kernel, talk, rows_count, group_rows),
        grid_spec=pltpu.PrefetchScalarGridSpec(
            num_scalar_prefetch=3,
            grid=(PAIRS, blocks),
            in_specs=in_specs,
            out_specs=out_specs,
            scratch_shapes=scratch + edges,
        ),
        out_shape=out_shape,
        compiler_params=params(**more),
        cost_estimate=pl.CostEstimate(
            flops=16 * rows_count * BLOCK * width,
            bytes_accessed=16 * rows_count * width,
            transcendentals=HEADS * rows_count * BLOCK,
        ),
        name="local_forward",
    )(*scalars, *operands)


def put_grouped(ref, value):
    seq, batch, rows, lanes = ref.shape
    for part in range(batch):
        piece = value[:, part * lanes : (part + 1) * lanes].astype(bf16)
        ref[:, part] = piece.reshape(seq, rows, lanes)


def put_unit(ref, value):
    batch, rows, lanes = ref.shape[4:]
    for part in range(batch):
        piece = value[:, part * lanes : (part + 1) * lanes].astype(bf16)
        ref[:, :, :, :, part] = piece.reshape(ref.shape[:4] + (rows, lanes))


TICKS = 3
DELAYS = (0, 2, 3, 4, 6)


def branch_kernel(
    tile,
    talk,
    x_ref,
    o_ref,
    ct_ref,
    gx_ref,
    go_in_ref,
    gstat_in_ref,
    gct_ref,
    wo_ref,
    w1_ref,
    b1_ref,
    w2_ref,
    b2_ref,
    norms_ref,
    z_ref,
    dy_ref,
    do_ref,
    gz_ref,
    gdy_ref,
    gdo_ref,
    dwo_ref,
    db1_ref,
    db2_ref,
    dgain_ref,
    doffset_ref,
    first_ref,
    second_ref,
    *refs,
):
    if talk:
        message_ref, rest_ref = refs[:2]
        refs = refs[2:]
    os_ref, cts_ref, y_ref, h_ref, z_sum_ref, dh_ref, dft_ref, a_ref, du_ref, load_sem = refs[:10]
    refs = refs[10:]
    step = pl.program_id(0)
    steps = pl.num_programs(0)
    count, width = x_ref.shape
    own = gx_ref.shape[0]
    extra = os_ref.shape[0] - count
    tiles = count // tile
    tail = pl.ds(count, extra)

    def rows_at(i):
        return pl.ds(i * tile, tile)

    def padded(value):
        return jnp.concatenate([value, jnp.zeros((extra - own, width), value.dtype)], axis=0)

    if talk:
        units_ref = refs[0]
        landings = refs[1:6]
        send_sem, recv_sem = refs[6:8]
        half_ref, half_stat_ref = refs[8:10]
        slot_sums = refs[10:12]
        slot_stats = refs[12:14]
        turned_ref, go_land, gstat_land, stat_ref, slot_send, slot_recv = refs[14:]
        last_step = 4
        bits, partners = my_place()
        core = bits["core"]
        chunks = last_step - 1
        slots = units_ref.shape[0]
        plan = [
            (TICKS * chunk + DELAYS[stage], chunk, stage)
            for chunk in range(chunks)
            for stage in range(STAGES if chunk < chunks - 1 else 2)
        ]

        def source(unit):
            return lambda side: units_ref.at[unit % slots, :, :, :, side]

        engine = WeightSum(
            [source(unit) for unit in range(2 * chunks)],
            landings,
            None,
            send_sem,
            recv_sem,
            None,
            first_ref,
            bits,
            partners,
        )

        def advance(tick):
            for when, chunk, stage in sorted(plan, key=lambda entry: -entry[2]):
                if when == tick:
                    for unit in (2 * chunk, 2 * chunk + 1):
                        engine.advance(unit, stage, stop=chunk == chunks - 1 and stage == 1)

        def tick_at(position):
            for number in range(1, last_step):
                tick = TICKS * (number - 1) + position

                @pl.when(step == number)
                def _():
                    advance(tick)

        slot_sum = SlotSum(
            None,
            (None, half_ref) + tuple(slot_sums),
            (None, half_stat_ref) + tuple(slot_stats),
            slot_send,
            slot_recv,
            bits,
            partners,
        )
        half_pairs = PAIRS // 2
        lanes = half_pairs * LANES
        my_lanes = pl.ds(pl.multiple_of(core * lanes, LANES), lanes)

        def final_copies():
            theirs = pl.ds(pl.multiple_of((1 - core) * own, own), own)
            return (
                remote(
                    turned_ref.at[theirs],
                    go_land.at[:, my_lanes],
                    slot_send.at[4, 0],
                    slot_recv.at[4, 0],
                    partners["core"],
                ),
                remote(
                    gstat_land.at[core],
                    gstat_land.at[core],
                    slot_send.at[4, 1],
                    slot_recv.at[4, 1],
                    partners["core"],
                ),
            )

        def finish_slots():
            slot_sum.merge(3)
            for which in range(half_pairs):
                stat = slot_stats[1][which]
                total = stat[2:4]
                sums = slot_sums[1][which].astype(f32)
                mean = jnp.concatenate(
                    [sums[:HEAD_DIM] / total[0:1], sums[HEAD_DIM:] / total[1:2]], 0
                )
                turned_ref[:, which * LANES : (which + 1) * LANES] = mean.T.astype(bf16)
                whole = stat[0:2] + jnp.log(total)
                gstat_land[core, which] = jnp.concatenate(
                    [whole, jnp.zeros((6, GLOBALS), f32)], 0
                )
            mine = pl.ds(pl.multiple_of(core * own, own), own)
            go_land[:, my_lanes] = turned_ref[mine, :]
            for copy in final_copies():
                copy.start()

        def put_message():
            product = gdo_ref[...].astype(f32) * go_land[...].astype(f32)
            head_of = iota((width, LANES), 0) // HEAD_DIM == iota((width, LANES), 1)
            head_of = jnp.where(head_of, 1.0, 0.0).astype(bf16)
            first = product.astype(bf16)
            second = (product - first.astype(f32)).astype(bf16)
            centre = nn(first, head_of) + nn(second, head_of)
            lines = [gstat_land[half, which, 0:2] for half in (0, 1) for which in range(half_pairs)]
            lines = jnp.concatenate(lines + [jnp.zeros((LANES - HEADS, GLOBALS), f32)], 0)
            stat_ref[...] = lines.T
            total = stat_ref[pl.ds(pl.multiple_of(core * own, own), own), :]
            spread = jnp.zeros((own, LANES), f32)
            for number, value in enumerate((total, centre)):
                for piece in range(3):
                    low = value.astype(bf16)
                    value = value - low.astype(f32)
                    start_lane = (3 * number + piece) * HEADS
                    source_lane = iota((LANES, LANES), 0)
                    moved = iota((LANES, LANES), 1) == source_lane + start_lane
                    moved = jnp.where(moved & (source_lane < HEADS), 1.0, 0.0).astype(bf16)
                    spread = spread + nn(low, moved)
            message_ref[:, :width] = gdo_ref[...]
            message_ref[:, width:] = spread.astype(bf16)

    else:

        def tick_at(position):
            pass

    loads = [
        pltpu.make_async_copy(o_ref, os_ref.at[pl.ds(0, count)], load_sem.at[0]),
        pltpu.make_async_copy(ct_ref, cts_ref.at[pl.ds(0, count)], load_sem.at[1]),
    ]

    def start(at, size, x, sums):
        y = x.astype(f32) + nn(os_ref[at, :], wo_ref[...])
        unit, unused = normalize_rows(y)
        h_ref[at, :] = (unit * norms_ref[4:5] + norms_ref[5:6]).astype(bf16)
        y_ref[at, :] = y
        sums[...] = y + b2_ref[...]
        dh_ref[at, :] = jnp.zeros((size, width), f32)

    @pl.when(step == 0)
    def _():
        for load in loads:
            load.start()
        if talk:
            half_ref[...] = go_in_ref[...]
            half_stat_ref[...] = gstat_in_ref[...]
            meet([partners[name] for name in ORDERS[0]])
            slot_sum.begin(2)
        cts_ref[count:] = padded(gct_ref[...])
        loads[0].wait()

        def start_tile(i, carry):
            at = pl.ds(pl.multiple_of(i * tile, tile), tile)
            start(at, tile, x_ref[at, :], dy_ref.at[at])
            return carry

        lax.fori_loop(0, tiles, start_tile, 0)
        loads[1].wait()
        dft_ref[...] = cts_ref[...].T
        if talk:
            slot_sum.merge(2)
            slot_sum.begin(3)

    db1_ref[...] = jnp.zeros_like(db1_ref)
    w1 = w1_ref[...].reshape(width, width)
    w2 = w2_ref[...].reshape(width, width)

    def chunk_of(at, sums):
        u = nt(h_ref[at, :], w1) + b1_ref[0]
        da = nt(cts_ref[at, :], w2)
        area, density = gelu_parts(u)
        a = (u * area).astype(bf16)
        du = (da * (area + u * density)).astype(bf16)
        a_ref[at, :] = a
        du_ref[at, :] = du
        db1_ref[0] += jnp.sum(du.astype(f32), axis=0, keepdims=True)
        sums[...] = sums[...] + nn(a, w2)
        dh_ref[at, :] = dh_ref[at, :] + nn(du, w1)

    chunk_of(rows_at(0), dy_ref.at[rows_at(0)])
    if talk:

        @pl.when(step == 0)
        def _():
            finish_slots()

    tick_at(0)
    for i in range(1, tiles):
        chunk_of(rows_at(i), dy_ref.at[rows_at(i)])

    @pl.when(step == 0)
    def _():
        if talk:
            for copy in final_copies():
                copy.wait_recv()
            os_ref[count:] = padded(go_land[...])
        else:
            os_ref[count:] = padded(go_in_ref[...])
        start(tail, extra, padded(gx_ref[...]), z_sum_ref)

    chunk_of(tail, z_sum_ref)
    tick_at(1)
    dw1 = tn(du_ref[...], h_ref[...])
    dw2 = nn(dft_ref[...], a_ref[...])
    if talk:
        for number in range(chunks):

            @pl.when(step == number)
            def _():
                for which, value in ((0, dw1), (1, dw2)):
                    unit = 2 * number + which
                    if unit >= slots:
                        engine.sent(unit - slots, 0)
                    put_unit(units_ref.at[unit % slots], value)

        @pl.when(step == chunks)
        def _():
            put_unit(second_ref.at[0], dw1)
            put_unit(second_ref.at[1], dw2)

        tick_at(2)
        for number in range(chunks):

            @pl.when(step == number)
            def _():
                engine.begin(2 * number)
                engine.begin(2 * number + 1)

    else:
        first_ref[...] = dw1.astype(bf16)
        second_ref[...] = dw2.astype(bf16)

    @pl.when(step == steps - 1)
    def _():
        db2_ref[...] = jnp.zeros_like(db2_ref)
        dgain_ref[...] = jnp.zeros_like(dgain_ref)
        doffset_ref[...] = jnp.zeros_like(doffset_ref)

        def finish(at, size, sums, put):
            z = sums[...].astype(bf16)
            unit, scale = normalize_rows(y_ref[at, :])
            dh = dh_ref[at, :]
            ct = cts_ref[at, :].astype(f32)
            dy = ct + norm_back(unit, scale, norms_ref[4:5], dh)
            db2_ref[...] += jnp.sum(ct, axis=0, keepdims=True)
            doffset_ref[...] += jnp.sum(dh, axis=0, keepdims=True)
            dgain_ref[...] += jnp.sum(dh * unit, axis=0, keepdims=True)
            low = dy.astype(bf16)
            h_ref[at, :] = low
            put(z, dy, nt(low, wo_ref[...]).astype(bf16))

        def finish_tile(i, carry):
            at = pl.ds(pl.multiple_of(i * tile, tile), tile)

            def put(z, dy, do):
                z_ref[at, :] = z
                dy_ref[at, :] = dy
                do_ref[at, :] = do

            finish(at, tile, dy_ref.at[at], put)
            return carry

        lax.fori_loop(0, tiles, finish_tile, 0)

        def put_tail(z, dy, do):
            gz_ref[...] = z[:own]
            gdy_ref[...] = dy[:own]
            gdo_ref[...] = do[:own]

        finish(tail, extra, z_sum_ref, put_tail)
        if talk:
            put_message()
        dwo = tn(h_ref[...], os_ref[...])
        if talk:
            put_grouped(dwo_ref, dwo)
            advance(TICKS * chunks)
            rest_ref[...] = landings[1][2 * chunks - 2 :]
            for when, chunk, stage in plan:
                for unit in (2 * chunk, 2 * chunk + 1):
                    if stage > 0 or unit + slots >= 2 * chunks:
                        engine.sent(unit, stage)
            slot_sum.sent(2)
            slot_sum.sent(3)
            for copy in final_copies():
                copy.wait_send()
        else:
            dwo_ref[...] = dwo.astype(bf16)


def branch(grid_of, x, o, ct, gx, go, gstat, gct, wo, w1t, b1, w2, b2, norms):
    count, width = x.shape
    own = gx.shape[0]
    hidden = w2.shape[0]
    steps = hidden // FF_CHUNK
    total = count + -(-own // LANES) * LANES
    row = once((count, width))
    few = once((own, width))
    line = full((1, width))
    anywhere = pl.BlockSpec(memory_space=pl.ANY)
    scratch = []
    more = {}
    if grid_of is None:
        weight_spec = pl.BlockSpec((FF_CHUNK, width), lambda j: (j, 0))
        b1 = b1.reshape(steps, 1, FF_CHUNK)
        dw_shapes = [(hidden, width), (width, hidden)]
        dw_types = [bf16, bf16]
        dw_specs = [weight_spec, pl.BlockSpec((width, FF_CHUNK), lambda j: (0, j))]
        dwo_shape = (width, width)
    else:
        seq, batch = grid_of
        rows, lanes = width // seq, width // batch
        weight_spec = pl.BlockSpec((seq, 1, rows, width), lambda j: (0, j, 0, 0))
        w1t = w1t.reshape(seq, steps, rows, width)
        w2 = w2.reshape(seq, steps, rows, width)
        b1 = b1.reshape(seq, steps, rows).transpose(1, 0, 2).reshape(steps, 1, FF_CHUNK)
        units = 2 * (steps - 1)
        sums, stats = go.shape[2:], gstat.shape[2:]
        dw_shapes = [
            ((units - 2) * rows, lanes),
            (2, 2, 2, 2, 2, batch, rows, lanes),
            (own, width + LANES),
            (2, 2, 2, 2, rows, lanes),
        ]
        dw_types = [f32, bf16, bf16, bf16]
        dw_specs = [once(shape) for shape in dw_shapes]
        dwo_shape = (seq, batch, rows, lanes)
        dma = pltpu.SemaphoreType.DMA
        scratch = (
            [pltpu.VMEM((4,) + dw_shapes[1][1:], bf16)]
            + sum_scratch(units, rows, lanes, False)
            + [
                pltpu.VMEM(go.shape, bf16),
                pltpu.VMEM(gstat.shape, f32),
                pltpu.VMEM((2,) + sums, bf16),
                pltpu.VMEM(sums, bf16),
                pltpu.VMEM((2,) + stats, f32),
                pltpu.VMEM(stats, f32),
                pltpu.VMEM((GLOBALS, PAIRS // 2 * LANES), bf16),
                pltpu.VMEM((own, width), bf16),
                pltpu.VMEM((2,) + stats, f32),
                pltpu.VMEM((GLOBALS, LANES), f32),
                dma((5, 2)),
                dma((5, 2)),
            ]
        )
        more = {"collective_id": 3, "has_side_effects": True}
    out = pl.pallas_call(
        functools.partial(branch_kernel, BLOCK, grid_of is not None),
        grid=(steps,),
        in_specs=[
            row,
            anywhere,
            anywhere,
            few,
            once(go.shape),
            once(gstat.shape),
            few,
            once((width, width)),
            weight_spec,
            pl.BlockSpec((1, 1, FF_CHUNK), lambda j: (j, 0, 0)),
            weight_spec,
            line,
            full(norms.shape),
        ],
        out_specs=[row, row, row, few, few, few]
        + [once(dwo_shape), pl.BlockSpec((1, 1, FF_CHUNK), lambda j: (j, 0, 0)), line, line, line]
        + dw_specs,
        out_shape=[
            jax.ShapeDtypeStruct((count, width), bf16),
            jax.ShapeDtypeStruct((count, width), f32),
            jax.ShapeDtypeStruct((count, width), bf16),
            jax.ShapeDtypeStruct((own, width), bf16),
            jax.ShapeDtypeStruct((own, width), f32),
            jax.ShapeDtypeStruct((own, width), bf16),
            jax.ShapeDtypeStruct(dwo_shape, bf16),
            jax.ShapeDtypeStruct((steps, 1, FF_CHUNK), f32),
            jax.ShapeDtypeStruct((1, width), f32),
            jax.ShapeDtypeStruct((1, width), f32),
            jax.ShapeDtypeStruct((1, width), f32),
        ]
        + [jax.ShapeDtypeStruct(shape, kind) for shape, kind in zip(dw_shapes, dw_types)],
        scratch_shapes=[
            pltpu.VMEM((total, width), bf16),
            pltpu.VMEM((total, width), bf16),
            pltpu.VMEM((total, width), f32),
            pltpu.VMEM((total, width), bf16),
            pltpu.VMEM((total - count, width), f32),
            pltpu.VMEM((total, width), f32),
            pltpu.VMEM((width, total), bf16),
            pltpu.VMEM((total, FF_CHUNK), bf16),
            pltpu.VMEM((total, FF_CHUNK), bf16),
            pltpu.SemaphoreType.DMA((2,)),
        ]
        + scratch,
        compiler_params=params(**more),
        cost_estimate=pl.CostEstimate(
            flops=6 * total * width * (2 * hidden + width),
            bytes_accessed=8 * width * hidden + 16 * total * width,
            transcendentals=2 * total * hidden,
        ),
        name="branch",
    )(x, o, ct, gx, go, gstat, gct, wo, w1t, b1, w2, b2, norms)
    db1 = out[7].reshape(steps, FF_CHUNK)
    if grid_of is not None:
        db1 = db1.reshape(steps, seq, rows).transpose(1, 0, 2).reshape(-1, width)
    return [*out[:7], db1, *out[8:]]


def local_backward_kernel(
    talk,
    rows_count,
    group_rows,
    lengths,
    bucket_of,
    place,
    q_ref,
    k_ref,
    v_ref,
    do_ref,
    o_ref,
    line_ref,
    *refs,
):
    if talk:
        message_ref, rest_ref, last_ref, dwo_ref = refs[:4]
        refs = refs[4:]
    dq_ref, dk_ref, dv_ref, centre_ref = refs[:4]
    refs = refs[4:]
    if talk:
        everyone_ref, sums_ref, rest_out_ref = refs[:3]
        refs = refs[3:]
    edges, query_columns, key_columns = refs[:3]
    pair = pl.program_id(0)
    block = pl.program_id(1)
    blocks = rows_count // BLOCK
    step = pair * blocks + block

    @pl.when(step == 0)
    def _():
        read_edges(lengths, bucket_of, place, edges)

    if talk:
        all_ref, gather_send, gather_recv, own_ref = refs[3:7]
        landings = refs[7:12]
        send_sem, recv_sem, own_sem = refs[12:]
        bits, partners = my_place()
        gather = RowGather(all_ref, 3 * LANES, gather_send, gather_recv, bits, partners)
        engine = WeightSum(
            [
                None,
                None,
                lambda side: last_ref.at[0, :, :, :, side],
                lambda side: last_ref.at[1, :, :, :, side],
                lambda side: dwo_ref.at[:, :, :, side],
            ],
            landings,
            own_ref,
            send_sem,
            recv_sem,
            own_sem,
            sums_ref,
            bits,
            partners,
        )
        plan = {
            1: [(2, 0), (3, 0), (4, 0)],
            3: [(0, 2), (1, 2)],
            6: [(0, 3), (1, 3)],
            11: [(0, 4), (1, 4), (2, 1), (3, 1), (4, 1)],
        }
        gather_plan = {2: 0, 5: 1, 8: 2, 11: 3}

        @pl.when(step == 0)
        def _():
            all_ref[bits["z1"], bits["z0"], bits["y"], bits["core"]] = message_ref[...]
            landings[1][:2] = rest_ref[...]
            meet([partners[name] for name in ORDERS[0]])
            gather.begin()
            for unit in (2, 3, 4):
                engine.begin(unit)
            for unit in (0, 1):
                engine.copy(unit, 2).start()

        for number in range(PAIRS * blocks):
            if number in plan or number in gather_plan:

                @pl.when(step == number)
                def _():
                    if number in gather_plan:
                        gather.advance(gather_plan[number])
                    for unit, stage in plan.get(number, ()):
                        engine.advance(unit, stage, stop=unit > 1 and stage == 1)

    block_columns(
        place, edges, rows_count, group_rows, block, step, blocks, query_columns, key_columns
    )
    extra = query_columns[block]
    upstream = do_ref[...]
    product = upstream.astype(f32) * o_ref[...].astype(f32)
    first = product.astype(bf16)
    second = (product - first.astype(f32)).astype(bf16)
    head = jnp.where(iota((8, LANES), 1) // HEAD_DIM == iota((8, LANES), 0), 1.0, 0.0).astype(bf16)
    by_head = nt(head, first) + nt(head, second)
    centre = jnp.concatenate([by_head[0:1], by_head[1:2]], axis=1)
    centre_ref[0, 0] = jnp.broadcast_to(centre, (8, 2 * BLOCK))
    queries = stack_pair(q_ref[...])
    grads = stack_pair(upstream)
    keys = k_ref[...]
    score = nt(
        jnp.concatenate([keys, key_columns[block]], 1),
        jnp.concatenate([queries, jnp.concatenate([extra, extra], 0)], 1),
    )
    weights = jnp.exp(score - line_ref[0, 0, 0:1])
    along = nt(v_ref[...], grads) - centre
    score_grad = (weights * along).astype(bf16)
    dv_ref[...] = nn(weights.astype(bf16), grads)
    dk_ref[...] = nn(score_grad, queries)
    low, high = side_by_side(tn(keys, score_grad))
    dq_ref[:HEAD_DIM] = low
    dq_ref[HEAD_DIM:] = high

    if talk:

        @pl.when(step == PAIRS * blocks - 1)
        def _():
            everyone_ref[...] = all_ref[...].reshape(everyone_ref.shape)
            gather.end()
            rest_out_ref[...] = landings[1][2:]
            for entries in plan.values():
                for unit, stage in entries:
                    engine.sent(unit, stage)


def local_backward(
    talk, scalars, rows_count, group_rows, q, k, v, do, o, line, message, rest, last, dwo
):
    blocks = rows_count // BLOCK
    width = q.shape[1]
    block_spec = pl.BlockSpec((BLOCK, LANES), lambda p, b, *unused: (b, p))
    operands = [q, k, v, do, o, line]
    in_specs = [block_spec] * 5 + [line_spec()]
    out_specs = (
        [pl.BlockSpec((LANES, BLOCK), lambda p, b, *unused: (p, b))]
        + [block_spec] * 2
        + [line_spec()]
    )
    out_shape = [
        jax.ShapeDtypeStruct((width, rows_count), f32),
        jax.ShapeDtypeStruct((rows_count, width), f32),
        jax.ShapeDtypeStruct((rows_count, width), f32),
        jax.ShapeDtypeStruct((PAIRS, blocks, 8, 2 * BLOCK), f32),
    ]
    scratch = column_scratch(blocks)
    more = {}
    if talk:
        own, wide = message.shape
        rows, lanes = last.shape[-2:]
        units = 5
        operands += [message, rest, last, dwo.reshape(last.shape[1:])]
        in_specs += [full(message.shape), once(rest.shape)]
        in_specs += [pl.BlockSpec(memory_space=pl.ANY)] * 2
        everyone = (16 * own, wide)
        rest_out = (units - 2,) + rest.shape[1:]
        out_specs += [once(everyone), once((2 * rows, lanes)), once(rest_out)]
        out_shape += [
            jax.ShapeDtypeStruct(everyone, bf16),
            jax.ShapeDtypeStruct((2 * rows, lanes), f32),
            jax.ShapeDtypeStruct(rest_out, bf16),
        ]
        dma = pltpu.SemaphoreType.DMA
        scratch += [pltpu.VMEM((2, 2, 2, 2, own, wide), bf16), dma((4, 2)), dma((4, 2))]
        scratch += sum_scratch(units, rows, lanes, True)
        more = {"collective_id": 4, "has_side_effects": True}
    return pl.pallas_call(
        functools.partial(local_backward_kernel, talk, rows_count, group_rows),
        grid_spec=pltpu.PrefetchScalarGridSpec(
            num_scalar_prefetch=3,
            grid=(PAIRS, blocks),
            in_specs=in_specs,
            out_specs=out_specs,
            scratch_shapes=scratch,
        ),
        out_shape=out_shape,
        compiler_params=params(**more),
        cost_estimate=pl.CostEstimate(
            flops=40 * rows_count * BLOCK * width,
            bytes_accessed=30 * rows_count * width,
            transcendentals=HEADS * rows_count * BLOCK,
        ),
        name="local_backward",
    )(*scalars, *operands)


def slot_backward_kernel(
    rows_count,
    group_rows,
    lengths,
    bucket_of,
    place,
    q_ref,
    k_ref,
    v_ref,
    do_ref,
    line_ref,
    centre_ref,
    dqt_ref,
    dk_in_ref,
    dv_in_ref,
    gq_ref,
    gk_ref,
    gv_ref,
    gdo_ref,
    gstat_ref,
    gx_ref,
    gh_ref,
    wq_ref,
    wk_ref,
    wv_ref,
    dq_ref,
    dk_ref,
    dv_ref,
    dw_ref,
    dgh_ref,
    dnorm_ref,
    edges,
    query_columns,
    key_columns,
    keys_ref,
    queries_ref,
    grads_ref,
    dqt_sum,
    dk_sum,
    dv_sum,
    dgqt_sum,
    dgk_sum,
    dgv_sum,
    lines_ref,
    dw_sum,
    dgh_sum,
):
    pair = pl.program_id(0)
    block = pl.program_id(1)
    blocks = rows_count // BLOCK
    step = pair * blocks + block

    @pl.when(step == 0)
    def _():
        read_edges(lengths, bucket_of, place, edges)

        def turn(slot, carry):
            at = pl.ds(pl.multiple_of(slot * GLOBALS, GLOBALS), GLOBALS)
            lines_ref[slot] = gstat_ref[at, :].astype(f32).T
            return carry

        lax.fori_loop(0, SLOTS, turn, 0)
        dgh_sum[...] = jnp.zeros_like(dgh_sum)
        dnorm_ref[...] = jnp.zeros_like(dnorm_ref)

    @pl.when(block == 0)
    def _():
        dgqt_sum[...] = jnp.zeros_like(dgqt_sum)
        dgk_sum[...] = jnp.zeros_like(dgk_sum)
        dgv_sum[...] = jnp.zeros_like(dgv_sum)

    block_columns(
        place, edges, rows_count, group_rows, block, step, blocks, query_columns, key_columns
    )
    extra = query_columns[block]
    keys_ref[:, :LANES] = k_ref[...]
    keys_ref[:, LANES:] = key_columns[block]
    queries_ref[:, :LANES] = stack_pair(q_ref[...])
    queries_ref[:BLOCK, LANES:] = extra
    queries_ref[BLOCK:, LANES:] = extra
    grads_ref[...] = stack_pair(do_ref[...])
    dqt_sum[...] = dqt_ref[...]
    dk_sum[...] = dk_in_ref[...]
    dv_sum[...] = dv_in_ref[...]

    def line_of(slot, first):
        halves = []
        for which in range(2):
            spot = first + 2 * pair + which
            halves.append(
                lines_ref[slot, pl.ds(spot, 1)]
                + lines_ref[slot, pl.ds(spot + HEADS, 1)]
                + lines_ref[slot, pl.ds(spot + 2 * HEADS, 1)]
            )
        return jnp.concatenate(halves, axis=1)

    def from_global(slot, keys, values):
        at = pl.ds(pl.multiple_of(slot * GLOBALS, GLOBALS), GLOBALS)
        extra = global_query_extra(slot).astype(bf16)
        queries = stack_pair(gq_ref[at, :])
        grads = stack_pair(gdo_ref[at, :])
        score = nt(keys, jnp.concatenate([queries, jnp.concatenate([extra, extra], 0)], 1))
        weights = jnp.exp(score - line_of(slot, 0))
        along = nt(values, grads) - line_of(slot, 3 * HEADS)
        score_grad = (weights * along).astype(bf16)
        low, high = side_by_side(tn(keys[:, :LANES], score_grad))
        dgqt_sum[slot, :HEAD_DIM] += low
        dgqt_sum[slot, HEAD_DIM:] += high
        return nn(score_grad, queries), nn(weights.astype(bf16), grads)

    def one_slot(slot, carry):
        @pl.when(slot_present(slot, place, edges, rows_count, group_rows, block))
        def _():
            key_grad, value_grad = from_global(slot, keys_ref[...], v_ref[...])
            dk_sum[...] += key_grad
            dv_sum[...] += value_grad
            at = pl.ds(pl.multiple_of(slot * GLOBALS, GLOBALS), GLOBALS)
            slot_keys = jnp.concatenate([gk_ref[at, :], global_key_extra(slot).astype(bf16)], 1)
            weights = jnp.exp(nt(slot_keys, queries_ref[...]) - line_ref[0, 0, 0:1])
            along = nt(gv_ref[at, :], grads_ref[...]) - centre_ref[0, 0, 0:1]
            score_grad = (weights * along).astype(bf16)
            dgv_sum[at, :] += nn(weights.astype(bf16), grads_ref[...])
            dgk_sum[at, :] += nn(score_grad, queries_ref[:, :LANES])
            low, high = side_by_side(tn(gk_ref[at, :], score_grad))
            dqt_sum[:HEAD_DIM] += low
            dqt_sum[HEAD_DIM:] += high

        return carry

    lax.fori_loop(0, SLOTS, one_slot, 0)
    dq_ref[...] = dqt_sum[...].T.astype(bf16)
    dk_ref[...] = dk_sum[...].astype(bf16)
    dv_ref[...] = dv_sum[...].astype(bf16)

    @pl.when((block == blocks - 1) & (place[2] >= 0))
    def _():
        slot = place[2]
        at = pl.ds(pl.multiple_of(slot * GLOBALS, GLOBALS), GLOBALS)
        keys = jnp.concatenate([gk_ref[at, :], global_key_extra(slot).astype(bf16)], axis=1)
        key_grad, value_grad = from_global(slot, keys, gv_ref[at, :])
        dgk_sum[at, :] += key_grad
        dgv_sum[at, :] += value_grad

    @pl.when(block == blocks - 1)
    def _():
        dw_sum[...] = jnp.zeros_like(dw_sum)

        def through(slot, carry):
            needed = slot == place[2]
            for number in range(blocks):
                needed = needed | slot_present(
                    slot, place, edges, rows_count, group_rows, number
                )

            @pl.when(needed)
            def _():
                at = pl.ds(pl.multiple_of(slot * GLOBALS, GLOBALS), GLOBALS)
                grads = (
                    (dgqt_sum[slot].T * query_scale).astype(bf16),
                    dgk_sum[at, :].astype(bf16),
                    dgv_sum[at, :].astype(bf16),
                )
                rows = gh_ref[at, :]
                total = dgh_sum[at, :]
                for index, weight in enumerate((wq_ref, wk_ref, wv_ref)):
                    dw_sum[index] += tn(grads[index], rows)
                    total = total + nt(grads[index], weight[...])
                dgh_sum[at, :] = total

                @pl.when(pair == PAIRS - 1)
                def _():
                    unit, unused = normalize_rows(gx_ref[at, :].astype(f32))
                    dnorm_ref[0:1] += jnp.sum(total * unit, axis=0, keepdims=True)
                    dnorm_ref[1:2] += jnp.sum(total, axis=0, keepdims=True)

            return carry

        lax.fori_loop(0, SLOTS, through, 0)
        dw_ref[...] = dw_sum[...].astype(bf16)

    @pl.when(step == PAIRS * blocks - 1)
    def _():
        dgh_ref[...] = dgh_sum[...].astype(bf16)


def slot_backward(
    scalars,
    rows_count,
    group_rows,
    q,
    k,
    v,
    do,
    line,
    centre,
    dqt,
    dk,
    dv,
    gq,
    gk,
    gv,
    everyone,
    gx,
    gh,
    wq,
    wk,
    wv,
):
    blocks = rows_count // BLOCK
    all_globals, width = gk.shape
    block_spec = pl.BlockSpec((BLOCK, LANES), lambda p, b, *unused: (b, p))
    pair_spec = pl.BlockSpec((all_globals, LANES), lambda p, b, *unused: (0, p))
    local = jax.ShapeDtypeStruct((rows_count, width), bf16)
    glob = jax.ShapeDtypeStruct((all_globals, width), bf16)
    return pl.pallas_call(
        functools.partial(slot_backward_kernel, rows_count, group_rows),
        grid_spec=pltpu.PrefetchScalarGridSpec(
            num_scalar_prefetch=3,
            grid=(PAIRS, blocks),
            in_specs=[block_spec] * 4
            + [line_spec()] * 2
            + [pl.BlockSpec((LANES, BLOCK), lambda p, b, *unused: (p, b))]
            + [block_spec] * 2
            + [pair_spec] * 4
            + [pl.BlockSpec((all_globals, LANES), lambda p, b, *unused: (0, PAIRS))]
            + [once((all_globals, width))] * 2
            + [pl.BlockSpec((width, LANES), lambda p, b, *unused: (0, p))] * 3,
            out_specs=[block_spec] * 3
            + [
                pl.BlockSpec((3, LANES, width), lambda p, b, *unused: (0, p, 0)),
                once((all_globals, width)),
                full((8, width)),
            ],
            scratch_shapes=column_scratch(blocks)
            + [
                pltpu.VMEM((BLOCK, 2 * LANES), bf16),
                pltpu.VMEM((2 * BLOCK, 2 * LANES), bf16),
                pltpu.VMEM((2 * BLOCK, LANES), bf16),
                pltpu.VMEM((LANES, BLOCK), f32),
                pltpu.VMEM((BLOCK, LANES), f32),
                pltpu.VMEM((BLOCK, LANES), f32),
                pltpu.VMEM((SLOTS, LANES, GLOBALS), f32),
                pltpu.VMEM((all_globals, LANES), f32),
                pltpu.VMEM((all_globals, LANES), f32),
                pltpu.VMEM((SLOTS, LANES, GLOBALS), f32),
                pltpu.VMEM((3, LANES, width), f32),
                pltpu.VMEM((all_globals, width), f32),
            ],
        ),
        out_shape=[local] * 3
        + [
            jax.ShapeDtypeStruct((3, width, width), bf16),
            glob,
            jax.ShapeDtypeStruct((8, width), f32),
        ],
        compiler_params=params(),
        cost_estimate=pl.CostEstimate(
            flops=80 * rows_count * GLOBALS * width,
            bytes_accessed=40 * rows_count * width,
            transcendentals=2 * HEADS * rows_count * GLOBALS,
        ),
        name="slot_backward",
    )(
        *scalars,
        q,
        k,
        v,
        do,
        line,
        centre,
        dqt,
        dk,
        dv,
        gq,
        gk,
        gv,
        everyone,
        everyone,
        gx,
        gh,
        wq,
        wk,
        wv,
    )


def project_back_kernel(
    tile,
    x_ref,
    dy_ref,
    h_ref,
    dq_ref,
    dk_ref,
    dv_ref,
    dwg_ref,
    wq_ref,
    wk_ref,
    wv_ref,
    gain_ref,
    dx_ref,
    dw_ref,
    dnorm_ref,
):
    count, width = x_ref.shape
    dnorm_ref[...] = jnp.zeros_like(dnorm_ref)

    def one_tile(i, carry):
        at = pl.ds(pl.multiple_of(i * tile, tile), tile)
        dh = (
            nt(dq_ref[at, :], wq_ref[...]) * query_scale
            + nt(dk_ref[at, :], wk_ref[...])
            + nt(dv_ref[at, :], wv_ref[...])
        )
        unit, scale = normalize_rows(x_ref[at, :].astype(f32))
        dnorm_ref[0:1] += jnp.sum(dh * unit, axis=0, keepdims=True)
        dnorm_ref[1:2] += jnp.sum(dh, axis=0, keepdims=True)
        dx_ref[at, :] = dy_ref[at, :] + norm_back(unit, scale, gain_ref[...], dh)
        return carry

    lax.fori_loop(0, count // tile, one_tile, 0)
    for index, source in enumerate((dq_ref, dk_ref, dv_ref)):
        value = tn(source[...], h_ref[...])
        if index == 0:
            value = value * query_scale
        dw_ref[index] = (value + dwg_ref[index].astype(f32)).astype(bf16)


def project_back(x, dy, h, dq, dk, dv, dwg, wq, wk, wv, gain):
    count, width = x.shape
    vmem = pl.BlockSpec(memory_space=pltpu.VMEM)
    return pl.pallas_call(
        functools.partial(project_back_kernel, BLOCK),
        in_specs=[vmem] * 11,
        out_specs=[vmem] * 3,
        out_shape=[
            jax.ShapeDtypeStruct((count, width), f32),
            jax.ShapeDtypeStruct((3, width, width), bf16),
            jax.ShapeDtypeStruct((8, width), f32),
        ],
        compiler_params=params(),
        cost_estimate=pl.CostEstimate(
            flops=12 * count * width * width, bytes_accessed=30 * count * width, transcendentals=0
        ),
        name="project_back",
    )(x, dy, h, dq, dk, dv, dwg, wq, wk, wv, gain)


class RowSum:
    ORDER = ("core", "y", "z0", "z1")

    def __init__(self, source, own, landings, send_sem, recv_sem, own_sem, bits, partners):
        self.source = source
        self.own = own
        self.landings = landings
        self.send_sem = send_sem
        self.recv_sem = recv_sem
        self.own_sem = own_sem
        self.bits = bits
        self.partners = partners

    def part(self, stage, other):
        bit = self.bits[self.ORDER[stage]]
        side = 1 - bit if other else bit
        if stage == 0:
            return self.source.at[:, :, :, side] if other else self.own
        ref = self.landings[stage - 1]
        if stage == 1:
            return ref.at[:, :, side]
        if stage == 2:
            return ref.at[:, side]
        return ref.at[side]

    def copy(self, stage):
        return remote(
            self.part(stage, True),
            self.landings[stage],
            self.send_sem.at[stage],
            self.recv_sem.at[stage],
            self.partners[self.ORDER[stage]],
        )

    def own_copy(self):
        return pltpu.make_async_copy(
            self.source.at[:, :, :, self.bits["core"]], self.own, self.own_sem
        )

    def begin(self):
        self.own_copy().start()
        self.copy(0).start()

    def advance(self, stage):
        if stage == 0:
            self.own_copy().wait()
        self.copy(stage).wait_recv()
        if stage < 3:
            add_into(self.landings[stage], self.part(stage, False))
            self.copy(stage + 1).start()
            return None
        return self.landings[3][...].astype(f32) + self.part(3, False)[...].astype(f32)

    def end(self):
        for stage in range(4):
            self.copy(stage).wait_send()


def finish_kernel(
    rest_ref,
    x_in,
    dy_in,
    h_in,
    dq_in,
    dk_in,
    dv_in,
    dwg_in,
    dgh_ref,
    z_in,
    wq_in,
    wk_in,
    wv_in,
    db1_ref,
    db2_ref,
    dnorm_global_ref,
    dgain2_ref,
    doffset2_ref,
    gx_ref,
    gdy_ref,
    norms_ref,
    out_ref,
    small_out_ref,
    grad_out_ref,
    layer_ref,
    token_ref,
    x_ref,
    dy_ref,
    h_ref,
    dq_ref,
    dk_ref,
    dv_ref,
    dwg_ref,
    wq_ref,
    wk_ref,
    wv_ref,
    load_sem,
    units_ref,
    one_ref,
    two_ref,
    three_ref,
    four_ref,
    five_ref,
    send_sem,
    recv_sem,
    gown_ref,
    gone_ref,
    gtwo_ref,
    gthree_ref,
    gfour_ref,
    gsend_sem,
    grecv_sem,
    gown_sem,
    sums_ref,
    here_ref,
    ssend_sem,
    srecv_sem,
    halo_out,
    halo_z,
    halo_dx,
    halo_send,
    halo_recv,
    dnorm_ref,
):
    bits, partners = my_place()
    count, width = x_ref.shape
    came = rest_ref.shape[0]
    units = came + 3
    batch = lax.axis_index("batch")
    seq = lax.axis_index("seq")
    places = lax.axis_size("seq")
    after = (batch, lax.rem(seq + 1, places))
    before = (batch, lax.rem(seq + places - 1, places))

    pairs = [
        (dq_in, dq_ref),
        (h_in, h_ref),
        (dwg_in, dwg_ref),
        (dk_in, dk_ref),
        (dv_in, dv_ref),
        (wq_in, wq_ref),
        (wk_in, wk_ref),
        (wv_in, wv_ref),
        (x_in, x_ref),
        (dy_in, dy_ref),
        (z_in.at[pl.ds(HALF, count - HALF)], layer_ref.at[pl.ds(0, count - HALF)]),
    ]
    loads = [
        pltpu.make_async_copy(source, target, load_sem.at[number])
        for number, (source, target) in enumerate(pairs)
    ]
    for load in loads:
        load.start()

    def source(unit):
        return lambda side: units_ref.at[unit - came, :, :, :, side]

    engine = WeightSum(
        [source(unit) for unit in range(units)],
        (one_ref, two_ref, three_ref, four_ref, five_ref),
        None,
        send_sem,
        recv_sem,
        None,
        out_ref,
        bits,
        partners,
    )
    row_sum = RowSum(
        dgh_ref,
        gown_ref,
        (gone_ref, gtwo_ref, gthree_ref, gfour_ref),
        gsend_sem,
        grecv_sem,
        gown_sem,
        bits,
        partners,
    )

    def scopy(stage):
        return remote(
            sums_ref.at[stage],
            here_ref.at[stage],
            ssend_sem.at[stage],
            srecv_sem.at[stage],
            partners[ORDERS[0][stage]],
        )

    def small_advance(stage):
        scopy(stage).wait_recv()
        total = sums_ref[stage] + here_ref[stage]
        if stage < STAGES - 1:
            sums_ref[stage + 1] = total
            scopy(stage + 1).start()
        else:
            small_out_ref[...] = total

    head = pl.ds(0, HALF)
    halos = [
        remote(z_in.at[head], halo_z, halo_send.at[0], halo_recv.at[0], before),
        remote(halo_out, halo_dx, halo_send.at[1], halo_recv.at[1], before),
    ]
    two_ref[:came] = rest_ref[...]
    meet([partners[name] for name in ORDERS[0]] + [before, after])
    for unit in range(came):
        engine.copy(unit, 2).start()
    row_sum.begin()
    halos[0].start()

    def weight_gradient(index, grads_ref):
        value = tn(grads_ref[...], h_ref[...])
        if index == 0:
            value = value * query_scale
        put_unit(units_ref.at[index], value + dwg_ref[index].astype(f32))
        engine.begin(came + index)

    for number in range(3):
        loads[number].wait()
    weight_gradient(0, dq_ref)
    row_sum.advance(0)
    loads[3].wait()
    weight_gradient(1, dk_ref)
    loads[4].wait()
    weight_gradient(2, dv_ref)
    for unit in range(came):
        engine.advance(unit, 2)
    for number in range(5, 10):
        loads[number].wait()
    dnorm_ref[...] = jnp.zeros_like(dnorm_ref)

    def back(index):
        at = pl.ds(index * HALF, HALF)
        dh = (
            nt(dq_ref[at, :], wq_ref[...]) * query_scale
            + nt(dk_ref[at, :], wk_ref[...])
            + nt(dv_ref[at, :], wv_ref[...])
        )
        unit, scale = normalize_rows(x_ref[at, :].astype(f32))
        dnorm_ref[0:1] += jnp.sum(dh * unit, axis=0, keepdims=True)
        dnorm_ref[1:2] += jnp.sum(dh, axis=0, keepdims=True)
        dx = dy_ref[at, :] + norm_back(unit, scale, norms_ref[0:1], dh)
        if index == 0:
            halo_out[...] = dx.astype(bf16)
        else:
            token_ref[pl.ds((index - 1) * HALF, HALF), :] = dx

    for index in range(count // HALF):
        back(index)
        if index == 0:
            halos[1].start()
            for unit in range(came, units):
                engine.advance(unit, 0)
        if index == 1:
            row_sum.advance(1)
        if index == 2:
            for unit in range(came):
                engine.advance(unit, 3)

    hidden_rows = db1_ref.shape[0]
    parts = [
        db1_ref[...],
        db2_ref[...],
        dnorm_ref[0:2],
        dnorm_global_ref[0:2],
        dgain2_ref[...],
        doffset2_ref[...],
    ]
    filled = hidden_rows + 7
    parts.append(jnp.zeros((sums_ref.shape[1] - filled, width), f32))
    sums_ref[0] = jnp.concatenate(parts, 0)
    scopy(0).start()
    row_sum.advance(2)
    for unit in range(came, units):
        engine.advance(unit, 1)
    small_advance(0)
    dgh = row_sum.advance(3)
    unit_rows, scale = normalize_rows(gx_ref[...].astype(f32))
    grad_out_ref[...] = gdy_ref[...] + norm_back(unit_rows, scale, norms_ref[2:3], dgh)
    small_advance(1)
    for unit in range(came):
        engine.advance(unit, 4)
    for unit in range(came, units):
        engine.advance(unit, 2)
    small_advance(2)
    halos[0].wait_recv()
    halos[1].wait_recv()
    loads[10].wait()
    layer_ref[count - HALF :, :] = halo_z[...]
    token_ref[count - HALF :, :] = halo_dx[...].astype(f32)
    for unit in range(came, units):
        engine.advance(unit, 3)
    small_advance(3)
    for unit in range(came, units):
        engine.advance(unit, 4)
    small_advance(4)

    for unit in range(units):
        for stage in range(2 if unit < came else 0, STAGES):
            engine.sent(unit, stage)
    for stage in range(STAGES):
        scopy(stage).wait_send()
    row_sum.end()
    for halo in halos:
        halo.wait_send()


def finish_all(rest, x, dy, h, dq, dk, dv, dwg, dgh, z, wq, wk, wv, small, gx, gdy, norms):
    count, width = x.shape
    rows, lanes = rest.shape[-2:]
    units = rest.shape[0] + 3
    own = gx.shape[0]
    place = (2, 2, 2, 2)
    small_rows = small[0].shape[0] + 7
    small_rows += -small_rows % 8
    anywhere = pl.BlockSpec(memory_space=pl.ANY)
    vmem = pl.BlockSpec(memory_space=pltpu.VMEM)
    dma = pltpu.SemaphoreType.DMA
    row = pltpu.VMEM((count, width), bf16)
    weight = pltpu.VMEM((width, width), bf16)
    half = pltpu.VMEM((HALF, width), bf16)
    return pl.pallas_call(
        finish_kernel,
        in_specs=[vmem] + [anywhere] * 12 + [vmem] * 8,
        out_specs=[vmem] * 5,
        out_shape=[
            jax.ShapeDtypeStruct((units * rows, lanes), f32),
            jax.ShapeDtypeStruct((small_rows, width), f32),
            jax.ShapeDtypeStruct((own, width), f32),
            jax.ShapeDtypeStruct((count, width), bf16),
            jax.ShapeDtypeStruct((count, width), f32),
        ],
        scratch_shapes=[
            row,
            pltpu.VMEM((count, width), f32),
            row,
            row,
            row,
            row,
            pltpu.VMEM((3, width, width), bf16),
            weight,
            weight,
            weight,
            dma((11,)),
            pltpu.VMEM((3, 2, 2, 2, 2, 2, rows, lanes), bf16),
        ]
        + sum_scratch(units, rows, lanes, False)
        + [
            pltpu.VMEM((2, 2, 2, own, width), bf16),
            pltpu.VMEM((2, 2, 2, own, width), bf16),
            pltpu.VMEM((2, 2, own, width), bf16),
            pltpu.VMEM((2, own, width), bf16),
            pltpu.VMEM((own, width), bf16),
            dma((4,)),
            dma((4,)),
            dma,
            pltpu.VMEM((STAGES, small_rows, width), f32),
            pltpu.VMEM((STAGES, small_rows, width), f32),
            dma((STAGES,)),
            dma((STAGES,)),
            half,
            half,
            half,
            dma((2,)),
            dma((2,)),
            pltpu.VMEM((8, width), f32),
        ],
        compiler_params=params(collective_id=0, has_side_effects=True),
        cost_estimate=pl.CostEstimate(
            flops=12 * count * width * width, bytes_accessed=30 * count * width, transcendentals=0
        ),
        name="finish_all",
    )(
        rest,
        x,
        dy,
        h,
        dq,
        dk,
        dv,
        dwg,
        dgh.reshape(place + (own, width)),
        z,
        wq,
        wk,
        wv,
        *small,
        gx,
        gdy,
        norms,
    )


def from_behind(value, axis, steps):
    count = lax.axis_size(axis)
    pairs = [(source, (source + steps) % count) for source in range(count)]
    return lax.ppermute(value, axis, pairs)


def pieces(value):
    first = lax.reduce_precision(value, 8, 7)
    second = lax.reduce_precision(value - first, 8, 7)
    return [first.astype(bf16), second.astype(bf16), (value - first - second).astype(bf16)]


def scatter_sum(value):
    half = lax.psum_scatter(value, "batch", scatter_dimension=1, tiled=True)
    part = lax.psum_scatter(half, "seq", scatter_dimension=0, tiled=True)
    return part.T.astype(f32)


def on_device(
    tokens,
    global_states,
    lengths,
    bucket_of,
    wq,
    wk,
    wv,
    wo,
    w1,
    b1,
    w2,
    b2,
    norm_params,
    cotangent,
    global_cotangent,
):
    rows = tokens.shape[1]
    width = tokens.shape[2]
    own = global_states.shape[1]
    seq_count = lax.axis_size("seq")
    seq_place = lax.axis_index("seq")
    group_rows = rows * seq_count
    own_start = seq_place * own
    first_of_slot = own_start % GLOBALS == 0
    place = jnp.stack(
        [
            lax.axis_index("batch"),
            seq_place,
            jnp.where(first_of_slot, own_start // GLOBALS, -1),
        ]
    ).astype(jnp.int32)
    scalars = (lengths, bucket_of, place)
    norms = [norm_params[i : i + 1] for i in range(6)]
    b2_line = b2[None]

    batch_count = lax.axis_size("batch")
    grid_of = None
    if seq_count == 16 and batch_count == 2 and 2 * own == GLOBALS and rows == 2 * BLOCK:
        grid_of = (seq_count, batch_count)

    if grid_of is None:
        arrived_tokens, arrived_grads = from_behind(
            (tokens[0, rows - HALF :], cotangent[0, rows - HALF :]), "seq", 1
        )
        x = jnp.concatenate([arrived_tokens, tokens[0, : rows - HALF]], 0)
        ct = jnp.concatenate([arrived_grads, cotangent[0, : rows - HALF]], 0)
        all_states = lax.all_gather(global_states[0], "seq", axis=0, tiled=True)
        w1t = w1.T
        h, q, k, v = project_local(x, norms[0], norms[1], wq, wk, wv)
        gh, gq, gk, gv = project_global(
            scalars, rows, group_rows, all_states, norms[2], norms[3], wq, wk, wv
        )
    else:
        h, q, k, v, x, ct, all_states, gh, gq, gk, gv, w1t = gather_project(
            tokens[0], cotangent[0], global_states[0], w1, norm_params, wq, wk, wv
        )
        all_states = all_states.reshape(-1, width)
    far, far_stat, part, part_stat = slot_forward(scalars, rows, group_rows, q, k, v, gq, gk, gv)
    if grid_of is None:
        o, line = local_forward(
            False, scalars, rows, group_rows, q, k, v, far, far_stat, None, None
        )
        part_peak = part_stat[:, :, 0:2]
        peak = jnp.max(lax.all_gather(part_peak, "seq"), axis=0)
        factor = jnp.exp(part_peak - peak)
        scaled = part.reshape(SLOTS, PAIRS, 2, HEAD_DIM, GLOBALS).astype(f32) * factor[:, :, :, None]
        scaled = scaled.reshape(SLOTS, width, GLOBALS)
        scaled_total = (part_stat[:, :, 2:4] * factor).reshape(SLOTS, HEADS, GLOBALS)
        payload = jnp.concatenate(
            [scaled, scaled_total, jnp.zeros((SLOTS, 4, GLOBALS), f32)], 1
        ).transpose(0, 2, 1)
        sums = lax.psum_scatter(
            payload.astype(bf16).reshape(SLOTS * GLOBALS, -1), "seq", scatter_dimension=0, tiled=True
        ).astype(f32)
        own_total = sums[:, width : width + HEADS]
        all_peak = peak.reshape(SLOTS, HEADS, GLOBALS).transpose(0, 2, 1).reshape(-1, HEADS)
        own_peak = lax.dynamic_slice_in_dim(all_peak, own_start, own, 0)
        go = (
            (sums[:, :width].reshape(own, HEADS, HEAD_DIM) / own_total[:, :, None])
            .reshape(own, width)
            .astype(bf16)
        )
        gstat = own_peak + jnp.log(own_total)
    else:
        o, line, half_sum, half_stat = local_forward(
            True, scalars, rows, group_rows, q, k, v, far, far_stat, part, part_stat
        )

    z, dy, do, gz, gdy, gdo, dwo, db1, db2, dgain2, doffset2, *dws = branch(
        grid_of,
        x,
        o,
        ct,
        global_states[0],
        go if grid_of is None else half_sum,
        gstat if grid_of is None else half_stat,
        global_cotangent[0],
        wo,
        w1t,
        b1,
        w2,
        b2_line,
        norm_params,
    )
    if grid_of is None:
        gcentre = jnp.sum(
            (gdo.astype(f32) * go.astype(f32)).reshape(own, HEADS, HEAD_DIM), axis=-1
        )
        message = jnp.concatenate(
            [gdo]
            + pieces(gstat)
            + pieces(gcentre)
            + [jnp.zeros((own, LANES - 6 * HEADS), bf16)],
            axis=1,
        )
        everyone = lax.all_gather(message, "seq", axis=0, tiled=True)
        dqt, dk, dv, centre = local_backward(
            False, scalars, rows, group_rows, q, k, v, do, o, line, None, None, None, None
        )
    else:
        sum_first, last, message, rest = dws
        dqt, dk, dv, centre, everyone, sum_second, rest = local_backward(
            True, scalars, rows, group_rows, q, k, v, do, o, line, message, rest, last, dwo
        )
    dq, dk, dv, dwg, dgh, dnorm_global = slot_backward(
        scalars,
        rows,
        group_rows,
        q,
        k,
        v,
        do,
        line,
        centre,
        dqt,
        dk,
        dv,
        gq,
        gk,
        gv,
        everyone,
        all_states,
        gh,
        wq,
        wk,
        wv,
    )
    if grid_of is None:
        dx, dqkv, dnorm = project_back(x, dy, h, dq, dk, dv, dwg, wq, wk, wv, norms[0])
        back_z, back_grad = from_behind((z[:HALF], dx[:HALF].astype(bf16)), "seq", -1)
        layer_out = jnp.concatenate([z[HALF:], back_z], 0)
        token_grad = jnp.concatenate([dx[HALF:], back_grad.astype(f32)], 0)
        small = jnp.concatenate([db1, db2, dnorm[:2], dnorm_global[:2], dgain2, doffset2], 0)
        dgh = lax.psum_scatter(dgh, "seq", scatter_dimension=0, tiled=True).astype(f32)
        gunit, gscale = normalize_rows(global_states[0].astype(f32))
        global_grad = gdy + norm_back(gunit, gscale, norms[2], dgh)
        small = lax.psum(small, ("batch", "seq"))
        dw1, dw2 = dws
        weights = [scatter_sum(value) for value in (dqkv[0], dqkv[1], dqkv[2], dwo, dw1, dw2)]
    else:
        sum_third, small, global_grad, layer_out, token_grad = finish_all(
            rest,
            x,
            dy,
            h,
            dq,
            dk,
            dv,
            dwg,
            dgh,
            z,
            wq,
            wk,
            wv,
            (db1, db2, dnorm_global, dgain2, doffset2),
            global_states[0],
            gdy,
            norm_params,
        )
        piece = width // seq_count
        lanes = width // batch_count
        steps = w1.shape[1] // FF_CHUNK
        chunks = jnp.concatenate([sum_first, sum_second, sum_third[: 2 * piece]], 0)
        chunks = chunks.reshape(steps, 2, piece, lanes)
        part1 = chunks[:, 0].reshape(steps * piece, lanes)
        part2 = chunks[:, 1].reshape(steps, piece, lanes // piece, piece)
        part2 = part2.transpose(1, 2, 0, 3).reshape(piece, -1)
        parts = [sum_third[i * piece : (i + 1) * piece] for i in (3, 4, 5, 2)] + [part1, part2]
        weights = [value.T for value in parts]
    hidden_rows = w1.shape[1] // width
    return (
        layer_out[None],
        gz[None],
        token_grad[None],
        global_grad[None],
        *weights,
        small[:hidden_rows].reshape(-1),
        small[hidden_rows],
        small[hidden_rows + 1 : hidden_rows + 7],
    )


def solution(mesh):
    split = P("batch", "seq", None)
    return jax.shard_map(
        on_device,
        mesh=mesh,
        in_specs=(split, split) + (P(),) * 11 + (split, split),
        out_specs=(split,) * 4 + (P("batch", "seq"),) * 6 + (P(),) * 3,
        check_vma=False,
    )
```

time: 1050 us -> 346 us (0.33)
  waiting for transfers between devices: 600 us -> 0 us
  blocking collectives: 63.1 us -> 0 us
  Pallas kernels: 260 us -> 323 us
  other arithmetic: 44.1 us -> 1.37 us
  local copies, waits for them, and re-layouts: 50.7 us -> 18.1 us
  between operations: 14.9 us -> 1.03 us
    reduce_scatter x9 -> x0, waiting for transfers between devices: 458 us -> none  [the longest x6 296 us: scatter_sum(): part = lax.psum_scatter(half, 'seq', scatter_dimension=0, tiled=True)]
    unnamed x21 -> x0, waiting for transfers between devices: 99.7 us -> none
    pallas_call x9 -> x7, Pallas kernels: 260 us -> 323 us  [the longest x1 88.6 us: branch(): pl.pallas_call(functools.partial(branch_kernel, BLOCK, grid_of is not Non...]
    psum x1 -> x0, blocking collectives: 41.2 us -> none  [on_device(): lax.psum((db1[0] + gdb1[0], db2[0] + gdb2[0], norm_grad), ('batch', 'seq'))]
    unnamed x59 -> x16, local copies, waits for them, and re-layouts: 29.2 us -> 4.85 us
    all_gather x2 -> x0, waiting for transfers between devices: 23.6 us -> none  [the longest x1 23.6 us: on_device(): all_states = lax.all_gather(global_states[0], 'seq', axis=0, tiled=True)]
    all_gather x1 -> x0, blocking collectives: 21.9 us -> none  [on_device(): peak = jnp.max(lax.all_gather(part_peak, 'seq'), axis=0)]
    ppermute x4 -> x0, waiting for transfers between devices: 17.8 us -> none  [from_behind(): return lax.ppermute(value, axis, pairs)]
  transfers between devices with their start and end apart: 20 -> 0, of which waited for: 16 -> 0; matrix products, arithmetic and copies ran while one was open for 7% -> 0% of each run, Pallas kernels for 20% -> 0%
where the time goes in v2:
time: 346 us; the launch traced here: 344 us
  Pallas kernels  323 us (93%)
  local copies, waits for them, and re-layouts  18.1 us (5%)
    pallas_call x1, Pallas kernels, branch(): pl.pallas_call(functools.partial(branch_kernel, BLOCK, grid_of is not Non...  88.6 us
    pallas_call x1, Pallas kernels, finish_all(): pl.pallas_call(finish_kernel, in_specs=[vmem] + [anywhere] * 12 + [vmem]...  72.5 us
    pallas_call x1, Pallas kernels, gather_project(): pl.pallas_call(gather_project_kernel, in_specs=[vmem, anywhere, vmem, any...  46.4 us
    pallas_call x1, Pallas kernels, slot_backward(): pl.pallas_call(functools.partial(slot_backward_kernel, rows_count, group_...  35.6 us
    pallas_call x1, Pallas kernels, local_backward(): pl.pallas_call(functools.partial(local_backward_kernel, talk, rows_count,...  34.7 us
    pallas_call x1, Pallas kernels, slot_forward(): pl.pallas_call(functools.partial(slot_forward_kernel, rows_count, group_r...  22.9 us
    pallas_call x1, Pallas kernels, local_forward(): pl.pallas_call(functools.partial(local_forward_kernel, talk, rows_count,...  22.5 us

profile of v2, /device:TPU:0, one launch (start us, length us, event | category | flops | bytes accessed | tf_op | source)
XLA Modules:
  0.0 343.9 jit_solution(14509095687954439547)
XLA Ops:
  0.7 0.6 pad_add_fusion.place
  1.3 1.3 broadcast_in_dim.15.b2_ref
  2.5 0.8 reshape.68
  3.3 0.7 reshape.69.b1_ref
  4.0 46.4 %gather_project.1 = (bf16[1024,768]{1,0:T(8,128)(2,1)}, bf16[1024,768]{1,0:T(8,128)(2,1)}, bf16[1024,768]{1,0:T(8,128)(2,1)}, bf16[1024,768]{1,0:T(8,128)(2,1)},...) custom-call(bf16[1024,768]{1,0:T(8,128)(2,1)} %bitcast.52, ...), custom_call_target="tpu_custom_call" | custom-call | flops 7247757312 | bytes 18874368 | tf_op jit(solution)/shard_map/gather_project/pallas_call | solution.py:495
  50.4 22.9 %slot_forward.1 = (f32[768,1024]{1,0:T(8,128)}, f32[6,2,8,1024]{3,2,1,0:T(8,128)}, bf16[8,6,128,128]{3,2,1,0:T(8,128)(2,1)}, f32[8,6,8,128]{3,2,1,0:T(8,128)}) custom-call(s32[2,8]{1,0:T(2,128)} %lengths.7, s32[2]{0:T(128)} %bucket_of.7, s32[3]{0:T(128)} %pad_add_fusion.place, bf16[1024,768]{1,0:T(8,128)(2,1)} %get-tuple-element.65.q_ref, ...), custom_call_target="tpu_custom_call" | custom-call | flops 3221225472 | bytes 15728640 | tf_op jit(solution)/shard_map/slot_forward/pallas_call | solution.py:729
  73.4 22.5 %local_forward.1 = (bf16[1024,768]{1,0:T(8,128)(2,1)}, f32[6,2,8,1024]{3,2,1,0:T(8,128)}, bf16[2,2,3,128,128]{4,3,2,1,0:T(8,128)(2,1)}, f32[2,2,3,8,128]{4,3,2,1,0:T(8,128)}) custom-call(s32[2,8]{1,0:T(2,128)} %lengths.7, s32[2]{0:T(128)} %bucket_of.7, s32[3]{0:T(128)} %pad_add_fusion.place, bf16[1024,768]{1,0:T(8,128)(2,1)} %get-tuple-element.65.q_ref, ...), custom_call_target="tpu_custom_call" | custom-call | flops 6442450944 | bytes 12582912 | tf_op jit(solution)/shard_map/local_forward/pallas_call | solution.py:981
  95.9 88.6 %branch.1 = (bf16[1024,768]{1,0:T(8,128)(2,1)}, f32[1024,768]{1,0:T(8,128)}, bf16[1024,768]{1,0:T(8,128)(2,1)}, bf16[64,768]{1,0:T(8,128)(2,1)}, f32[64,768]{1,0...) custom-call(bf16[1024,768]{1,0:T(8,128)(2,1)} %get-tuple-element.68., ...), custom_call_target="tpu_custom_call" | custom-call | flops 36691771392 | bytes 33030144 | tf_op jit(solution)/shard_map/branch/pallas_call | solution.py:1417
  184.5 0.7 reduce
  185.3 0.1 reshape_reshape.3
  185.4 0.7 reshape.74.db1_ref
  186.1 34.7 %local_backward.1 = (f32[768,1024]{1,0:T(8,128)}, f32[1024,768]{1,0:T(8,128)}, f32[1024,768]{1,0:T(8,128)}, f32[6,2,8,1024]{3,2,1,0:T(8,128)}, bf16[1024,896]{1,...) custom-call(s32[2,8]{1,0:T(2,128)} %lengths.7, s32[2]{0:T(128)} %bucket_of.7, ...), custom_call_target="tpu_custom_call" | custom-call | flops 16106127360 | bytes 23592960 | tf_op jit(solution)/shard_map/local_backward/pallas_call | solution.py:1644
  220.8 35.6 %slot_backward.1 = (bf16[1024,768]{1,0:T(8,128)(2,1)}, bf16[1024,768]{1,0:T(8,128)(2,1)}, bf16[1024,768]{1,0:T(8,128)(2,1)}, bf16[3,768,768]{2,1,0:T(8,128)(2,1)...) custom-call(s32[2,8]{1,0:T(2,128)} %lengths.7, s32[2]{0:T(128)} %bucket_of.7, s32[3]{0:T(128)} %pad_add_fusion.place, ...), custom_call_target="tpu_custom_call" | custom-call | flops 8053063680 | bytes 31457280 | tf_op jit(solution)/shard_map/slot_backward/pallas_call | solution.py:1878
  256.4 0.0 copy-start.2
  256.4 0.0 copy-start.4
  256.4 72.5 %finish_all.1 = (f32[288,384]{1,0:T(8,128)}, f32[16,768]{1,0:T(8,128)}, f32[64,768]{1,0:T(8,128)}, bf16[1024,768]{1,0:T(8,128)(2,1)}, f32[1024,768]{1,0:T(8,128)}) custom-call(bf16[3,2,2,2,48,384]{5,4,3,2,1,0:T(8,128)(2,1)} %get-tuple-element.87.rest_ref, bf16[1024,768]{1,0:T(8,128)(2,1)} %get-tuple-element.68.x_ref.x_in, ...), custom_call_target="tpu_custom_call" | custom-call | flops 7247757312 | bytes 23592960 | tf_op jit(solution)/shard_map/finish_all/pallas_call | solution.py:2330
  329.0 1.3 slice_reduce_fusion
  330.3 0.7 slice.37
  331.1 1.4 slice.39
  332.5 0.6 reshape.77
  333.1 0.9 slice.34
  334.0 1.7 slice_bitcast_fusion
  335.7 0.0 copy-done.2
  335.7 0.0 copy-done.4
  335.8 0.8 fusion
  336.5 0.3 reshape_squeeze.7
  336.8 0.0 copy-start.1
  336.8 0.0 copy-start.5
  336.8 0.5 copy.35
  337.3 1.5 reshape.76
  338.8 0.0 copy-done.1
  338.8 0.0 copy-start
  338.8 1.1 copy.41
  340.0 0.0 copy-done.5
  340.0 0.6 copy.42
  340.6 0.7 copy-done
  341.3 0.0 copy-start.3
  341.3 1.7 copy.43
  343.0 0.0 copy-done.3
  343.0 0.7 copy.44
  (3 shorter events, 0.1 us)
Async XLA Ops:
  256.4 79.3 %copy-start.2 = (f32[192,384]{1,0:T(8,128)S(1)}, f32[192,384]{1,0:T(8,128)}, u32[]{:S(2)}) copy-start(f32[192,384]{1,0:T(8,128)} %get-tuple-element.114) | copy-start | bytes 884740
  256.4 79.3 %copy-start.4 = (f32[96,384]{1,0:T(8,128)S(1)}, f32[96,384]{1,0:T(8,128)}, u32[]{:S(2)}) copy-start(f32[96,384]{1,0:T(8,128)} %get-tuple-element.115) | copy-start | bytes 442372
  336.8 2.0 copy-start.1
  336.8 3.1 copy-start.5
  338.8 2.5 copy-start
  341.3 1.7 copy-start.3

commit v3 on v2

--- a/solution.py
+++ b/solution.py
@@ -16,6 +16,7 @@
 GLOBALS = 128
 SLOTS = 8
 FF_CHUNK = 768
+TOGETHER = 3
 
 norm_eps = 1e-05
 masked_score = -1e30
@@ -247,36 +248,38 @@
                 copy.wait_send()
 
 
-ORDERS = (("core", "x", "y", "z0", "z1"), ("core", "y", "x", "z0", "z1"))
-
-
-class WeightSum:
-    def __init__(self, sources, landings, own, send_sem, recv_sem, own_sem, out, bits, partners):
+X_FIRST = ("core", "x", "y", "z0", "z1")
+Y_FIRST = ("core", "y", "x", "z0", "z1")
+Z_FIRST = ("core", "z0", "x", "z1", "y")
+AXES = ("z1", "z0", "y", "core", "x")
+
+
+class HalvingSum:
+    def __init__(
+        self, orders, sources, landings, own, send_sem, recv_sem, own_sem, put, bits, partners
+    ):
+        self.orders = orders
         self.sources = sources
         self.landings = landings
         self.own = own
         self.send_sem = send_sem
         self.recv_sem = recv_sem
         self.own_sem = own_sem
-        self.out = out
+        self.put = put
         self.bits = bits
         self.partners = partners
 
     def part(self, unit, stage, other):
-        name = ORDERS[unit % 2][stage]
+        order = self.orders[unit]
+        name = order[stage]
         side = 1 - self.bits[name] if other else self.bits[name]
         if stage == 0:
             if not other and self.own is not None:
                 return self.own.at[unit]
             return self.sources[unit](side)
-        ref = self.landings[stage - 1].at[unit]
-        if stage == 1:
-            return ref.at[:, :, :, side] if name == "x" else ref.at[:, :, side]
-        if stage == 2:
-            return ref.at[:, :, side]
-        if stage == 3:
-            return ref.at[:, side]
-        return ref.at[side]
+        left = [axis for axis in AXES if axis in order[stage:]]
+        index = (slice(None),) * left.index(name) + (side,)
+        return self.landings[stage - 1].at[unit].at[index]
 
     def copy(self, unit, stage):
         return remote(
@@ -284,7 +287,7 @@
             self.landings[stage].at[unit],
             self.send_sem.at[unit, stage],
             self.recv_sem.at[unit, stage],
-            self.partners[ORDERS[unit % 2][stage]],
+            self.partners[self.orders[unit][stage]],
         )
 
     def own_copy(self, unit):
@@ -303,18 +306,22 @@
         self.copy(unit, stage).wait_recv()
         landing = self.landings[stage].at[unit]
         kept = self.part(unit, stage, False)
-        if stage < STAGES - 1:
+        if stage < len(self.orders[unit]) - 1:
             add_into(landing, kept)
             if not stop:
                 self.copy(unit, stage + 1).start()
         else:
-            rows = landing.shape[0]
-            self.out[unit * rows : (unit + 1) * rows] = landing[...].astype(f32) + kept[
-                ...
-            ].astype(f32)
+            self.put(unit, landing[...].astype(f32) + kept[...].astype(f32))
 
     def sent(self, unit, stage):
         self.copy(unit, stage).wait_send()
+
+
+def put_rows(ref, rows):
+    def put(unit, value):
+        ref[unit * rows : (unit + 1) * rows] = value
+
+    return put
 
 
 def add_into(target, more):
@@ -377,61 +384,88 @@
     states_ref,
     w1_ref,
     norms_ref,
+    wq_in,
+    wk_in,
+    wv_in,
+    h_out,
+    q_out,
+    k_out,
+    v_out,
+    x_out,
+    ct_out,
+    all_out,
+    gh_out,
+    gq_out,
+    gk_out,
+    gv_out,
+    w1t_out,
     wq_ref,
     wk_ref,
     wv_ref,
-    h_ref,
-    q_ref,
-    k_ref,
-    v_ref,
     x_ref,
-    ct_out_ref,
     all_ref,
-    gh_ref,
-    gq_ref,
-    gk_ref,
-    gv_ref,
+    local_ref,
+    global_ref,
+    w1s_ref,
     w1t_ref,
-    w1s_ref,
     halo_send,
     halo_recv,
-    move_sem,
-    w1_sem,
+    load_sem,
+    store_sem,
+    gstore_sem,
+    more_sem,
     send_sem,
     recv_sem,
 ):
     bits, partners = my_place()
     batch = lax.axis_index("batch")
     seq = lax.axis_index("seq")
-    count = lax.axis_size("seq")
-    after = (batch, lax.rem(seq + 1, count))
-    before = (batch, lax.rem(seq + count - 1, count))
+    places = lax.axis_size("seq")
+    after = (batch, lax.rem(seq + 1, places))
+    before = (batch, lax.rem(seq + places - 1, places))
     rows, width = tokens_ref.shape
     own = states_ref.shape[0]
     core, y, z0, z1 = (bits[name] for name in ("core", "y", "z0", "z1"))
-    w1_copy = pltpu.make_async_copy(w1_ref, w1s_ref, w1_sem)
-    w1_copy.start()
-    ct_copy = pltpu.make_async_copy(
-        ct_ref.at[pl.ds(0, rows - HALF)], ct_out_ref.at[pl.ds(HALF, rows - HALF)], move_sem
-    )
-    ct_copy.start()
+    start = pl.ds(0, HALF)
+    most = pl.ds(0, rows - HALF)
+    end = pl.ds(rows - HALF, HALF)
+    shifted = pl.ds(HALF, rows - HALF)
+    loads = [
+        pltpu.make_async_copy(source, target, load_sem.at[number])
+        for number, (source, target) in enumerate(
+            (
+                (tokens_ref.at[most], x_ref.at[shifted]),
+                (wq_in, wq_ref),
+                (wk_in, wk_ref),
+                (wv_in, wv_ref),
+                (w1_ref, w1s_ref),
+                (ct_ref.at[most], ct_out.at[shifted]),
+            )
+        )
+    ]
+    for load in loads:
+        load.start()
     all_ref[z1, z0, y, core] = states_ref[...]
     meet([partners[name] for name, unused in WEIGHTS] + [before, after])
-    end = pl.ds(rows - HALF, HALF)
-    start = pl.ds(0, HALF)
     halo = [
-        remote(
-            tokens_ref.at[end], x_ref.at[start], halo_send.at[0], halo_recv.at[0], after
-        ),
-        remote(
-            ct_ref.at[end], ct_out_ref.at[start], halo_send.at[1], halo_recv.at[1], after
-        ),
+        remote(tokens_ref.at[end], x_ref.at[start], halo_send.at[0], halo_recv.at[0], after),
+        remote(ct_ref.at[end], ct_out.at[start], halo_send.at[1], halo_recv.at[1], after),
     ]
+    gather = RowGather(all_ref, width // 2, send_sem, recv_sem, bits, partners)
+    gather.begin()
     halo[0].start()
 
-    gather = RowGather(all_ref, width // 2, send_sem, recv_sem, bits, partners)
-
-    def project(at):
+    outs = (h_out, q_out, k_out, v_out)
+
+    def stores(index):
+        at = pl.ds(index * HALF, HALF)
+        return [
+            pltpu.make_async_copy(local_ref.at[which, at], out.at[at], store_sem.at[which, index])
+            for which, out in enumerate(outs)
+        ]
+
+    def project(index):
+        at = pl.ds(index * HALF, HALF)
         project_rows(
             x_ref.at[at],
             norms_ref.at[0:1],
@@ -439,21 +473,24 @@
             wq_ref,
             wk_ref,
             wv_ref,
-            [ref.at[at] for ref in (h_ref, q_ref, k_ref, v_ref)],
+            [local_ref.at[which, at] for which in range(4)],
         )
-
-    gather.begin()
-    halo[1].start()
-    x_ref[HALF:] = tokens_ref[: rows - HALF]
-    project(pl.ds(HALF, HALF))
+        for store in stores(index):
+            store.start()
+
+    for number in range(4):
+        loads[number].wait()
+    tiles = rows // HALF
+    project(1)
     gather.advance(0)
-    project(pl.ds(2 * HALF, HALF))
-    for index in range(3, rows // HALF):
-        project(pl.ds(index * HALF, HALF))
+    for index in range(2, tiles):
+        project(index)
     gather.advance(1)
     halo[0].wait_recv()
-    project(start)
-    w1_copy.wait()
+    x_store = pltpu.make_async_copy(x_ref, x_out, more_sem.at[0])
+    x_store.start()
+    project(0)
+    loads[4].wait()
 
     def turn(i, carry):
         at = pl.ds(pl.multiple_of(i * HALF, HALF), HALF)
@@ -461,22 +498,58 @@
         return carry
 
     lax.fori_loop(0, w1t_ref.shape[0] // HALF, turn, 0)
+    w1t_store = pltpu.make_async_copy(w1t_ref, w1t_out, more_sem.at[1])
+    w1t_store.start()
     gather.advance(2)
+    halo[1].start()
+
+    gouts = (gh_out, gq_out, gk_out, gv_out)
+
+    def gstores(first, side):
+        return [
+            pltpu.make_async_copy(
+                global_ref.at[which, first, :, :, side],
+                out.at[first, :, :, side],
+                gstore_sem.at[which, first, number],
+            )
+            for which, out in enumerate(gouts)
+            for number in ((0 if side is core else 1),)
+        ]
+
+    def project_states(side):
+        for first in range(2):
+            piece = all_ref[first, :, :, side].reshape(4 * own, width)
+            unit, unused = normalize_rows(piece.astype(f32))
+            normed = (unit * norms_ref[2:3] + norms_ref[3:4]).astype(bf16)
+            values = (
+                normed,
+                (nn(normed, wq_ref[...]) * query_scale).astype(bf16),
+                nn(normed, wk_ref[...]).astype(bf16),
+                nn(normed, wv_ref[...]).astype(bf16),
+            )
+            for which, value in enumerate(values):
+                global_ref[which, first, :, :, side] = value.reshape(2, 2, own, width)
+            for store in gstores(first, side):
+                store.start()
+
+    other = 1 - core
+    project_states(core)
     gather.advance(3)
-
-    def project_states(i, carry):
-        at = pl.ds(pl.multiple_of(i * HALF, HALF), HALF)
-        piece = all_ref[i // 2, i % 2].reshape(HALF, width)
-        unit, unused = normalize_rows(piece.astype(f32))
-        normed = (unit * norms_ref[2:3] + norms_ref[3:4]).astype(bf16)
-        gh_ref[at, :] = normed
-        gq_ref[at, :] = (nn(normed, wq_ref[...]) * query_scale).astype(bf16)
-        gk_ref[at, :] = nn(normed, wk_ref[...]).astype(bf16)
-        gv_ref[at, :] = nn(normed, wv_ref[...]).astype(bf16)
-        return carry
-
-    lax.fori_loop(0, 4, project_states, 0)
-    ct_copy.wait()
+    all_store = pltpu.make_async_copy(all_ref, all_out, more_sem.at[2])
+    all_store.start()
+    project_states(other)
+
+    for index in range(tiles):
+        for store in stores(index):
+            store.wait()
+    for side in (core, other):
+        for first in range(2):
+            for store in gstores(first, side):
+                store.wait()
+    x_store.wait()
+    w1t_store.wait()
+    all_store.wait()
+    loads[5].wait()
     halo[1].wait_recv()
     for copy in halo:
         copy.wait_send()
@@ -486,32 +559,40 @@
 def gather_project(tokens, ct, states, w1, norms, wq, wk, wv):
     rows, width = tokens.shape
     own = states.shape[0]
-    all_globals = 16 * own
     vmem = pl.BlockSpec(memory_space=pltpu.VMEM)
     anywhere = pl.BlockSpec(memory_space=pl.ANY)
     dma = pltpu.SemaphoreType.DMA
     local = jax.ShapeDtypeStruct((rows, width), bf16)
-    glob = jax.ShapeDtypeStruct((all_globals, width), bf16)
+    glob = jax.ShapeDtypeStruct((2, 2, 2, 2, own, width), bf16)
+    turned = (w1.shape[1], width)
+    weight = pltpu.VMEM((width, width), bf16)
     return pl.pallas_call(
         gather_project_kernel,
-        in_specs=[vmem, anywhere, vmem, anywhere] + [vmem] * 4,
-        out_specs=[vmem] * 5 + [anywhere] + [vmem] * 6,
-        out_shape=[local] * 6
-        + [jax.ShapeDtypeStruct((2, 2, 2, 2, own, width), bf16)]
-        + [glob] * 4
-        + [jax.ShapeDtypeStruct((w1.shape[1], width), bf16)],
+        in_specs=[anywhere, anywhere, vmem, anywhere, vmem] + [anywhere] * 3,
+        out_specs=[anywhere] * 12,
+        out_shape=[local] * 6 + [glob] * 5 + [jax.ShapeDtypeStruct(turned, bf16)],
         scratch_shapes=[
+            weight,
+            weight,
+            weight,
+            pltpu.VMEM((rows, width), bf16),
+            pltpu.VMEM(glob.shape, bf16),
+            pltpu.VMEM((4, rows, width), bf16),
+            pltpu.VMEM((4,) + glob.shape, bf16),
             pltpu.VMEM(w1.shape, bf16),
+            pltpu.VMEM(turned, bf16),
             dma((2,)),
             dma((2,)),
-            dma,
-            dma,
+            dma((6,)),
+            dma((4, rows // HALF)),
+            dma((4, 2, 2)),
+            dma((3,)),
             dma((4, 2)),
             dma((4, 2)),
         ],
         compiler_params=params(collective_id=1, has_side_effects=True),
         cost_estimate=pl.CostEstimate(
-            flops=6 * (rows + all_globals) * width * width,
+            flops=6 * (rows + 16 * own) * width * width,
             bytes_accessed=24 * rows * width,
             transcendentals=0,
         ),
@@ -618,11 +699,13 @@
     keys_ref,
     queries_ref,
     sum_ref,
+    far_sum,
 ):
-    pair = pl.program_id(0)
+    group = pl.program_id(0)
     block = pl.program_id(1)
     blocks = rows_count // BLOCK
-    step = pair * blocks + block
+    step = group * blocks + block
+    together = range(TOGETHER)
 
     @pl.when(step == 0)
     def _():
@@ -639,82 +722,105 @@
         place, edges, rows_count, group_rows, block, step, blocks, query_columns, key_columns
     )
     extra = query_columns[block]
-    keys_ref[:, :LANES] = k_ref[...]
-    keys_ref[:, LANES:] = key_columns[block]
-    queries_ref[:, :LANES] = stack_pair(q_ref[...])
-    queries_ref[:BLOCK, LANES:] = extra
-    queries_ref[BLOCK:, LANES:] = extra
+    for which in together:
+        lanes = pl.ds(which * LANES, LANES)
+        keys_ref[which, :, :LANES] = k_ref[:, lanes]
+        keys_ref[which, :, LANES:] = key_columns[block]
+        queries_ref[which, :, :LANES] = stack_pair(q_ref[:, lanes])
+        queries_ref[which, :BLOCK, LANES:] = extra
+        queries_ref[which, BLOCK:, LANES:] = extra
     line = slot_line(place, edges, rows_count, group_rows, block)
     both_lines = jnp.concatenate([line, line], 1)
 
-    def add(slot, keys, values):
+    def add(slot, keys_of, values_of):
         at = pl.ds(pl.multiple_of(slot * GLOBALS, GLOBALS), GLOBALS)
         extra = global_query_extra(slot).astype(bf16)
-        queries = jnp.concatenate(
-            [stack_pair(gq_ref[at, :]), jnp.concatenate([extra, extra], 0)], axis=1
-        )
-        score = nt(keys, queries)
-        stat = part_stat_ref[slot, 0]
-        old = jnp.concatenate([stat[0:1], stat[1:2]], axis=1)
-        peak = jnp.maximum(old, jnp.max(score, axis=0, keepdims=True))
-        weights = jnp.exp(score - peak)
-        keep = jnp.exp(old - peak)
-        total = jnp.concatenate([stat[2:3], stat[3:4]], axis=1) * keep + jnp.sum(
-            weights, axis=0, keepdims=True
-        )
-        part_stat_ref[slot, 0] = jnp.concatenate(
-            [
-                peak[:, :GLOBALS],
-                peak[:, GLOBALS:],
-                total[:, :GLOBALS],
-                total[:, GLOBALS:],
-                jnp.zeros((4, GLOBALS), f32),
-            ],
-            axis=0,
-        )
-        low, high = side_by_side(tn(values, weights.astype(bf16)))
-        sum_ref[slot, :HEAD_DIM] = sum_ref[slot, :HEAD_DIM] * keep[:, :GLOBALS] + low
-        sum_ref[slot, HEAD_DIM:] = sum_ref[slot, HEAD_DIM:] * keep[:, GLOBALS:] + high
-
-    far_ref[...] = jnp.zeros_like(far_ref)
+        for which in together:
+            lanes = pl.ds(which * LANES, LANES)
+            queries = jnp.concatenate(
+                [stack_pair(gq_ref[at, lanes]), jnp.concatenate([extra, extra], 0)], axis=1
+            )
+            score = nt(keys_of(which), queries)
+            stat = part_stat_ref[slot, which]
+            old = jnp.concatenate([stat[0:1], stat[1:2]], axis=1)
+            peak = jnp.maximum(old, jnp.max(score, axis=0, keepdims=True))
+            weights = jnp.exp(score - peak)
+            keep = jnp.exp(old - peak)
+            total = jnp.concatenate([stat[2:3], stat[3:4]], axis=1) * keep + jnp.sum(
+                weights, axis=0, keepdims=True
+            )
+            part_stat_ref[slot, which] = jnp.concatenate(
+                [
+                    peak[:, :GLOBALS],
+                    peak[:, GLOBALS:],
+                    total[:, :GLOBALS],
+                    total[:, GLOBALS:],
+                    jnp.zeros((4, GLOBALS), f32),
+                ],
+                axis=0,
+            )
+            low, high = side_by_side(tn(values_of(which), weights.astype(bf16)))
+            sums = sum_ref.at[which, slot]
+            sums[:HEAD_DIM] = sums[:HEAD_DIM] * keep[:, :GLOBALS] + low
+            sums[HEAD_DIM:] = sums[HEAD_DIM:] * keep[:, GLOBALS:] + high
+
+    far_sum[...] = jnp.zeros_like(far_sum)
     far_stat_ref[...] = jnp.zeros_like(far_stat_ref)
 
     def one_slot(slot, carry):
         @pl.when(slot_present(slot, place, edges, rows_count, group_rows, block))
         def _():
-            add(slot, keys_ref[...], v_ref[...])
+            add(
+                slot,
+                lambda which: keys_ref[which],
+                lambda which: v_ref[:, pl.ds(which * LANES, LANES)],
+            )
             at = pl.ds(pl.multiple_of(slot * GLOBALS, GLOBALS), GLOBALS)
-            slot_keys = jnp.concatenate([gk_ref[at, :], global_key_extra(slot).astype(bf16)], 1)
-            score = nt(slot_keys, queries_ref[...])
-            peak = jnp.max(score, axis=0, keepdims=True)
-            weights = jnp.exp(score - peak)
-            total = jnp.sum(weights, axis=0, keepdims=True)
+            columns = global_key_extra(slot).astype(bf16)
             mine = both_lines == slot
-            far_stat_ref[0, 0, 0:1] = jnp.where(mine, peak, far_stat_ref[0, 0, 0:1])
-            far_stat_ref[0, 0, 1:2] = jnp.where(mine, total, far_stat_ref[0, 0, 1:2])
-            low, high = side_by_side(tn(gv_ref[at, :], weights.astype(bf16)))
             here = line == slot
-            far_ref[:HEAD_DIM] = jnp.where(here, low, far_ref[:HEAD_DIM])
-            far_ref[HEAD_DIM:] = jnp.where(here, high, far_ref[HEAD_DIM:])
+            for which in together:
+                lanes = pl.ds(which * LANES, LANES)
+                slot_keys = jnp.concatenate([gk_ref[at, lanes], columns], 1)
+                score = nt(slot_keys, queries_ref[which])
+                peak = jnp.max(score, axis=0, keepdims=True)
+                weights = jnp.exp(score - peak)
+                total = jnp.sum(weights, axis=0, keepdims=True)
+                stat = far_stat_ref.at[which, 0]
+                stat[0:1] = jnp.where(mine, peak, stat[0:1])
+                stat[1:2] = jnp.where(mine, total, stat[1:2])
+                low, high = side_by_side(tn(gv_ref[at, lanes], weights.astype(bf16)))
+                first = pl.ds(which * LANES, HEAD_DIM)
+                second = pl.ds(which * LANES + HEAD_DIM, HEAD_DIM)
+                far_sum[first] = jnp.where(here, low, far_sum[first])
+                far_sum[second] = jnp.where(here, high, far_sum[second])
 
         return carry
 
     lax.fori_loop(0, SLOTS, one_slot, 0)
+    far_ref[...] = far_sum[...].astype(bf16)
 
     @pl.when((block == blocks - 1) & (place[2] >= 0))
     def _():
         slot = place[2]
         at = pl.ds(pl.multiple_of(slot * GLOBALS, GLOBALS), GLOBALS)
-        keys = jnp.concatenate([gk_ref[at, :], global_key_extra(slot).astype(bf16)], axis=1)
-        add(slot, keys, gv_ref[at, :])
+        columns = global_key_extra(slot).astype(bf16)
+        add(
+            slot,
+            lambda which: jnp.concatenate(
+                [gk_ref[at, pl.ds(which * LANES, LANES)], columns], axis=1
+            ),
+            lambda which: gv_ref[at, pl.ds(which * LANES, LANES)],
+        )
 
     @pl.when(block == blocks - 1)
     def _():
-        part_ref[:, 0] = sum_ref[...].astype(bf16)
-
-
-def line_spec():
-    return pl.BlockSpec((1, 1, 8, 2 * BLOCK), lambda p, b, *unused: (p, b, 0, 0))
+        for which in together:
+            part_ref[:, which] = sum_ref[which].astype(bf16)
+
+
+def line_spec(pairs=1):
+    return pl.BlockSpec((pairs, 1, 8, 2 * BLOCK), lambda p, b, *unused: (p, b, 0, 0))
 
 
 def column_scratch(blocks):
@@ -724,29 +830,30 @@
 def slot_forward(scalars, rows_count, group_rows, q, k, v, gq, gk, gv):
     blocks = rows_count // BLOCK
     all_globals, width = gq.shape
-    block_spec = pl.BlockSpec((BLOCK, LANES), lambda p, b, *unused: (b, p))
-    pair_spec = pl.BlockSpec((all_globals, LANES), lambda p, b, *unused: (0, p))
+    block_spec = pl.BlockSpec((BLOCK, TOGETHER * LANES), lambda p, b, *unused: (b, p))
+    pair_spec = pl.BlockSpec((all_globals, TOGETHER * LANES), lambda p, b, *unused: (0, p))
     return pl.pallas_call(
         functools.partial(slot_forward_kernel, rows_count, group_rows),
         grid_spec=pltpu.PrefetchScalarGridSpec(
             num_scalar_prefetch=3,
-            grid=(PAIRS, blocks),
+            grid=(PAIRS // TOGETHER, blocks),
             in_specs=[block_spec] * 3 + [pair_spec] * 3,
             out_specs=[
-                pl.BlockSpec((LANES, BLOCK), lambda p, b, *unused: (p, b)),
-                line_spec(),
-                pl.BlockSpec((SLOTS, 1, LANES, GLOBALS), lambda p, b, *unused: (0, p, 0, 0)),
-                pl.BlockSpec((SLOTS, 1, 8, GLOBALS), lambda p, b, *unused: (0, p, 0, 0)),
+                pl.BlockSpec((TOGETHER * LANES, BLOCK), lambda p, b, *unused: (p, b)),
+                line_spec(TOGETHER),
+                pl.BlockSpec((SLOTS, TOGETHER, LANES, GLOBALS), lambda p, b, *unused: (0, p, 0, 0)),
+                pl.BlockSpec((SLOTS, TOGETHER, 8, GLOBALS), lambda p, b, *unused: (0, p, 0, 0)),
             ],
             scratch_shapes=column_scratch(blocks)
             + [
-                pltpu.VMEM((BLOCK, 2 * LANES), bf16),
-                pltpu.VMEM((2 * BLOCK, 2 * LANES), bf16),
-                pltpu.VMEM((SLOTS, LANES, GLOBALS), f32),
+                pltpu.VMEM((TOGETHER, BLOCK, 2 * LANES), bf16),
+                pltpu.VMEM((TOGETHER, 2 * BLOCK, 2 * LANES), bf16),
+                pltpu.VMEM((TOGETHER, SLOTS, LANES, GLOBALS), f32),
+                pltpu.VMEM((TOGETHER * LANES, BLOCK), f32),
             ],
         ),
         out_shape=[
-            jax.ShapeDtypeStruct((width, rows_count), f32),
+            jax.ShapeDtypeStruct((width, rows_count), bf16),
             jax.ShapeDtypeStruct((PAIRS, blocks, 8, 2 * BLOCK), f32),
             jax.ShapeDtypeStruct((SLOTS, PAIRS, LANES, GLOBALS), bf16),
             jax.ShapeDtypeStruct((SLOTS, PAIRS, 8, GLOBALS), f32),
@@ -1088,14 +1195,15 @@
         def source(unit):
             return lambda side: units_ref.at[unit % slots, :, :, :, side]
 
-        engine = WeightSum(
+        engine = HalvingSum(
+            (X_FIRST, Y_FIRST) * chunks,
             [source(unit) for unit in range(2 * chunks)],
             landings,
             None,
             send_sem,
             recv_sem,
             None,
-            first_ref,
+            put_rows(first_ref, landings[4].shape[1]),
             bits,
             partners,
         )
@@ -1214,7 +1322,7 @@
         if talk:
             half_ref[...] = go_in_ref[...]
             half_stat_ref[...] = gstat_in_ref[...]
-            meet([partners[name] for name in ORDERS[0]])
+            meet([partners[name] for name in AXES])
             slot_sum.begin(2)
         cts_ref[count:] = padded(gct_ref[...])
         loads[0].wait()
@@ -1515,7 +1623,8 @@
         send_sem, recv_sem, own_sem = refs[12:]
         bits, partners = my_place()
         gather = RowGather(all_ref, 3 * LANES, gather_send, gather_recv, bits, partners)
-        engine = WeightSum(
+        engine = HalvingSum(
+            (X_FIRST, Y_FIRST) * 2 + (X_FIRST,),
             [
                 None,
                 None,
@@ -1528,28 +1637,28 @@
             send_sem,
             recv_sem,
             own_sem,
-            sums_ref,
+            put_rows(sums_ref, landings[4].shape[1]),
             bits,
             partners,
         )
         plan = {
-            1: [(2, 0), (3, 0), (4, 0)],
-            3: [(0, 2), (1, 2)],
-            6: [(0, 3), (1, 3)],
+            3: [(2, 0), (3, 0), (4, 0)],
+            4: [(0, 2), (1, 2)],
+            7: [(0, 3), (1, 3)],
             11: [(0, 4), (1, 4), (2, 1), (3, 1), (4, 1)],
         }
-        gather_plan = {2: 0, 5: 1, 8: 2, 11: 3}
+        gather_plan = {2: 0, 5: 1, 8: 2, 10: 3}
 
         @pl.when(step == 0)
         def _():
             all_ref[bits["z1"], bits["z0"], bits["y"], bits["core"]] = message_ref[...]
             landings[1][:2] = rest_ref[...]
-            meet([partners[name] for name in ORDERS[0]])
+            meet([partners[name] for name in AXES])
             gather.begin()
+            for unit in (0, 1):
+                engine.copy(unit, 2).start()
             for unit in (2, 3, 4):
                 engine.begin(unit)
-            for unit in (0, 1):
-                engine.copy(unit, 2).start()
 
         for number in range(PAIRS * blocks):
             if number in plan or number in gather_plan:
@@ -1583,11 +1692,11 @@
     weights = jnp.exp(score - line_ref[0, 0, 0:1])
     along = nt(v_ref[...], grads) - centre
     score_grad = (weights * along).astype(bf16)
-    dv_ref[...] = nn(weights.astype(bf16), grads)
-    dk_ref[...] = nn(score_grad, queries)
+    dv_ref[...] = nn(weights.astype(bf16), grads).astype(bf16)
+    dk_ref[...] = nn(score_grad, queries).astype(bf16)
     low, high = side_by_side(tn(keys, score_grad))
-    dq_ref[:HEAD_DIM] = low
-    dq_ref[HEAD_DIM:] = high
+    dq_ref[:HEAD_DIM] = low.astype(bf16)
+    dq_ref[HEAD_DIM:] = high.astype(bf16)
 
     if talk:
 
@@ -1615,9 +1724,9 @@
         + [line_spec()]
     )
     out_shape = [
-        jax.ShapeDtypeStruct((width, rows_count), f32),
-        jax.ShapeDtypeStruct((rows_count, width), f32),
-        jax.ShapeDtypeStruct((rows_count, width), f32),
+        jax.ShapeDtypeStruct((width, rows_count), bf16),
+        jax.ShapeDtypeStruct((rows_count, width), bf16),
+        jax.ShapeDtypeStruct((rows_count, width), bf16),
         jax.ShapeDtypeStruct((PAIRS, blocks, 8, 2 * BLOCK), f32),
     ]
     scratch = column_scratch(blocks)
@@ -1708,10 +1817,14 @@
     dw_sum,
     dgh_sum,
 ):
-    pair = pl.program_id(0)
+    group = pl.program_id(0)
     block = pl.program_id(1)
     blocks = rows_count // BLOCK
-    step = pair * blocks + block
+    step = group * blocks + block
+    together = range(TOGETHER)
+
+    def lanes_of(which):
+        return pl.ds(which * LANES, LANES)
 
     @pl.when(step == 0)
     def _():
@@ -1736,20 +1849,22 @@
         place, edges, rows_count, group_rows, block, step, blocks, query_columns, key_columns
     )
     extra = query_columns[block]
-    keys_ref[:, :LANES] = k_ref[...]
-    keys_ref[:, LANES:] = key_columns[block]
-    queries_ref[:, :LANES] = stack_pair(q_ref[...])
-    queries_ref[:BLOCK, LANES:] = extra
-    queries_ref[BLOCK:, LANES:] = extra
-    grads_ref[...] = stack_pair(do_ref[...])
-    dqt_sum[...] = dqt_ref[...]
-    dk_sum[...] = dk_in_ref[...]
-    dv_sum[...] = dv_in_ref[...]
-
-    def line_of(slot, first):
+    for which in together:
+        lanes = lanes_of(which)
+        keys_ref[which, :, :LANES] = k_ref[:, lanes]
+        keys_ref[which, :, LANES:] = key_columns[block]
+        queries_ref[which, :, :LANES] = stack_pair(q_ref[:, lanes])
+        queries_ref[which, :BLOCK, LANES:] = extra
+        queries_ref[which, BLOCK:, LANES:] = extra
+        grads_ref[which] = stack_pair(do_ref[:, lanes])
+    dqt_sum[...] = dqt_ref[...].astype(f32)
+    dk_sum[...] = dk_in_ref[...].astype(f32)
+    dv_sum[...] = dv_in_ref[...].astype(f32)
+
+    def line_of(slot, which, first):
         halves = []
-        for which in range(2):
-            spot = first + 2 * pair + which
+        for head in range(2):
+            spot = first + 2 * (group * TOGETHER + which) + head
             halves.append(
                 lines_ref[slot, pl.ds(spot, 1)]
                 + lines_ref[slot, pl.ds(spot + HEADS, 1)]
@@ -1757,36 +1872,41 @@
             )
         return jnp.concatenate(halves, axis=1)
 
-    def from_global(slot, keys, values):
+    def from_global(slot, which, keys, values):
         at = pl.ds(pl.multiple_of(slot * GLOBALS, GLOBALS), GLOBALS)
         extra = global_query_extra(slot).astype(bf16)
-        queries = stack_pair(gq_ref[at, :])
-        grads = stack_pair(gdo_ref[at, :])
+        queries = stack_pair(gq_ref[at, lanes_of(which)])
+        grads = stack_pair(gdo_ref[at, lanes_of(which)])
         score = nt(keys, jnp.concatenate([queries, jnp.concatenate([extra, extra], 0)], 1))
-        weights = jnp.exp(score - line_of(slot, 0))
-        along = nt(values, grads) - line_of(slot, 3 * HEADS)
+        weights = jnp.exp(score - line_of(slot, which, 0))
+        along = nt(values, grads) - line_of(slot, which, 3 * HEADS)
         score_grad = (weights * along).astype(bf16)
         low, high = side_by_side(tn(keys[:, :LANES], score_grad))
-        dgqt_sum[slot, :HEAD_DIM] += low
-        dgqt_sum[slot, HEAD_DIM:] += high
+        dgqt_sum[which, slot, :HEAD_DIM] += low
+        dgqt_sum[which, slot, HEAD_DIM:] += high
         return nn(score_grad, queries), nn(weights.astype(bf16), grads)
 
     def one_slot(slot, carry):
         @pl.when(slot_present(slot, place, edges, rows_count, group_rows, block))
         def _():
-            key_grad, value_grad = from_global(slot, keys_ref[...], v_ref[...])
-            dk_sum[...] += key_grad
-            dv_sum[...] += value_grad
             at = pl.ds(pl.multiple_of(slot * GLOBALS, GLOBALS), GLOBALS)
-            slot_keys = jnp.concatenate([gk_ref[at, :], global_key_extra(slot).astype(bf16)], 1)
-            weights = jnp.exp(nt(slot_keys, queries_ref[...]) - line_ref[0, 0, 0:1])
-            along = nt(gv_ref[at, :], grads_ref[...]) - centre_ref[0, 0, 0:1]
-            score_grad = (weights * along).astype(bf16)
-            dgv_sum[at, :] += nn(weights.astype(bf16), grads_ref[...])
-            dgk_sum[at, :] += nn(score_grad, queries_ref[:, :LANES])
-            low, high = side_by_side(tn(gk_ref[at, :], score_grad))
-            dqt_sum[:HEAD_DIM] += low
-            dqt_sum[HEAD_DIM:] += high
+            columns = global_key_extra(slot).astype(bf16)
+            for which in together:
+                lanes = lanes_of(which)
+                key_grad, value_grad = from_global(slot, which, keys_ref[which], v_ref[:, lanes])
+                dk_sum[:, lanes] += key_grad
+                dv_sum[:, lanes] += value_grad
+                keys = gk_ref[at, lanes]
+                grads = grads_ref[which]
+                score = nt(jnp.concatenate([keys, columns], 1), queries_ref[which])
+                weights = jnp.exp(score - line_ref[which, 0, 0:1])
+                along = nt(gv_ref[at, lanes], grads) - centre_ref[which, 0, 0:1]
+                score_grad = (weights * along).astype(bf16)
+                dgv_sum[at, lanes] += nn(weights.astype(bf16), grads)
+                dgk_sum[at, lanes] += nn(score_grad, queries_ref[which, :, :LANES])
+                low, high = side_by_side(tn(keys, score_grad))
+                dqt_sum[pl.ds(which * LANES, HEAD_DIM)] += low
+                dqt_sum[pl.ds(which * LANES + HEAD_DIM, HEAD_DIM)] += high
 
         return carry
 
@@ -1799,10 +1919,13 @@
     def _():
         slot = place[2]
         at = pl.ds(pl.multiple_of(slot * GLOBALS, GLOBALS), GLOBALS)
-        keys = jnp.concatenate([gk_ref[at, :], global_key_extra(slot).astype(bf16)], axis=1)
-        key_grad, value_grad = from_global(slot, keys, gv_ref[at, :])
-        dgk_sum[at, :] += key_grad
-        dgv_sum[at, :] += value_grad
+        columns = global_key_extra(slot).astype(bf16)
+        for which in together:
+            lanes = lanes_of(which)
+            keys = jnp.concatenate([gk_ref[at, lanes], columns], axis=1)
+            key_grad, value_grad = from_global(slot, which, keys, gv_ref[at, lanes])
+            dgk_sum[at, lanes] += key_grad
+            dgv_sum[at, lanes] += value_grad
 
     @pl.when(block == blocks - 1)
     def _():
@@ -1819,7 +1942,10 @@
             def _():
                 at = pl.ds(pl.multiple_of(slot * GLOBALS, GLOBALS), GLOBALS)
                 grads = (
-                    (dgqt_sum[slot].T * query_scale).astype(bf16),
+                    (
+                        jnp.concatenate([dgqt_sum[which, slot].T for which in together], 1)
+                        * query_scale
+                    ).astype(bf16),
                     dgk_sum[at, :].astype(bf16),
                     dgv_sum[at, :].astype(bf16),
                 )
@@ -1830,7 +1956,7 @@
                     total = total + nt(grads[index], weight[...])
                 dgh_sum[at, :] = total
 
-                @pl.when(pair == PAIRS - 1)
+                @pl.when(group == PAIRS // TOGETHER - 1)
                 def _():
                     unit, unused = normalize_rows(gx_ref[at, :].astype(f32))
                     dnorm_ref[0:1] += jnp.sum(total * unit, axis=0, keepdims=True)
@@ -1841,7 +1967,7 @@
         lax.fori_loop(0, SLOTS, through, 0)
         dw_ref[...] = dw_sum[...].astype(bf16)
 
-    @pl.when(step == PAIRS * blocks - 1)
+    @pl.when(step == PAIRS // TOGETHER * blocks - 1)
     def _():
         dgh_ref[...] = dgh_sum[...].astype(bf16)
 
@@ -1871,42 +1997,42 @@
 ):
     blocks = rows_count // BLOCK
     all_globals, width = gk.shape
-    block_spec = pl.BlockSpec((BLOCK, LANES), lambda p, b, *unused: (b, p))
-    pair_spec = pl.BlockSpec((all_globals, LANES), lambda p, b, *unused: (0, p))
+    block_spec = pl.BlockSpec((BLOCK, TOGETHER * LANES), lambda p, b, *unused: (b, p))
+    pair_spec = pl.BlockSpec((all_globals, TOGETHER * LANES), lambda p, b, *unused: (0, p))
     local = jax.ShapeDtypeStruct((rows_count, width), bf16)
     glob = jax.ShapeDtypeStruct((all_globals, width), bf16)
     return pl.pallas_call(
         functools.partial(slot_backward_kernel, rows_count, group_rows),
         grid_spec=pltpu.PrefetchScalarGridSpec(
             num_scalar_prefetch=3,
-            grid=(PAIRS, blocks),
+            grid=(PAIRS // TOGETHER, blocks),
             in_specs=[block_spec] * 4
-            + [line_spec()] * 2
-            + [pl.BlockSpec((LANES, BLOCK), lambda p, b, *unused: (p, b))]
+            + [line_spec(TOGETHER)] * 2
+            + [pl.BlockSpec((TOGETHER * LANES, BLOCK), lambda p, b, *unused: (p, b))]
             + [block_spec] * 2
             + [pair_spec] * 4
             + [pl.BlockSpec((all_globals, LANES), lambda p, b, *unused: (0, PAIRS))]
             + [once((all_globals, width))] * 2
-            + [pl.BlockSpec((width, LANES), lambda p, b, *unused: (0, p))] * 3,
+            + [pl.BlockSpec((width, TOGETHER * LANES), lambda p, b, *unused: (0, p))] * 3,
             out_specs=[block_spec] * 3
             + [
-                pl.BlockSpec((3, LANES, width), lambda p, b, *unused: (0, p, 0)),
+                pl.BlockSpec((3, TOGETHER * LANES, width), lambda p, b, *unused: (0, p, 0)),
                 once((all_globals, width)),
                 full((8, width)),
             ],
             scratch_shapes=column_scratch(blocks)
             + [
-                pltpu.VMEM((BLOCK, 2 * LANES), bf16),
-                pltpu.VMEM((2 * BLOCK, 2 * LANES), bf16),
-                pltpu.VMEM((2 * BLOCK, LANES), bf16),
-                pltpu.VMEM((LANES, BLOCK), f32),
-                pltpu.VMEM((BLOCK, LANES), f32),
-                pltpu.VMEM((BLOCK, LANES), f32),
+                pltpu.VMEM((TOGETHER, BLOCK, 2 * LANES), bf16),
+                pltpu.VMEM((TOGETHER, 2 * BLOCK, 2 * LANES), bf16),
+                pltpu.VMEM((TOGETHER, 2 * BLOCK, LANES), bf16),
+                pltpu.VMEM((TOGETHER * LANES, BLOCK), f32),
+                pltpu.VMEM((BLOCK, TOGETHER * LANES), f32),
+                pltpu.VMEM((BLOCK, TOGETHER * LANES), f32),
+                pltpu.VMEM((TOGETHER, SLOTS, LANES, GLOBALS), f32),
+                pltpu.VMEM((all_globals, TOGETHER * LANES), f32),
+                pltpu.VMEM((all_globals, TOGETHER * LANES), f32),
                 pltpu.VMEM((SLOTS, LANES, GLOBALS), f32),
-                pltpu.VMEM((all_globals, LANES), f32),
-                pltpu.VMEM((all_globals, LANES), f32),
-                pltpu.VMEM((SLOTS, LANES, GLOBALS), f32),
-                pltpu.VMEM((3, LANES, width), f32),
+                pltpu.VMEM((3, TOGETHER * LANES, width), f32),
                 pltpu.VMEM((all_globals, width), f32),
             ],
         ),
@@ -2006,64 +2132,6 @@
         ),
         name="project_back",
     )(x, dy, h, dq, dk, dv, dwg, wq, wk, wv, gain)
-
-
-class RowSum:
-    ORDER = ("core", "y", "z0", "z1")
-
-    def __init__(self, source, own, landings, send_sem, recv_sem, own_sem, bits, partners):
-        self.source = source
-        self.own = own
-        self.landings = landings
-        self.send_sem = send_sem
-        self.recv_sem = recv_sem
-        self.own_sem = own_sem
-        self.bits = bits
-        self.partners = partners
-
-    def part(self, stage, other):
-        bit = self.bits[self.ORDER[stage]]
-        side = 1 - bit if other else bit
-        if stage == 0:
-            return self.source.at[:, :, :, side] if other else self.own
-        ref = self.landings[stage - 1]
-        if stage == 1:
-            return ref.at[:, :, side]
-        if stage == 2:
-            return ref.at[:, side]
-        return ref.at[side]
-
-    def copy(self, stage):
-        return remote(
-            self.part(stage, True),
-            self.landings[stage],
-            self.send_sem.at[stage],
-            self.recv_sem.at[stage],
-            self.partners[self.ORDER[stage]],
-        )
-
-    def own_copy(self):
-        return pltpu.make_async_copy(
-            self.source.at[:, :, :, self.bits["core"]], self.own, self.own_sem
-        )
-
-    def begin(self):
-        self.own_copy().start()
-        self.copy(0).start()
-
-    def advance(self, stage):
-        if stage == 0:
-            self.own_copy().wait()
-        self.copy(stage).wait_recv()
-        if stage < 3:
-            add_into(self.landings[stage], self.part(stage, False))
-            self.copy(stage + 1).start()
-            return None
-        return self.landings[3][...].astype(f32) + self.part(3, False)[...].astype(f32)
-
-    def end(self):
-        for stage in range(4):
-            self.copy(stage).wait_send()
 
 
 def finish_kernel(
@@ -2130,6 +2198,7 @@
     halo_send,
     halo_recv,
     dnorm_ref,
+    dgh_sum_ref,
 ):
     bits, partners = my_place()
     count, width = x_ref.shape
@@ -2164,27 +2233,43 @@
     def source(unit):
         return lambda side: units_ref.at[unit - came, :, :, :, side]
 
-    engine = WeightSum(
+    engine = HalvingSum(
+        (X_FIRST, Y_FIRST, X_FIRST, X_FIRST, Y_FIRST, Z_FIRST),
         [source(unit) for unit in range(units)],
         (one_ref, two_ref, three_ref, four_ref, five_ref),
         None,
         send_sem,
         recv_sem,
         None,
-        out_ref,
+        put_rows(out_ref, five_ref.shape[1]),
         bits,
         partners,
     )
-    row_sum = RowSum(
-        dgh_ref,
+    wide = gone_ref.shape[-1]
+
+    def row_source(unit):
+        lanes = pl.ds(unit * wide, wide)
+        return lambda side: dgh_ref.at[:, :, :, side, :, lanes]
+
+    def put_dgh(unit, value):
+        dgh_sum_ref[:, unit * wide : (unit + 1) * wide] = value
+
+    row_sum = HalvingSum(
+        (("core", "y", "z0", "z1"), ("core", "z0", "y", "z1")),
+        [row_source(unit) for unit in range(2)],
+        (gone_ref, gtwo_ref, gthree_ref, gfour_ref),
         gown_ref,
-        (gone_ref, gtwo_ref, gthree_ref, gfour_ref),
         gsend_sem,
         grecv_sem,
         gown_sem,
+        put_dgh,
         bits,
         partners,
     )
+
+    def rows_advance(stage):
+        for unit in range(2):
+            row_sum.advance(unit, stage)
 
     def scopy(stage):
         return remote(
@@ -2192,7 +2277,7 @@
             here_ref.at[stage],
             ssend_sem.at[stage],
             srecv_sem.at[stage],
-            partners[ORDERS[0][stage]],
+            partners[X_FIRST[stage]],
         )
 
     def small_advance(stage):
@@ -2210,10 +2295,11 @@
         remote(halo_out, halo_dx, halo_send.at[1], halo_recv.at[1], before),
     ]
     two_ref[:came] = rest_ref[...]
-    meet([partners[name] for name in ORDERS[0]] + [before, after])
+    meet([partners[name] for name in AXES] + [before, after])
     for unit in range(came):
         engine.copy(unit, 2).start()
-    row_sum.begin()
+    for unit in range(2):
+        row_sum.begin(unit)
     halos[0].start()
 
     def weight_gradient(index, grads_ref):
@@ -2226,7 +2312,7 @@
     for number in range(3):
         loads[number].wait()
     weight_gradient(0, dq_ref)
-    row_sum.advance(0)
+    rows_advance(0)
     loads[3].wait()
     weight_gradient(1, dk_ref)
     loads[4].wait()
@@ -2260,7 +2346,7 @@
             for unit in range(came, units):
                 engine.advance(unit, 0)
         if index == 1:
-            row_sum.advance(1)
+            rows_advance(1)
         if index == 2:
             for unit in range(came):
                 engine.advance(unit, 3)
@@ -2278,11 +2364,12 @@
     parts.append(jnp.zeros((sums_ref.shape[1] - filled, width), f32))
     sums_ref[0] = jnp.concatenate(parts, 0)
     scopy(0).start()
-    row_sum.advance(2)
+    rows_advance(2)
     for unit in range(came, units):
         engine.advance(unit, 1)
     small_advance(0)
-    dgh = row_sum.advance(3)
+    rows_advance(3)
+    dgh = dgh_sum_ref[...]
     unit_rows, scale = normalize_rows(gx_ref[...].astype(f32))
     grad_out_ref[...] = gdy_ref[...] + norm_back(unit_rows, scale, norms_ref[2:3], dgh)
     small_advance(1)
@@ -2308,7 +2395,9 @@
             engine.sent(unit, stage)
     for stage in range(STAGES):
         scopy(stage).wait_send()
-    row_sum.end()
+    for unit in range(2):
+        for stage in range(4):
+            row_sum.sent(unit, stage)
     for halo in halos:
         halo.wait_send()
 
@@ -2354,14 +2443,14 @@
         ]
         + sum_scratch(units, rows, lanes, False)
         + [
-            pltpu.VMEM((2, 2, 2, own, width), bf16),
-            pltpu.VMEM((2, 2, 2, own, width), bf16),
-            pltpu.VMEM((2, 2, own, width), bf16),
-            pltpu.VMEM((2, own, width), bf16),
-            pltpu.VMEM((own, width), bf16),
-            dma((4,)),
-            dma((4,)),
-            dma,
+            pltpu.VMEM((2, 2, 2, 2, own, width // 2), bf16),
+            pltpu.VMEM((2, 2, 2, 2, own, width // 2), bf16),
+            pltpu.VMEM((2, 2, 2, own, width // 2), bf16),
+            pltpu.VMEM((2, 2, own, width // 2), bf16),
+            pltpu.VMEM((2, own, width // 2), bf16),
+            dma((2, 4)),
+            dma((2, 4)),
+            dma((2,)),
             pltpu.VMEM((STAGES, small_rows, width), f32),
             pltpu.VMEM((STAGES, small_rows, width), f32),
             dma((STAGES,)),
@@ -2372,6 +2461,7 @@
             dma((2,)),
             dma((2,)),
             pltpu.VMEM((8, width), f32),
+            pltpu.VMEM((own, width), f32),
         ],
         compiler_params=params(collective_id=0, has_side_effects=True),
         cost_estimate=pl.CostEstimate(
@@ -2474,7 +2564,9 @@
         h, q, k, v, x, ct, all_states, gh, gq, gk, gv, w1t = gather_project(
             tokens[0], cotangent[0], global_states[0], w1, norm_params, wq, wk, wv
         )
-        all_states = all_states.reshape(-1, width)
+        all_states, gh, gq, gk, gv = (
+            value.reshape(-1, width) for value in (all_states, gh, gq, gk, gv)
+        )
     far, far_stat, part, part_stat = slot_forward(scalars, rows, group_rows, q, k, v, gq, gk, gv)
     if grid_of is None:
         o, line = local_forward(

time: 346 us -> 320 us (0.925); the launches traced: 344 us -> 322 us
  Pallas kernels: 323 us -> 302 us
    pallas_call x1, Pallas kernels: 72.5 us -> 60.5 us  [finish_all(): pl.pallas_call(finish_kernel, in_specs=[vmem] + [anywhere] * 12 + [vmem]...]
    pallas_call x1, Pallas kernels: 46.4 us -> 38.3 us  [gather_project(): pl.pallas_call(gather_project_kernel, in_specs=[anywhere, anywhere, vmem,...]
where the time goes in v3:
time: 320 us; the launch traced here: 322 us
  Pallas kernels  302 us (94%)
  local copies, waits for them, and re-layouts  18.1 us (6%)
    pallas_call x1, Pallas kernels, branch(): pl.pallas_call(functools.partial(branch_kernel, BLOCK, grid_of is not Non...  86.4 us
    pallas_call x1, Pallas kernels, finish_all(): pl.pallas_call(finish_kernel, in_specs=[vmem] + [anywhere] * 12 + [vmem]...  60.5 us
    pallas_call x1, Pallas kernels, gather_project(): pl.pallas_call(gather_project_kernel, in_specs=[anywhere, anywhere, vmem,...  38.3 us
    pallas_call x1, Pallas kernels, slot_backward(): pl.pallas_call(functools.partial(slot_backward_kernel, rows_count, group_...  37.8 us
    pallas_call x1, Pallas kernels, local_backward(): pl.pallas_call(functools.partial(local_backward_kernel, talk, rows_count,...  32.9 us
    pallas_call x1, Pallas kernels, slot_forward(): pl.pallas_call(functools.partial(slot_forward_kernel, rows_count, group_r...  23.1 us
    pallas_call x1, Pallas kernels, local_forward(): pl.pallas_call(functools.partial(local_forward_kernel, talk, rows_count,...  22.5 us

profile of v3, /device:TPU:0, one launch (start us, length us, event | category | flops | bytes accessed | tf_op | source)
XLA Modules:
  0.0 322.1 jit_solution(9742554135132996118)
XLA Ops:
  0.7 0.6 pad_add_fusion.place
  1.3 1.3 broadcast_in_dim.15.b2_ref
  2.5 0.8 reshape.83
  3.3 0.7 reshape.84.b1_ref
  4.0 38.3 %gather_project.1 = (bf16[1024,768]{1,0:T(8,128)(2,1)}, bf16[1024,768]{1,0:T(8,128)(2,1)}, bf16[1024,768]{1,0:T(8,128)(2,1)}, bf16[1024,768]{1,0:T(8,128)(2,1)},...) custom-call(bf16[1024,768]{1,0:T(8,128)(2,1)} %bitcast.55, ...), custom_call_target="tpu_custom_call" | custom-call | flops 7247757312 | bytes 18874368 | tf_op jit(solution)/shard_map/gather_project/pallas_call | solution.py:569
  42.3 23.1 %slot_forward.1 = (bf16[768,1024]{1,0:T(8,128)(2,1)}, f32[6,2,8,1024]{3,2,1,0:T(8,128)}, bf16[8,6,128,128]{3,2,1,0:T(8,128)(2,1)}, f32[8,6,8,128]{3,2,1,0:T(8,128)}) custom-call(s32[2,8]{1,0:T(2,128)} %lengths.7, s32[2]{0:T(128)} %bucket_of.7, s32[3]{0:T(128)} %pad_add_fusion.place, bf16[1024,768]{1,0:T(8,128)(2,1)} %get-tuple-element.65.q_ref, ...), custom_call_target="tpu_custom_call" | custom-call | flops 3221225472 | bytes 15728640 | tf_op jit(solution)/shard_map/slot_forward/pallas_call | solution.py:835
  65.4 22.5 %local_forward.1 = (bf16[1024,768]{1,0:T(8,128)(2,1)}, f32[6,2,8,1024]{3,2,1,0:T(8,128)}, bf16[2,2,3,128,128]{4,3,2,1,0:T(8,128)(2,1)}, f32[2,2,3,8,128]{4,3,2,1,0:T(8,128)}) custom-call(s32[2,8]{1,0:T(2,128)} %lengths.7, s32[2]{0:T(128)} %bucket_of.7, s32[3]{0:T(128)} %pad_add_fusion.place, bf16[1024,768]{1,0:T(8,128)(2,1)} %get-tuple-element.65.q_ref, ...), custom_call_target="tpu_custom_call" | custom-call | flops 6442450944 | bytes 12582912 | tf_op jit(solution)/shard_map/local_forward/pallas_call | solution.py:1088
  87.9 86.4 %branch.1 = (bf16[1024,768]{1,0:T(8,128)(2,1)}, f32[1024,768]{1,0:T(8,128)}, bf16[1024,768]{1,0:T(8,128)(2,1)}, bf16[64,768]{1,0:T(8,128)(2,1)}, f32[64,768]{1,0...) custom-call(bf16[1024,768]{1,0:T(8,128)(2,1)} %get-tuple-element.68., ...), custom_call_target="tpu_custom_call" | custom-call | flops 36691771392 | bytes 33030144 | tf_op jit(solution)/shard_map/branch/pallas_call | solution.py:1525
  174.4 0.7 reduce
  175.1 0.1 reshape_reshape.3
  175.2 0.7 reshape.90.db1_ref
  175.9 32.9 %local_backward.1 = (bf16[768,1024]{1,0:T(8,128)(2,1)}, bf16[1024,768]{1,0:T(8,128)(2,1)}, bf16[1024,768]{1,0:T(8,128)(2,1)}, f32[6,2,8,1024]{3,2,1,0:T(8,128)},...) custom-call(s32[2,8]{1,0:T(2,128)} %lengths.7, s32[2]{0:T(128)} %bucket_of.7, ...), custom_call_target="tpu_custom_call" | custom-call | flops 16106127360 | bytes 23592960 | tf_op jit(solution)/shard_map/local_backward/pallas_call | solution.py:1753
  208.9 37.8 %slot_backward.1 = (bf16[1024,768]{1,0:T(8,128)(2,1)}, bf16[1024,768]{1,0:T(8,128)(2,1)}, bf16[1024,768]{1,0:T(8,128)(2,1)}, bf16[3,768,768]{2,1,0:T(8,128)(2,1)...) custom-call(s32[2,8]{1,0:T(2,128)} %lengths.7, s32[2]{0:T(128)} %bucket_of.7, s32[3]{0:T(128)} %pad_add_fusion.place, ...), custom_call_target="tpu_custom_call" | custom-call | flops 8053063680 | bytes 31457280 | tf_op jit(solution)/shard_map/slot_backward/pallas_call | solution.py:2004
  246.6 0.0 copy-start.2
  246.7 0.0 copy-start.4
  246.7 60.5 %finish_all.1 = (f32[288,384]{1,0:T(8,128)}, f32[16,768]{1,0:T(8,128)}, f32[64,768]{1,0:T(8,128)}, bf16[1024,768]{1,0:T(8,128)(2,1)}, f32[1024,768]{1,0:T(8,128)}) custom-call(bf16[3,2,2,2,48,384]{5,4,3,2,1,0:T(8,128)(2,1)} %get-tuple-element.87.rest_ref, bf16[1024,768]{1,0:T(8,128)(2,1)} %get-tuple-element.68.x_ref.x_in, ...), custom_call_target="tpu_custom_call" | custom-call | flops 7247757312 | bytes 23592960 | tf_op jit(solution)/shard_map/finish_all/pallas_call | solution.py:2419
  307.2 1.3 slice_reduce_fusion
  308.5 0.7 slice.37
  309.3 1.4 slice.39
  310.7 0.6 reshape.93
  311.3 0.9 slice.34
  312.2 1.7 slice_bitcast_fusion
  313.9 0.0 copy-done.2
  313.9 0.0 copy-done.4
  314.0 0.8 fusion
  314.7 0.3 reshape_squeeze.7
  315.0 0.0 copy-start.1
  315.0 0.0 copy-start.5
  315.1 0.5 copy.35
  315.6 1.5 reshape.92
  317.0 0.0 copy-done.1
  317.0 0.0 copy-start
  317.0 1.1 copy.41
  318.2 0.0 copy-done.5
  318.2 0.6 copy.42
  318.8 0.7 copy-done
  319.5 0.0 copy-start.3
  319.5 1.7 copy.43
  321.2 0.0 copy-done.3
  321.2 0.7 copy.44
  (3 shorter events, 0.1 us)
Async XLA Ops:
  246.6 67.3 %copy-start.2 = (f32[192,384]{1,0:T(8,128)S(1)}, f32[192,384]{1,0:T(8,128)}, u32[]{:S(2)}) copy-start(f32[192,384]{1,0:T(8,128)} %get-tuple-element.114) | copy-start | bytes 884740
  246.7 67.3 %copy-start.4 = (f32[96,384]{1,0:T(8,128)S(1)}, f32[96,384]{1,0:T(8,128)}, u32[]{:S(2)}) copy-start(f32[96,384]{1,0:T(8,128)} %get-tuple-element.115) | copy-start | bytes 442372
  315.0 2.0 copy-start.1
  315.0 3.1 copy-start.5
  317.0 2.5 copy-start
  319.5 1.7 copy-start.3

commit v4 on v3

--- a/solution.py
+++ b/solution.py
@@ -203,12 +203,12 @@
         if number == 0:
             moves = [
                 (ref.at[z1, z0, y, core, rows, left], "z1"),
-                (ref.at[z1, z0, y, core, rows, right], "y"),
+                (ref.at[z1, z0, y, core, rows, right], "z1"),
             ]
         elif number == 1:
             moves = [
                 (ref.at[:, z0, y, core, rows, left], "z0"),
-                (ref.at[z1, z0, :, core, rows, right], "z1"),
+                (ref.at[:, z0, y, core, rows, right], "y"),
             ]
         elif number == 2:
             moves = [
@@ -380,7 +380,6 @@
 
 def gather_project_kernel(
     tokens_ref,
-    ct_ref,
     states_ref,
     w1_ref,
     norms_ref,
@@ -392,7 +391,6 @@
     k_out,
     v_out,
     x_out,
-    ct_out,
     all_out,
     gh_out,
     gq_out,
@@ -439,7 +437,6 @@
                 (wk_in, wk_ref),
                 (wv_in, wv_ref),
                 (w1_ref, w1s_ref),
-                (ct_ref.at[most], ct_out.at[shifted]),
             )
         )
     ]
@@ -447,13 +444,10 @@
         load.start()
     all_ref[z1, z0, y, core] = states_ref[...]
     meet([partners[name] for name, unused in WEIGHTS] + [before, after])
-    halo = [
-        remote(tokens_ref.at[end], x_ref.at[start], halo_send.at[0], halo_recv.at[0], after),
-        remote(ct_ref.at[end], ct_out.at[start], halo_send.at[1], halo_recv.at[1], after),
-    ]
+    halo = remote(tokens_ref.at[end], x_ref.at[start], halo_send, halo_recv, after)
     gather = RowGather(all_ref, width // 2, send_sem, recv_sem, bits, partners)
     gather.begin()
-    halo[0].start()
+    halo.start()
 
     outs = (h_out, q_out, k_out, v_out)
 
@@ -481,27 +475,24 @@
     for number in range(4):
         loads[number].wait()
     tiles = rows // HALF
-    project(1)
-    gather.advance(0)
-    for index in range(2, tiles):
-        project(index)
-    gather.advance(1)
-    halo[0].wait_recv()
-    x_store = pltpu.make_async_copy(x_ref, x_out, more_sem.at[0])
-    x_store.start()
-    project(0)
-    loads[4].wait()
-
     def turn(i, carry):
         at = pl.ds(pl.multiple_of(i * HALF, HALF), HALF)
         w1t_ref[at, :] = w1s_ref[:, at].T
         return carry
 
-    lax.fori_loop(0, w1t_ref.shape[0] // HALF, turn, 0)
+    project(1)
+    project(2)
+    gather.advance(0)
+    for index in range(3, tiles):
+        project(index)
+    loads[4].wait()
+    turns = w1t_ref.shape[0] // HALF
+    lax.fori_loop(0, turns // 2, turn, 0)
+    gather.advance(1)
+    lax.fori_loop(turns // 2, turns, turn, 0)
     w1t_store = pltpu.make_async_copy(w1t_ref, w1t_out, more_sem.at[1])
     w1t_store.start()
     gather.advance(2)
-    halo[1].start()
 
     gouts = (gh_out, gq_out, gk_out, gv_out)
 
@@ -538,6 +529,10 @@
     all_store = pltpu.make_async_copy(all_ref, all_out, more_sem.at[2])
     all_store.start()
     project_states(other)
+    halo.wait_recv()
+    x_store = pltpu.make_async_copy(x_ref, x_out, more_sem.at[0])
+    x_store.start()
+    project(0)
 
     for index in range(tiles):
         for store in stores(index):
@@ -549,14 +544,11 @@
     x_store.wait()
     w1t_store.wait()
     all_store.wait()
-    loads[5].wait()
-    halo[1].wait_recv()
-    for copy in halo:
-        copy.wait_send()
+    halo.wait_send()
     gather.end()
 
 
-def gather_project(tokens, ct, states, w1, norms, wq, wk, wv):
+def gather_project(tokens, states, w1, norms, wq, wk, wv):
     rows, width = tokens.shape
     own = states.shape[0]
     vmem = pl.BlockSpec(memory_space=pltpu.VMEM)
@@ -568,9 +560,9 @@
     weight = pltpu.VMEM((width, width), bf16)
     return pl.pallas_call(
         gather_project_kernel,
-        in_specs=[anywhere, anywhere, vmem, anywhere, vmem] + [anywhere] * 3,
-        out_specs=[anywhere] * 12,
-        out_shape=[local] * 6 + [glob] * 5 + [jax.ShapeDtypeStruct(turned, bf16)],
+        in_specs=[anywhere, vmem, anywhere, vmem] + [anywhere] * 3,
+        out_specs=[anywhere] * 11,
+        out_shape=[local] * 5 + [glob] * 5 + [jax.ShapeDtypeStruct(turned, bf16)],
         scratch_shapes=[
             weight,
             weight,
@@ -581,9 +573,9 @@
             pltpu.VMEM((4,) + glob.shape, bf16),
             pltpu.VMEM(w1.shape, bf16),
             pltpu.VMEM(turned, bf16),
-            dma((2,)),
-            dma((2,)),
-            dma((6,)),
+            dma,
+            dma,
+            dma((5,)),
             dma((4, rows // HALF)),
             dma((4, 2, 2)),
             dma((3,)),
@@ -597,7 +589,7 @@
             transcendentals=0,
         ),
         name="gather_project",
-    )(tokens, ct, states, w1, norms, wq, wk, wv)
+    )(tokens, states, w1, norms, wq, wk, wv)
 
 
 def project_global_kernel(
@@ -972,11 +964,13 @@
     *refs,
 ):
     if talk:
-        part_ref, part_stat_ref, o_ref, line_ref, half_ref, half_stat_ref = refs[:6]
-        own_ref, own_stat_ref = refs[6:8]
-        sums_refs = refs[8:10]
-        stat_refs = refs[10:12]
-        edges, query_columns, key_columns, send_sem, recv_sem, own_sem = refs[12:]
+        part_ref, part_stat_ref, ct_ref = refs[:3]
+        o_ref, line_ref, half_ref, half_stat_ref, ct_head_ref = refs[3:8]
+        own_ref, own_stat_ref = refs[8:10]
+        sums_refs = refs[10:12]
+        stat_refs = refs[12:14]
+        edges, query_columns, key_columns, send_sem, recv_sem, own_sem = refs[14:20]
+        ct_land, halo_send, halo_recv = refs[20:]
     else:
         o_ref, line_ref, edges, query_columns, key_columns = refs
     pair = pl.program_id(0)
@@ -1005,12 +999,25 @@
             pltpu.make_async_copy(own_parts[1], own_stat_ref, own_sem.at[1]),
         ]
 
+        batch = lax.axis_index("batch")
+        seq = lax.axis_index("seq")
+        places = lax.axis_size("seq")
+        after = (batch, lax.rem(seq + 1, places))
+        before = (batch, lax.rem(seq + places - 1, places))
+        halo = remote(
+            ct_ref.at[pl.ds(ct_ref.shape[0] - HALF, HALF)], ct_land, halo_send, halo_recv, after
+        )
+
         @pl.when(step == 0)
         def _():
-            meet([partners["core"], partners["y"]])
+            meet([partners["core"], partners["y"], before, after])
             for copy in own_copies:
                 copy.start()
             slot_sum.begin(0)
+
+        @pl.when(step == 4)
+        def _():
+            halo.start()
 
         @pl.when(step == 3)
         def _():
@@ -1024,6 +1031,9 @@
             slot_sum.merge(1)
             half_ref[...] = sums_refs[1][...]
             half_stat_ref[...] = stat_refs[1][...]
+            halo.wait_recv()
+            ct_head_ref[...] = ct_land[...]
+            halo.wait_send()
             slot_sum.sent(0)
             slot_sum.sent(1)
 
@@ -1048,7 +1058,9 @@
     line_ref[0, 0] = jnp.broadcast_to(peak + jnp.log(total), (8, 2 * BLOCK))
 
 
-def local_forward(talk, scalars, rows_count, group_rows, q, k, v, far, far_stat, part, part_stat):
+def local_forward(
+    talk, scalars, rows_count, group_rows, q, k, v, far, far_stat, part, part_stat, ct
+):
     blocks = rows_count // BLOCK
     width = q.shape[1]
     block_spec = pl.BlockSpec((BLOCK, LANES), lambda p, b, *unused: (b, p))
@@ -1067,16 +1079,21 @@
     edges = column_scratch(blocks)
     if talk:
         cut = (2, 2, 2, 2, PAIRS // 2)
-        operands += [part.reshape(cut + part.shape[2:]), part_stat.reshape(cut + part_stat.shape[2:])]
-        in_specs += [pl.BlockSpec(memory_space=pl.ANY)] * 2
+        operands += [
+            part.reshape(cut + part.shape[2:]),
+            part_stat.reshape(cut + part_stat.shape[2:]),
+            ct,
+        ]
+        in_specs += [pl.BlockSpec(memory_space=pl.ANY)] * 3
         shapes = [
             (2, 2, PAIRS // 2, LANES, GLOBALS),
             (2, 2, PAIRS // 2, 8, GLOBALS),
         ]
-        out_specs += [full(shape) for shape in shapes]
+        out_specs += [full(shape) for shape in shapes] + [full((HALF, width))]
         out_shape += [
             jax.ShapeDtypeStruct(shapes[0], bf16),
             jax.ShapeDtypeStruct(shapes[1], f32),
+            jax.ShapeDtypeStruct((HALF, width), bf16),
         ]
         leads = [(2, 2, 2), (2, 2, 2), (2, 2)]
         sums = [pltpu.VMEM(lead + shapes[0][2:], bf16) for lead in leads]
@@ -1084,6 +1101,7 @@
         dma = pltpu.SemaphoreType.DMA
         scratch = [sums[0], stats[0]] + sums[1:] + stats[1:]
         edges += [dma((2, 2)), dma((2, 2)), dma((2,))]
+        edges += [pltpu.VMEM((HALF, width), bf16), dma, dma]
         more = {"collective_id": 2, "has_side_effects": True}
     return pl.pallas_call(
         functools.partial(local_forward_kernel, talk, rows_count, group_rows),
@@ -1129,6 +1147,7 @@
     x_ref,
     o_ref,
     ct_ref,
+    ct_head_ref,
     gx_ref,
     go_in_ref,
     gstat_in_ref,
@@ -1304,7 +1323,12 @@
 
     loads = [
         pltpu.make_async_copy(o_ref, os_ref.at[pl.ds(0, count)], load_sem.at[0]),
-        pltpu.make_async_copy(ct_ref, cts_ref.at[pl.ds(0, count)], load_sem.at[1]),
+        pltpu.make_async_copy(
+            ct_ref.at[pl.ds(0, count - HALF)],
+            cts_ref.at[pl.ds(HALF, count - HALF)],
+            load_sem.at[1],
+        ),
+        pltpu.make_async_copy(ct_head_ref, cts_ref.at[pl.ds(0, HALF)], load_sem.at[2]),
     ]
 
     def start(at, size, x, sums):
@@ -1334,6 +1358,7 @@
 
         lax.fori_loop(0, tiles, start_tile, 0)
         loads[1].wait()
+        loads[2].wait()
         dft_ref[...] = cts_ref[...].T
         if talk:
             slot_sum.merge(2)
@@ -1465,7 +1490,7 @@
             dwo_ref[...] = dwo.astype(bf16)
 
 
-def branch(grid_of, x, o, ct, gx, go, gstat, gct, wo, w1t, b1, w2, b2, norms):
+def branch(grid_of, x, o, ct, ct_head, gx, go, gstat, gct, wo, w1t, b1, w2, b2, norms):
     count, width = x.shape
     own = gx.shape[0]
     hidden = w2.shape[0]
@@ -1529,6 +1554,7 @@
             row,
             anywhere,
             anywhere,
+            anywhere,
             few,
             once(go.shape),
             once(gstat.shape),
@@ -1567,7 +1593,7 @@
             pltpu.VMEM((width, total), bf16),
             pltpu.VMEM((total, FF_CHUNK), bf16),
             pltpu.VMEM((total, FF_CHUNK), bf16),
-            pltpu.SemaphoreType.DMA((2,)),
+            pltpu.SemaphoreType.DMA((3,)),
         ]
         + scratch,
         compiler_params=params(**more),
@@ -1577,7 +1603,7 @@
             transcendentals=2 * total * hidden,
         ),
         name="branch",
-    )(x, o, ct, gx, go, gstat, gct, wo, w1t, b1, w2, b2, norms)
+    )(x, o, ct, ct_head, gx, go, gstat, gct, wo, w1t, b1, w2, b2, norms)
     db1 = out[7].reshape(steps, FF_CHUNK)
     if grid_of is not None:
         db1 = db1.reshape(steps, seq, rows).transpose(1, 0, 2).reshape(-1, width)
@@ -1647,7 +1673,7 @@
             7: [(0, 3), (1, 3)],
             11: [(0, 4), (1, 4), (2, 1), (3, 1), (4, 1)],
         }
-        gather_plan = {2: 0, 5: 1, 8: 2, 10: 3}
+        gather_plan = {3: 0, 6: 1, 9: 2, 11: 3}
 
         @pl.when(step == 0)
         def _():
@@ -2159,8 +2185,9 @@
     out_ref,
     small_out_ref,
     grad_out_ref,
-    layer_ref,
     token_ref,
+    halo_dx_out,
+    halo_z_out,
     x_ref,
     dy_ref,
     h_ref,
@@ -2193,8 +2220,8 @@
     ssend_sem,
     srecv_sem,
     halo_out,
+    halo_dx,
     halo_z,
-    halo_dx,
     halo_send,
     halo_recv,
     dnorm_ref,
@@ -2221,7 +2248,6 @@
         (wv_in, wv_ref),
         (x_in, x_ref),
         (dy_in, dy_ref),
-        (z_in.at[pl.ds(HALF, count - HALF)], layer_ref.at[pl.ds(0, count - HALF)]),
     ]
     loads = [
         pltpu.make_async_copy(source, target, load_sem.at[number])
@@ -2289,10 +2315,11 @@
         else:
             small_out_ref[...] = total
 
-    head = pl.ds(0, HALF)
     halos = [
-        remote(z_in.at[head], halo_z, halo_send.at[0], halo_recv.at[0], before),
-        remote(halo_out, halo_dx, halo_send.at[1], halo_recv.at[1], before),
+        remote(halo_out, halo_dx, halo_send.at[0], halo_recv.at[0], before),
+        remote(
+            z_in.at[pl.ds(0, HALF)], halo_z, halo_send.at[1], halo_recv.at[1], before
+        ),
     ]
     two_ref[:came] = rest_ref[...]
     meet([partners[name] for name in AXES] + [before, after])
@@ -2300,7 +2327,6 @@
         engine.copy(unit, 2).start()
     for unit in range(2):
         row_sum.begin(unit)
-    halos[0].start()
 
     def weight_gradient(index, grads_ref):
         value = tn(grads_ref[...], h_ref[...])
@@ -2315,8 +2341,10 @@
     rows_advance(0)
     loads[3].wait()
     weight_gradient(1, dk_ref)
+    engine.advance(came, 0)
     loads[4].wait()
     weight_gradient(2, dv_ref)
+    engine.advance(came + 1, 0)
     for unit in range(came):
         engine.advance(unit, 2)
     for number in range(5, 10):
@@ -2342,9 +2370,8 @@
     for index in range(count // HALF):
         back(index)
         if index == 0:
-            halos[1].start()
-            for unit in range(came, units):
-                engine.advance(unit, 0)
+            engine.advance(came + 2, 0)
+            halos[0].start()
         if index == 1:
             rows_advance(1)
         if index == 2:
@@ -2364,6 +2391,7 @@
     parts.append(jnp.zeros((sums_ref.shape[1] - filled, width), f32))
     sums_ref[0] = jnp.concatenate(parts, 0)
     scopy(0).start()
+    halos[1].start()
     rows_advance(2)
     for unit in range(came, units):
         engine.advance(unit, 1)
@@ -2378,11 +2406,10 @@
     for unit in range(came, units):
         engine.advance(unit, 2)
     small_advance(2)
-    halos[0].wait_recv()
-    halos[1].wait_recv()
-    loads[10].wait()
-    layer_ref[count - HALF :, :] = halo_z[...]
-    token_ref[count - HALF :, :] = halo_dx[...].astype(f32)
+    for halo in halos:
+        halo.wait_recv()
+    halo_dx_out[...] = halo_dx[...]
+    halo_z_out[...] = halo_z[...]
     for unit in range(came, units):
         engine.advance(unit, 3)
     small_advance(3)
@@ -2419,13 +2446,14 @@
     return pl.pallas_call(
         finish_kernel,
         in_specs=[vmem] + [anywhere] * 12 + [vmem] * 8,
-        out_specs=[vmem] * 5,
+        out_specs=[vmem] * 6,
         out_shape=[
             jax.ShapeDtypeStruct((units * rows, lanes), f32),
             jax.ShapeDtypeStruct((small_rows, width), f32),
             jax.ShapeDtypeStruct((own, width), f32),
-            jax.ShapeDtypeStruct((count, width), bf16),
-            jax.ShapeDtypeStruct((count, width), f32),
+            jax.ShapeDtypeStruct((count - HALF, width), f32),
+            jax.ShapeDtypeStruct((HALF, width), bf16),
+            jax.ShapeDtypeStruct((HALF, width), bf16),
         ],
         scratch_shapes=[
             row,
@@ -2438,7 +2466,7 @@
             weight,
             weight,
             weight,
-            dma((11,)),
+            dma((10,)),
             pltpu.VMEM((3, 2, 2, 2, 2, 2, rows, lanes), bf16),
         ]
         + sum_scratch(units, rows, lanes, False)
@@ -2489,6 +2517,125 @@
     )
 
 
+def unpack_kernel(
+    z_ref,
+    halo_z_ref,
+    dx_ref,
+    halo_dx_ref,
+    gz_ref,
+    ggrad_ref,
+    first_ref,
+    second_ref,
+    third_ref,
+    small_ref,
+    layer_ref,
+    gz_out,
+    token_ref,
+    ggrad_out,
+    wq_ref,
+    wk_ref,
+    wv_ref,
+    wo_ref,
+    w1_ref,
+    w2_ref,
+    b1_ref,
+    b2_ref,
+    norms_ref,
+    turned_ref,
+):
+    step = pl.program_id(0)
+    last = pl.num_programs(0) - 1
+
+    @pl.when(step < last)
+    def _():
+        layer_ref[0] = z_ref[...]
+        token_ref[0] = dx_ref[...]
+
+    @pl.when(step == last)
+    def _():
+        layer_ref[0] = halo_z_ref[...]
+        token_ref[0] = halo_dx_ref[...].astype(f32)
+
+    rows = wq_ref.shape[0]
+
+    @pl.when(step == 0)
+    def _():
+        gz_out[0] = gz_ref[...]
+        ggrad_out[0] = ggrad_ref[...]
+        for ref, unit in ((wo_ref, 2), (wq_ref, 3), (wk_ref, 4), (wv_ref, 5)):
+            ref[...] = third_ref[unit * rows : (unit + 1) * rows]
+        chunks = w1_ref.shape[0] // rows
+        for chunk in range(chunks):
+            for ref, unit in ((first_ref, chunk), (second_ref, chunk - 2), (third_ref, chunk - 3)):
+                if 0 <= unit < ref.shape[0] // (2 * rows):
+                    break
+            start = 2 * unit * rows
+            w1_ref[chunk * rows : (chunk + 1) * rows] = ref[start : start + rows]
+            part = ref[start + rows : start + 2 * rows].T
+            for place in range(part.shape[0] // rows):
+                spot = (place * chunks + chunk) * rows
+                turned_ref[spot : spot + rows, :] = part[place * rows : (place + 1) * rows, :]
+        w2_ref[...] = turned_ref[...].T
+        pieces_in_row = small_ref.shape[1] // LANES
+        hidden_rows = b1_ref.shape[0] // pieces_in_row
+        for row in range(hidden_rows + 1):
+            for piece in range(pieces_in_row):
+                value = small_ref[row : row + 1, piece * LANES : (piece + 1) * LANES]
+                if row < hidden_rows:
+                    b1_ref[row * pieces_in_row + piece : row * pieces_in_row + piece + 1] = value
+                else:
+                    b2_ref[piece : piece + 1] = value
+        norms_ref[...] = small_ref[hidden_rows + 1 : hidden_rows + 7]
+
+
+def unpack(z, halo_z, dx, halo_dx, gz, ggrad, first, second, third, small, rows, hidden):
+    count, width = z.shape
+    own = gz.shape[0]
+    lanes = first.shape[1]
+    steps = count // HALF
+    shapes = [
+        ((1, count, width), bf16),
+        ((1, own, width), bf16),
+        ((1, count, width), f32),
+        ((1, own, width), f32),
+    ]
+    shapes += [((rows, lanes), f32)] * 4
+    shapes += [
+        ((hidden // width * rows, lanes), f32),
+        ((rows, hidden // width * lanes), f32),
+        ((hidden // LANES, LANES), f32),
+        ((width // LANES, LANES), f32),
+        ((6, width), f32),
+    ]
+    tile = pl.BlockSpec((1, HALF, width), lambda i: (0, i, 0))
+    return pl.pallas_call(
+        unpack_kernel,
+        grid=(steps,),
+        in_specs=[
+            pl.BlockSpec((HALF, width), lambda i: (jnp.minimum(i + 1, steps - 1), 0)),
+            full(halo_z.shape),
+            pl.BlockSpec((HALF, width), lambda i: (jnp.minimum(i, steps - 2), 0)),
+            full(halo_dx.shape),
+            full(gz.shape),
+            full(ggrad.shape),
+            full(first.shape),
+            full(second.shape),
+            full(third.shape),
+            full(small.shape),
+        ],
+        out_specs=[
+            tile if shape[1] == count else full(shape) for shape, unused in shapes
+        ],
+        out_shape=[jax.ShapeDtypeStruct(shape, kind) for shape, kind in shapes],
+        scratch_shapes=[pltpu.VMEM((hidden // width * lanes, rows), f32)],
+        compiler_params=params(),
+        cost_estimate=pl.CostEstimate(
+            flops=0, bytes_accessed=14 * count * width, transcendentals=0
+        ),
+        name="unpack",
+    )(z, halo_z, dx, halo_dx, gz, ggrad, first, second, third, small)
+
+
 def from_behind(value, axis, steps):
     count = lax.axis_size(axis)
     pairs = [(source, (source + steps) % count) for source in range(count)]
@@ -2553,7 +2700,7 @@
             (tokens[0, rows - HALF :], cotangent[0, rows - HALF :]), "seq", 1
         )
         x = jnp.concatenate([arrived_tokens, tokens[0, : rows - HALF]], 0)
-        ct = jnp.concatenate([arrived_grads, cotangent[0, : rows - HALF]], 0)
+        ct_head = arrived_grads
         all_states = lax.all_gather(global_states[0], "seq", axis=0, tiled=True)
         w1t = w1.T
         h, q, k, v = project_local(x, norms[0], norms[1], wq, wk, wv)
@@ -2561,8 +2708,8 @@
             scalars, rows, group_rows, all_states, norms[2], norms[3], wq, wk, wv
         )
     else:
-        h, q, k, v, x, ct, all_states, gh, gq, gk, gv, w1t = gather_project(
-            tokens[0], cotangent[0], global_states[0], w1, norm_params, wq, wk, wv
+        h, q, k, v, x, all_states, gh, gq, gk, gv, w1t = gather_project(
+            tokens[0], global_states[0], w1, norm_params, wq, wk, wv
         )
         all_states, gh, gq, gk, gv = (
             value.reshape(-1, width) for value in (all_states, gh, gq, gk, gv)
@@ -2570,7 +2717,7 @@
     far, far_stat, part, part_stat = slot_forward(scalars, rows, group_rows, q, k, v, gq, gk, gv)
     if grid_of is None:
         o, line = local_forward(
-            False, scalars, rows, group_rows, q, k, v, far, far_stat, None, None
+            False, scalars, rows, group_rows, q, k, v, far, far_stat, None, None, None
         )
         part_peak = part_stat[:, :, 0:2]
         peak = jnp.max(lax.all_gather(part_peak, "seq"), axis=0)
@@ -2594,15 +2741,16 @@
         )
         gstat = own_peak + jnp.log(own_total)
     else:
-        o, line, half_sum, half_stat = local_forward(
-            True, scalars, rows, group_rows, q, k, v, far, far_stat, part, part_stat
+        o, line, half_sum, half_stat, ct_head = local_forward(
+            True, scalars, rows, group_rows, q, k, v, far, far_stat, part, part_stat, cotangent[0]
         )
 
     z, dy, do, gz, gdy, gdo, dwo, db1, db2, dgain2, doffset2, *dws = branch(
         grid_of,
         x,
         o,
-        ct,
+        cotangent[0],
+        ct_head,
         global_states[0],
         go if grid_of is None else half_sum,
         gstat if grid_of is None else half_stat,
@@ -2670,7 +2818,7 @@
         dw1, dw2 = dws
         weights = [scatter_sum(value) for value in (dqkv[0], dqkv[1], dqkv[2], dwo, dw1, dw2)]
     else:
-        sum_third, small, global_grad, layer_out, token_grad = finish_all(
+        sum_third, small, global_grad, dx, halo_dx, halo_z = finish_all(
             rest,
             x,
             dy,
@@ -2689,16 +2837,23 @@
             gdy,
             norm_params,
         )
-        piece = width // seq_count
-        lanes = width // batch_count
-        steps = w1.shape[1] // FF_CHUNK
-        chunks = jnp.concatenate([sum_first, sum_second, sum_third[: 2 * piece]], 0)
-        chunks = chunks.reshape(steps, 2, piece, lanes)
-        part1 = chunks[:, 0].reshape(steps * piece, lanes)
-        part2 = chunks[:, 1].reshape(steps, piece, lanes // piece, piece)
-        part2 = part2.transpose(1, 2, 0, 3).reshape(piece, -1)
-        parts = [sum_third[i * piece : (i + 1) * piece] for i in (3, 4, 5, 2)] + [part1, part2]
-        weights = [value.T for value in parts]
+        results = unpack(
+            z,
+            halo_z,
+            dx,
+            halo_dx,
+            gz,
+            global_grad,
+            sum_first,
+            sum_second,
+            sum_third,
+            small,
+            width // seq_count,
+            w1.shape[1],
+        )
+        weights = [value.T for value in results[4:10]]
+        biases = [value.reshape(-1) for value in results[10:12]]
+        return (*results[:4], *weights, *biases, results[12])
     hidden_rows = w1.shape[1] // width
     return (
         layer_out[None],

time: 320 us -> 301 us (0.941)
  local copies, waits for them, and re-layouts: 18.1 us -> 3.55 us
  Pallas kernels: 302 us -> 298 us
    pallas_call x1, Pallas kernels: 60.5 us -> 54.9 us  [finish_all(): pl.pallas_call(finish_kernel, in_specs=[vmem] + [anywhere] * 12 + [vmem]...]
    slice x5 -> x0, local copies, waits for them, and re-layouts: 5.16 us -> none  [the longest x1 1.41 us: on_device(): small[hidden_rows + 1:hidden_rows + 7]]
    unnamed x16 -> x0, local copies, waits for them, and re-layouts: 4.85 us -> none
    pallas_call x1 -> x2, Pallas kernels: 38.3 us -> 39.4 us  [the longest x1 32.9 us: gather_project(): pl.pallas_call(gather_project_kernel, in_specs=[anywhere, vmem, anywhere,...]
where the time goes in v4:
time: 301 us; the launch traced here: 303 us
  Pallas kernels  298 us (99%)
  local copies, waits for them, and re-layouts  3.55 us (1%)
    pallas_call x1, Pallas kernels, branch(): pl.pallas_call(functools.partial(branch_kernel, BLOCK, grid_of is not Non...  83.9 us
    pallas_call x1, Pallas kernels, finish_all(): pl.pallas_call(finish_kernel, in_specs=[vmem] + [anywhere] * 12 + [vmem]...  54.9 us
    pallas_call x1, Pallas kernels, slot_backward(): pl.pallas_call(functools.partial(slot_backward_kernel, rows_count, group_...  37.8 us
    pallas_call x1, Pallas kernels, gather_project(): pl.pallas_call(gather_project_kernel, in_specs=[anywhere, vmem, anywhere,...  32.9 us
    pallas_call x1, Pallas kernels, local_backward(): pl.pallas_call(functools.partial(local_backward_kernel, talk, rows_count,...  32.9 us
    pallas_call x1, Pallas kernels, local_forward(): pl.pallas_call(functools.partial(local_forward_kernel, talk, rows_count,...  25.6 us
    pallas_call x1, Pallas kernels, slot_forward(): pl.pallas_call(functools.partial(slot_forward_kernel, rows_count, group_r...  23.1 us
    pallas_call x1, Pallas kernels, unpack(): pl.pallas_call(unpack_kernel, grid=(steps,), in_specs=[pl.BlockSpec((HALF...  6.46 us

profile of v4, /device:TPU:0, one launch (start us, length us, event | category | flops | bytes accessed | tf_op | source)
XLA Modules:
  0.0 303.4 jit_solution(4943743406868593150)
XLA Ops:
  0.7 0.6 pad_add_fusion.place
  1.3 1.3 broadcast_in_dim.3.b2_ref
  2.5 0.8 reshape.80
  3.3 0.7 reshape.81.b1_ref
  4.0 32.9 %gather_project.1 = (bf16[1024,768]{1,0:T(8,128)(2,1)}, bf16[1024,768]{1,0:T(8,128)(2,1)}, bf16[1024,768]{1,0:T(8,128)(2,1)}, bf16[1024,768]{1,0:T(8,128)(2,1)},...) custom-call(bf16[1024,768]{1,0:T(8,128)(2,1)} %bitcast.33, ...), custom_call_target="tpu_custom_call" | custom-call | flops 7247757312 | bytes 18874368 | tf_op jit(solution)/shard_map/gather_project/pallas_call | solution.py:561
  37.0 23.1 %slot_forward.1 = (bf16[768,1024]{1,0:T(8,128)(2,1)}, f32[6,2,8,1024]{3,2,1,0:T(8,128)}, bf16[8,6,128,128]{3,2,1,0:T(8,128)(2,1)}, f32[8,6,8,128]{3,2,1,0:T(8,128)}) custom-call(s32[2,8]{1,0:T(2,128)} %lengths.7, s32[2]{0:T(128)} %bucket_of.7, s32[3]{0:T(128)} %pad_add_fusion.place, bf16[1024,768]{1,0:T(8,128)(2,1)} %get-tuple-element.80.q_ref, ...), custom_call_target="tpu_custom_call" | custom-call | flops 3221225472 | bytes 15728640 | tf_op jit(solution)/shard_map/slot_forward/pallas_call | solution.py:827
  60.1 25.6 %local_forward.1 = (bf16[1024,768]{1,0:T(8,128)(2,1)}, f32[6,2,8,1024]{3,2,1,0:T(8,128)}, bf16[2,2,3,128,128]{4,3,2,1,0:T(8,128)(2,1)}, f32[2,2,3,8,128]{4,3,2,1,0:T(8,128)}, bf16[256,768]{1,0:T(8,128)(2,1)}) custom-call(s32[2,8]{1,0:T(2,128)} %lengths.7, s32[2]{0:T(128)} %bucket_of.7, s32[3]{0:T(128)} %pad_add_fusion.place, ...), custom_call_target="tpu_custom_call" | custom-call | flops 6442450944 | bytes 12582912 | tf_op jit(solution)/shard_map/local_forward/pallas_call | solution.py:1106
  85.7 83.9 %branch.1 = (bf16[1024,768]{1,0:T(8,128)(2,1)}, f32[1024,768]{1,0:T(8,128)}, bf16[1024,768]{1,0:T(8,128)(2,1)}, bf16[64,768]{1,0:T(8,128)(2,1)}, f32[64,768]{1,0...) custom-call(bf16[1024,768]{1,0:T(8,128)(2,1)} %get-tuple-element.79., ...), custom_call_target="tpu_custom_call" | custom-call | flops 36691771392 | bytes 33030144 | tf_op jit(solution)/shard_map/branch/pallas_call | solution.py:1550
  169.5 0.7 reduce
  170.3 0.1 reshape_reshape.3
  170.4 0.7 reshape.87.db1_ref
  171.1 32.9 %local_backward.1 = (bf16[768,1024]{1,0:T(8,128)(2,1)}, bf16[1024,768]{1,0:T(8,128)(2,1)}, bf16[1024,768]{1,0:T(8,128)(2,1)}, f32[6,2,8,1024]{3,2,1,0:T(8,128)},...) custom-call(s32[2,8]{1,0:T(2,128)} %lengths.7, s32[2]{0:T(128)} %bucket_of.7, ...), custom_call_target="tpu_custom_call" | custom-call | flops 16106127360 | bytes 23592960 | tf_op jit(solution)/shard_map/local_backward/pallas_call | solution.py:1779
  204.0 37.8 %slot_backward.1 = (bf16[1024,768]{1,0:T(8,128)(2,1)}, bf16[1024,768]{1,0:T(8,128)(2,1)}, bf16[1024,768]{1,0:T(8,128)(2,1)}, bf16[3,768,768]{2,1,0:T(8,128)(2,1)...) custom-call(s32[2,8]{1,0:T(2,128)} %lengths.7, s32[2]{0:T(128)} %bucket_of.7, s32[3]{0:T(128)} %pad_add_fusion.place, ...), custom_call_target="tpu_custom_call" | custom-call | flops 8053063680 | bytes 31457280 | tf_op jit(solution)/shard_map/slot_backward/pallas_call | solution.py:2030
  241.8 54.9 %finish_all.1 = (f32[288,384]{1,0:T(8,128)}, f32[16,768]{1,0:T(8,128)}, f32[64,768]{1,0:T(8,128)}, f32[768,768]{1,0:T(8,128)}, bf16[256,768]{1,0:T(8,128)(2,1)}, /*index=5*/bf16[256,768]{1,0:T(8,128)(2,1)}) custom-call(bf16[3,2,2,2,48,384]{5,4,3,2,1,0:T(8,128)(2,1)} %get-tuple-element.102.rest_ref, bf16[1024,768]{1,0:T(8,128)(2,1)} %get-tuple-element.79.x_ref.x_in, ...), custom_call_target="tpu_custom_call" | custom-call | flops 7247757312 | bytes 23592960 | tf_op jit(solution)/shard_map/finish_all/pallas_call | solution.py:2446
  296.7 6.5 %unpack.1 = (bf16[1,1024,768]{2,1,0:T(8,128)(2,1)}, bf16[1,64,768]{2,1,0:T(8,128)(2,1)}, f32[1,1024,768]{2,1,0:T(8,128)}, f32[1,64,768]{2,1,0:T(8,128)}, f32[48,...) custom-call(bf16[1024,768]{1,0:T(8,128)(2,1)} %get-tuple-element.95., ...), custom_call_target="tpu_custom_call" | custom-call | bytes 11010048 | tf_op jit(solution)/shard_map/unpack/pallas_call | solution.py:2611
  (2 shorter events, 0.0 us)

commit v5 on v4

--- a/solution.py
+++ b/solution.py
@@ -231,25 +231,25 @@
             for side, (part, name) in enumerate(moves)
         ]
 
-    def begin(self):
-        for copy in self.copies(0):
+    def begin(self, number=0):
+        for copy in self.copies(number):
             copy.start()
 
     def advance(self, number):
         for copy in self.copies(number):
             copy.wait_recv()
         if number < 3:
-            for copy in self.copies(number + 1):
-                copy.start()
-
-    def end(self):
-        for number in range(4):
+            self.begin(number + 1)
+
+    def end(self, first=0):
+        for number in range(first, 4):
             for copy in self.copies(number):
                 copy.wait_send()
 
 
 X_FIRST = ("core", "x", "y", "z0", "z1")
 Y_FIRST = ("core", "y", "x", "z0", "z1")
+X_Z_FIRST = ("core", "x", "z0", "y", "z1")
 Z_FIRST = ("core", "z0", "x", "z1", "y")
 AXES = ("z1", "z0", "y", "core", "x")
 
@@ -964,13 +964,12 @@
     *refs,
 ):
     if talk:
-        part_ref, part_stat_ref, ct_ref = refs[:3]
-        o_ref, line_ref, half_ref, half_stat_ref, ct_head_ref = refs[3:8]
-        own_ref, own_stat_ref = refs[8:10]
-        sums_refs = refs[10:12]
-        stat_refs = refs[12:14]
-        edges, query_columns, key_columns, send_sem, recv_sem, own_sem = refs[14:20]
-        ct_land, halo_send, halo_recv = refs[20:]
+        part_ref, part_stat_ref = refs[:2]
+        o_ref, line_ref, half_ref, half_stat_ref = refs[2:6]
+        own_ref, own_stat_ref = refs[6:8]
+        sums_refs = refs[8:10]
+        stat_refs = refs[10:12]
+        edges, query_columns, key_columns, send_sem, recv_sem, own_sem = refs[12:]
     else:
         o_ref, line_ref, edges, query_columns, key_columns = refs
     pair = pl.program_id(0)
@@ -999,25 +998,12 @@
             pltpu.make_async_copy(own_parts[1], own_stat_ref, own_sem.at[1]),
         ]
 
-        batch = lax.axis_index("batch")
-        seq = lax.axis_index("seq")
-        places = lax.axis_size("seq")
-        after = (batch, lax.rem(seq + 1, places))
-        before = (batch, lax.rem(seq + places - 1, places))
-        halo = remote(
-            ct_ref.at[pl.ds(ct_ref.shape[0] - HALF, HALF)], ct_land, halo_send, halo_recv, after
-        )
-
         @pl.when(step == 0)
         def _():
-            meet([partners["core"], partners["y"], before, after])
+            meet([partners["core"], partners["y"]])
             for copy in own_copies:
                 copy.start()
             slot_sum.begin(0)
-
-        @pl.when(step == 4)
-        def _():
-            halo.start()
 
         @pl.when(step == 3)
         def _():
@@ -1031,9 +1017,6 @@
             slot_sum.merge(1)
             half_ref[...] = sums_refs[1][...]
             half_stat_ref[...] = stat_refs[1][...]
-            halo.wait_recv()
-            ct_head_ref[...] = ct_land[...]
-            halo.wait_send()
             slot_sum.sent(0)
             slot_sum.sent(1)
 
@@ -1059,7 +1042,7 @@
 
 
 def local_forward(
-    talk, scalars, rows_count, group_rows, q, k, v, far, far_stat, part, part_stat, ct
+    talk, scalars, rows_count, group_rows, q, k, v, far, far_stat, part, part_stat
 ):
     blocks = rows_count // BLOCK
     width = q.shape[1]
@@ -1082,18 +1065,16 @@
         operands += [
             part.reshape(cut + part.shape[2:]),
             part_stat.reshape(cut + part_stat.shape[2:]),
-            ct,
         ]
-        in_specs += [pl.BlockSpec(memory_space=pl.ANY)] * 3
+        in_specs += [pl.BlockSpec(memory_space=pl.ANY)] * 2
         shapes = [
             (2, 2, PAIRS // 2, LANES, GLOBALS),
             (2, 2, PAIRS // 2, 8, GLOBALS),
         ]
-        out_specs += [full(shape) for shape in shapes] + [full((HALF, width))]
+        out_specs += [full(shape) for shape in shapes]
         out_shape += [
             jax.ShapeDtypeStruct(shapes[0], bf16),
             jax.ShapeDtypeStruct(shapes[1], f32),
-            jax.ShapeDtypeStruct((HALF, width), bf16),
         ]
         leads = [(2, 2, 2), (2, 2, 2), (2, 2)]
         sums = [pltpu.VMEM(lead + shapes[0][2:], bf16) for lead in leads]
@@ -1101,7 +1082,6 @@
         dma = pltpu.SemaphoreType.DMA
         scratch = [sums[0], stats[0]] + sums[1:] + stats[1:]
         edges += [dma((2, 2)), dma((2, 2)), dma((2,))]
-        edges += [pltpu.VMEM((HALF, width), bf16), dma, dma]
         more = {"collective_id": 2, "has_side_effects": True}
     return pl.pallas_call(
         functools.partial(local_forward_kernel, talk, rows_count, group_rows),
@@ -1138,7 +1118,7 @@
 
 
 TICKS = 3
-DELAYS = (0, 2, 3, 4, 6)
+ENDINGS = ((0, 2, 4, 6, 8), (3, 5, 7, 9, 10), (6, 8))
 
 
 def branch_kernel(
@@ -1199,16 +1179,17 @@
         half_ref, half_stat_ref = refs[8:10]
         slot_sums = refs[10:12]
         slot_stats = refs[12:14]
-        turned_ref, go_land, gstat_land, stat_ref, slot_send, slot_recv = refs[14:]
+        turned_ref, go_land, gstat_land, stat_ref, slot_send, slot_recv = refs[14:20]
+        message_land, message_send, message_recv, halo_send, halo_recv = refs[20:]
         last_step = 4
         bits, partners = my_place()
         core = bits["core"]
         chunks = last_step - 1
         slots = units_ref.shape[0]
         plan = [
-            (TICKS * chunk + DELAYS[stage], chunk, stage)
-            for chunk in range(chunks)
-            for stage in range(STAGES if chunk < chunks - 1 else 2)
+            (tick, chunk, stage)
+            for chunk, ticks in enumerate(ENDINGS)
+            for stage, tick in enumerate(ticks)
         ]
 
         def source(unit):
@@ -1313,14 +1294,33 @@
                     moved = iota((LANES, LANES), 1) == source_lane + start_lane
                     moved = jnp.where(moved & (source_lane < HEADS), 1.0, 0.0).astype(bf16)
                     spread = spread + nn(low, moved)
-            message_ref[:, :width] = gdo_ref[...]
-            message_ref[:, width:] = spread.astype(bf16)
+            mine = message_land.at[bits["z1"]]
+            mine[:, :width] = gdo_ref[...]
+            mine[:, width:] = spread.astype(bf16)
+            message_copy().start()
+
+        def message_copy():
+            mine = message_land.at[bits["z1"]]
+            return remote(mine, mine, message_send, message_recv, partners["z1"])
 
     else:
 
         def tick_at(position):
             pass
 
+    if talk:
+        batch = lax.axis_index("batch")
+        seq_place = lax.axis_index("seq")
+        places = lax.axis_size("seq")
+        after = (batch, lax.rem(seq_place + 1, places))
+        before = (batch, lax.rem(seq_place + places - 1, places))
+        halo = remote(
+            ct_ref.at[pl.ds(count - HALF, HALF)],
+            cts_ref.at[pl.ds(0, HALF)],
+            halo_send,
+            halo_recv,
+            after,
+        )
     loads = [
         pltpu.make_async_copy(o_ref, os_ref.at[pl.ds(0, count)], load_sem.at[0]),
         pltpu.make_async_copy(
@@ -1328,15 +1328,19 @@
             cts_ref.at[pl.ds(HALF, count - HALF)],
             load_sem.at[1],
         ),
-        pltpu.make_async_copy(ct_head_ref, cts_ref.at[pl.ds(0, HALF)], load_sem.at[2]),
     ]
+    if not talk:
+        loads.append(
+            pltpu.make_async_copy(ct_head_ref, cts_ref.at[pl.ds(0, HALF)], load_sem.at[2])
+        )
 
     def start(at, size, x, sums):
         y = x.astype(f32) + nn(os_ref[at, :], wo_ref[...])
         unit, unused = normalize_rows(y)
         h_ref[at, :] = (unit * norms_ref[4:5] + norms_ref[5:6]).astype(bf16)
         y_ref[at, :] = y
-        sums[...] = y + b2_ref[...]
+        b2 = jnp.concatenate([b2_ref[i : i + 1] for i in range(width // LANES)], axis=1)
+        sums[...] = y + b2
         dh_ref[at, :] = jnp.zeros((size, width), f32)
 
     @pl.when(step == 0)
@@ -1346,8 +1350,9 @@
         if talk:
             half_ref[...] = go_in_ref[...]
             half_stat_ref[...] = gstat_in_ref[...]
-            meet([partners[name] for name in AXES])
+            meet([partners[name] for name in AXES] + [before, after])
             slot_sum.begin(2)
+            halo.start()
         cts_ref[count:] = padded(gct_ref[...])
         loads[0].wait()
 
@@ -1357,12 +1362,8 @@
             return carry
 
         lax.fori_loop(0, tiles, start_tile, 0)
-        loads[1].wait()
-        loads[2].wait()
-        dft_ref[...] = cts_ref[...].T
-        if talk:
-            slot_sum.merge(2)
-            slot_sum.begin(3)
+        for load in loads[1:]:
+            load.wait()
 
     db1_ref[...] = jnp.zeros_like(db1_ref)
     w1 = w1_ref[...].reshape(width, width)
@@ -1380,19 +1381,26 @@
         sums[...] = sums[...] + nn(a, w2)
         dh_ref[at, :] = dh_ref[at, :] + nn(du, w1)
 
-    chunk_of(rows_at(0), dy_ref.at[rows_at(0)])
+    for i in range(1, tiles):
+        chunk_of(rows_at(i), dy_ref.at[rows_at(i)])
+
     if talk:
 
         @pl.when(step == 0)
         def _():
-            finish_slots()
+            slot_sum.merge(2)
+            slot_sum.begin(3)
+            halo.wait_recv()
 
     tick_at(0)
-    for i in range(1, tiles):
-        chunk_of(rows_at(i), dy_ref.at[rows_at(i)])
+    chunk_of(rows_at(0), dy_ref.at[rows_at(0)])
 
     @pl.when(step == 0)
     def _():
+        if talk:
+            finish_slots()
+            halo.wait_send()
+        dft_ref[...] = cts_ref[...].T
         if talk:
             for copy in final_copies():
                 copy.wait_recv()
@@ -1463,8 +1471,6 @@
             finish(at, tile, dy_ref.at[at], put)
             return carry
 
-        lax.fori_loop(0, tiles, finish_tile, 0)
-
         def put_tail(z, dy, do):
             gz_ref[...] = z[:own]
             gdy_ref[...] = dy[:own]
@@ -1473,10 +1479,12 @@
         finish(tail, extra, z_sum_ref, put_tail)
         if talk:
             put_message()
+            advance(TICKS * chunks)
+        lax.fori_loop(0, tiles, finish_tile, 0)
         dwo = tn(h_ref[...], os_ref[...])
         if talk:
             put_grouped(dwo_ref, dwo)
-            advance(TICKS * chunks)
+            advance(TICKS * chunks + 1)
             rest_ref[...] = landings[1][2 * chunks - 2 :]
             for when, chunk, stage in plan:
                 for unit in (2 * chunk, 2 * chunk + 1):
@@ -1486,6 +1494,9 @@
             slot_sum.sent(3)
             for copy in final_copies():
                 copy.wait_send()
+            message_copy().wait_recv()
+            message_ref[...] = message_land[...]
+            message_copy().wait_send()
         else:
             dwo_ref[...] = dwo.astype(bf16)
 
@@ -1521,7 +1532,7 @@
         dw_shapes = [
             ((units - 2) * rows, lanes),
             (2, 2, 2, 2, 2, batch, rows, lanes),
-            (own, width + LANES),
+            (2, own, width + LANES),
             (2, 2, 2, 2, rows, lanes),
         ]
         dw_types = [f32, bf16, bf16, bf16]
@@ -1544,6 +1555,11 @@
                 pltpu.VMEM((GLOBALS, LANES), f32),
                 dma((5, 2)),
                 dma((5, 2)),
+                pltpu.VMEM((2, own, width + LANES), bf16),
+                dma,
+                dma,
+                dma,
+                dma,
             ]
         )
         more = {"collective_id": 3, "has_side_effects": True}
@@ -1563,7 +1579,7 @@
             weight_spec,
             pl.BlockSpec((1, 1, FF_CHUNK), lambda j: (j, 0, 0)),
             weight_spec,
-            line,
+            full(b2.shape),
             full(norms.shape),
         ],
         out_specs=[row, row, row, few, few, few]
@@ -1669,18 +1685,18 @@
         )
         plan = {
             3: [(2, 0), (3, 0), (4, 0)],
-            4: [(0, 2), (1, 2)],
-            7: [(0, 3), (1, 3)],
+            5: [(0, 2), (1, 2)],
+            8: [(0, 3), (1, 3)],
             11: [(0, 4), (1, 4), (2, 1), (3, 1), (4, 1)],
         }
-        gather_plan = {3: 0, 6: 1, 9: 2, 11: 3}
+        gather_plan = {4: 1, 8: 2, 10: 3}
 
         @pl.when(step == 0)
         def _():
-            all_ref[bits["z1"], bits["z0"], bits["y"], bits["core"]] = message_ref[...]
+            all_ref[:, bits["z0"], bits["y"], bits["core"]] = message_ref[...]
             landings[1][:2] = rest_ref[...]
             meet([partners[name] for name in AXES])
-            gather.begin()
+            gather.begin(1)
             for unit in (0, 1):
                 engine.copy(unit, 2).start()
             for unit in (2, 3, 4):
@@ -1729,7 +1745,7 @@
         @pl.when(step == PAIRS * blocks - 1)
         def _():
             everyone_ref[...] = all_ref[...].reshape(everyone_ref.shape)
-            gather.end()
+            gather.end(1)
             rest_out_ref[...] = landings[1][2:]
             for entries in plan.values():
                 for unit, stage in entries:
@@ -1758,7 +1774,7 @@
     scratch = column_scratch(blocks)
     more = {}
     if talk:
-        own, wide = message.shape
+        unused, own, wide = message.shape
         rows, lanes = last.shape[-2:]
         units = 5
         operands += [message, rest, last, dwo.reshape(last.shape[1:])]
@@ -1955,9 +1971,7 @@
 
     @pl.when(block == blocks - 1)
     def _():
-        dw_sum[...] = jnp.zeros_like(dw_sum)
-
-        def through(slot, carry):
+        def through(slot, found):
             needed = slot == place[2]
             for number in range(blocks):
                 needed = needed | slot_present(
@@ -1978,9 +1992,18 @@
                 rows = gh_ref[at, :]
                 total = dgh_sum[at, :]
                 for index, weight in enumerate((wq_ref, wk_ref, wv_ref)):
-                    dw_sum[index] += tn(grads[index], rows)
                     total = total + nt(grads[index], weight[...])
                 dgh_sum[at, :] = total
+
+                @pl.when(found == 0)
+                def _():
+                    for index in range(3):
+                        dw_sum[index] = tn(grads[index], rows)
+
+                @pl.when(found > 0)
+                def _():
+                    for index in range(3):
+                        dw_sum[index] += tn(grads[index], rows)
 
                 @pl.when(group == PAIRS // TOGETHER - 1)
                 def _():
@@ -1988,9 +2011,9 @@
                     dnorm_ref[0:1] += jnp.sum(total * unit, axis=0, keepdims=True)
                     dnorm_ref[1:2] += jnp.sum(total, axis=0, keepdims=True)
 
-            return carry
-
-        lax.fori_loop(0, SLOTS, through, 0)
+            return jnp.where(needed, 1, found)
+
+        lax.fori_loop(0, SLOTS, through, jnp.int32(0))
         dw_ref[...] = dw_sum[...].astype(bf16)
 
     @pl.when(step == PAIRS // TOGETHER * blocks - 1)
@@ -2260,7 +2283,7 @@
         return lambda side: units_ref.at[unit - came, :, :, :, side]
 
     engine = HalvingSum(
-        (X_FIRST, Y_FIRST, X_FIRST, X_FIRST, Y_FIRST, Z_FIRST),
+        (X_Z_FIRST, Y_FIRST, X_FIRST, X_FIRST, Y_FIRST, Z_FIRST),
         [source(unit) for unit in range(units)],
         (one_ref, two_ref, three_ref, four_ref, five_ref),
         None,
@@ -2688,7 +2711,7 @@
     ).astype(jnp.int32)
     scalars = (lengths, bucket_of, place)
     norms = [norm_params[i : i + 1] for i in range(6)]
-    b2_line = b2[None]
+    b2_rows = b2.reshape(-1, LANES)
 
     batch_count = lax.axis_size("batch")
     grid_of = None
@@ -2717,7 +2740,7 @@
     far, far_stat, part, part_stat = slot_forward(scalars, rows, group_rows, q, k, v, gq, gk, gv)
     if grid_of is None:
         o, line = local_forward(
-            False, scalars, rows, group_rows, q, k, v, far, far_stat, None, None, None
+            False, scalars, rows, group_rows, q, k, v, far, far_stat, None, None
         )
         part_peak = part_stat[:, :, 0:2]
         peak = jnp.max(lax.all_gather(part_peak, "seq"), axis=0)
@@ -2741,8 +2764,8 @@
         )
         gstat = own_peak + jnp.log(own_total)
     else:
-        o, line, half_sum, half_stat, ct_head = local_forward(
-            True, scalars, rows, group_rows, q, k, v, far, far_stat, part, part_stat, cotangent[0]
+        o, line, half_sum, half_stat = local_forward(
+            True, scalars, rows, group_rows, q, k, v, far, far_stat, part, part_stat
         )
 
     z, dy, do, gz, gdy, gdo, dwo, db1, db2, dgain2, doffset2, *dws = branch(
@@ -2750,7 +2773,7 @@
         x,
         o,
         cotangent[0],
-        ct_head,
+        ct_head if grid_of is None else cotangent[0],
         global_states[0],
         go if grid_of is None else half_sum,
         gstat if grid_of is None else half_stat,
@@ -2759,7 +2782,7 @@
         w1t,
         b1,
         w2,
-        b2_line,
+        b2_rows,
         norm_params,
     )
     if grid_of is None:

time: 301 us -> 300 us (level)
    pallas_call x1, Pallas kernels: 83.9 us -> 88.8 us  [branch(): pl.pallas_call(functools.partial(branch_kernel, BLOCK, grid_of is not Non...]
    pallas_call x1, Pallas kernels: 25.6 us -> 21.3 us  [local_forward(): pl.pallas_call(functools.partial(local_forward_kernel, talk, rows_count,...]
where the time goes in v5:
time: 300 us; the launch traced here: 303 us
  Pallas kernels  298 us (99%)
    pallas_call x1, Pallas kernels, branch(): pl.pallas_call(functools.partial(branch_kernel, BLOCK, grid_of is not Non...  88.8 us
    pallas_call x1, Pallas kernels, finish_all(): pl.pallas_call(finish_kernel, in_specs=[vmem] + [anywhere] * 12 + [vmem]...  55.9 us
    pallas_call x1, Pallas kernels, slot_backward(): pl.pallas_call(functools.partial(slot_backward_kernel, rows_count, group_...  38.4 us
    pallas_call x1, Pallas kernels, gather_project(): pl.pallas_call(gather_project_kernel, in_specs=[anywhere, vmem, anywhere,...  33 us
    pallas_call x1, Pallas kernels, local_backward(): pl.pallas_call(functools.partial(local_backward_kernel, talk, rows_count,...  31.5 us
    pallas_call x1, Pallas kernels, slot_forward(): pl.pallas_call(functools.partial(slot_forward_kernel, rows_count, group_r...  23.1 us
    pallas_call x1, Pallas kernels, local_forward(): pl.pallas_call(functools.partial(local_forward_kernel, talk, rows_count,...  21.3 us
    pallas_call x1, Pallas kernels, unpack(): pl.pallas_call(unpack_kernel, grid=(steps,), in_specs=[pl.BlockSpec((HALF...  6.46 us

profile of v5, /device:TPU:0, one launch (start us, length us, event | category | flops | bytes accessed | tf_op | source)
XLA Modules:
  0.0 302.9 jit_solution(4220704482595756387)
XLA Ops:
  0.7 0.6 pad_add_fusion.place
  1.3 0.8 reshape.83
  2.1 0.7 reshape.84.b1_ref
  2.8 33.0 %gather_project.1 = (bf16[1024,768]{1,0:T(8,128)(2,1)}, bf16[1024,768]{1,0:T(8,128)(2,1)}, bf16[1024,768]{1,0:T(8,128)(2,1)}, bf16[1024,768]{1,0:T(8,128)(2,1)},...) custom-call(bf16[1024,768]{1,0:T(8,128)(2,1)} %bitcast.34, ...), custom_call_target="tpu_custom_call" | custom-call | flops 7247757312 | bytes 18874368 | tf_op jit(solution)/shard_map/gather_project/pallas_call | solution.py:561
  35.7 23.1 %slot_forward.1 = (bf16[768,1024]{1,0:T(8,128)(2,1)}, f32[6,2,8,1024]{3,2,1,0:T(8,128)}, bf16[8,6,128,128]{3,2,1,0:T(8,128)(2,1)}, f32[8,6,8,128]{3,2,1,0:T(8,128)}) custom-call(s32[2,8]{1,0:T(2,128)} %lengths.7, s32[2]{0:T(128)} %bucket_of.7, s32[3]{0:T(128)} %pad_add_fusion.place, bf16[1024,768]{1,0:T(8,128)(2,1)} %get-tuple-element.79.q_ref, ...), custom_call_target="tpu_custom_call" | custom-call | flops 3221225472 | bytes 15728640 | tf_op jit(solution)/shard_map/slot_forward/pallas_call | solution.py:827
  58.8 21.3 %local_forward.1 = (bf16[1024,768]{1,0:T(8,128)(2,1)}, f32[6,2,8,1024]{3,2,1,0:T(8,128)}, bf16[2,2,3,128,128]{4,3,2,1,0:T(8,128)(2,1)}, f32[2,2,3,8,128]{4,3,2,1,0:T(8,128)}) custom-call(s32[2,8]{1,0:T(2,128)} %lengths.7, s32[2]{0:T(128)} %bucket_of.7, s32[3]{0:T(128)} %pad_add_fusion.place, bf16[1024,768]{1,0:T(8,128)(2,1)} %get-tuple-element.79.q_ref, ...), custom_call_target="tpu_custom_call" | custom-call | flops 6442450944 | bytes 12582912 | tf_op jit(solution)/shard_map/local_forward/pallas_call | solution.py:1086
  80.1 88.8 %branch.1 = (bf16[1024,768]{1,0:T(8,128)(2,1)}, f32[1024,768]{1,0:T(8,128)}, bf16[1024,768]{1,0:T(8,128)(2,1)}, bf16[64,768]{1,0:T(8,128)(2,1)}, f32[64,768]{1,0...) custom-call(bf16[1024,768]{1,0:T(8,128)(2,1)} %get-tuple-element.78., ...), custom_call_target="tpu_custom_call" | custom-call | flops 36691771392 | bytes 33030144 | tf_op jit(solution)/shard_map/branch/pallas_call | solution.py:1566
  168.9 0.7 reduce
  169.6 0.1 reshape_reshape.3
  169.7 0.7 reshape.91.db1_ref
  170.4 31.5 %local_backward.1 = (bf16[768,1024]{1,0:T(8,128)(2,1)}, bf16[1024,768]{1,0:T(8,128)(2,1)}, bf16[1024,768]{1,0:T(8,128)(2,1)}, f32[6,2,8,1024]{3,2,1,0:T(8,128)},...) custom-call(s32[2,8]{1,0:T(2,128)} %lengths.7, s32[2]{0:T(128)} %bucket_of.7, ...), custom_call_target="tpu_custom_call" | custom-call | flops 16106127360 | bytes 23592960 | tf_op jit(solution)/shard_map/local_backward/pallas_call | solution.py:1795
  201.9 38.4 %slot_backward.1 = (bf16[1024,768]{1,0:T(8,128)(2,1)}, bf16[1024,768]{1,0:T(8,128)(2,1)}, bf16[1024,768]{1,0:T(8,128)(2,1)}, bf16[3,768,768]{2,1,0:T(8,128)(2,1)...) custom-call(s32[2,8]{1,0:T(2,128)} %lengths.7, s32[2]{0:T(128)} %bucket_of.7, s32[3]{0:T(128)} %pad_add_fusion.place, ...), custom_call_target="tpu_custom_call" | custom-call | flops 8053063680 | bytes 31457280 | tf_op jit(solution)/shard_map/slot_backward/pallas_call | solution.py:2053
  240.4 55.9 %finish_all.1 = (f32[288,384]{1,0:T(8,128)}, f32[16,768]{1,0:T(8,128)}, f32[64,768]{1,0:T(8,128)}, f32[768,768]{1,0:T(8,128)}, bf16[256,768]{1,0:T(8,128)(2,1)}, /*index=5*/bf16[256,768]{1,0:T(8,128)(2,1)}) custom-call(bf16[3,2,2,2,48,384]{5,4,3,2,1,0:T(8,128)(2,1)} %get-tuple-element.100.rest_ref, bf16[1024,768]{1,0:T(8,128)(2,1)} %get-tuple-element.78.x_ref.x_in, ...), custom_call_target="tpu_custom_call" | custom-call | flops 7247757312 | bytes 23592960 | tf_op jit(solution)/shard_map/finish_all/pallas_call | solution.py:2469
  296.2 6.5 %unpack.1 = (bf16[1,1024,768]{2,1,0:T(8,128)(2,1)}, bf16[1,64,768]{2,1,0:T(8,128)(2,1)}, f32[1,1024,768]{2,1,0:T(8,128)}, f32[1,64,768]{2,1,0:T(8,128)}, f32[48,...) custom-call(bf16[1024,768]{1,0:T(8,128)(2,1)} %get-tuple-element.93., ...), custom_call_target="tpu_custom_call" | custom-call | bytes 11010048 | tf_op jit(solution)/shard_map/unpack/pallas_call | solution.py:2634
  (2 shorter events, 0.0 us)

commit v6 on v5

--- a/solution.py
+++ b/solution.py
@@ -1103,6 +1103,14 @@
     )(*scalars, *operands)
 
 
+def join_rows(ref):
+    return jnp.concatenate([ref[i : i + 1] for i in range(ref.shape[0])], axis=1)
+
+
+def take_lanes(row, starts, length):
+    return jnp.concatenate([row[:, start : start + length] for start in starts], axis=1)
+
+
 def put_grouped(ref, value):
     seq, batch, rows, lanes = ref.shape
     for part in range(batch):
@@ -1123,7 +1131,7 @@
 
 def branch_kernel(
     tile,
-    talk,
+    seq_size,
     x_ref,
     o_ref,
     ct_ref,
@@ -1153,11 +1161,13 @@
     second_ref,
     *refs,
 ):
+    talk = seq_size > 0
     if talk:
-        message_ref, rest_ref = refs[:2]
-        refs = refs[2:]
+        message_ref, rest_ref, z_head_ref = refs[:3]
+        refs = refs[3:]
     os_ref, cts_ref, y_ref, h_ref, z_sum_ref, dh_ref, dft_ref, a_ref, du_ref, load_sem = refs[:10]
-    refs = refs[10:]
+    b1s_ref = refs[10]
+    refs = refs[11:]
     step = pl.program_id(0)
     steps = pl.num_programs(0)
     count, width = x_ref.shape
@@ -1339,8 +1349,7 @@
         unit, unused = normalize_rows(y)
         h_ref[at, :] = (unit * norms_ref[4:5] + norms_ref[5:6]).astype(bf16)
         y_ref[at, :] = y
-        b2 = jnp.concatenate([b2_ref[i : i + 1] for i in range(width // LANES)], axis=1)
-        sums[...] = y + b2
+        sums[...] = y + join_rows(b2_ref)
         dh_ref[at, :] = jnp.zeros((size, width), f32)
 
     @pl.when(step == 0)
@@ -1365,19 +1374,32 @@
         for load in loads[1:]:
             load.wait()
 
-    db1_ref[...] = jnp.zeros_like(db1_ref)
+    @pl.when(step == 0)
+    def _():
+        row = join_rows(b1_ref)
+        for number in range(b1s_ref.shape[0]):
+            if talk:
+                share = FF_CHUNK // seq_size
+                starts = [place * b1s_ref.shape[0] * share for place in range(seq_size)]
+                starts = [start + number * share for start in starts]
+                b1s_ref[number : number + 1] = take_lanes(row, starts, share)
+            else:
+                b1s_ref[number : number + 1] = row[:, number * FF_CHUNK : (number + 1) * FF_CHUNK]
+
+    my_row = pl.ds(step, 1)
+    db1_ref[my_row, :] = jnp.zeros((1, FF_CHUNK), f32)
     w1 = w1_ref[...].reshape(width, width)
     w2 = w2_ref[...].reshape(width, width)
 
     def chunk_of(at, sums):
-        u = nt(h_ref[at, :], w1) + b1_ref[0]
+        u = nt(h_ref[at, :], w1) + b1s_ref[my_row, :]
         da = nt(cts_ref[at, :], w2)
         area, density = gelu_parts(u)
         a = (u * area).astype(bf16)
         du = (da * (area + u * density)).astype(bf16)
         a_ref[at, :] = a
         du_ref[at, :] = du
-        db1_ref[0] += jnp.sum(du.astype(f32), axis=0, keepdims=True)
+        db1_ref[my_row, :] += jnp.sum(du.astype(f32), axis=0, keepdims=True)
         sums[...] = sums[...] + nn(a, w2)
         dh_ref[at, :] = dh_ref[at, :] + nn(du, w1)
 
@@ -1486,6 +1508,7 @@
             put_grouped(dwo_ref, dwo)
             advance(TICKS * chunks + 1)
             rest_ref[...] = landings[1][2 * chunks - 2 :]
+            z_head_ref[...] = z_ref[:HALF]
             for when, chunk, stage in plan:
                 for unit in (2 * chunk, 2 * chunk + 1):
                     if stage > 0 or unit + slots >= 2 * chunks:
@@ -1515,7 +1538,6 @@
     more = {}
     if grid_of is None:
         weight_spec = pl.BlockSpec((FF_CHUNK, width), lambda j: (j, 0))
-        b1 = b1.reshape(steps, 1, FF_CHUNK)
         dw_shapes = [(hidden, width), (width, hidden)]
         dw_types = [bf16, bf16]
         dw_specs = [weight_spec, pl.BlockSpec((width, FF_CHUNK), lambda j: (0, j))]
@@ -1526,7 +1548,6 @@
         weight_spec = pl.BlockSpec((seq, 1, rows, width), lambda j: (0, j, 0, 0))
         w1t = w1t.reshape(seq, steps, rows, width)
         w2 = w2.reshape(seq, steps, rows, width)
-        b1 = b1.reshape(seq, steps, rows).transpose(1, 0, 2).reshape(steps, 1, FF_CHUNK)
         units = 2 * (steps - 1)
         sums, stats = go.shape[2:], gstat.shape[2:]
         dw_shapes = [
@@ -1534,8 +1555,9 @@
             (2, 2, 2, 2, 2, batch, rows, lanes),
             (2, own, width + LANES),
             (2, 2, 2, 2, rows, lanes),
+            (HALF, width),
         ]
-        dw_types = [f32, bf16, bf16, bf16]
+        dw_types = [f32, bf16, bf16, bf16, bf16]
         dw_specs = [once(shape) for shape in dw_shapes]
         dwo_shape = (seq, batch, rows, lanes)
         dma = pltpu.SemaphoreType.DMA
@@ -1564,7 +1586,7 @@
         )
         more = {"collective_id": 3, "has_side_effects": True}
     out = pl.pallas_call(
-        functools.partial(branch_kernel, BLOCK, grid_of is not None),
+        functools.partial(branch_kernel, BLOCK, grid_of[0] if grid_of else 0),
         grid=(steps,),
         in_specs=[
             row,
@@ -1577,13 +1599,13 @@
             few,
             once((width, width)),
             weight_spec,
-            pl.BlockSpec((1, 1, FF_CHUNK), lambda j: (j, 0, 0)),
+            full(b1.shape),
             weight_spec,
             full(b2.shape),
             full(norms.shape),
         ],
         out_specs=[row, row, row, few, few, few]
-        + [once(dwo_shape), pl.BlockSpec((1, 1, FF_CHUNK), lambda j: (j, 0, 0)), line, line, line]
+        + [once(dwo_shape), full((steps, FF_CHUNK)), line, line, line]
         + dw_specs,
         out_shape=[
             jax.ShapeDtypeStruct((count, width), bf16),
@@ -1593,7 +1615,7 @@
             jax.ShapeDtypeStruct((own, width), f32),
             jax.ShapeDtypeStruct((own, width), bf16),
             jax.ShapeDtypeStruct(dwo_shape, bf16),
-            jax.ShapeDtypeStruct((steps, 1, FF_CHUNK), f32),
+            jax.ShapeDtypeStruct((steps, FF_CHUNK), f32),
             jax.ShapeDtypeStruct((1, width), f32),
             jax.ShapeDtypeStruct((1, width), f32),
             jax.ShapeDtypeStruct((1, width), f32),
@@ -1610,6 +1632,7 @@
             pltpu.VMEM((total, FF_CHUNK), bf16),
             pltpu.VMEM((total, FF_CHUNK), bf16),
             pltpu.SemaphoreType.DMA((3,)),
+            pltpu.VMEM((steps, FF_CHUNK), f32),
         ]
         + scratch,
         compiler_params=params(**more),
@@ -1620,10 +1643,7 @@
         ),
         name="branch",
     )(x, o, ct, ct_head, gx, go, gstat, gct, wo, w1t, b1, w2, b2, norms)
-    db1 = out[7].reshape(steps, FF_CHUNK)
-    if grid_of is not None:
-        db1 = db1.reshape(steps, seq, rows).transpose(1, 0, 2).reshape(-1, width)
-    return [*out[:7], db1, *out[8:]]
+    return out
 
 
 def local_backward_kernel(
@@ -1813,6 +1833,7 @@
 
 
 def slot_backward_kernel(
+    grouped,
     rows_count,
     group_rows,
     lengths,
@@ -1832,8 +1853,9 @@
     gv_ref,
     gdo_ref,
     gstat_ref,
-    gx_ref,
-    gh_ref,
+    gx_in,
+    gh_in,
+    h_in,
     wq_ref,
     wk_ref,
     wv_ref,
@@ -1858,6 +1880,11 @@
     lines_ref,
     dw_sum,
     dgh_sum,
+    rows_ref,
+    gx_ref,
+    gh_ref,
+    h_ref,
+    load_sem,
 ):
     group = pl.program_id(0)
     block = pl.program_id(1)
@@ -1868,8 +1895,17 @@
     def lanes_of(which):
         return pl.ds(which * LANES, LANES)
 
+    loads = [
+        pltpu.make_async_copy(source, target, load_sem.at[number])
+        for number, (source, target) in enumerate(
+            ((gx_in, gx_ref), (gh_in, gh_ref), (h_in, h_ref))
+        )
+    ]
+
     @pl.when(step == 0)
     def _():
+        for load in loads:
+            load.start()
         read_edges(lengths, bucket_of, place, edges)
 
         def turn(slot, carry):
@@ -1953,9 +1989,18 @@
         return carry
 
     lax.fori_loop(0, SLOTS, one_slot, 0)
-    dq_ref[...] = dqt_sum[...].T.astype(bf16)
-    dk_ref[...] = dk_sum[...].astype(bf16)
-    dv_ref[...] = dv_sum[...].astype(bf16)
+    here = pl.ds(pl.multiple_of(block * BLOCK, BLOCK), BLOCK)
+    for index, (ref, value) in enumerate(
+        ((dq_ref, dqt_sum[...].T), (dk_ref, dk_sum[...]), (dv_ref, dv_sum[...]))
+    ):
+        low = value.astype(bf16)
+        ref[...] = low
+        rows_ref[index, here, :] = low
+
+    @pl.when(step == blocks - 1)
+    def _():
+        for load in loads:
+            load.wait()
 
     @pl.when((block == blocks - 1) & (place[2] >= 0))
     def _():
@@ -1971,7 +2016,11 @@
 
     @pl.when(block == blocks - 1)
     def _():
-        def through(slot, found):
+        for index in range(3):
+            local = tn(rows_ref[index], h_ref[...])
+            dw_sum[index] = local * query_scale if index == 0 else local
+
+        def through(slot, carry):
             needed = slot == place[2]
             for number in range(blocks):
                 needed = needed | slot_present(
@@ -1995,15 +2044,8 @@
                     total = total + nt(grads[index], weight[...])
                 dgh_sum[at, :] = total
 
-                @pl.when(found == 0)
-                def _():
-                    for index in range(3):
-                        dw_sum[index] = tn(grads[index], rows)
-
-                @pl.when(found > 0)
-                def _():
-                    for index in range(3):
-                        dw_sum[index] += tn(grads[index], rows)
+                for index in range(3):
+                    dw_sum[index] += tn(grads[index], rows)
 
                 @pl.when(group == PAIRS // TOGETHER - 1)
                 def _():
@@ -2011,10 +2053,14 @@
                     dnorm_ref[0:1] += jnp.sum(total * unit, axis=0, keepdims=True)
                     dnorm_ref[1:2] += jnp.sum(total, axis=0, keepdims=True)
 
-            return jnp.where(needed, 1, found)
-
-        lax.fori_loop(0, SLOTS, through, jnp.int32(0))
-        dw_ref[...] = dw_sum[...].astype(bf16)
+            return carry
+
+        lax.fori_loop(0, SLOTS, through, 0)
+        if grouped:
+            for index in range(3):
+                put_grouped(dw_ref.at[index], dw_sum[index])
+        else:
+            dw_ref[...] = dw_sum[...].astype(bf16)
 
     @pl.when(step == PAIRS // TOGETHER * blocks - 1)
     def _():
@@ -2022,6 +2068,7 @@
 
 
 def slot_backward(
+    grid_of,
     scalars,
     rows_count,
     group_rows,
@@ -2040,6 +2087,7 @@
     everyone,
     gx,
     gh,
+    h,
     wq,
     wk,
     wv,
@@ -2050,8 +2098,17 @@
     pair_spec = pl.BlockSpec((all_globals, TOGETHER * LANES), lambda p, b, *unused: (0, p))
     local = jax.ShapeDtypeStruct((rows_count, width), bf16)
     glob = jax.ShapeDtypeStruct((all_globals, width), bf16)
+    if grid_of is None:
+        dw_shape = (3, width, width)
+        dw_spec = pl.BlockSpec((3, TOGETHER * LANES, width), lambda p, b, *unused: (0, p, 0))
+    else:
+        seq, batch = grid_of
+        piece = (batch, width // seq, width // batch)
+        dw_shape = (3, seq) + piece
+        share = TOGETHER * LANES // piece[1]
+        dw_spec = pl.BlockSpec((3, share) + piece, lambda p, b, *unused: (0, p, 0, 0, 0))
     return pl.pallas_call(
-        functools.partial(slot_backward_kernel, rows_count, group_rows),
+        functools.partial(slot_backward_kernel, grid_of is not None, rows_count, group_rows),
         grid_spec=pltpu.PrefetchScalarGridSpec(
             num_scalar_prefetch=3,
             grid=(PAIRS // TOGETHER, blocks),
@@ -2061,11 +2118,11 @@
             + [block_spec] * 2
             + [pair_spec] * 4
             + [pl.BlockSpec((all_globals, LANES), lambda p, b, *unused: (0, PAIRS))]
-            + [once((all_globals, width))] * 2
+            + [pl.BlockSpec(memory_space=pl.ANY)] * 3
             + [pl.BlockSpec((width, TOGETHER * LANES), lambda p, b, *unused: (0, p))] * 3,
             out_specs=[block_spec] * 3
             + [
-                pl.BlockSpec((3, TOGETHER * LANES, width), lambda p, b, *unused: (0, p, 0)),
+                dw_spec,
                 once((all_globals, width)),
                 full((8, width)),
             ],
@@ -2083,11 +2140,16 @@
                 pltpu.VMEM((SLOTS, LANES, GLOBALS), f32),
                 pltpu.VMEM((3, TOGETHER * LANES, width), f32),
                 pltpu.VMEM((all_globals, width), f32),
+                pltpu.VMEM((3, rows_count, TOGETHER * LANES), bf16),
+                pltpu.VMEM((all_globals, width), bf16),
+                pltpu.VMEM((all_globals, width), bf16),
+                pltpu.VMEM((rows_count, width), bf16),
+                pltpu.SemaphoreType.DMA((3,)),
             ],
         ),
         out_shape=[local] * 3
         + [
-            jax.ShapeDtypeStruct((3, width, width), bf16),
+            jax.ShapeDtypeStruct(dw_shape, bf16),
             glob,
             jax.ShapeDtypeStruct((8, width), f32),
         ],
@@ -2116,6 +2178,7 @@
         everyone,
         gx,
         gh,
+        h,
         wq,
         wk,
         wv,
@@ -2126,17 +2189,14 @@
     tile,
     x_ref,
     dy_ref,
-    h_ref,
     dq_ref,
     dk_ref,
     dv_ref,
-    dwg_ref,
     wq_ref,
     wk_ref,
     wv_ref,
     gain_ref,
     dx_ref,
-    dw_ref,
     dnorm_ref,
 ):
     count, width = x_ref.shape
@@ -2156,23 +2216,17 @@
         return carry
 
     lax.fori_loop(0, count // tile, one_tile, 0)
-    for index, source in enumerate((dq_ref, dk_ref, dv_ref)):
-        value = tn(source[...], h_ref[...])
-        if index == 0:
-            value = value * query_scale
-        dw_ref[index] = (value + dwg_ref[index].astype(f32)).astype(bf16)
-
-
-def project_back(x, dy, h, dq, dk, dv, dwg, wq, wk, wv, gain):
+
+
+def project_back(x, dy, dq, dk, dv, wq, wk, wv, gain):
     count, width = x.shape
     vmem = pl.BlockSpec(memory_space=pltpu.VMEM)
     return pl.pallas_call(
         functools.partial(project_back_kernel, BLOCK),
-        in_specs=[vmem] * 11,
-        out_specs=[vmem] * 3,
+        in_specs=[vmem] * 9,
+        out_specs=[vmem] * 2,
         out_shape=[
             jax.ShapeDtypeStruct((count, width), f32),
-            jax.ShapeDtypeStruct((3, width, width), bf16),
             jax.ShapeDtypeStruct((8, width), f32),
         ],
         compiler_params=params(),
@@ -2180,20 +2234,18 @@
             flops=12 * count * width * width, bytes_accessed=30 * count * width, transcendentals=0
         ),
         name="project_back",
-    )(x, dy, h, dq, dk, dv, dwg, wq, wk, wv, gain)
+    )(x, dy, dq, dk, dv, wq, wk, wv, gain)
 
 
 def finish_kernel(
     rest_ref,
     x_in,
     dy_in,
-    h_in,
     dq_in,
     dk_in,
     dv_in,
-    dwg_in,
+    dqkv_ref,
     dgh_ref,
-    z_in,
     wq_in,
     wk_in,
     wv_in,
@@ -2210,19 +2262,16 @@
     grad_out_ref,
     token_ref,
     halo_dx_out,
-    halo_z_out,
     x_ref,
     dy_ref,
-    h_ref,
     dq_ref,
     dk_ref,
     dv_ref,
-    dwg_ref,
     wq_ref,
     wk_ref,
     wv_ref,
     load_sem,
-    units_ref,
+    own_ref,
     one_ref,
     two_ref,
     three_ref,
@@ -2230,6 +2279,7 @@
     five_ref,
     send_sem,
     recv_sem,
+    own_sem,
     gown_ref,
     gone_ref,
     gtwo_ref,
@@ -2244,7 +2294,6 @@
     srecv_sem,
     halo_out,
     halo_dx,
-    halo_z,
     halo_send,
     halo_recv,
     dnorm_ref,
@@ -2262,8 +2311,6 @@
 
     pairs = [
         (dq_in, dq_ref),
-        (h_in, h_ref),
-        (dwg_in, dwg_ref),
         (dk_in, dk_ref),
         (dv_in, dv_ref),
         (wq_in, wq_ref),
@@ -2276,20 +2323,17 @@
         pltpu.make_async_copy(source, target, load_sem.at[number])
         for number, (source, target) in enumerate(pairs)
     ]
-    for load in loads:
-        load.start()
-
     def source(unit):
-        return lambda side: units_ref.at[unit - came, :, :, :, side]
+        return lambda side: dqkv_ref.at[unit - came, :, :, :, side]
 
     engine = HalvingSum(
         (X_Z_FIRST, Y_FIRST, X_FIRST, X_FIRST, Y_FIRST, Z_FIRST),
         [source(unit) for unit in range(units)],
         (one_ref, two_ref, three_ref, four_ref, five_ref),
-        None,
+        own_ref,
         send_sem,
         recv_sem,
-        None,
+        own_sem,
         put_rows(out_ref, five_ref.shape[1]),
         bits,
         partners,
@@ -2338,40 +2382,21 @@
         else:
             small_out_ref[...] = total
 
-    halos = [
-        remote(halo_out, halo_dx, halo_send.at[0], halo_recv.at[0], before),
-        remote(
-            z_in.at[pl.ds(0, HALF)], halo_z, halo_send.at[1], halo_recv.at[1], before
-        ),
-    ]
+    halo = remote(halo_out, halo_dx, halo_send, halo_recv, before)
     two_ref[:came] = rest_ref[...]
     meet([partners[name] for name in AXES] + [before, after])
+    for unit in range(came, units):
+        engine.begin(unit)
+    for load in loads:
+        load.start()
     for unit in range(came):
         engine.copy(unit, 2).start()
     for unit in range(2):
         row_sum.begin(unit)
-
-    def weight_gradient(index, grads_ref):
-        value = tn(grads_ref[...], h_ref[...])
-        if index == 0:
-            value = value * query_scale
-        put_unit(units_ref.at[index], value + dwg_ref[index].astype(f32))
-        engine.begin(came + index)
-
-    for number in range(3):
-        loads[number].wait()
-    weight_gradient(0, dq_ref)
-    rows_advance(0)
-    loads[3].wait()
-    weight_gradient(1, dk_ref)
-    engine.advance(came, 0)
-    loads[4].wait()
-    weight_gradient(2, dv_ref)
-    engine.advance(came + 1, 0)
-    for unit in range(came):
-        engine.advance(unit, 2)
-    for number in range(5, 10):
-        loads[number].wait()
+    for unit in range(came, units):
+        engine.advance(unit, 0)
+    for load in loads:
+        load.wait()
     dnorm_ref[...] = jnp.zeros_like(dnorm_ref)
 
     def back(index):
@@ -2393,11 +2418,12 @@
     for index in range(count // HALF):
         back(index)
         if index == 0:
-            engine.advance(came + 2, 0)
-            halos[0].start()
-        if index == 1:
+            halo.start()
+            rows_advance(0)
+            for unit in range(came):
+                engine.advance(unit, 2)
+        if index == 2:
             rows_advance(1)
-        if index == 2:
             for unit in range(came):
                 engine.advance(unit, 3)
 
@@ -2414,31 +2440,29 @@
     parts.append(jnp.zeros((sums_ref.shape[1] - filled, width), f32))
     sums_ref[0] = jnp.concatenate(parts, 0)
     scopy(0).start()
-    halos[1].start()
+
+    def weights_advance(stage):
+        for unit in range(came, units):
+            engine.advance(unit, stage)
+
+    small_advance(0)
+    weights_advance(1)
+    small_advance(1)
     rows_advance(2)
-    for unit in range(came, units):
-        engine.advance(unit, 1)
-    small_advance(0)
+    small_advance(2)
+    weights_advance(2)
+    small_advance(3)
+    for unit in range(came):
+        engine.advance(unit, 4)
     rows_advance(3)
     dgh = dgh_sum_ref[...]
     unit_rows, scale = normalize_rows(gx_ref[...].astype(f32))
     grad_out_ref[...] = gdy_ref[...] + norm_back(unit_rows, scale, norms_ref[2:3], dgh)
-    small_advance(1)
-    for unit in range(came):
-        engine.advance(unit, 4)
-    for unit in range(came, units):
-        engine.advance(unit, 2)
-    small_advance(2)
-    for halo in halos:
-        halo.wait_recv()
+    small_advance(4)
+    halo.wait_recv()
     halo_dx_out[...] = halo_dx[...]
-    halo_z_out[...] = halo_z[...]
-    for unit in range(came, units):
-        engine.advance(unit, 3)
-    small_advance(3)
-    for unit in range(came, units):
-        engine.advance(unit, 4)
-    small_advance(4)
+    weights_advance(3)
+    weights_advance(4)
 
     for unit in range(units):
         for stage in range(2 if unit < came else 0, STAGES):
@@ -2448,11 +2472,10 @@
     for unit in range(2):
         for stage in range(4):
             row_sum.sent(unit, stage)
-    for halo in halos:
-        halo.wait_send()
-
-
-def finish_all(rest, x, dy, h, dq, dk, dv, dwg, dgh, z, wq, wk, wv, small, gx, gdy, norms):
+    halo.wait_send()
+
+
+def finish_all(rest, x, dy, dq, dk, dv, dqkv, dgh, wq, wk, wv, small, gx, gdy, norms):
     count, width = x.shape
     rows, lanes = rest.shape[-2:]
     units = rest.shape[0] + 3
@@ -2468,14 +2491,13 @@
     half = pltpu.VMEM((HALF, width), bf16)
     return pl.pallas_call(
         finish_kernel,
-        in_specs=[vmem] + [anywhere] * 12 + [vmem] * 8,
-        out_specs=[vmem] * 6,
+        in_specs=[vmem] + [anywhere] * 10 + [vmem] * 8,
+        out_specs=[vmem] * 5,
         out_shape=[
             jax.ShapeDtypeStruct((units * rows, lanes), f32),
             jax.ShapeDtypeStruct((small_rows, width), f32),
             jax.ShapeDtypeStruct((own, width), f32),
             jax.ShapeDtypeStruct((count - HALF, width), f32),
-            jax.ShapeDtypeStruct((HALF, width), bf16),
             jax.ShapeDtypeStruct((HALF, width), bf16),
         ],
         scratch_shapes=[
@@ -2484,15 +2506,12 @@
             row,
             row,
             row,
-            row,
-            pltpu.VMEM((3, width, width), bf16),
             weight,
             weight,
             weight,
-            dma((10,)),
-            pltpu.VMEM((3, 2, 2, 2, 2, 2, rows, lanes), bf16),
+            dma((8,)),
         ]
-        + sum_scratch(units, rows, lanes, False)
+        + sum_scratch(units, rows, lanes, True)
         + [
             pltpu.VMEM((2, 2, 2, 2, own, width // 2), bf16),
             pltpu.VMEM((2, 2, 2, 2, own, width // 2), bf16),
@@ -2508,9 +2527,8 @@
             dma((STAGES,)),
             half,
             half,
-            half,
-            dma((2,)),
-            dma((2,)),
+            dma,
+            dma,
             pltpu.VMEM((8, width), f32),
             pltpu.VMEM((own, width), f32),
         ],
@@ -2523,13 +2541,11 @@
         rest,
         x,
         dy,
-        h,
         dq,
         dk,
         dv,
-        dwg,
+        dqkv.reshape((3,) + place + (2, rows, lanes)),
         dgh.reshape(place + (own, width)),
-        z,
         wq,
         wk,
         wv,
@@ -2601,13 +2617,21 @@
         w2_ref[...] = turned_ref[...].T
         pieces_in_row = small_ref.shape[1] // LANES
         hidden_rows = b1_ref.shape[0] // pieces_in_row
-        for row in range(hidden_rows + 1):
-            for piece in range(pieces_in_row):
-                value = small_ref[row : row + 1, piece * LANES : (piece + 1) * LANES]
-                if row < hidden_rows:
-                    b1_ref[row * pieces_in_row + piece : row * pieces_in_row + piece + 1] = value
-                else:
-                    b2_ref[piece : piece + 1] = value
+        per_chunk = small_ref.shape[1] // rows
+        natural = jnp.concatenate(
+            [
+                small_ref[chunk : chunk + 1, place * rows : (place + 1) * rows]
+                for place in range(per_chunk)
+                for chunk in range(hidden_rows)
+            ],
+            axis=1,
+        )
+        for piece in range(hidden_rows * pieces_in_row):
+            b1_ref[piece : piece + 1] = natural[:, piece * LANES : (piece + 1) * LANES]
+        for piece in range(pieces_in_row):
+            b2_ref[piece : piece + 1] = small_ref[
+                hidden_rows : hidden_rows + 1, piece * LANES : (piece + 1) * LANES
+            ]
         norms_ref[...] = small_ref[hidden_rows + 1 : hidden_rows + 7]
 
 
@@ -2780,7 +2804,7 @@
         global_cotangent[0],
         wo,
         w1t,
-        b1,
+        b1.reshape(-1, LANES),
         w2,
         b2_rows,
         norm_params,
@@ -2801,11 +2825,14 @@
             False, scalars, rows, group_rows, q, k, v, do, o, line, None, None, None, None
         )
     else:
-        sum_first, last, message, rest = dws
+        sum_first, last, message, rest, z_head = dws
         dqt, dk, dv, centre, everyone, sum_second, rest = local_backward(
             True, scalars, rows, group_rows, q, k, v, do, o, line, message, rest, last, dwo
         )
-    dq, dk, dv, dwg, dgh, dnorm_global = slot_backward(
+        z_head, rest = lax.optimization_barrier((z_head, rest))
+        halo_z = from_behind(z_head, "seq", -1)
+    dq, dk, dv, dqkv, dgh, dnorm_global = slot_backward(
+        grid_of,
         scalars,
         rows,
         group_rows,
@@ -2824,12 +2851,13 @@
         everyone,
         all_states,
         gh,
+        h,
         wq,
         wk,
         wv,
     )
     if grid_of is None:
-        dx, dqkv, dnorm = project_back(x, dy, h, dq, dk, dv, dwg, wq, wk, wv, norms[0])
+        dx, dnorm = project_back(x, dy, dq, dk, dv, wq, wk, wv, norms[0])
         back_z, back_grad = from_behind((z[:HALF], dx[:HALF].astype(bf16)), "seq", -1)
         layer_out = jnp.concatenate([z[HALF:], back_z], 0)
         token_grad = jnp.concatenate([dx[HALF:], back_grad.astype(f32)], 0)
@@ -2841,17 +2869,15 @@
         dw1, dw2 = dws
         weights = [scatter_sum(value) for value in (dqkv[0], dqkv[1], dqkv[2], dwo, dw1, dw2)]
     else:
-        sum_third, small, global_grad, dx, halo_dx, halo_z = finish_all(
+        sum_third, small, global_grad, dx, halo_dx = finish_all(
             rest,
             x,
             dy,
-            h,
             dq,
             dk,
             dv,
-            dwg,
+            dqkv,
             dgh,
-            z,
             wq,
             wk,
             wv,

time: 300 us -> 294 us (0.980); the launches traced: 303 us -> 290 us
  Pallas kernels: 298 us -> 286 us
    pallas_call x3, Pallas kernels: 183 us -> 176 us  [the longest x1 83.5 us: branch(): pl.pallas_call(functools.partial(branch_kernel, BLOCK, grid_of[0] if grid...]
    pallas_call x1, Pallas kernels: 23.1 us -> 18.4 us  [slot_forward(): pl.pallas_call(functools.partial(slot_forward_kernel, rows_count, group_r...]
  transfers between devices with their start and end apart: 0 -> 1, of which waited for: 0 -> 0; matrix products, arithmetic and copies ran while one was open for 0% -> 0% of each run, Pallas kernels for 0% -> 32%
where the time goes in v6:
time: 294 us; the launch traced here: 290 us
  Pallas kernels  286 us (97%)
    pallas_call x1, Pallas kernels, branch(): pl.pallas_call(functools.partial(branch_kernel, BLOCK, grid_of[0] if grid...  83.5 us
    pallas_call x1, Pallas kernels, finish_all(): pl.pallas_call(finish_kernel, in_specs=[vmem] + [anywhere] * 10 + [vmem]...  58.8 us
    pallas_call x1, Pallas kernels, slot_backward(): pl.pallas_call(functools.partial(slot_backward_kernel, grid_of is not Non...  33.5 us
    pallas_call x1, Pallas kernels, gather_project(): pl.pallas_call(gather_project_kernel, in_specs=[anywhere, vmem, anywhere,...  32.8 us
    pallas_call x1, Pallas kernels, local_backward(): pl.pallas_call(functools.partial(local_backward_kernel, talk, rows_count,...  31.1 us
    pallas_call x1, Pallas kernels, local_forward(): pl.pallas_call(functools.partial(local_forward_kernel, talk, rows_count,...  21.4 us
    pallas_call x1, Pallas kernels, slot_forward(): pl.pallas_call(functools.partial(slot_forward_kernel, rows_count, group_r...  18.4 us
    pallas_call x1, Pallas kernels, unpack(): pl.pallas_call(unpack_kernel, grid=(steps,), in_specs=[pl.BlockSpec((HALF...  6.56 us
  transfers between devices with their start and end apart: 1, of which 0 were waited for; matrix products, arithmetic and copies ran while one was open for 0% of the time, Pallas kernels for 32%

profile of v6, /device:TPU:0, one launch (start us, length us, event | category | flops | bytes accessed | tf_op | source)
XLA Modules:
  0.0 290.3 jit_solution(12815444539162910891)
XLA Ops:
  0.7 0.6 pad_add_fusion.place
  1.3 32.8 %gather_project.1 = (bf16[1024,768]{1,0:T(8,128)(2,1)}, bf16[1024,768]{1,0:T(8,128)(2,1)}, bf16[1024,768]{1,0:T(8,128)(2,1)}, bf16[1024,768]{1,0:T(8,128)(2,1)},...) custom-call(bf16[1024,768]{1,0:T(8,128)(2,1)} %bitcast.30, ...), custom_call_target="tpu_custom_call" | custom-call | flops 7247757312 | bytes 18874368 | tf_op jit(solution)/shard_map/gather_project/pallas_call | solution.py:561
  34.1 18.4 %slot_forward.1 = (bf16[768,1024]{1,0:T(8,128)(2,1)}, f32[6,2,8,1024]{3,2,1,0:T(8,128)}, bf16[8,6,128,128]{3,2,1,0:T(8,128)(2,1)}, f32[8,6,8,128]{3,2,1,0:T(8,128)}) custom-call(s32[2,8]{1,0:T(2,128)} %lengths.7, s32[2]{0:T(128)} %bucket_of.7, s32[3]{0:T(128)} %pad_add_fusion.place, bf16[1024,768]{1,0:T(8,128)(2,1)} %get-tuple-element.81.q_ref, ...), custom_call_target="tpu_custom_call" | custom-call | flops 3221225472 | bytes 15728640 | tf_op jit(solution)/shard_map/slot_forward/pallas_call | solution.py:827
  52.5 21.4 %local_forward.1 = (bf16[1024,768]{1,0:T(8,128)(2,1)}, f32[6,2,8,1024]{3,2,1,0:T(8,128)}, bf16[2,2,3,128,128]{4,3,2,1,0:T(8,128)(2,1)}, f32[2,2,3,8,128]{4,3,2,1,0:T(8,128)}) custom-call(s32[2,8]{1,0:T(2,128)} %lengths.7, s32[2]{0:T(128)} %bucket_of.7, s32[3]{0:T(128)} %pad_add_fusion.place, bf16[1024,768]{1,0:T(8,128)(2,1)} %get-tuple-element.81.q_ref, ...), custom_call_target="tpu_custom_call" | custom-call | flops 6442450944 | bytes 12582912 | tf_op jit(solution)/shard_map/local_forward/pallas_call | solution.py:1086
  74.0 83.5 %branch.1 = (bf16[1024,768]{1,0:T(8,128)(2,1)}, f32[1024,768]{1,0:T(8,128)}, bf16[1024,768]{1,0:T(8,128)(2,1)}, bf16[64,768]{1,0:T(8,128)(2,1)}, f32[64,768]{1,0...) custom-call(bf16[1024,768]{1,0:T(8,128)(2,1)} %get-tuple-element.80., ...), custom_call_target="tpu_custom_call" | custom-call | flops 36691771392 | bytes 33030144 | tf_op jit(solution)/shard_map/branch/pallas_call | solution.py:1588
  157.5 0.0 copy-start.1
  157.5 31.1 %local_backward.1 = (bf16[768,1024]{1,0:T(8,128)(2,1)}, bf16[1024,768]{1,0:T(8,128)(2,1)}, bf16[1024,768]{1,0:T(8,128)(2,1)}, f32[6,2,8,1024]{3,2,1,0:T(8,128)},...) custom-call(s32[2,8]{1,0:T(2,128)} %lengths.7, s32[2]{0:T(128)} %bucket_of.7, ...), custom_call_target="tpu_custom_call" | custom-call | flops 16106127360 | bytes 23592960 | tf_op jit(solution)/shard_map/local_backward/pallas_call | solution.py:1815
  188.6 0.0 copy-done.1
  188.7 1.7 collective-permute-start
  190.4 33.5 %slot_backward.1 = (bf16[1024,768]{1,0:T(8,128)(2,1)}, bf16[1024,768]{1,0:T(8,128)(2,1)}, bf16[1024,768]{1,0:T(8,128)(2,1)}, bf16[3,16,2,48,384]{4,3,2,1,0:T(8,1...) custom-call(s32[2,8]{1,0:T(2,128)} %lengths.7, s32[2]{0:T(128)} %bucket_of.7, s32[3]{0:T(128)} %pad_add_fusion.place, ...), custom_call_target="tpu_custom_call" | custom-call | flops 8053063680 | bytes 31457280 | tf_op jit(solution)/shard_map/slot_backward/pallas_call | solution.py:2110
  223.9 58.8 %finish_all.1 = (f32[288,384]{1,0:T(8,128)}, f32[16,768]{1,0:T(8,128)}, f32[64,768]{1,0:T(8,128)}, f32[768,768]{1,0:T(8,128)}, bf16[256,768]{1,0:T(8,128)(2,1)}) custom-call(bf16[3,2,2,2,48,384]{5,4,3,2,1,0:T(8,128)(2,1)} %get-tuple-element.105.rest_ref, bf16[1024,768]{1,0:T(8,128)(2,1)} %get-tuple-element.80.x_ref.x_in, ...), custom_call_target="tpu_custom_call" | custom-call | flops 7247757312 | bytes 23592960 | tf_op jit(solution)/shard_map/finish_all/pallas_call | solution.py:2492
  282.7 0.0 collective-permute-done.halo_z_ref
  282.7 0.0 copy-start
  282.7 0.7 copy-done
  283.5 6.6 %unpack.1 = (bf16[1,1024,768]{2,1,0:T(8,128)(2,1)}, bf16[1,64,768]{2,1,0:T(8,128)(2,1)}, f32[1,1024,768]{2,1,0:T(8,128)}, f32[1,64,768]{2,1,0:T(8,128)}, f32[48,...) custom-call(bf16[1024,768]{1,0:T(8,128)(2,1)} %get-tuple-element.95., ...), custom_call_target="tpu_custom_call" | custom-call | bytes 11010048 | tf_op jit(solution)/shard_map/unpack/pallas_call | solution.py:2658
Async XLA Ops:
  157.5 31.1 %copy-start.1 = (bf16[256,768]{1,0:T(8,128)(2,1)S(1)}, bf16[256,768]{1,0:T(8,128)(2,1)}, u32[]{:S(2)}) copy-start(bf16[256,768]{1,0:T(8,128)(2,1)} %get-tuple-element.104) | copy-start | bytes 1179652
  188.7 94.1 %collective-permute-start = (bf16[256,768]{1,0:T(8,128)(2,1)S(1)}, bf16[256,768]{1,0:T(8,128)(2,1)S(1)}, u32[]{:S(2)}, u32[]{:S(2)}) collective-permute-start(bf16[256,768]{1,0:T(8,128)(2,1)S(1)} %copy-done.1), channel_id=1, source_target_pairs={{0,15},{1,0},{2,1},{3,2},{4,3},{5,4},{6,5},{7,6},{8,7},{9,8},{10,9... | collective-permute-start | bytes 1179656 | tf_op jit(solution)/shard_map/ppermute | solution.py:2689
  282.7 0.7 copy-start

commit v7 on v6

--- a/solution.py
+++ b/solution.py
@@ -2420,12 +2420,9 @@
         if index == 0:
             halo.start()
             rows_advance(0)
+        if index == 2:
             for unit in range(came):
                 engine.advance(unit, 2)
-        if index == 2:
-            rows_advance(1)
-            for unit in range(came):
-                engine.advance(unit, 3)
 
     hidden_rows = db1_ref.shape[0]
     parts = [
@@ -2446,7 +2443,10 @@
             engine.advance(unit, stage)
 
     small_advance(0)
+    rows_advance(1)
     weights_advance(1)
+    for unit in range(came):
+        engine.advance(unit, 3)
     small_advance(1)
     rows_advance(2)
     small_advance(2)

time: 294 us -> 290 us (0.986)
  Pallas kernels: 286 us -> 281 us
    pallas_call x1, Pallas kernels: 58.8 us -> 54 us  [finish_all(): pl.pallas_call(finish_kernel, in_specs=[vmem] + [anywhere] * 10 + [vmem]...]
  transfers between devices with their start and end apart: 1 -> 1, of which waited for: 0 -> 0; matrix products, arithmetic and copies ran while one was open for 0% -> 0% of each run, Pallas kernels for 32% -> 31%
where the time goes in v7:
time: 290 us; the launch traced here: 285 us
  Pallas kernels  281 us (97%)
    pallas_call x1, Pallas kernels, branch(): pl.pallas_call(functools.partial(branch_kernel, BLOCK, grid_of[0] if grid...  82.7 us
    pallas_call x1, Pallas kernels, finish_all(): pl.pallas_call(finish_kernel, in_specs=[vmem] + [anywhere] * 10 + [vmem]...  54 us
    pallas_call x1, Pallas kernels, slot_backward(): pl.pallas_call(functools.partial(slot_backward_kernel, grid_of is not Non...  33.5 us
    pallas_call x1, Pallas kernels, gather_project(): pl.pallas_call(gather_project_kernel, in_specs=[anywhere, vmem, anywhere,...  32.8 us
    pallas_call x1, Pallas kernels, local_backward(): pl.pallas_call(functools.partial(local_backward_kernel, talk, rows_count,...  31.6 us
    pallas_call x1, Pallas kernels, local_forward(): pl.pallas_call(functools.partial(local_forward_kernel, talk, rows_count,...  21.4 us
    pallas_call x1, Pallas kernels, slot_forward(): pl.pallas_call(functools.partial(slot_forward_kernel, rows_count, group_r...  18.4 us
    pallas_call x1, Pallas kernels, unpack(): pl.pallas_call(unpack_kernel, grid=(steps,), in_specs=[pl.BlockSpec((HALF...  6.56 us
  transfers between devices with their start and end apart: 1, of which 0 were waited for; matrix products, arithmetic and copies ran while one was open for 0% of the time, Pallas kernels for 31%

profile of v7, /device:TPU:0, one launch (start us, length us, event | category | flops | bytes accessed | tf_op | source)
XLA Modules:
  0.0 284.5 jit_solution(6119292204997135458)
XLA Ops:
  0.7 0.6 pad_add_fusion.place
  1.3 32.8 %gather_project.1 = (bf16[1024,768]{1,0:T(8,128)(2,1)}, bf16[1024,768]{1,0:T(8,128)(2,1)}, bf16[1024,768]{1,0:T(8,128)(2,1)}, bf16[1024,768]{1,0:T(8,128)(2,1)},...) custom-call(bf16[1024,768]{1,0:T(8,128)(2,1)} %bitcast.30, ...), custom_call_target="tpu_custom_call" | custom-call | flops 7247757312 | bytes 18874368 | tf_op jit(solution)/shard_map/gather_project/pallas_call | solution.py:561
  34.1 18.4 %slot_forward.1 = (bf16[768,1024]{1,0:T(8,128)(2,1)}, f32[6,2,8,1024]{3,2,1,0:T(8,128)}, bf16[8,6,128,128]{3,2,1,0:T(8,128)(2,1)}, f32[8,6,8,128]{3,2,1,0:T(8,128)}) custom-call(s32[2,8]{1,0:T(2,128)} %lengths.7, s32[2]{0:T(128)} %bucket_of.7, s32[3]{0:T(128)} %pad_add_fusion.place, bf16[1024,768]{1,0:T(8,128)(2,1)} %get-tuple-element.81.q_ref, ...), custom_call_target="tpu_custom_call" | custom-call | flops 3221225472 | bytes 15728640 | tf_op jit(solution)/shard_map/slot_forward/pallas_call | solution.py:827
  52.5 21.4 %local_forward.1 = (bf16[1024,768]{1,0:T(8,128)(2,1)}, f32[6,2,8,1024]{3,2,1,0:T(8,128)}, bf16[2,2,3,128,128]{4,3,2,1,0:T(8,128)(2,1)}, f32[2,2,3,8,128]{4,3,2,1,0:T(8,128)}) custom-call(s32[2,8]{1,0:T(2,128)} %lengths.7, s32[2]{0:T(128)} %bucket_of.7, s32[3]{0:T(128)} %pad_add_fusion.place, bf16[1024,768]{1,0:T(8,128)(2,1)} %get-tuple-element.81.q_ref, ...), custom_call_target="tpu_custom_call" | custom-call | flops 6442450944 | bytes 12582912 | tf_op jit(solution)/shard_map/local_forward/pallas_call | solution.py:1086
  74.0 82.7 %branch.1 = (bf16[1024,768]{1,0:T(8,128)(2,1)}, f32[1024,768]{1,0:T(8,128)}, bf16[1024,768]{1,0:T(8,128)(2,1)}, bf16[64,768]{1,0:T(8,128)(2,1)}, f32[64,768]{1,0...) custom-call(bf16[1024,768]{1,0:T(8,128)(2,1)} %get-tuple-element.80., ...), custom_call_target="tpu_custom_call" | custom-call | flops 36691771392 | bytes 33030144 | tf_op jit(solution)/shard_map/branch/pallas_call | solution.py:1588
  156.7 0.0 copy-start.1
  156.7 31.6 %local_backward.1 = (bf16[768,1024]{1,0:T(8,128)(2,1)}, bf16[1024,768]{1,0:T(8,128)(2,1)}, bf16[1024,768]{1,0:T(8,128)(2,1)}, f32[6,2,8,1024]{3,2,1,0:T(8,128)},...) custom-call(s32[2,8]{1,0:T(2,128)} %lengths.7, s32[2]{0:T(128)} %bucket_of.7, ...), custom_call_target="tpu_custom_call" | custom-call | flops 16106127360 | bytes 23592960 | tf_op jit(solution)/shard_map/local_backward/pallas_call | solution.py:1815
  188.3 0.0 copy-done.1
  188.3 1.2 collective-permute-start
  189.5 33.5 %slot_backward.1 = (bf16[1024,768]{1,0:T(8,128)(2,1)}, bf16[1024,768]{1,0:T(8,128)(2,1)}, bf16[1024,768]{1,0:T(8,128)(2,1)}, bf16[3,16,2,48,384]{4,3,2,1,0:T(8,1...) custom-call(s32[2,8]{1,0:T(2,128)} %lengths.7, s32[2]{0:T(128)} %bucket_of.7, s32[3]{0:T(128)} %pad_add_fusion.place, ...), custom_call_target="tpu_custom_call" | custom-call | flops 8053063680 | bytes 31457280 | tf_op jit(solution)/shard_map/slot_backward/pallas_call | solution.py:2110
  223.0 54.0 %finish_all.1 = (f32[288,384]{1,0:T(8,128)}, f32[16,768]{1,0:T(8,128)}, f32[64,768]{1,0:T(8,128)}, f32[768,768]{1,0:T(8,128)}, bf16[256,768]{1,0:T(8,128)(2,1)}) custom-call(bf16[3,2,2,2,48,384]{5,4,3,2,1,0:T(8,128)(2,1)} %get-tuple-element.105.rest_ref, bf16[1024,768]{1,0:T(8,128)(2,1)} %get-tuple-element.80.x_ref.x_in, ...), custom_call_target="tpu_custom_call" | custom-call | flops 7247757312 | bytes 23592960 | tf_op jit(solution)/shard_map/finish_all/pallas_call | solution.py:2492
  277.0 0.0 collective-permute-done.halo_z_ref
  277.0 0.0 copy-start
  277.0 0.7 copy-done
  277.7 6.6 %unpack.1 = (bf16[1,1024,768]{2,1,0:T(8,128)(2,1)}, bf16[1,64,768]{2,1,0:T(8,128)(2,1)}, f32[1,1024,768]{2,1,0:T(8,128)}, f32[1,64,768]{2,1,0:T(8,128)}, f32[48,...) custom-call(bf16[1024,768]{1,0:T(8,128)(2,1)} %get-tuple-element.95., ...), custom_call_target="tpu_custom_call" | custom-call | bytes 11010048 | tf_op jit(solution)/shard_map/unpack/pallas_call | solution.py:2658
Async XLA Ops:
  156.7 31.6 %copy-start.1 = (bf16[256,768]{1,0:T(8,128)(2,1)S(1)}, bf16[256,768]{1,0:T(8,128)(2,1)}, u32[]{:S(2)}) copy-start(bf16[256,768]{1,0:T(8,128)(2,1)} %get-tuple-element.104) | copy-start | bytes 1179652
  188.3 88.7 %collective-permute-start = (bf16[256,768]{1,0:T(8,128)(2,1)S(1)}, bf16[256,768]{1,0:T(8,128)(2,1)S(1)}, u32[]{:S(2)}, u32[]{:S(2)}) collective-permute-start(bf16[256,768]{1,0:T(8,128)(2,1)S(1)} %copy-done.1), channel_id=1, source_target_pairs={{0,15},{1,0},{2,1},{3,2},{4,3},{5,4},{6,5},{7,6},{8,7},{9,8},{10,9... | collective-permute-start | bytes 1179656 | tf_op jit(solution)/shard_map/ppermute | solution.py:2689
  277.0 0.7 copy-start

commit v8 on v7

--- a/solution.py
+++ b/solution.py
@@ -1005,7 +1005,7 @@
                 copy.start()
             slot_sum.begin(0)
 
-        @pl.when(step == 3)
+        @pl.when(step == 2)
         def _():
             for copy in own_copies:
                 copy.wait()

time: 290 us -> 290 us (level)
  no operation moved by 1% of the time
where the time goes in v8:
time: 290 us; the launch traced here: 284 us
  Pallas kernels  282 us (97%)
    pallas_call x1, Pallas kernels, branch(): pl.pallas_call(functools.partial(branch_kernel, BLOCK, grid_of[0] if grid...  83 us
    pallas_call x1, Pallas kernels, finish_all(): pl.pallas_call(finish_kernel, in_specs=[vmem] + [anywhere] * 10 + [vmem]...  54.2 us
    pallas_call x1, Pallas kernels, slot_backward(): pl.pallas_call(functools.partial(slot_backward_kernel, grid_of is not Non...  33.5 us
    pallas_call x1, Pallas kernels, gather_project(): pl.pallas_call(gather_project_kernel, in_specs=[anywhere, vmem, anywhere,...  32.8 us
    pallas_call x1, Pallas kernels, local_backward(): pl.pallas_call(functools.partial(local_backward_kernel, talk, rows_count,...  32.8 us
    pallas_call x1, Pallas kernels, local_forward(): pl.pallas_call(functools.partial(local_forward_kernel, talk, rows_count,...  20.3 us
    pallas_call x1, Pallas kernels, slot_forward(): pl.pallas_call(functools.partial(slot_forward_kernel, rows_count, group_r...  18.4 us
    pallas_call x1, Pallas kernels, unpack(): pl.pallas_call(unpack_kernel, grid=(steps,), in_specs=[pl.BlockSpec((HALF...  6.56 us
  transfers between devices with their start and end apart: 1, of which 0 were waited for; matrix products, arithmetic and copies ran while one was open for 0% of the time, Pallas kernels for 31%

profile of v8, /device:TPU:0, one launch (start us, length us, event | category | flops | bytes accessed | tf_op | source)
XLA Modules:
  0.0 284.4 jit_solution(16243975698995668389)
XLA Ops:
  0.7 0.6 pad_add_fusion.place
  1.3 32.8 %gather_project.1 = (bf16[1024,768]{1,0:T(8,128)(2,1)}, bf16[1024,768]{1,0:T(8,128)(2,1)}, bf16[1024,768]{1,0:T(8,128)(2,1)}, bf16[1024,768]{1,0:T(8,128)(2,1)},...) custom-call(bf16[1024,768]{1,0:T(8,128)(2,1)} %bitcast.30, ...), custom_call_target="tpu_custom_call" | custom-call | flops 7247757312 | bytes 18874368 | tf_op jit(solution)/shard_map/gather_project/pallas_call | solution.py:561
  34.1 18.4 %slot_forward.1 = (bf16[768,1024]{1,0:T(8,128)(2,1)}, f32[6,2,8,1024]{3,2,1,0:T(8,128)}, bf16[8,6,128,128]{3,2,1,0:T(8,128)(2,1)}, f32[8,6,8,128]{3,2,1,0:T(8,128)}) custom-call(s32[2,8]{1,0:T(2,128)} %lengths.7, s32[2]{0:T(128)} %bucket_of.7, s32[3]{0:T(128)} %pad_add_fusion.place, bf16[1024,768]{1,0:T(8,128)(2,1)} %get-tuple-element.81.q_ref, ...), custom_call_target="tpu_custom_call" | custom-call | flops 3221225472 | bytes 15728640 | tf_op jit(solution)/shard_map/slot_forward/pallas_call | solution.py:827
  52.5 20.3 %local_forward.1 = (bf16[1024,768]{1,0:T(8,128)(2,1)}, f32[6,2,8,1024]{3,2,1,0:T(8,128)}, bf16[2,2,3,128,128]{4,3,2,1,0:T(8,128)(2,1)}, f32[2,2,3,8,128]{4,3,2,1,0:T(8,128)}) custom-call(s32[2,8]{1,0:T(2,128)} %lengths.7, s32[2]{0:T(128)} %bucket_of.7, s32[3]{0:T(128)} %pad_add_fusion.place, bf16[1024,768]{1,0:T(8,128)(2,1)} %get-tuple-element.81.q_ref, ...), custom_call_target="tpu_custom_call" | custom-call | flops 6442450944 | bytes 12582912 | tf_op jit(solution)/shard_map/local_forward/pallas_call | solution.py:1086
  72.8 83.0 %branch.1 = (bf16[1024,768]{1,0:T(8,128)(2,1)}, f32[1024,768]{1,0:T(8,128)}, bf16[1024,768]{1,0:T(8,128)(2,1)}, bf16[64,768]{1,0:T(8,128)(2,1)}, f32[64,768]{1,0...) custom-call(bf16[1024,768]{1,0:T(8,128)(2,1)} %get-tuple-element.80., ...), custom_call_target="tpu_custom_call" | custom-call | flops 36691771392 | bytes 33030144 | tf_op jit(solution)/shard_map/branch/pallas_call | solution.py:1588
  155.8 0.0 copy-start.1
  155.8 32.8 %local_backward.1 = (bf16[768,1024]{1,0:T(8,128)(2,1)}, bf16[1024,768]{1,0:T(8,128)(2,1)}, bf16[1024,768]{1,0:T(8,128)(2,1)}, f32[6,2,8,1024]{3,2,1,0:T(8,128)},...) custom-call(s32[2,8]{1,0:T(2,128)} %lengths.7, s32[2]{0:T(128)} %bucket_of.7, ...), custom_call_target="tpu_custom_call" | custom-call | flops 16106127360 | bytes 23592960 | tf_op jit(solution)/shard_map/local_backward/pallas_call | solution.py:1815
  188.6 0.0 copy-done.1
  188.6 0.5 collective-permute-start
  189.1 33.5 %slot_backward.1 = (bf16[1024,768]{1,0:T(8,128)(2,1)}, bf16[1024,768]{1,0:T(8,128)(2,1)}, bf16[1024,768]{1,0:T(8,128)(2,1)}, bf16[3,16,2,48,384]{4,3,2,1,0:T(8,1...) custom-call(s32[2,8]{1,0:T(2,128)} %lengths.7, s32[2]{0:T(128)} %bucket_of.7, s32[3]{0:T(128)} %pad_add_fusion.place, ...), custom_call_target="tpu_custom_call" | custom-call | flops 8053063680 | bytes 31457280 | tf_op jit(solution)/shard_map/slot_backward/pallas_call | solution.py:2110
  222.6 54.2 %finish_all.1 = (f32[288,384]{1,0:T(8,128)}, f32[16,768]{1,0:T(8,128)}, f32[64,768]{1,0:T(8,128)}, f32[768,768]{1,0:T(8,128)}, bf16[256,768]{1,0:T(8,128)(2,1)}) custom-call(bf16[3,2,2,2,48,384]{5,4,3,2,1,0:T(8,128)(2,1)} %get-tuple-element.105.rest_ref, bf16[1024,768]{1,0:T(8,128)(2,1)} %get-tuple-element.80.x_ref.x_in, ...), custom_call_target="tpu_custom_call" | custom-call | flops 7247757312 | bytes 23592960 | tf_op jit(solution)/shard_map/finish_all/pallas_call | solution.py:2492
  276.9 0.0 collective-permute-done.halo_z_ref
  276.9 0.0 copy-start
  276.9 0.7 copy-done
  277.6 6.6 %unpack.1 = (bf16[1,1024,768]{2,1,0:T(8,128)(2,1)}, bf16[1,64,768]{2,1,0:T(8,128)(2,1)}, f32[1,1024,768]{2,1,0:T(8,128)}, f32[1,64,768]{2,1,0:T(8,128)}, f32[48,...) custom-call(bf16[1024,768]{1,0:T(8,128)(2,1)} %get-tuple-element.95., ...), custom_call_target="tpu_custom_call" | custom-call | bytes 11010048 | tf_op jit(solution)/shard_map/unpack/pallas_call | solution.py:2658
Async XLA Ops:
  155.8 32.8 %copy-start.1 = (bf16[256,768]{1,0:T(8,128)(2,1)S(1)}, bf16[256,768]{1,0:T(8,128)(2,1)}, u32[]{:S(2)}) copy-start(bf16[256,768]{1,0:T(8,128)(2,1)} %get-tuple-element.104) | copy-start | bytes 1179652
  188.6 88.2 %collective-permute-start = (bf16[256,768]{1,0:T(8,128)(2,1)S(1)}, bf16[256,768]{1,0:T(8,128)(2,1)S(1)}, u32[]{:S(2)}, u32[]{:S(2)}) collective-permute-start(bf16[256,768]{1,0:T(8,128)(2,1)S(1)} %copy-done.1), channel_id=1, source_target_pairs={{0,15},{1,0},{2,1},{3,2},{4,3},{5,4},{6,5},{7,6},{8,7},{9,8},{10,9... | collective-permute-start | bytes 1179656 | tf_op jit(solution)/shard_map/ppermute | solution.py:2689
  276.9 0.7 copy-start
